TPU v7x, 32 devices: a whole 2x2x4 slice. The times are simulated.
32 devices in a mesh: feat: 4 (over y, x), batch: 8 (over z, core).
Axes of the slice: x: 2, y: 2, z: 4, core: 2. Of those that a mesh axis runs over, the one named last changes fastest.
Arguments:
- store: bfloat16 [65536, 1024], P('batch', 'feat'), may hold values from -6 to 6
- input_owner: int32 [8, 6144, 1], P('batch'), may hold values from 0 to 7; in each aligned block of 6144 rows (0 to 6143, 6144 to 12287, ..., all dimensions but the last counted through in order) at most 1536 rows name the same one
- input_row: int32 [8, 6144], P('batch'), may hold values from 0 to 8191
- nbr_one: int32 [8, 3072, 15], P('batch'), may hold values from 0 to 6143
- deg_one: int32 [8, 3072], P('batch'), may hold values from 1 to 15
- nbr_two: int32 [8, 512, 10], P('batch', 'feat'), may hold values from 0 to 3071
- deg_two: int32 [8, 512], P('batch', 'feat'), may hold values from 1 to 10
- cotangent: bfloat16 [8, 512, 256], P('batch', 'feat'), may hold values from -0.09375 to 0.09375
- w1_self: bfloat16 [1024, 256], P('feat'), may hold values from -0.1875 to 0.1875
- w1_neigh: bfloat16 [1024, 256], P('feat'), may hold values from -0.1875 to 0.1875
- bias_one: float32 [256], replicated, may hold values from -3 to 3
- w2_self: bfloat16 [256, 256], replicated, may hold values from -0.375 to 0.375
- w2_neigh: bfloat16 [256, 256], replicated, may hold values from -0.375 to 0.375
- bias_two: float32 [256], replicated, may hold values from -3 to 3
Outputs:
- activations: bfloat16 [8, 512, 256], P('batch', 'feat')
- grad_w2_self: float32 [256, 256], replicated
- grad_w2_neigh: float32 [256, 256], replicated
- grad_w1_self: float32 [1024, 256], P('feat')
- grad_w1_neigh: float32 [1024, 256], P('feat')
Inputs may be any that keep to these rules, and one draw needn't show every extreme that they name: `input_owner`: in each group, no index of batch is named by more than 1536 input nodes, and one is named by exactly 1536.
All inputs are finite; a program needn't handle non-finite values.
Results may differ from a plain program's by a relative error of at most 0.006.
Values may be sent and summed in bfloat16 or wider, within the bound.
No kernel may reach another device: no remote copies, remote signals or barrier semaphores. Data moves between devices by JAX's collectives and lax.ppermute only.
A program may use at most 64 MiB of HBM per device.

v0:
```python
import math

import jax
import jax.numpy as jnp
from jax import lax
from jax.sharding import PartitionSpec as P


def silu_grad(values):
    sig = jax.nn.sigmoid(values)
    return sig * (1.0 + values * (1.0 - sig))


def mean_rows(table, index, counts):
    rows_all, fanout = index.shape
    block = math.gcd(rows_all, 512)

    def one_block(pieces):
        positions, numbers = pieces
        gathered = jnp.take(table, positions, axis=0)
        keep = (jnp.arange(fanout)[None, :] < numbers[:, None]).astype(table.dtype)
        total = jnp.einsum("rk,rkw->rw", keep, gathered, preferred_element_type=jnp.float32)
        return (total / numbers[:, None].astype(jnp.float32)).astype(jnp.bfloat16)

    result = lax.map(
        one_block,
        (index.reshape(rows_all // block, block, fanout), counts.reshape(rows_all // block, block)),
    )
    return result.reshape(rows_all, table.shape[1])


def contract_rows(left_side, right_side):
    return lax.dot_general(
        left_side, right_side, (((0,), (0,)), ((), ())), preferred_element_type=jnp.float32
    )


def contract_cols(left_side, right_side):
    return lax.dot_general(
        left_side, right_side, (((1,), (1,)), ((), ())), preferred_element_type=jnp.float32
    )


def local(
    store,
    input_owner,
    input_row,
    nbr_one,
    deg_one,
    nbr_two,
    deg_two,
    cotangent,
    w1_self,
    w1_neigh,
    bias_one,
    w2_self,
    w2_neigh,
    bias_two,
):
    batch_count = lax.axis_size("batch")
    feat_index = lax.axis_index("feat")
    owners = input_owner[0, :, 0]
    wanted = input_row[0]
    input_count = owners.shape[0]
    capacity = 2 * input_count // batch_count
    onehot = (owners[:, None] == jnp.arange(batch_count)[None, :]).astype(jnp.int32)
    before = jnp.cumsum(onehot, axis=0) - onehot
    slots = jnp.sum(before * onehot, axis=1)
    bucket = owners * capacity + slots
    requests = (
        jnp.zeros((batch_count * capacity,), jnp.int32)
        .at[bucket]
        .set(wanted)
        .reshape(batch_count, capacity)
    )
    received = lax.all_to_all(requests, "batch", split_axis=0, concat_axis=0, tiled=True)
    looked = jnp.take(store, received, axis=0)
    answered = lax.all_to_all(looked, "batch", split_axis=0, concat_axis=0, tiled=True)
    inputs = jnp.take(answered.reshape(batch_count * capacity, store.shape[1]), bucket, axis=0)
    layer_rows = nbr_one.shape[1]
    agg_one = mean_rows(inputs, nbr_one[0], deg_one[0])
    self_one = inputs[:layer_rows]
    z_share = (
        lax.psum_scatter(
            jnp.dot(self_one, w1_self, preferred_element_type=jnp.float32)
            + jnp.dot(agg_one, w1_neigh, preferred_element_type=jnp.float32),
            "feat",
            scatter_dimension=0,
            tiled=True,
        )
        + bias_one
    )
    hidden_share = jax.nn.silu(z_share).astype(jnp.bfloat16)
    hidden = lax.all_gather(hidden_share, "feat", axis=0, tiled=True)
    seed_rows = nbr_two.shape[1]
    hidden_width = hidden.shape[1]
    seed_start = feat_index * seed_rows
    self_two = lax.dynamic_slice_in_dim(hidden, seed_start, seed_rows, 0)
    agg_two = mean_rows(hidden, nbr_two[0], deg_two[0])
    z_two = (
        jnp.dot(self_two, w2_self, preferred_element_type=jnp.float32)
        + jnp.dot(agg_two, w2_neigh, preferred_element_type=jnp.float32)
        + bias_two
    )
    activations = jax.nn.silu(z_two).astype(jnp.bfloat16)[None]
    dz_two = (cotangent[0].astype(jnp.float32) * silu_grad(z_two)).astype(jnp.bfloat16)
    gw2_self = contract_rows(self_two, dz_two)
    gw2_neigh = contract_rows(agg_two, dz_two)
    back_self = contract_cols(dz_two, w2_self)
    count_two = deg_two[0]
    back_neigh = contract_cols(dz_two, w2_neigh) / count_two[:, None].astype(jnp.float32)
    fanout_two = nbr_two.shape[2]
    keep_two = (jnp.arange(fanout_two)[None, :] < count_two[:, None]).astype(jnp.float32)
    spread = (back_neigh[:, None, :] * keep_two[:, :, None]).reshape(
        seed_rows * fanout_two, hidden_width
    )
    partial_grad = jnp.zeros((layer_rows, hidden_width), jnp.float32)
    partial_grad = partial_grad.at[seed_start + jnp.arange(seed_rows)].add(back_self)
    partial_grad = partial_grad.at[nbr_two[0].reshape(-1)].add(spread)
    dh_share = lax.psum_scatter(partial_grad, "feat", scatter_dimension=0, tiled=True)
    dz_share = (dh_share * silu_grad(z_share)).astype(jnp.bfloat16)
    dz_one = lax.all_gather(dz_share, "feat", axis=0, tiled=True)
    gw1_self = contract_rows(self_one, dz_one)
    gw1_neigh = contract_rows(agg_one, dz_one)
    gw2_self, gw2_neigh = lax.psum((gw2_self, gw2_neigh), ("feat", "batch"))
    gw1_self, gw1_neigh = lax.psum((gw1_self, gw1_neigh), "batch")
    return (activations, gw2_self, gw2_neigh, gw1_self, gw1_neigh)


def solution(mesh):
    in_specs = (
        P("batch", "feat"),
        P("batch", None, None),
        P("batch", None),
        P("batch", None, None),
        P("batch", None),
        P("batch", "feat", None),
        P("batch", "feat"),
        P("batch", "feat", None),
        P("feat", None),
        P("feat", None),
        P(),
        P(),
        P(),
        P(),
    )
    out_specs = (P("batch", "feat", None), P(), P(), P("feat", None), P("feat", None))
    return jax.shard_map(local, mesh=mesh, in_specs=in_specs, out_specs=out_specs, check_vma=False)
```

profile of v0, /device:TPU:0, one launch (start us, length us, event | category | flops | bytes accessed | tf_op | source)
XLA Modules:
  0.0 911.7 jit_solution(1363740317771601559)
XLA Ops:
  12.6 23.2 %scatter_custom_fusion = s32[12288]{0:T(1024)S(1)} fusion(s32[6144]{0:T(1024)S(1)} %bitcast.122, s32[6144]{0:T(1024)} %bitcast.126, s32[]{:T(128)} %constant.77.clone.1), kind=kCustom, calls=%fused_computation.78 | custom fusion | bytes 49664 | tf_op jit(solution)/shard_map/scatter | solution.py:73
  35.8 12.0 %all_to_all.20 = s32[8,1,1536]{2,1,0:T(1,128)S(1)} all-to-all(s32[8,1,1536]{2,1,0:T(1,128)S(1)} %bitcast.120), channel_id=1, replica_groups=mesh['feat'=4,'batch'=8] {'batch'}, dimensions={0} | all-to-all | bytes 98304 | tf_op jit(solution)/shard_map/all_to_all | solution.py:76
  47.9 48.6 %gather_fusion.1 = bf16[12288,256]{1,0:T(8,128)(2,1)} fusion(bf16[8192,256]{1,0:T(8,128)(2,1)} %param.16, s32[12288]{0:T(1024)S(1)} %broadcast_clamp_fusion), kind=kCustom, calls=%fused_computation.1 | custom fusion | bytes 12632064 | tf_op jit(solution)/shard_map/jit(_take)/gather | solution.py:77
  96.5 7.6 broadcast_select_fusion
  112.0 135.9 %all-to-all-done.1 = bf16[8,1536,256]{2,1,0:T(8,128)(2,1)} async-done(((bf16[8,1536,256]{2,1,0:T(8,128)(2,1)}), bf16[8,1536,256]{2,1,0:T(8,128)(2,1)}, u32[]{:S(2)}, u32[]{:S(2)}) %all-to-all-start.1) | async-done | bytes 6291488 | tf_op jit(solution)/shard_map/all_to_all | solution.py:78
  247.9 27.0 %gather_fusion.2 = bf16[6144,256]{1,0:T(8,128)(2,1)} fusion(bf16[12288,256]{1,0:T(8,128)(2,1)} %bitcast.17, s32[6144]{0:T(1024)S(1)} %broadcast_clamp_fusion.1), kind=kCustom, calls=%fused_computation.2 | custom fusion | bytes 6316032 | tf_op jit(solution)/shard_map/jit(_take)/gather | solution.py:79
  279.6 230.9 %while.2 = (s32[]{:T(128)}, bf16[6,512,256]{2,1,0:T(8,128)(2,1)}, s32[6,512]{1,0:T(8,128)S(1)}, s32[6,512,15]{2,1,0:T(8,128)}, bf16[6144,256]{1,0:T(8,128)(2,1)S(1)}, /*index=5*/s32[]{:T(128)}) while((s32[]{:T(128)}, bf16[6,512,256]{2,1,0:T(8,128)(2,1)}, s32[6,512]{1,0:T(8,128)S(1)}, s32[6,512,15]{2,1,0:T(8,128)}, ...), condition=%wide.region_5.6_spmd, body=%wide.region_4.5_spmd.sunk | while | flops 6245890 | bytes 21262928 | solution.py:25
  282.2 22.1 %gather_fusion = bf16[7680,256]{1,0:T(8,128)(2,1)} fusion(bf16[6144,256]{1,0:T(8,128)(2,1)S(1)} %get-tuple-element.113, s32[8192]{0:T(1024)S(1)} %pad_clamp_fusion.3), kind=kCustom, calls=%fused_computation.clone.1 | custom fusion | bytes 7895040 | tf_op jit(solution)/shard_map/while/body/eval_jaxpr/jit(_take)/gather | solution.py:20
  320.7 22.1 %gather_fusion = bf16[7680,256]{1,0:T(8,128)(2,1)} fusion(bf16[6144,256]{1,0:T(8,128)(2,1)S(1)} %get-tuple-element.113, s32[8192]{0:T(1024)S(1)} %pad_clamp_fusion.3), kind=kCustom, calls=%fused_computation.clone.1 | custom fusion | bytes 7895040 | tf_op jit(solution)/shard_map/while/body/eval_jaxpr/jit(_take)/gather | solution.py:20
  342.7 6.8 reshape.365
  359.1 22.1 %gather_fusion = bf16[7680,256]{1,0:T(8,128)(2,1)} fusion(bf16[6144,256]{1,0:T(8,128)(2,1)S(1)} %get-tuple-element.113, s32[8192]{0:T(1024)S(1)} %pad_clamp_fusion.3), kind=kCustom, calls=%fused_computation.clone.1 | custom fusion | bytes 7895040 | tf_op jit(solution)/shard_map/while/body/eval_jaxpr/jit(_take)/gather | solution.py:20
  381.2 6.8 reshape.365
  397.6 22.1 %gather_fusion = bf16[7680,256]{1,0:T(8,128)(2,1)} fusion(bf16[6144,256]{1,0:T(8,128)(2,1)S(1)} %get-tuple-element.113, s32[8192]{0:T(1024)S(1)} %pad_clamp_fusion.3), kind=kCustom, calls=%fused_computation.clone.1 | custom fusion | bytes 7895040 | tf_op jit(solution)/shard_map/while/body/eval_jaxpr/jit(_take)/gather | solution.py:20
  419.7 6.8 reshape.365
  436.1 22.1 %gather_fusion = bf16[7680,256]{1,0:T(8,128)(2,1)} fusion(bf16[6144,256]{1,0:T(8,128)(2,1)S(1)} %get-tuple-element.113, s32[8192]{0:T(1024)S(1)} %pad_clamp_fusion.3), kind=kCustom, calls=%fused_computation.clone.1 | custom fusion | bytes 7895040 | tf_op jit(solution)/shard_map/while/body/eval_jaxpr/jit(_take)/gather | solution.py:20
  458.2 6.8 reshape.365
  474.6 22.1 %gather_fusion = bf16[7680,256]{1,0:T(8,128)(2,1)} fusion(bf16[6144,256]{1,0:T(8,128)(2,1)S(1)} %get-tuple-element.113, s32[8192]{0:T(1024)S(1)} %pad_clamp_fusion.3), kind=kCustom, calls=%fused_computation.clone.1 | custom fusion | bytes 7895040 | tf_op jit(solution)/shard_map/while/body/eval_jaxpr/jit(_take)/gather | solution.py:20
  515.1 42.9 %reduce-scatter.3.cloned.1.call-done = f32[768,256]{1,0:T(8,128)} async-done(((f32[3072,256]{1,0:T(8,128)}), f32[768,256]{1,0:T(8,128)}) %reduce-scatter.3.cloned.1.call-update) | async-done | bytes 786448 | tf_op jit(solution)/shard_map/reduce_scatter | solution.py:84
  561.4 29.9 %all-gather.3.cloned.1.call-done = bf16[3072,256]{1,0:T(8,128)(2,1)} async-done(((bf16[768,256]{1,0:T(8,128)(2,1)}), bf16[3072,256]{1,0:T(8,128)(2,1)}) %all-gather.3.cloned.1.call-update) | async-done | bytes 1572880 | tf_op jit(solution)/shard_map/all_gather | solution.py:94
  612.2 16.0 %scatter_custom_fusion.2 = f32[3072,256]{1,0:T(8,128)} fusion(f32[3072,256]{1,0:T(8,128)} %scatter_custom_fusion.1, s32[1280]{0:T(1024)S(1)} %fusion.38, f32[1280,256]{1,0:T(8,128)} %mul.83, f32[1280]{0:T(1024)S(1)} %reshape.277), kind=kCustom, calls=%fused_computation.32 | custom fusion | flops 655360 | bytes 4464640 | tf_op jit(solution)/shard_map/scatter-add | solution.py:119
  628.4 44.1 %reduce-scatter.5.cloned.1.call-done = f32[768,256]{1,0:T(8,128)} async-done(((f32[3072,256]{1,0:T(8,128)}), f32[768,256]{1,0:T(8,128)}) %reduce-scatter.5.cloned.1.call-update) | async-done | bytes 786448 | tf_op jit(solution)/shard_map/reduce_scatter | solution.py:120
  677.7 28.2 %all-gather.5.cloned.1.call-done = bf16[3072,256]{1,0:T(8,128)(2,1)} async-done(((bf16[768,256]{1,0:T(8,128)(2,1)}), bf16[3072,256]{1,0:T(8,128)(2,1)}) %all-gather.5.cloned.1.call-update) | async-done | bytes 1572880 | tf_op jit(solution)/shard_map/all_gather | solution.py:122
  711.5 128.4 %all-reduce.5.cloned.1.call-done = (f32[256,256]{1,0:T(8,128)}, f32[256,256]{1,0:T(8,128)}) async-done(((f32[256,256]{1,0:T(8,128)}, f32[256,256]{1,0:T(8,128)}), (f32[256,256]{1,0:T(8,128)}, f32[256,256]{1,0:T(8,128)})) %all-reduce.5.cloned.1.call-update) | async-done | bytes 524304 | tf_op jit(solution)/shard_map/psum | solution.py:125
  839.9 58.2 %all-reduce.7.cloned.1.call-done = (f32[256,256]{1,0:T(8,128)}, f32[256,256]{1,0:T(8,128)}) async-done(((f32[256,256]{1,0:T(8,128)}, f32[256,256]{1,0:T(8,128)}), (f32[256,256]{1,0:T(8,128)}, f32[256,256]{1,0:T(8,128)})) %all-reduce.7.cloned.1.call-update) | async-done | bytes 524304 | tf_op jit(solution)/shard_map/psum | solution.py:126
  (150 shorter events, 135.7 us)
Async XLA Ops:
  7.2 503.3 %copy-start = (bf16[256,256]{1,0:T(8,128)(2,1)S(1)}, bf16[256,256]{1,0:T(8,128)(2,1)}, u32[]{:S(2)}) copy-start(bf16[256,256]{1,0:T(8,128)(2,1)} %param.24) | copy-start | bytes 393220
  104.1 5.0 copy-start.4
  104.1 7.2 copy-start.7
  104.1 7.9 copy-start.3
  104.1 143.8 %all-to-all-start.1 = ((bf16[8,1536,256]{2,1,0:T(8,128)(2,1)}), bf16[8,1536,256]{2,1,0:T(8,128)(2,1)}, u32[]{:S(2)}, u32[]{:S(2)}) async-start(bf16[8,1536,256]{2,1,0:T(8,128)(2,1)} %broadcast_select_fusion), calls=%async_computation.1 | async-start | bytes 12582912 | tf_op jit(solution)/shard_map/all_to_all | solution.py:78
  109.0 449.1 %reduce-scatter.3.cloned.1.call-start = ((), (), s32[]{:S(2)}) async-start(), calls=%async_computation.4 | async-start | bytes 3932160 | tf_op jit(solution)/shard_map/reduce_scatter | solution.py:84
  510.5 0.9 copy-start.5
  515.0 43.0 %copy-start.8 = (f32[256]{0:T(256)S(1)}, f32[256]{0:T(256)}, u32[]{:S(2)}) copy-start(f32[256]{0:T(256)} %param.26) | copy-start | bytes 3076
  515.1 45.4 %copy-start.6 = (s32[1,128,10]{1,0,2:T(1,128)S(1)}, s32[1,128,10]{1,0,2:T(1,128)}, u32[]{:S(2)}) copy-start(s32[1,128,10]{1,0,2:T(1,128)} %param.21) | copy-start | bytes 15364
  515.1 45.9 %copy-start.9 = (s32[1,128]{1,0:T(1,128)S(1)}, s32[1,128]{1,0:T(1,128)}, u32[]{:S(2)}) copy-start(s32[1,128]{1,0:T(1,128)} %param.22) | copy-start | bytes 1540
  515.1 76.2 %all-gather.3.cloned.1.call-start = ((), (), s32[]{:S(2)}) async-start(), calls=%async_computation.5 | async-start | bytes 1966080 | tf_op jit(solution)/shard_map/all_gather | solution.py:94
  560.2 112.2 %reduce-scatter.5.cloned.1.call-start = ((), (), s32[]{:S(2)}) async-start(), calls=%async_computation.6 | async-start | bytes 3932160 | tf_op jit(solution)/shard_map/reduce_scatter | solution.py:120
  596.9 3.9 copy-start.2
  596.9 5.0 copy-start.11
  599.0 4.6 copy-start.10
  600.8 2.9 copy-start.12
  628.3 48.4 %copy-start.13 = (f32[128,1,256]{2,1,0:T(1,128)S(1)}, f32[128,1,256]{2,1,0:T(1,128)}, u32[]{:S(2)}) copy-start(f32[128,1,256]{2,1,0:T(1,128)} %copy-done.12) | copy-start | bytes 393220
  628.3 77.7 %all-gather.5.cloned.1.call-start = ((), (), s32[]{:S(2)}) async-start(), calls=%async_computation.7 | async-start | bytes 1966080 | tf_op jit(solution)/shard_map/all_gather | solution.py:122
  674.9 165.1 %all-reduce.5.cloned.1.call-start = ((), (), s32[]{:S(2)}) async-start(), calls=%async_computation.8 | async-start | bytes 1048576 | tf_op jit(solution)/shard_map/psum | solution.py:125
  677.7 220.5 %all-reduce.7.cloned.1.call-start = ((), (), s32[]{:S(2)}) async-start(), calls=%async_computation.9 | async-start | bytes 1048576 | tf_op jit(solution)/shard_map/psum | solution.py:126
  706.0 2.8 copy-start.1
Sparse Core Ops, SparseCore 0:
  515.2 42.8 reduce-scatter.2
  560.3 30.9 all-gather.2
  628.4 43.9 reduce-scatter.4
  675.0 30.9 all-gather.4
  711.9 128.0 all-reduce.4
  842.9 55.2 all-reduce.6
where the time goes:
time: 915 us; the launch traced here: 912 us
  waiting for transfers between devices  468 us (51%)
  local copies, waits for them, and re-layouts  299 us (33%)
  other arithmetic  64.9 us (7%)
  matrix products  48.3 us (5%)
  between operations  14.4 us (2%)
  blocking collectives  12 us (1%)
    gather x14, local copies, waits for them, and re-layouts, one_block(): gathered = jnp.take(table, positions, axis=0)  181 us
    all_to_all x1, waiting for transfers between devices, local(): lax.all_to_all(looked, 'batch', split_axis=0, concat_axis=0, tiled=True)  136 us
    psum x1, waiting for transfers between devices, local(): gw2_self, gw2_neigh = lax.psum((gw2_self, gw2_neigh), ('feat', 'batch'))  128 us
    psum x1, waiting for transfers between devices, local(): gw1_self, gw1_neigh = lax.psum((gw1_self, gw1_neigh), 'batch')  58.2 us
    gather x1, local copies, waits for them, and re-layouts, local(): looked = jnp.take(store, received, axis=0)  48.6 us
    reduce_scatter x1, waiting for transfers between devices, local(): lax.psum_scatter(partial_grad, 'feat', scatter_dimension=0, tiled=True)  44.1 us
    reduce_scatter x1, waiting for transfers between devices, local(): lax.psum_scatter(jnp.dot(self_one, w1_self, preferred_element_type=jnp.fl...  42.9 us
    dot_general x7, matrix products, one_block(): jnp.einsum('rk,rkw->rw', keep, gathered, preferred_element_type=jnp.float32)  31.9 us
  transfers between devices with their start and end apart: 7, of which 7 were waited for; matrix products, arithmetic and copies ran while one was open for 1% of the time, Pallas kernels for 0%

commit v1 on v0

v1 whole, which is shorter than its diff:
```python
import functools

import jax
import jax.numpy as jnp
from jax import lax
from jax.experimental import pallas as pl
from jax.experimental.pallas import tpu as pltpu
from jax.sharding import PartitionSpec as P

TILE = 256
LANES = 128
SLOTS = 16
TILE_BITS, LANE_BITS, SLOT_BITS = 8, 7, 4
VMEM_BYTES = 56 * 1024 * 1024
VMEM = pl.BlockSpec(memory_space=pltpu.VMEM)
SMEM = pl.BlockSpec(memory_space=pltpu.SMEM)


def silu_grad(values):
    sig = jax.nn.sigmoid(values)
    return sig * (1.0 + values * (1.0 - sig))


def contract_rows(left_side, right_side):
    return lax.dot_general(
        left_side, right_side, (((0,), (0,)), ((), ())), preferred_element_type=jnp.float32
    )


def contract_cols(left_side, right_side):
    return lax.dot_general(
        left_side, right_side, (((1,), (1,)), ((), ())), preferred_element_type=jnp.float32
    )


def params(**more):
    return pltpu.CompilerParams(vmem_limit_bytes=VMEM_BYTES, **more)


def cost(flops, moved):
    return pl.CostEstimate(flops=int(flops), bytes_accessed=int(moved), transcendentals=0)


def requests_body(batch_count, capacity, owner_ref, row_ref, slot_ref, count_ref, request_ref):
    blocks, width = owner_ref.shape
    places = request_ref.shape[0]
    owner_id = lax.broadcasted_iota(jnp.int32, (batch_count, width), 0)
    earlier = lax.broadcasted_iota(jnp.int32, (width, width), 0)
    later = lax.broadcasted_iota(jnp.int32, (width, width), 1)
    upper = jnp.where(earlier <= later, 1.0, 0.0).astype(jnp.bfloat16)
    high_id = lax.broadcasted_iota(jnp.int32, (places, width), 0)
    low_id = lax.broadcasted_iota(jnp.int32, (LANES, width), 0)
    marks = [
        jnp.where(owner_ref[b : b + 1, :] == owner_id, 1.0, 0.0) for b in range(blocks)
    ]
    stacked = jnp.concatenate(marks, axis=0).astype(jnp.bfloat16)
    prefix = jnp.dot(stacked, upper, preferred_element_type=jnp.float32)
    running = jnp.zeros((batch_count, 1), jnp.float32)
    total = jnp.zeros((2 * places, LANES), jnp.float32)
    for b in range(blocks):
        part = prefix[b * batch_count : (b + 1) * batch_count]
        slots = jnp.sum(marks[b] * (part + running - 1.0), axis=0, keepdims=True)
        slots = slots.astype(jnp.int32)
        slot_ref[b : b + 1, :] = slots
        running = running + part[:, width - 1 : width]
        bucket = owner_ref[b : b + 1, :] * capacity + slots
        rows = row_ref[b : b + 1, :]
        hit = (bucket >> LANE_BITS) == high_id
        left = jnp.concatenate(
            [
                jnp.where(hit, (rows >> TILE_BITS).astype(jnp.float32), 0.0),
                jnp.where(hit, (rows & (TILE - 1)).astype(jnp.float32), 0.0),
            ],
            axis=0,
        ).astype(jnp.bfloat16)
        right = jnp.where((bucket & (LANES - 1)) == low_id, 1.0, 0.0).astype(jnp.bfloat16)
        total = total + contract_cols(left, right)
    count_ref[...] = jnp.broadcast_to(running, count_ref.shape).astype(jnp.int32)
    request_ref[...] = (total[:places] * TILE + total[places:]).astype(jnp.int32)


def make_requests(batch_count, capacity, owners, wanted):
    total = owners.shape[0]
    blocks = total // TILE
    places = batch_count * capacity // LANES
    return pl.pallas_call(
        functools.partial(requests_body, batch_count, capacity),
        out_shape=(
            jax.ShapeDtypeStruct((blocks, TILE), jnp.int32),
            jax.ShapeDtypeStruct((batch_count, LANES), jnp.int32),
            jax.ShapeDtypeStruct((places, LANES), jnp.int32),
        ),
        in_specs=[VMEM, VMEM],
        out_specs=(VMEM, VMEM, VMEM),
        compiler_params=params(),
        cost_estimate=cost(4 * total * places * LANES, 24 * total),
        name="requests",
    )(owners.reshape(blocks, TILE), wanted.reshape(blocks, TILE))


def lookup_body(first, width, want_ref, store_ref, out_ref, table, lines):
    group = pl.program_id(0)
    rows_all = store_ref.shape[0]

    @pl.when(group == 0)
    def _():
        @pl.loop(0, rows_all // TILE)
        def _(j):
            part = pl.ds(pl.multiple_of(j * TILE, TILE), TILE)
            table[part, :] = store_ref[part, :].astype(jnp.float32)

    @pl.loop(0, width // SLOTS)
    def _(j):
        for u in range(SLOTS):
            at = j * SLOTS + u
            lines[pl.ds(at, 1), :] = table[pl.ds(want_ref[group, first + at], 1), :]

    out_ref[0] = lines[...].astype(jnp.bfloat16)


def lookup(store, received, first, width):
    groups = received.shape[0]
    rows_all, features = store.shape
    return pl.pallas_call(
        functools.partial(lookup_body, first, width),
        out_shape=jax.ShapeDtypeStruct((groups, width, features), jnp.bfloat16),
        grid=(groups,),
        in_specs=[SMEM, pl.BlockSpec((rows_all, features), lambda g: (0, 0))],
        out_specs=pl.BlockSpec((1, width, features), lambda g: (g, 0, 0)),
        scratch_shapes=[
            pltpu.VMEM((rows_all, features), jnp.float32),
            pltpu.VMEM((width, features), jnp.float32),
        ],
        compiler_params=params(),
        cost_estimate=cost(groups * width * features * 40, 2 * rows_all * features),
        name="lookup",
    )(received, store)


def adjacency_body(tiles, near_ref, table_ref, out_ref):
    groups = near_ref.shape[0]
    node_high = lax.broadcasted_iota(jnp.int32, (LANES, TILE), 0)
    own_row = (
        lax.shift_right_logical(lax.broadcasted_iota(jnp.int32, (SLOTS, TILE), 1), SLOT_BITS)
        == lax.broadcasted_iota(jnp.int32, (SLOTS, TILE), 0)
    )
    low_id = lax.broadcasted_iota(jnp.int32, (TILE, TILE), 0).astype(jnp.float32)

    def one_group(g):
        near = near_ref[pl.ds(g, 1), :]
        pick = jnp.where((near >> LANE_BITS) == node_high, 1.0, 0.0).astype(jnp.bfloat16)
        found = jnp.dot(table_ref[...], pick, preferred_element_type=jnp.float32)
        here = (near & (LANES - 1)) == node_high
        high = jnp.sum(jnp.where(here, found[:LANES], 0.0), axis=0, keepdims=True)
        low = jnp.sum(jnp.where(here, found[LANES:], 0.0), axis=0, keepdims=True)
        high = jnp.where(near < 0, -1.0, high)
        rows = jnp.where(own_row, high, -1.0)
        left = jnp.concatenate(
            [jnp.where(rows == float(t), 1.0, 0.0) for t in range(tiles)], axis=0
        ).astype(jnp.bfloat16)
        right = jnp.where(low == low_id, 1.0, 0.0).astype(jnp.bfloat16)
        return contract_cols(left, right).reshape(tiles, SLOTS, TILE)

    @pl.loop(0, groups // 2)
    def _(j):
        pair = jnp.concatenate([one_group(2 * j), one_group(2 * j + 1)], axis=1)
        out_ref[:, pl.ds(pl.multiple_of(j * 2 * SLOTS, 2 * SLOTS), 2 * SLOTS), :] = pair.astype(
            out_ref.dtype
        )


def adjacency(near, table, tiles):
    groups = near.shape[0]
    nodes = groups * SLOTS
    step = TILE // SLOTS
    return pl.pallas_call(
        functools.partial(adjacency_body, tiles),
        out_shape=jax.ShapeDtypeStruct((tiles, nodes, TILE), jnp.float8_e4m3fn),
        grid=(groups // step,),
        in_specs=[
            pl.BlockSpec((step, TILE), lambda r: (r, 0)),
            pl.BlockSpec(table.shape, lambda r: (0, 0)),
        ],
        out_specs=pl.BlockSpec((tiles, TILE, TILE), lambda r: (0, r, 0)),
        compiler_params=params(),
        cost_estimate=cost(2 * nodes * TILE * TILE * tiles * 2, nodes * TILE * tiles),
        name="adjacency",
    )(near, table)


def collect(piece, counts_ref, starts_ref, answer_ref, packed):
    batch_count = answer_ref.shape[0]

    @pl.loop(0, batch_count)
    def _(o):
        base = starts_ref[o]

        @pl.loop(0, pl.cdiv(counts_ref[o], piece))
        def _(c):
            source = pl.ds(pl.multiple_of(c * piece, piece), piece)
            target = pl.ds(pl.multiple_of(base + c * piece, SLOTS), piece)
            packed[target, :] = answer_ref[o, source, :]

    end = starts_ref[batch_count]
    packed[pl.ds(pl.multiple_of(end, SLOTS), TILE), :] = jnp.zeros(
        (TILE, packed.shape[1]), packed.dtype
    )


def gather_sum_body(
    piece, last, spans_ref, counts_ref, starts_ref, answer_ref, column_ref, adj_ref, *refs
):
    if last:
        (total_in, own_in, deg_ref, wself_ref, wneigh_ref, own_ref, mean_ref, share_ref) = refs[:8]
        packed, tiles_ref, ready, total_ref = refs[8:]
    else:
        total_ref, own_ref, packed, tiles_ref, ready = refs
    nodes = own_ref.shape[0]
    begin, count = spans_ref[0], spans_ref[1]

    def fetch(step, slot):
        return pltpu.make_async_copy(adj_ref.at[begin + step], tiles_ref.at[slot], ready.at[slot])

    fetch(0, 0).start()
    collect(piece, counts_ref, starts_ref, answer_ref, packed)

    @pl.loop(0, nodes // TILE)
    def _(r):
        part = pl.ds(pl.multiple_of(r * TILE, TILE), TILE)
        if last:
            total_ref[part, :] = total_in[part, :]
            own_ref[part, :] = own_in[part, :]
        else:
            total_ref[part, :] = jnp.zeros((TILE, total_ref.shape[1]), jnp.float32)
            own_ref[part, :] = jnp.zeros((TILE, own_ref.shape[1]), jnp.bfloat16)

    @pl.loop(0, count)
    def _(step):
        slot = step & 1

        @pl.when(step + 1 < count)
        def _():
            fetch(step + 1, 1 - slot).start()

        fetch(step, slot).wait()
        block = packed[pl.ds(pl.multiple_of(step * TILE, TILE), TILE), :]
        lane = lax.broadcasted_iota(jnp.int32, (TILE, TILE), 1) + (begin + step) * TILE

        @pl.loop(0, nodes // TILE)
        def _(r):
            part = pl.ds(pl.multiple_of(r * TILE, TILE), TILE)
            near = tiles_ref[slot, part, :].astype(jnp.bfloat16)
            total_ref[part, :] += jnp.dot(near, block, preferred_element_type=jnp.float32)
            own = jnp.where(column_ref[part, :] == lane, 1.0, 0.0).astype(jnp.bfloat16)
            found = jnp.dot(own, block, preferred_element_type=jnp.float32)
            own_ref[part, :] = (own_ref[part, :].astype(jnp.float32) + found).astype(jnp.bfloat16)

    if last:

        @pl.loop(0, nodes // TILE)
        def _(r):
            part = pl.ds(pl.multiple_of(r * TILE, TILE), TILE)
            mean = (total_ref[part, :] / deg_ref[part, :]).astype(jnp.bfloat16)
            mean_ref[part, :] = mean
            share_ref[part, :] = (
                jnp.dot(own_ref[part, :], wself_ref[...], preferred_element_type=jnp.float32)
                + jnp.dot(mean, wneigh_ref[...], preferred_element_type=jnp.float32)
            ).astype(share_ref.dtype)


def gather_sum(spans, counts, starts, answer, column, adj, rest, share_type=jnp.bfloat16):
    batch_count, width, features = answer.shape
    tiles, nodes, _ = adj.shape
    piece = LANES if width % LANES == 0 else SLOTS
    last = rest is not None
    room = (min(batch_count * width, 2 * nodes) + SLOTS * batch_count + 3 * TILE) // TILE * TILE
    in_specs = [SMEM, SMEM, SMEM, VMEM, VMEM, pl.BlockSpec(memory_space=pl.ANY)]
    rows = lambda dtype: jax.ShapeDtypeStruct((nodes, features), dtype)
    scratch = [
        pltpu.VMEM((room, features), jnp.bfloat16),
        pltpu.VMEM((2, nodes, TILE), adj.dtype),
        pltpu.SemaphoreType.DMA((2,)),
    ]
    operands = [answer, column, adj]
    if last:
        operands += list(rest)
        in_specs += [VMEM] * len(rest)
        out_shape = (
            rows(jnp.bfloat16),
            rows(jnp.bfloat16),
            jax.ShapeDtypeStruct((nodes, rest[3].shape[1]), share_type),
        )
        scratch += [pltpu.VMEM((nodes, features), jnp.float32)]
    else:
        out_shape = (rows(jnp.float32), rows(jnp.bfloat16))
    return pl.pallas_call(
        functools.partial(gather_sum_body, piece, last),
        out_shape=out_shape,
        in_specs=in_specs,
        out_specs=(VMEM,) * len(out_shape),
        scratch_shapes=scratch,
        compiler_params=params(),
        cost_estimate=cost(2 * nodes * features * TILE * tiles, nodes * TILE * tiles // 2),
        name="gather_sum",
    )(spans, counts, starts, *operands)


def share_order(array, parts, seeds):
    others = array.shape[0] - seeds
    own, rest = seeds // parts, others // parts
    tail = array.shape[1:]
    return jnp.concatenate(
        [array[:seeds].reshape(parts, own, *tail), array[seeds:].reshape(parts, rest, *tail)],
        axis=1,
    ).reshape(array.shape)


def spread(part, axis, count):
    return lax.all_to_all(
        jnp.broadcast_to(part[None], (count,) + part.shape), axis, 0, 0, tiled=True
    )


def local(
    store,
    input_owner,
    input_row,
    nbr_one,
    deg_one,
    nbr_two,
    deg_two,
    cotangent,
    w1_self,
    w1_neigh,
    bias_one,
    w2_self,
    w2_neigh,
    bias_two,
):
    batch_count = lax.axis_size("batch")
    parts = lax.axis_size("feat")
    feat_index = lax.axis_index("feat")
    input_count = input_owner.shape[1]
    capacity = 2 * input_count // batch_count
    nodes = nbr_one.shape[1]
    seed_rows = nbr_two.shape[1]
    seeds = seed_rows * parts
    share = nodes // parts
    hidden_width = w1_self.shape[1]

    owners = input_owner[0, :, 0]
    slots, counts, requests = make_requests(batch_count, capacity, owners, input_row[0])
    received = lax.all_to_all(
        requests.reshape(batch_count, capacity), "batch", split_axis=0, concat_axis=0, tiled=True
    )
    first = capacity // 2
    looked = lookup(store, received, 0, first)
    answer_a = lax.all_to_all(looked, "batch", split_axis=0, concat_axis=0, tiled=True)
    looked = lookup(store, received, first, capacity - first)
    looked, answer_a = lax.optimization_barrier((looked, answer_a))
    answer_b = lax.all_to_all(looked, "batch", split_axis=0, concat_axis=0, tiled=True)

    tiles = -(-(input_count + 2 * (SLOTS - 1) * batch_count + TILE - 1) // TILE)
    tally = counts[:, 0]
    tally_a = jnp.minimum(tally, first)
    tally_b = tally - tally_a
    padded = lambda n: (n + SLOTS - 1) // SLOTS * SLOTS
    ends = lambda n: jnp.concatenate([jnp.zeros((1,), jnp.int32), jnp.cumsum(padded(n))])
    starts_a, starts_b = ends(tally_a), ends(tally_b)
    tiles_a = (starts_a[batch_count] + TILE - 1) // TILE
    tiles_b = (starts_b[batch_count] + TILE - 1) // TILE
    spans_a = jnp.stack([jnp.zeros_like(tiles_a), jnp.maximum(tiles_a, 1)])
    spans_b = jnp.stack([tiles_a, jnp.maximum(tiles_b, 1)])
    slot = slots.reshape(1, input_count)
    shifted = jnp.where(
        slot < first,
        slot + starts_a[:batch_count, None],
        slot - first + tiles_a * TILE + starts_b[:batch_count, None],
    )
    mine = owners[None, :] == jnp.arange(batch_count)[:, None]
    column = jnp.sum(jnp.where(mine, shifted, 0), axis=0)
    grid = jnp.pad(column.reshape(-1, LANES), ((0, LANES - input_count // LANES), (0, 0))).T
    table = jnp.concatenate([grid // TILE, grid % TILE], axis=0).astype(jnp.bfloat16)
    own_column = share_order(column[:nodes], parts, seeds).reshape(nodes, 1)

    fanout = nbr_one.shape[2]
    used = jnp.arange(fanout)[None, :] < deg_one[0][:, None]
    near = share_order(jnp.where(used, nbr_one[0], -1), parts, seeds)
    near = jnp.pad(near, ((0, 0), (0, SLOTS - fanout)), constant_values=-1)
    adj = adjacency(near.reshape(nodes // SLOTS, TILE), table, tiles)
    deg_first = share_order(deg_one[0], parts, seeds).astype(jnp.float32).reshape(nodes, 1)

    fanout_two = nbr_two.shape[2]
    used_two = jnp.arange(fanout_two)[None, :] < deg_two[0][:, None]
    near_two = lax.all_gather(jnp.where(used_two, nbr_two[0], -1), "feat", axis=0, tiled=True)
    deg_all = lax.all_gather(deg_two[0], "feat", axis=0, tiled=True)
    rest = share - seed_rows
    after = near_two - seeds
    place = jnp.where(
        near_two < seeds,
        near_two // seed_rows * share + near_two % seed_rows,
        after // rest * share + seed_rows + after % rest,
    )
    place = jnp.where(near_two < 0, -1, place - feat_index * share)
    adj_two = jnp.sum(
        place[:, :, None] == jnp.arange(share)[None, None, :], axis=1, dtype=jnp.float32
    ).astype(jnp.bfloat16)

    total, own = gather_sum(spans_a, tally_a, starts_a, answer_a, own_column, adj, None)
    self_one, agg_one, z_part = gather_sum(
        spans_b,
        tally_b,
        starts_b,
        answer_b,
        own_column,
        adj,
        (total, own, deg_first, w1_self, w1_neigh),
    )
    z_parts = lax.all_to_all(z_part.reshape(parts, share, hidden_width), "feat", 0, 0, tiled=True)
    z_share = jnp.sum(z_parts.astype(jnp.float32), axis=0) + bias_one
    hidden = jax.nn.silu(z_share).astype(jnp.bfloat16)

    agg_parts = jnp.dot(adj_two, hidden, preferred_element_type=jnp.float32)
    agg_parts = lax.all_to_all(
        agg_parts.reshape(parts, seed_rows, hidden_width), "feat", 0, 0, tiled=True
    )
    deg_second = deg_two[0].astype(jnp.float32)[:, None]
    agg_two = (jnp.sum(agg_parts, axis=0) / deg_second).astype(jnp.bfloat16)
    self_two = hidden[:seed_rows]
    z_two = (
        jnp.dot(self_two, w2_self, preferred_element_type=jnp.float32)
        + jnp.dot(agg_two, w2_neigh, preferred_element_type=jnp.float32)
        + bias_two
    )
    activations = jax.nn.silu(z_two).astype(jnp.bfloat16)[None]
    dz_two = (cotangent[0].astype(jnp.float32) * silu_grad(z_two)).astype(jnp.bfloat16)
    dz_two_all = spread(dz_two, "feat", parts).reshape(seeds, hidden_width)
    gw2 = jnp.concatenate([contract_rows(self_two, dz_two), contract_rows(agg_two, dz_two)])
    gw2 = lax.psum(gw2, ("feat", "batch"))

    back = contract_cols(dz_two_all, w2_neigh) / deg_all.astype(jnp.float32)[:, None]
    back_high = back.astype(jnp.bfloat16)
    back_low = (back - back_high.astype(jnp.float32)).astype(jnp.bfloat16)
    dh_share = contract_rows(adj_two, back_high) + contract_rows(adj_two, back_low)
    dh_share = dh_share + jnp.pad(contract_cols(dz_two, w2_self), ((0, rest), (0, 0)))
    dz_share = (dh_share * silu_grad(z_share)).astype(jnp.bfloat16)
    dz_one = spread(dz_share, "feat", parts).reshape(nodes, hidden_width)
    gw1 = jnp.concatenate([contract_rows(self_one, dz_one), contract_rows(agg_one, dz_one)])
    width = gw1.shape[0] // batch_count
    gw1 = lax.all_to_all(gw1.reshape(batch_count, width, hidden_width), "batch", 0, 0, tiled=True)
    gw1 = spread(jnp.sum(gw1, axis=0), "batch", batch_count).reshape(-1, hidden_width)
    half1, half2 = gw1.shape[0] // 2, gw2.shape[0] // 2
    return (activations, gw2[:half2], gw2[half2:], gw1[:half1], gw1[half1:])


def solution(mesh):
    in_specs = (
        P("batch", "feat"),
        P("batch", None, None),
        P("batch", None),
        P("batch", None, None),
        P("batch", None),
        P("batch", "feat", None),
        P("batch", "feat"),
        P("batch", "feat", None),
        P("feat", None),
        P("feat", None),
        P(),
        P(),
        P(),
        P(),
    )
    out_specs = (P("batch", "feat", None), P(), P(), P("feat", None), P("feat", None))
    return jax.shard_map(local, mesh=mesh, in_specs=in_specs, out_specs=out_specs, check_vma=False)
```

time: 915 us -> 549 us (0.60)
  waiting for transfers between devices: 468 us -> 178 us
  local copies, waits for them, and re-layouts: 299 us -> 15.7 us
  Pallas kernels: 0 us -> 223 us
  blocking collectives: 12 us -> 79 us
  other arithmetic: 64.9 us -> 9.75 us
  matrix products: 48.3 us -> 5.27 us
  starting transfers between devices: 5.32 us -> 22.4 us
    gather x16 -> x0, local copies, waits for them, and re-layouts: 256 us -> none  [the longest x14 181 us: one_block(): gathered = jnp.take(table, positions, axis=0)]
    pallas_call x0 -> x6, Pallas kernels: none -> 223 us  [the longest x2 94.7 us: gather_sum(): pl.pallas_call(functools.partial(gather_sum_body, piece, last), out_shape...]
    all_to_all x1 -> x2, waiting for transfers between devices: 136 us -> 33.7 us  [local(): lax.all_to_all(looked, 'batch', split_axis=0, concat_axis=0, tiled=True)]
    reduce_scatter x2 -> x0, waiting for transfers between devices: 87 us -> none  [the longest x1 44.1 us: local(): lax.psum_scatter(partial_grad, 'feat', scatter_dimension=0, tiled=True)]
    all_gather x2 -> x0, waiting for transfers between devices: 58.1 us -> none  [the longest x1 29.9 us: local(): hidden = lax.all_gather(hidden_share, 'feat', axis=0, tiled=True)]
    psum x2 -> x1, waiting for transfers between devices: 187 us -> 132 us  [local(): gw2 = lax.psum(gw2, ('feat', 'batch'))]
    all_to_all x1 -> x3, blocking collectives: 12 us -> 48.8 us  [the longest x1 19.8 us: local(): lax.all_to_all(gw1.reshape(batch_count, width, hidden_width), 'batch', 0,...]
    dot_general x9 -> x1, matrix products: 36.1 us -> 1.16 us  [local(): agg_parts = jnp.dot(adj_two, hidden, preferred_element_type=jnp.float32)]
  transfers between devices with their start and end apart: 7 -> 7, of which waited for: 7 -> 4; matrix products, arithmetic and copies ran while one was open for 1% -> 3% of each run, Pallas kernels for 0% -> 28%
where the time goes in v1:
time: 549 us; the launch traced here: 548 us
  Pallas kernels  223 us (41%)
  waiting for transfers between devices  178 us (32%)
  blocking collectives  79 us (14%)
  starting transfers between devices  22.4 us (4%)
  between operations  15.9 us (3%)
  local copies, waits for them, and re-layouts  15.7 us (3%)
  other arithmetic  9.75 us (2%)
    psum x1, waiting for transfers between devices, local(): gw2 = lax.psum(gw2, ('feat', 'batch'))  132 us
    pallas_call x2, Pallas kernels, gather_sum(): pl.pallas_call(functools.partial(gather_sum_body, piece, last), out_shape...  94.7 us
    pallas_call x2, Pallas kernels, lookup(): pl.pallas_call(functools.partial(lookup_body, first, width), out_shape=ja...  71 us
    pallas_call x1, Pallas kernels, adjacency(): pl.pallas_call(functools.partial(adjacency_body, tiles), out_shape=jax.Sh...  54.2 us
    all_to_all x2, waiting for transfers between devices, local(): lax.all_to_all(looked, 'batch', split_axis=0, concat_axis=0, tiled=True)  33.7 us
    all_gather x1, blocking collectives, local(): deg_all = lax.all_gather(deg_two[0], 'feat', axis=0, tiled=True)  21.4 us
    all_to_all x1, blocking collectives, local(): lax.all_to_all(gw1.reshape(batch_count, width, hidden_width), 'batch', 0,...  19.8 us
    all_to_all x1, blocking collectives, spread(): lax.all_to_all(jnp.broadcast_to(part[None], (count,) + part.shape), axis,...  16.9 us
  transfers between devices with their start and end apart: 7, of which 4 were waited for; matrix products, arithmetic and copies ran while one was open for 3% of the time, Pallas kernels for 28%

profile of v1, /device:TPU:0, one launch (start us, length us, event | category | flops | bytes accessed | tf_op | source)
XLA Modules:
  0.0 548.2 jit_solution(14128709845204467036)
XLA Ops:
  11.8 2.6 requests.1
  14.4 12.2 %all_to_all.51 = s32[8,1,1536]{2,1,0:T(1,128)S(1)} all-to-all(s32[8,1,1536]{2,1,0:T(1,128)} %bitcast.117), channel_id=1, replica_groups=mesh['feat'=4,'batch'=8] {'batch'}, dimensions={0} | all-to-all | bytes 98304 | tf_op jit(solution)/shard_map/all_to_all | solution.py:353
  27.2 34.7 %lookup.3 = bf16[8,768,256]{2,1,0:T(8,128)(2,1)} custom-call(s32[8,1536]{1,0:T(8,128)} %bitcast.104, bf16[8192,256]{1,0:T(8,128)(2,1)} %store_ref.3), custom_call_target="tpu_custom_call" | custom-call | flops 62914560 | bytes 4194304 | tf_op jit(solution)/shard_map/lookup/pallas_call | solution.py:124
  61.8 3.8 all-to-all-start.1
  67.1 36.3 %lookup.2 = bf16[8,768,256]{2,1,0:T(8,128)(2,1)} custom-call(s32[8,1536]{1,0:T(8,128)} %bitcast.105, bf16[8192,256]{1,0:T(8,128)(2,1)} %store_ref.3), custom_call_target="tpu_custom_call" | custom-call | flops 62914560 | bytes 4194304 | tf_op jit(solution)/shard_map/lookup/pallas_call | solution.py:124
  103.4 33.7 %all-to-all-done.1.answer_ref = bf16[8,768,256]{2,1,0:T(8,128)(2,1)S(1)} async-done(((bf16[8,768,256]{2,1,0:T(8,128)(2,1)}), bf16[8,768,256]{2,1,0:T(8,128)(2,1)S(1)}, u32[]{:S(2)}, u32[]{:S(2)}) %all-to-all-start.1) | async-done | bytes 3145760 | tf_op jit(solution)/shard_map/all_to_all | solution.py:358
  138.7 4.4 all-to-all-start.2
  147.2 1.7 copy.45
  153.0 54.2 %adjacency.1.adj_ref = f8e4m3fn[26,3072,256]{2,1,0:T(32,128)(4,1)} custom-call(s32[192,256]{1,0:T(8,128)} %reshape.144.near_ref, bf16[256,128]{1,0:T(8,128)(2,1)} %pad_maximum_fusion.2.table_ref), custom_call_target="tpu_custom_call" | custom-call | flops 20937965568 | bytes 20447232 | tf_op jit(solution)/shard_map/adjacency/pallas_call | solution.py:176
  207.2 62.3 %gather_sum.2 = (f32[3072,256]{1,0:T(8,128)}, bf16[3072,256]{1,0:T(8,128)(2,1)}) custom-call(s32[2]{0:T(128)} %pad_add_fusion.4.spans_ref, s32[8]{0:T(128)} %get-tuple-element.36.counts_ref, s32[9]{0:T(128)} %copy-done.12, bf16[8,768,256]{2,1,0:T(8,128)(2,1)} %copy-done.1, s32[3072,1]{1,0:T(8,128)} %bitcast.98, f8e4m3fn[26,3072,256]{2,1,0:T(32,128)(4,1)} %adjacency.1.adj_ref), custom_call_target="tpu_custom_call" | custom-call | flops 10468982784 | bytes 10223616 | tf_op jit(solution)/shard_map/gather_sum/pallas_call | solution.py:296
  269.5 32.5 %gather_sum.3 = (bf16[3072,256]{1,0:T(8,128)(2,1)}, bf16[3072,256]{1,0:T(8,128)(2,1)}, bf16[3072,256]{1,0:T(8,128)(2,1)}) custom-call(s32[2]{0:T(128)} %pad_add_fusion.3.spans_ref, s32[8]{0:T(128)} %get-tuple-element.37.counts_ref, s32[9]{0:T(128)} %copy-done.11, bf16[8,768,256]{2,1,0:T(8,128)(2,1)} %all-to-all-done.2.answer_ref, s32[3072,1]{1,0:T(8,128)} %bitcast.99, ...), custom_call_target="tpu_custom_call" | custom-call | flops 10468982784 | bytes 10223616 | tf_op jit(solution)/shard_map/gather_sum/pallas_call | solution.py:296
  302.0 3.7 all-to-all-start.3
  305.8 21.4 %all-gather = s32[1,512]{1,0:T(1,128)S(1)} all-gather(s32[1,128]{1,0:T(1,128)S(1)} %copy-done.9), channel_id=2, replica_groups=mesh['feat'=4,'batch'=8] {'feat'}, dimensions={1}, use_global_device_ids=true | all-gather | bytes 2560 | tf_op jit(solution)/shard_map/all_gather | solution.py:396
  327.2 8.8 %all_gather.6 = s32[512,10]{0,1:T(8,128)S(1)} all-gather(s32[128,10]{0,1:T(8,128)S(1)} %bitcast_select_fusion.1), channel_id=1, replica_groups=mesh['feat'=4,'batch'=8] {'feat'}, dimensions={0}, use_global_device_ids=true | all-gather | bytes 25600 | tf_op jit(solution)/shard_map/all_gather | solution.py:395
  336.1 2.2 convert_reduce_fusion
  339.9 3.5 all-to-all-start.4
  343.6 6.4 %all-to-all-done.4 = f32[4,128,256]{2,1,0:T(8,128)S(1)} async-done(((f32[4,128,256]{2,1,0:T(8,128)}), f32[4,128,256]{2,1,0:T(8,128)S(1)}, u32[]{:S(2)}, u32[]{:S(2)}) %all-to-all-start.4) | async-done | bytes 524320 | tf_op jit(solution)/shard_map/all_to_all | solution.py:424
  351.6 3.4 all-to-all-start.5
  355.2 5.1 all-to-all-done.5
  361.7 16.9 %all_to_all.52 = bf16[4,768,256]{2,1,0:T(8,128)(2,1)S(1)} all-to-all(bf16[4,768,256]{2,1,0:T(8,128)(2,1)S(1)} %broadcast_in_dim.63), channel_id=1, replica_groups=mesh['feat'=4,'batch'=8] {'feat'}, dimensions={0} | all-to-all | bytes 3145728 | tf_op jit(solution)/shard_map/all_to_all | solution.py:319
  380.7 19.8 %all_to_all.53 = f32[8,64,256]{2,1,0:T(8,128)S(1)} all-to-all(f32[8,64,256]{2,1,0:T(8,128)S(1)} %bitcast.97), channel_id=1, replica_groups=mesh['feat'=4,'batch'=8] {'batch'}, dimensions={0} | all-to-all | bytes 1048576 | tf_op jit(solution)/shard_map/all_to_all | solution.py:450
  401.3 3.5 all-to-all-start.8
  406.2 132.4 %all-reduce.5.cloned.1.call-done = f32[512,256]{1,0:T(8,128)} async-done(((f32[512,256]{1,0:T(8,128)}), f32[512,256]{1,0:T(8,128)}) %all-reduce.5.cloned.1.call-update) | async-done | bytes 524304 | tf_op jit(solution)/shard_map/psum | solution.py:439
  538.7 1.9 fusion.49
  (109 shorter events, 25.1 us)
Async XLA Ops:
  7.2 342.8 %copy-start = (bf16[256,256]{1,0:T(8,128)(2,1)S(1)}, bf16[256,256]{1,0:T(8,128)(2,1)}, u32[]{:S(2)}) copy-start(bf16[256,256]{1,0:T(8,128)(2,1)} %param.26) | copy-start | bytes 393220
  61.8 3.8 copy-start.8
  61.8 75.2 %all-to-all-start.1 = ((bf16[8,768,256]{2,1,0:T(8,128)(2,1)}), bf16[8,768,256]{2,1,0:T(8,128)(2,1)S(1)}, u32[]{:S(2)}, u32[]{:S(2)}) async-start(bf16[8,768,256]{2,1,0:T(8,128)(2,1)} %lookup.3), calls=%async_computation.1 | async-start | bytes 6291456 | tf_op jit(solution)/shard_map/all_to_all | solution.py:358
  103.4 39.8 %copy-start.3 = (s32[1,3072,15]{1,0,2:T(1,128)S(1)}, s32[1,3072,15]{1,0,2:T(1,128)}, u32[]{:S(2)}) copy-start(s32[1,3072,15]{1,0,2:T(1,128)} %param.17) | copy-start | bytes 552964
  103.4 39.8 %copy-start.5 = (s32[1,3072]{1,0:T(1,128)S(1)}, s32[1,3072]{1,0:T(1,128)}, u32[]{:S(2)}) copy-start(s32[1,3072]{1,0:T(1,128)} %param.18) | copy-start | bytes 36868
  103.4 41.2 %copy-start.6 = (s32[24,256]{1,0:T(8,128)S(1)}, s32[24,256]{1,0:T(8,128)}, u32[]{:S(2)}) copy-start(s32[24,256]{1,0:T(8,128)} %get-tuple-element.18) | copy-start | bytes 73732
  103.4 41.5 %copy-start.4 = (s32[1,6144,1]{1,2,0:T(1,128)S(1)}, s32[1,6144,1]{1,2,0:T(1,128)}, u32[]{:S(2)}) copy-start(s32[1,6144,1]{1,2,0:T(1,128)} %param.15) | copy-start | bytes 73732
  137.1 1.6 copy-start.1
  138.7 130.8 %all-to-all-start.2 = ((bf16[8,768,256]{2,1,0:T(8,128)(2,1)}), bf16[8,768,256]{2,1,0:T(8,128)(2,1)}, u32[]{:S(2)}, u32[]{:S(2)}) async-start(bf16[8,768,256]{2,1,0:T(8,128)(2,1)} %lookup.2), calls=%async_computation.2 | async-start | bytes 6291456 | tf_op jit(solution)/shard_map/all_to_all | solution.py:361
  144.8 1.1 copy-start.11
  144.8 1.1 copy-start.12
  302.0 3.8 copy-start.9
  302.0 25.2 %copy-start.7 = (s32[1,128,10]{1,0,2:T(1,128)S(1)}, s32[1,128,10]{1,0,2:T(1,128)}, u32[]{:S(2)}) copy-start(s32[1,128,10]{1,0,2:T(1,128)} %param.19) | copy-start | bytes 15364
  302.0 36.2 %all-to-all-start.3 = ((bf16[4,768,256]{2,1,0:T(8,128)(2,1)}), bf16[4,768,256]{2,1,0:T(8,128)(2,1)S(1)}, u32[]{:S(2)}, u32[]{:S(2)}) async-start(bf16[4,768,256]{2,1,0:T(8,128)(2,1)} %bitcast.101), calls=%async_computation.3 | async-start | bytes 3145728 | tf_op jit(solution)/shard_map/all_to_all | solution.py:419
  336.1 2.4 copy-start.10
  338.7 4.7 copy-start.2
  338.7 11.3 %copy-start.13 = (bf16[1,128,256]{2,1,0:T(8,128)(2,1)S(1)}, bf16[1,128,256]{2,1,0:T(8,128)(2,1)}, u32[]{:S(2)}) copy-start(bf16[1,128,256]{2,1,0:T(8,128)(2,1)} %param.21) | copy-start | bytes 196612
  338.7 11.3 %copy-start.14 = (f32[256]{0:T(256)S(1)}, f32[256]{0:T(256)}, u32[]{:S(2)}) copy-start(f32[256]{0:T(256)} %param.27) | copy-start | bytes 3076
  339.9 10.0 %all-to-all-start.4 = ((f32[4,128,256]{2,1,0:T(8,128)}), f32[4,128,256]{2,1,0:T(8,128)S(1)}, u32[]{:S(2)}, u32[]{:S(2)}) async-start(f32[4,128,256]{2,1,0:T(8,128)} %bitcast.15), calls=%async_computation.4 | async-start | bytes 1048576 | tf_op jit(solution)/shard_map/all_to_all | solution.py:424
  351.6 8.8 %all-to-all-start.5 = ((bf16[4,128,256]{2,1,0:T(8,128)(2,1)}), bf16[4,128,256]{2,1,0:T(8,128)(2,1)S(1)}, u32[]{:S(2)}, u32[]{:S(2)}) async-start(bf16[4,128,256]{2,1,0:T(8,128)(2,1)} %broadcast_in_dim.62), calls=%async_computation.5 | async-start | bytes 524288 | tf_op jit(solution)/shard_map/all_to_all | solution.py:319
  361.7 17.0 %copy-start.16 = (bf16[3072,256]{1,0:T(8,128)(2,1)S(1)}, bf16[3072,256]{1,0:T(8,128)(2,1)}, u32[]{:S(2)}) copy-start(bf16[3072,256]{1,0:T(8,128)(2,1)} %get-tuple-element.23) | copy-start | bytes 4718596
  378.6 1.4 copy-start.15
  401.3 139.2 %all-to-all-start.8 = ((f32[8,64,256]{2,1,0:T(8,128)}), f32[8,64,256]{2,1,0:T(8,128)S(1)}, u32[]{:S(2)}, u32[]{:S(2)}) async-start(f32[8,64,256]{2,1,0:T(8,128)} %broadcast_in_dim.64), calls=%async_computation.8 | async-start | bytes 1048576 | tf_op jit(solution)/shard_map/all_to_all | solution.py:319
  404.8 133.9 %all-reduce.5.cloned.1.call-start = ((), (), s32[]{:S(2)}) async-start(), calls=%async_computation.9 | async-start | bytes 1048576 | tf_op jit(solution)/shard_map/psum | solution.py:439
Sparse Core Ops, SparseCore 0:
  410.9 127.7 all-reduce.4

commit v2 on v1

--- a/solution.py
+++ b/solution.py
@@ -1,4 +1,5 @@
 import functools
+import math
 
 import jax
 import jax.numpy as jnp
@@ -10,6 +11,7 @@
 TILE = 256
 LANES = 128
 SLOTS = 16
+WIDE = 2
 TILE_BITS, LANE_BITS, SLOT_BITS = 8, 7, 4
 VMEM_BYTES = 56 * 1024 * 1024
 VMEM = pl.BlockSpec(memory_space=pltpu.VMEM)
@@ -42,8 +44,9 @@
 
 
 def requests_body(batch_count, capacity, owner_ref, row_ref, slot_ref, count_ref, request_ref):
-    blocks, width = owner_ref.shape
+    blocks, width = owner_ref.shape[0] // 2, TILE
     places = request_ref.shape[0]
+    line = lambda ref, b: jnp.concatenate([ref[2 * b : 2 * b + 1], ref[2 * b + 1 : 2 * b + 2]], axis=1)
     owner_id = lax.broadcasted_iota(jnp.int32, (batch_count, width), 0)
     earlier = lax.broadcasted_iota(jnp.int32, (width, width), 0)
     later = lax.broadcasted_iota(jnp.int32, (width, width), 1)
@@ -51,7 +54,7 @@
     high_id = lax.broadcasted_iota(jnp.int32, (places, width), 0)
     low_id = lax.broadcasted_iota(jnp.int32, (LANES, width), 0)
     marks = [
-        jnp.where(owner_ref[b : b + 1, :] == owner_id, 1.0, 0.0) for b in range(blocks)
+        jnp.where(line(owner_ref, b) == owner_id, 1.0, 0.0) for b in range(blocks)
     ]
     stacked = jnp.concatenate(marks, axis=0).astype(jnp.bfloat16)
     prefix = jnp.dot(stacked, upper, preferred_element_type=jnp.float32)
@@ -61,10 +64,11 @@
         part = prefix[b * batch_count : (b + 1) * batch_count]
         slots = jnp.sum(marks[b] * (part + running - 1.0), axis=0, keepdims=True)
         slots = slots.astype(jnp.int32)
-        slot_ref[b : b + 1, :] = slots
+        slot_ref[2 * b : 2 * b + 1, :] = slots[:, :LANES]
+        slot_ref[2 * b + 1 : 2 * b + 2, :] = slots[:, LANES:]
         running = running + part[:, width - 1 : width]
-        bucket = owner_ref[b : b + 1, :] * capacity + slots
-        rows = row_ref[b : b + 1, :]
+        bucket = line(owner_ref, b) * capacity + slots
+        rows = line(row_ref, b)
         hit = (bucket >> LANE_BITS) == high_id
         left = jnp.concatenate(
             [
@@ -80,13 +84,12 @@
 
 
 def make_requests(batch_count, capacity, owners, wanted):
-    total = owners.shape[0]
-    blocks = total // TILE
+    total = owners.shape[0] * LANES
     places = batch_count * capacity // LANES
     return pl.pallas_call(
         functools.partial(requests_body, batch_count, capacity),
         out_shape=(
-            jax.ShapeDtypeStruct((blocks, TILE), jnp.int32),
+            jax.ShapeDtypeStruct(owners.shape, jnp.int32),
             jax.ShapeDtypeStruct((batch_count, LANES), jnp.int32),
             jax.ShapeDtypeStruct((places, LANES), jnp.int32),
         ),
@@ -95,42 +98,44 @@
         compiler_params=params(),
         cost_estimate=cost(4 * total * places * LANES, 24 * total),
         name="requests",
-    )(owners.reshape(blocks, TILE), wanted.reshape(blocks, TILE))
+    )(owners, wanted)
 
 
 def lookup_body(first, width, want_ref, store_ref, out_ref, table, lines):
     group = pl.program_id(0)
     rows_all = store_ref.shape[0]
+    halves = store_ref.shape[1] // LANES
+    lane = lambda h: pl.ds(h * LANES, LANES)
 
     @pl.when(group == 0)
     def _():
         @pl.loop(0, rows_all // TILE)
         def _(j):
             part = pl.ds(pl.multiple_of(j * TILE, TILE), TILE)
-            table[part, :] = store_ref[part, :].astype(jnp.float32)
+            for h in range(halves):
+                table[part, h, :] = store_ref[part, lane(h)].astype(jnp.float32)
 
     @pl.loop(0, width // SLOTS)
     def _(j):
         for u in range(SLOTS):
             at = j * SLOTS + u
-            lines[pl.ds(at, 1), :] = table[pl.ds(want_ref[group, first + at], 1), :]
-
-    out_ref[0] = lines[...].astype(jnp.bfloat16)
+            lines[at] = table[want_ref[group, first + at]]
+
+    for h in range(halves):
+        out_ref[0, :, lane(h)] = lines[:, h, :].astype(jnp.bfloat16)
 
 
 def lookup(store, received, first, width):
     groups = received.shape[0]
     rows_all, features = store.shape
+    apart = lambda rows: pltpu.VMEM((rows, features // LANES, LANES), jnp.float32)
     return pl.pallas_call(
         functools.partial(lookup_body, first, width),
         out_shape=jax.ShapeDtypeStruct((groups, width, features), jnp.bfloat16),
         grid=(groups,),
         in_specs=[SMEM, pl.BlockSpec((rows_all, features), lambda g: (0, 0))],
         out_specs=pl.BlockSpec((1, width, features), lambda g: (g, 0, 0)),
-        scratch_shapes=[
-            pltpu.VMEM((rows_all, features), jnp.float32),
-            pltpu.VMEM((width, features), jnp.float32),
-        ],
+        scratch_shapes=[apart(rows_all), apart(width)],
         compiler_params=params(),
         cost_estimate=cost(groups * width * features * 40, 2 * rows_all * features),
         name="lookup",
@@ -161,7 +166,7 @@
         right = jnp.where(low == low_id, 1.0, 0.0).astype(jnp.bfloat16)
         return contract_cols(left, right).reshape(tiles, SLOTS, TILE)
 
-    @pl.loop(0, groups // 2)
+    @pl.loop(0, groups // 2, unroll=2)
     def _(j):
         pair = jnp.concatenate([one_group(2 * j), one_group(2 * j + 1)], axis=1)
         out_ref[:, pl.ds(pl.multiple_of(j * 2 * SLOTS, 2 * SLOTS), 2 * SLOTS), :] = pair.astype(
@@ -202,8 +207,8 @@
             packed[target, :] = answer_ref[o, source, :]
 
     end = starts_ref[batch_count]
-    packed[pl.ds(pl.multiple_of(end, SLOTS), TILE), :] = jnp.zeros(
-        (TILE, packed.shape[1]), packed.dtype
+    packed[pl.ds(pl.multiple_of(end, SLOTS), WIDE * TILE), :] = jnp.zeros(
+        (WIDE * TILE, packed.shape[1]), packed.dtype
     )
 
 
@@ -212,16 +217,22 @@
 ):
     if last:
         (total_in, own_in, deg_ref, wself_ref, wneigh_ref, own_ref, mean_ref, share_ref) = refs[:8]
-        packed, tiles_ref, ready, total_ref = refs[8:]
+        packed, tiles_ref, ready, found_ref, total_ref = refs[8:]
     else:
-        total_ref, own_ref, packed, tiles_ref, ready = refs
+        total_ref, own_ref, packed, tiles_ref, ready, found_ref = refs
     nodes = own_ref.shape[0]
+    rows = math.gcd(nodes, 3 * TILE)
     begin, count = spans_ref[0], spans_ref[1]
 
     def fetch(step, slot):
-        return pltpu.make_async_copy(adj_ref.at[begin + step], tiles_ref.at[slot], ready.at[slot])
-
-    fetch(0, 0).start()
+        return pltpu.make_async_copy(
+            adj_ref.at[pl.ds(begin + step * WIDE, WIDE)], tiles_ref.at[slot], ready.at[slot]
+        )
+
+    @pl.when(count > 0)
+    def _():
+        fetch(0, 0).start()
+
     collect(piece, counts_ref, starts_ref, answer_ref, packed)
 
     @pl.loop(0, nodes // TILE)
@@ -229,10 +240,10 @@
         part = pl.ds(pl.multiple_of(r * TILE, TILE), TILE)
         if last:
             total_ref[part, :] = total_in[part, :]
-            own_ref[part, :] = own_in[part, :]
+            found_ref[part, :] = own_in[part, :].astype(jnp.float32)
         else:
             total_ref[part, :] = jnp.zeros((TILE, total_ref.shape[1]), jnp.float32)
-            own_ref[part, :] = jnp.zeros((TILE, own_ref.shape[1]), jnp.bfloat16)
+            found_ref[part, :] = jnp.zeros((TILE, found_ref.shape[1]), jnp.float32)
 
     @pl.loop(0, count)
     def _(step):
@@ -243,17 +254,27 @@
             fetch(step + 1, 1 - slot).start()
 
         fetch(step, slot).wait()
-        block = packed[pl.ds(pl.multiple_of(step * TILE, TILE), TILE), :]
-        lane = lax.broadcasted_iota(jnp.int32, (TILE, TILE), 1) + (begin + step) * TILE
-
-        @pl.loop(0, nodes // TILE)
+        depth = WIDE * TILE
+        block = packed[pl.ds(pl.multiple_of(step * depth, depth), depth), :]
+        lane = lax.broadcasted_iota(jnp.int32, (rows, depth), 1) + (begin * TILE + step * depth)
+
+        @pl.loop(0, nodes // rows)
         def _(r):
-            part = pl.ds(pl.multiple_of(r * TILE, TILE), TILE)
-            near = tiles_ref[slot, part, :].astype(jnp.bfloat16)
-            total_ref[part, :] += jnp.dot(near, block, preferred_element_type=jnp.float32)
+            part = pl.ds(pl.multiple_of(r * rows, rows), rows)
+            near = jnp.concatenate(
+                [tiles_ref[slot, w, part, :].astype(jnp.bfloat16) for w in range(WIDE)], axis=1
+            )
             own = jnp.where(column_ref[part, :] == lane, 1.0, 0.0).astype(jnp.bfloat16)
-            found = jnp.dot(own, block, preferred_element_type=jnp.float32)
-            own_ref[part, :] = (own_ref[part, :].astype(jnp.float32) + found).astype(jnp.bfloat16)
+            both = jnp.dot(
+                jnp.concatenate([near, own], axis=0), block, preferred_element_type=jnp.float32
+            )
+            total_ref[part, :] += both[:rows]
+            found_ref[part, :] += both[rows:]
+
+    @pl.loop(0, nodes // TILE)
+    def _(r):
+        part = pl.ds(pl.multiple_of(r * TILE, TILE), TILE)
+        own_ref[part, :] = found_ref[part, :].astype(jnp.bfloat16)
 
     if last:
 
@@ -268,18 +289,19 @@
             ).astype(share_ref.dtype)
 
 
-def gather_sum(spans, counts, starts, answer, column, adj, rest, share_type=jnp.bfloat16):
+def gather_sum(inputs, spans, counts, starts, answer, column, adj, rest, share_type=jnp.bfloat16):
     batch_count, width, features = answer.shape
     tiles, nodes, _ = adj.shape
     piece = LANES if width % LANES == 0 else SLOTS
     last = rest is not None
-    room = (min(batch_count * width, 2 * nodes) + SLOTS * batch_count + 3 * TILE) // TILE * TILE
+    room = min(batch_count * width, inputs) + SLOTS * batch_count + 2 * WIDE * TILE
     in_specs = [SMEM, SMEM, SMEM, VMEM, VMEM, pl.BlockSpec(memory_space=pl.ANY)]
     rows = lambda dtype: jax.ShapeDtypeStruct((nodes, features), dtype)
     scratch = [
         pltpu.VMEM((room, features), jnp.bfloat16),
-        pltpu.VMEM((2, nodes, TILE), adj.dtype),
+        pltpu.VMEM((2, WIDE, nodes, TILE), adj.dtype),
         pltpu.SemaphoreType.DMA((2,)),
+        pltpu.VMEM((nodes, features), jnp.float32),
     ]
     operands = [answer, column, adj]
     if last:
@@ -319,6 +341,16 @@
     return lax.all_to_all(
         jnp.broadcast_to(part[None], (count,) + part.shape), axis, 0, 0, tiled=True
     )
+
+
+def total_over_batch(one, two):
+    count = lax.axis_size("batch")
+    both = jnp.concatenate([one, two]).astype(jnp.bfloat16)
+    pieces = both.reshape(count, both.shape[0] // count, both.shape[1])
+    pieces = lax.all_to_all(pieces, "batch", 0, 0, tiled=True)
+    total = spread(jnp.sum(pieces.astype(jnp.float32), axis=0), "batch", count)
+    total = total.reshape(both.shape)
+    return total[: one.shape[0]], total[one.shape[0] :]
 
 
 def local(
@@ -348,52 +380,60 @@
     share = nodes // parts
     hidden_width = w1_self.shape[1]
 
-    owners = input_owner[0, :, 0]
-    slots, counts, requests = make_requests(batch_count, capacity, owners, input_row[0])
+    owners = input_owner.reshape(input_count // LANES, LANES)
+    wanted = input_row.reshape(input_count // LANES, LANES)
+    slots, counts, requests = make_requests(batch_count, capacity, owners, wanted)
+    owners = owners.reshape(1, input_count)
     received = lax.all_to_all(
         requests.reshape(batch_count, capacity), "batch", split_axis=0, concat_axis=0, tiled=True
     )
     first = capacity // 2
-    looked = lookup(store, received, 0, first)
-    answer_a = lax.all_to_all(looked, "batch", split_axis=0, concat_axis=0, tiled=True)
+    looked_a = lookup(store, received, 0, first)
+    near_first, looked_a = lax.optimization_barrier((nbr_one[0], looked_a))
+    answer_a = lax.all_to_all(looked_a, "batch", split_axis=0, concat_axis=0, tiled=True)
     looked = lookup(store, received, first, capacity - first)
-    looked, answer_a = lax.optimization_barrier((looked, answer_a))
-    answer_b = lax.all_to_all(looked, "batch", split_axis=0, concat_axis=0, tiled=True)
-
-    tiles = -(-(input_count + 2 * (SLOTS - 1) * batch_count + TILE - 1) // TILE)
+
+    depth = WIDE * TILE
+    steps = -(-(input_count + 2 * (SLOTS - 1) * batch_count + depth - 1) // depth)
     tally = counts[:, 0]
     tally_a = jnp.minimum(tally, first)
     tally_b = tally - tally_a
     padded = lambda n: (n + SLOTS - 1) // SLOTS * SLOTS
     ends = lambda n: jnp.concatenate([jnp.zeros((1,), jnp.int32), jnp.cumsum(padded(n))])
     starts_a, starts_b = ends(tally_a), ends(tally_b)
-    tiles_a = (starts_a[batch_count] + TILE - 1) // TILE
-    tiles_b = (starts_b[batch_count] + TILE - 1) // TILE
-    spans_a = jnp.stack([jnp.zeros_like(tiles_a), jnp.maximum(tiles_a, 1)])
-    spans_b = jnp.stack([tiles_a, jnp.maximum(tiles_b, 1)])
+    steps_a = (starts_a[batch_count] + depth - 1) // depth
+    steps_b = (starts_b[batch_count] + depth - 1) // depth
+    spans_a = jnp.stack([jnp.zeros_like(steps_a), steps_a])
+    spans_b = jnp.stack([steps_a * WIDE, steps_b])
     slot = slots.reshape(1, input_count)
     shifted = jnp.where(
         slot < first,
         slot + starts_a[:batch_count, None],
-        slot - first + tiles_a * TILE + starts_b[:batch_count, None],
-    )
-    mine = owners[None, :] == jnp.arange(batch_count)[:, None]
+        slot - first + steps_a * depth + starts_b[:batch_count, None],
+    )
+    mine = owners == jnp.arange(batch_count)[:, None]
     column = jnp.sum(jnp.where(mine, shifted, 0), axis=0)
     grid = jnp.pad(column.reshape(-1, LANES), ((0, LANES - input_count // LANES), (0, 0))).T
     table = jnp.concatenate([grid // TILE, grid % TILE], axis=0).astype(jnp.bfloat16)
     own_column = share_order(column[:nodes], parts, seeds).reshape(nodes, 1)
 
+    fanout_two = nbr_two.shape[2]
+    used_two = jnp.arange(fanout_two)[:, None] < deg_two
+    lists = jnp.concatenate([jnp.where(used_two, nbr_two[0].T, -1), deg_two], axis=0)
+    lists = spread(lists, "feat", parts)
+
     fanout = nbr_one.shape[2]
     used = jnp.arange(fanout)[None, :] < deg_one[0][:, None]
-    near = share_order(jnp.where(used, nbr_one[0], -1), parts, seeds)
+    near = share_order(jnp.where(used, near_first, -1), parts, seeds)
     near = jnp.pad(near, ((0, 0), (0, SLOTS - fanout)), constant_values=-1)
-    adj = adjacency(near.reshape(nodes // SLOTS, TILE), table, tiles)
+    near, lists = lax.optimization_barrier((near, lists))
+    adj = adjacency(near.reshape(nodes // SLOTS, TILE), table, steps * WIDE)
+    looked, answer_a, adj = lax.optimization_barrier((looked, answer_a, adj))
+    answer_b = lax.all_to_all(looked, "batch", split_axis=0, concat_axis=0, tiled=True)
     deg_first = share_order(deg_one[0], parts, seeds).astype(jnp.float32).reshape(nodes, 1)
 
-    fanout_two = nbr_two.shape[2]
-    used_two = jnp.arange(fanout_two)[None, :] < deg_two[0][:, None]
-    near_two = lax.all_gather(jnp.where(used_two, nbr_two[0], -1), "feat", axis=0, tiled=True)
-    deg_all = lax.all_gather(deg_two[0], "feat", axis=0, tiled=True)
+    near_two = lists[:, :fanout_two].transpose(1, 0, 2).reshape(fanout_two, seeds)
+    deg_all = lists[:, fanout_two].reshape(seeds)
     rest = share - seed_rows
     after = near_two - seeds
     place = jnp.where(
@@ -403,11 +443,12 @@
     )
     place = jnp.where(near_two < 0, -1, place - feat_index * share)
     adj_two = jnp.sum(
-        place[:, :, None] == jnp.arange(share)[None, None, :], axis=1, dtype=jnp.float32
+        place[:, :, None] == jnp.arange(share)[None, None, :], axis=0, dtype=jnp.float32
     ).astype(jnp.bfloat16)
 
-    total, own = gather_sum(spans_a, tally_a, starts_a, answer_a, own_column, adj, None)
+    total, own = gather_sum(input_count, spans_a, tally_a, starts_a, answer_a, own_column, adj, None)
     self_one, agg_one, z_part = gather_sum(
+        input_count,
         spans_b,
         tally_b,
         starts_b,
@@ -434,9 +475,9 @@
     )
     activations = jax.nn.silu(z_two).astype(jnp.bfloat16)[None]
     dz_two = (cotangent[0].astype(jnp.float32) * silu_grad(z_two)).astype(jnp.bfloat16)
-    dz_two_all = spread(dz_two, "feat", parts).reshape(seeds, hidden_width)
-    gw2 = jnp.concatenate([contract_rows(self_two, dz_two), contract_rows(agg_two, dz_two)])
-    gw2 = lax.psum(gw2, ("feat", "batch"))
+    group = spread(jnp.stack([self_two, agg_two, dz_two]), "feat", parts)
+    self_all, agg_all, dz_two_all = (group[:, i].reshape(seeds, hidden_width) for i in range(3))
+    gw2 = total_over_batch(contract_rows(self_all, dz_two_all), contract_rows(agg_all, dz_two_all))
 
     back = contract_cols(dz_two_all, w2_neigh) / deg_all.astype(jnp.float32)[:, None]
     back_high = back.astype(jnp.bfloat16)
@@ -445,12 +486,8 @@
     dh_share = dh_share + jnp.pad(contract_cols(dz_two, w2_self), ((0, rest), (0, 0)))
     dz_share = (dh_share * silu_grad(z_share)).astype(jnp.bfloat16)
     dz_one = spread(dz_share, "feat", parts).reshape(nodes, hidden_width)
-    gw1 = jnp.concatenate([contract_rows(self_one, dz_one), contract_rows(agg_one, dz_one)])
-    width = gw1.shape[0] // batch_count
-    gw1 = lax.all_to_all(gw1.reshape(batch_count, width, hidden_width), "batch", 0, 0, tiled=True)
-    gw1 = spread(jnp.sum(gw1, axis=0), "batch", batch_count).reshape(-1, hidden_width)
-    half1, half2 = gw1.shape[0] // 2, gw2.shape[0] // 2
-    return (activations, gw2[:half2], gw2[half2:], gw1[:half1], gw1[half1:])
+    gw1 = total_over_batch(contract_rows(self_one, dz_one), contract_rows(agg_one, dz_one))
+    return (activations, *gw2, *gw1)
 
 
 def solution(mesh):

time: 549 us -> 388 us (0.71)
  blocking collectives: 79 us -> 0 us
  Pallas kernels: 223 us -> 164 us
  waiting for transfers between devices: 178 us -> 138 us
  starting transfers between devices: 22.4 us -> 50.5 us
  between operations: 15.9 us -> 2.51 us
    psum x1 -> x0, waiting for transfers between devices: 132 us -> none  [local(): gw2 = lax.psum(gw2, ('feat', 'batch'))]
    all_to_all x2 -> x5, waiting for transfers between devices: 5.15 us -> 55.3 us  [spread(): lax.all_to_all(jnp.broadcast_to(part[None], (count,) + part.shape), axis,...]
    all_to_all x3 -> x0, blocking collectives: 48.8 us -> none  [the longest x1 19.8 us: local(): lax.all_to_all(gw1.reshape(batch_count, width, hidden_width), 'batch', 0,...]
    pallas_call x2, Pallas kernels: 94.7 us -> 47.4 us  [gather_sum(): pl.pallas_call(functools.partial(gather_sum_body, piece, last), out_shape...]
    all_gather x2 -> x0, blocking collectives: 30.2 us -> none  [the longest x1 21.4 us: local(): deg_all = lax.all_gather(deg_two[0], 'feat', axis=0, tiled=True)]
    all_to_all x0 -> x4, waiting for transfers between devices: none -> 20.3 us  [the longest x2 15.8 us: total_over_batch(): pieces = lax.all_to_all(pieces, 'batch', 0, 0, tiled=True)]
    all_to_all x0 -> x4, starting transfers between devices: none -> 19.8 us  [the longest x2 8.85 us: total_over_batch(): pieces = lax.all_to_all(pieces, 'batch', 0, 0, tiled=True)]
    all_to_all x1, waiting for transfers between devices: 0.01 us -> 16.7 us  [local(): lax.all_to_all(z_part.reshape(parts, share, hidden_width), 'feat', 0, 0,...]
  transfers between devices with their start and end apart: 7 -> 12, of which waited for: 4 -> 10; matrix products, arithmetic and copies ran while one was open for 3% -> 5% of each run, Pallas kernels for 28% -> 37%
where the time goes in v2:
time: 388 us; the launch traced here: 387 us
  Pallas kernels  164 us (42%)
  waiting for transfers between devices  138 us (36%)
  starting transfers between devices  50.5 us (13%)
  local copies, waits for them, and re-layouts  16.2 us (4%)
  other arithmetic  8.84 us (2%)
  matrix products  6.89 us (2%)
    pallas_call x2, Pallas kernels, lookup(): pl.pallas_call(functools.partial(lookup_body, first, width), out_shape=ja...  66 us
    all_to_all x5, waiting for transfers between devices, spread(): lax.all_to_all(jnp.broadcast_to(part[None], (count,) + part.shape), axis,...  55.3 us
    pallas_call x1, Pallas kernels, adjacency(): pl.pallas_call(functools.partial(adjacency_body, tiles), out_shape=jax.Sh...  48.2 us
    pallas_call x2, Pallas kernels, gather_sum(): pl.pallas_call(functools.partial(gather_sum_body, piece, last), out_shape...  47.4 us
    all_to_all x1, waiting for transfers between devices, local(): lax.all_to_all(looked, 'batch', split_axis=0, concat_axis=0, tiled=True)  38 us
    all_to_all x5, starting transfers between devices, spread(): lax.all_to_all(jnp.broadcast_to(part[None], (count,) + part.shape), axis,...  17.9 us
    all_to_all x1, waiting for transfers between devices, local(): lax.all_to_all(z_part.reshape(parts, share, hidden_width), 'feat', 0, 0,...  16.7 us
    all_to_all x2, waiting for transfers between devices, total_over_batch(): pieces = lax.all_to_all(pieces, 'batch', 0, 0, tiled=True)  15.8 us
  transfers between devices with their start and end apart: 12, of which 10 were waited for; matrix products, arithmetic and copies ran while one was open for 5% of the time, Pallas kernels for 37%

profile of v2, /device:TPU:0, one launch (start us, length us, event | category | flops | bytes accessed | tf_op | source)
XLA Modules:
  0.0 386.7 jit_solution(4743659320965851963)
XLA Ops:
  3.3 6.3 %all-to-all-start = ((s32[8,1,1536]{2,1,0:T(1,128)}), s32[8,1,1536]{2,1,0:T(1,128)S(1)}, u32[]{:S(2)}, u32[]{:S(2)}) async-start(s32[8,1,1536]{2,1,0:T(1,128)} %bitcast.161), calls=%async_computation | async-start | bytes 98304 | tf_op jit(solution)/shard_map/all_to_all | solution.py:387
  10.9 4.5 %all-to-all-done = s32[8,1,1536]{2,1,0:T(1,128)S(1)} async-done(((s32[8,1,1536]{2,1,0:T(1,128)}), s32[8,1,1536]{2,1,0:T(1,128)S(1)}, u32[]{:S(2)}, u32[]{:S(2)}) %all-to-all-start) | async-done | bytes 49184 | tf_op jit(solution)/shard_map/all_to_all | solution.py:387
  16.0 3.7 all-to-all-start.2
  21.3 32.9 %lookup.3 = bf16[8,768,256]{2,1,0:T(8,128)(2,1)} custom-call(s32[8,1536]{1,0:T(8,128)} %bitcast.146, bf16[8192,256]{1,0:T(8,128)(2,1)} %store_ref.3), custom_call_target="tpu_custom_call" | custom-call | flops 62914560 | bytes 4194304 | tf_op jit(solution)/shard_map/lookup/pallas_call | solution.py:132
  54.3 4.6 %all-to-all-start.1 = ((bf16[8,768,256]{2,1,0:T(8,128)(2,1)}), bf16[8,768,256]{2,1,0:T(8,128)(2,1)}, u32[]{:S(2)}, u32[]{:S(2)}) async-start(bf16[8,768,256]{2,1,0:T(8,128)(2,1)} %lookup.3), calls=%async_computation.1 | async-start | bytes 6291456 | tf_op jit(solution)/shard_map/all_to_all | solution.py:393
  63.7 33.1 %lookup.2 = bf16[8,768,256]{2,1,0:T(8,128)(2,1)} custom-call(s32[8,1536]{1,0:T(8,128)} %bitcast.147, bf16[8192,256]{1,0:T(8,128)(2,1)} %store_ref.3), custom_call_target="tpu_custom_call" | custom-call | flops 62914560 | bytes 4194304 | tf_op jit(solution)/shard_map/lookup/pallas_call | solution.py:132
  96.7 48.2 %adjacency.1.adj_ref = f8e4m3fn[28,3072,256]{2,1,0:T(32,128)(4,1)} custom-call(s32[192,256]{1,0:T(8,128)} %reshape.275.near_ref, bf16[256,128]{1,0:T(8,128)(2,1)} %pad_maximum_fusion.3.table_ref), custom_call_target="tpu_custom_call" | custom-call | flops 22548578304 | bytes 22020096 | tf_op jit(solution)/shard_map/adjacency/pallas_call | solution.py:181
  144.9 5.0 %all-to-all-start.3 = ((bf16[8,768,256]{2,1,0:T(8,128)(2,1)}), bf16[8,768,256]{2,1,0:T(8,128)(2,1)S(1)}, u32[]{:S(2)}, u32[]{:S(2)}) async-start(bf16[8,768,256]{2,1,0:T(8,128)(2,1)} %lookup.2), calls=%async_computation.3 | async-start | bytes 6291456 | tf_op jit(solution)/shard_map/all_to_all | solution.py:432
  156.3 27.1 %gather_sum.2 = (f32[3072,256]{1,0:T(8,128)}, bf16[3072,256]{1,0:T(8,128)(2,1)}) custom-call(s32[2]{0:T(128)} %pad_add_fusion.5.spans_ref, s32[8]{0:T(128)} %get-tuple-element.46.counts_ref, s32[9]{0:T(128)} %copy-done.8, bf16[8,768,256]{2,1,0:T(8,128)(2,1)} %all-to-all-done.1.answer_ref, s32[3072,1]{1,0:T(8,128)} %bitcast.139, ...), custom_call_target="tpu_custom_call" | custom-call | flops 11274289152 | bytes 11010048 | tf_op jit(solution)/shard_map/gather_sum/pallas_call | solution.py:318
  183.5 38.0 %all-to-all-done.3.answer_ref = bf16[8,768,256]{2,1,0:T(8,128)(2,1)S(1)} async-done(((bf16[8,768,256]{2,1,0:T(8,128)(2,1)}), bf16[8,768,256]{2,1,0:T(8,128)(2,1)S(1)}, u32[]{:S(2)}, u32[]{:S(2)}) %all-to-all-start.3) | async-done | bytes 3145760 | tf_op jit(solution)/shard_map/all_to_all | solution.py:432
  223.2 20.3 %gather_sum.3 = (bf16[3072,256]{1,0:T(8,128)(2,1)}, bf16[3072,256]{1,0:T(8,128)(2,1)}, bf16[3072,256]{1,0:T(8,128)(2,1)}) custom-call(s32[2]{0:T(128)} %pad_add_fusion.4.spans_ref, s32[8]{0:T(128)} %get-tuple-element.47.counts_ref, s32[9]{0:T(128)} %copy-done.7, bf16[8,768,256]{2,1,0:T(8,128)(2,1)} %copy-done.1, s32[3072,1]{1,0:T(8,128)} %bitcast.140, ...), custom_call_target="tpu_custom_call" | custom-call | flops 11274289152 | bytes 11010048 | tf_op jit(solution)/shard_map/gather_sum/pallas_call | solution.py:318
  243.5 4.2 %all-to-all-start.4 = ((bf16[4,768,256]{2,1,0:T(8,128)(2,1)}), bf16[4,768,256]{2,1,0:T(8,128)(2,1)S(1)}, u32[]{:S(2)}, u32[]{:S(2)}) async-start(bf16[4,768,256]{2,1,0:T(8,128)(2,1)} %bitcast.141), calls=%async_computation.4 | async-start | bytes 3145728 | tf_op jit(solution)/shard_map/all_to_all | solution.py:460
  250.0 16.7 %all-to-all-done.4 = bf16[4,768,256]{2,1,0:T(8,128)(2,1)S(1)} async-done(((bf16[4,768,256]{2,1,0:T(8,128)(2,1)}), bf16[4,768,256]{2,1,0:T(8,128)(2,1)S(1)}, u32[]{:S(2)}, u32[]{:S(2)}) %all-to-all-start.4) | async-done | bytes 1572896 | tf_op jit(solution)/shard_map/all_to_all | solution.py:460
  268.4 3.6 all-to-all-start.5
  272.2 7.2 %all-to-all-done.5 = f32[4,128,256]{2,1,0:T(8,128)S(1)} async-done(((f32[4,128,256]{2,1,0:T(8,128)}), f32[4,128,256]{2,1,0:T(8,128)S(1)}, u32[]{:S(2)}, u32[]{:S(2)}) %all-to-all-start.5) | async-done | bytes 524320 | tf_op jit(solution)/shard_map/all_to_all | solution.py:465
  281.5 3.7 all-to-all-start.6
  285.4 9.0 %all-to-all-done.6 = bf16[4,3,128,256]{3,2,1,0:T(8,128)(2,1)S(1)} async-done(((bf16[4,3,128,256]{3,2,1,0:T(8,128)(2,1)}), bf16[4,3,128,256]{3,2,1,0:T(8,128)(2,1)S(1)}, u32[]{:S(2)}, u32[]{:S(2)}) %all-to-all-start.6) | async-done | bytes 786464 | tf_op jit(solution)/shard_map/all_to_all | solution.py:341
  296.8 3.6 all-to-all-start.9
  301.7 16.6 %all-to-all-done.9 = bf16[4,768,256]{2,1,0:T(8,128)(2,1)S(1)} async-done(((bf16[4,768,256]{2,1,0:T(8,128)(2,1)}), bf16[4,768,256]{2,1,0:T(8,128)(2,1)S(1)}, u32[]{:S(2)}, u32[]{:S(2)}) %all-to-all-start.9) | async-done | bytes 1572896 | tf_op jit(solution)/shard_map/all_to_all | solution.py:341
  318.3 5.4 %all-to-all-start.7 = ((bf16[8,64,256]{2,1,0:T(8,128)(2,1)}), bf16[8,64,256]{2,1,0:T(8,128)(2,1)S(1)}, u32[]{:S(2)}, u32[]{:S(2)}) async-start(bf16[8,64,256]{2,1,0:T(8,128)(2,1)} %bitcast.31), calls=%async_computation.7 | async-start | bytes 524288 | tf_op jit(solution)/shard_map/all_to_all | solution.py:350
  327.3 6.2 %all-to-all-done.7 = bf16[8,64,256]{2,1,0:T(8,128)(2,1)S(1)} async-done(((bf16[8,64,256]{2,1,0:T(8,128)(2,1)}), bf16[8,64,256]{2,1,0:T(8,128)(2,1)S(1)}, u32[]{:S(2)}, u32[]{:S(2)}) %all-to-all-start.7) | async-done | bytes 262176 | tf_op jit(solution)/shard_map/all_to_all | solution.py:350
  337.0 9.6 %all-to-all-done.10 = bf16[8,64,256]{2,1,0:T(8,128)(2,1)S(1)} async-done(((bf16[8,64,256]{2,1,0:T(8,128)(2,1)}), bf16[8,64,256]{2,1,0:T(8,128)(2,1)S(1)}, u32[]{:S(2)}, u32[]{:S(2)}) %all-to-all-start.10) | async-done | bytes 262176 | tf_op jit(solution)/shard_map/all_to_all | solution.py:350
  351.0 15.2 %all-to-all-done.8 = f32[8,64,256]{2,1,0:T(8,128)S(1)} async-done(((f32[8,64,256]{2,1,0:T(8,128)}), f32[8,64,256]{2,1,0:T(8,128)S(1)}, u32[]{:S(2)}, u32[]{:S(2)}) %all-to-all-start.8) | async-done | bytes 524320 | tf_op jit(solution)/shard_map/all_to_all | solution.py:341
  371.4 14.4 %all-to-all-done.11 = f32[8,64,256]{2,1,0:T(8,128)S(1)} async-done(((f32[8,64,256]{2,1,0:T(8,128)}), f32[8,64,256]{2,1,0:T(8,128)S(1)}, u32[]{:S(2)}, u32[]{:S(2)}) %all-to-all-start.11) | async-done | bytes 524320 | tf_op jit(solution)/shard_map/all_to_all | solution.py:341
  (113 shorter events, 44.9 us)
Async XLA Ops:
  0.6 278.9 %copy-start = (bf16[256,256]{1,0:T(8,128)(2,1)S(1)}, bf16[256,256]{1,0:T(8,128)(2,1)}, u32[]{:S(2)}) copy-start(bf16[256,256]{1,0:T(8,128)(2,1)} %param.26) | copy-start | bytes 393220
  3.3 12.2 %all-to-all-start = ((s32[8,1,1536]{2,1,0:T(1,128)}), s32[8,1,1536]{2,1,0:T(1,128)S(1)}, u32[]{:S(2)}, u32[]{:S(2)}) async-start(s32[8,1,1536]{2,1,0:T(1,128)} %bitcast.161), calls=%async_computation | async-start | bytes 98304 | tf_op jit(solution)/shard_map/all_to_all | solution.py:387
  16.0 38.2 %all-to-all-start.2 = ((s32[4,11,128]{2,1,0:T(8,128)}), s32[4,11,128]{2,1,0:T(8,128)S(1)}, u32[]{:S(2)}, u32[]{:S(2)}) async-start(s32[4,11,128]{2,1,0:T(8,128)} %broadcast_in_dim.38), calls=%async_computation.2 | async-start | bytes 65536 | tf_op jit(solution)/shard_map/all_to_all | solution.py:341
  54.2 4.6 %copy-start.6 = (s32[8,128]{1,0:T(8,128)S(1)}, s32[8,128]{1,0:T(8,128)}, u32[]{:S(2)}) copy-start(s32[8,128]{1,0:T(8,128)} %get-tuple-element.20) | copy-start | bytes 12292
  54.2 6.3 %copy-start.3 = (s32[48,128]{1,0:T(8,128)S(1)}, s32[48,128]{1,0:T(8,128)}, u32[]{:S(2)}) copy-start(s32[48,128]{1,0:T(8,128)} %get-tuple-element.25) | copy-start | bytes 73732
  54.2 6.3 %copy-start.5 = (s32[1,6144,1]{1,2,0:T(1,128)S(1)}, s32[1,6144,1]{1,2,0:T(1,128)}, u32[]{:S(2)}) copy-start(s32[1,6144,1]{1,2,0:T(1,128)} %param.15) | copy-start | bytes 73732
  54.2 7.3 %copy-start.4 = (s32[1,3072]{1,0:T(1,128)S(1)}, s32[1,3072]{1,0:T(1,128)}, u32[]{:S(2)}) copy-start(s32[1,3072]{1,0:T(1,128)} %param.18) | copy-start | bytes 36868
  54.3 90.7 %all-to-all-start.1 = ((bf16[8,768,256]{2,1,0:T(8,128)(2,1)}), bf16[8,768,256]{2,1,0:T(8,128)(2,1)}, u32[]{:S(2)}, u32[]{:S(2)}) async-start(bf16[8,768,256]{2,1,0:T(8,128)(2,1)} %lookup.3), calls=%async_computation.1 | async-start | bytes 6291456 | tf_op jit(solution)/shard_map/all_to_all | solution.py:393
  60.5 1.7 copy-start.8
  144.9 76.5 %all-to-all-start.3 = ((bf16[8,768,256]{2,1,0:T(8,128)(2,1)}), bf16[8,768,256]{2,1,0:T(8,128)(2,1)S(1)}, u32[]{:S(2)}, u32[]{:S(2)}) async-start(bf16[8,768,256]{2,1,0:T(8,128)(2,1)} %lookup.2), calls=%async_computation.3 | async-start | bytes 6291456 | tf_op jit(solution)/shard_map/all_to_all | solution.py:432
  243.5 4.2 %copy-start.9 = (s32[1,128]{1,0:T(1,128)S(1)}, s32[1,128]{1,0:T(1,128)}, u32[]{:S(2)}) copy-start(s32[1,128]{1,0:T(1,128)} %param.20) | copy-start | bytes 1540
  243.5 23.3 %all-to-all-start.4 = ((bf16[4,768,256]{2,1,0:T(8,128)(2,1)}), bf16[4,768,256]{2,1,0:T(8,128)(2,1)S(1)}, u32[]{:S(2)}, u32[]{:S(2)}) async-start(bf16[4,768,256]{2,1,0:T(8,128)(2,1)} %bitcast.141), calls=%async_computation.4 | async-start | bytes 3145728 | tf_op jit(solution)/shard_map/all_to_all | solution.py:460
  247.8 19.1 %copy-start.10 = (f32[256]{0:T(256)S(1)}, f32[256]{0:T(256)}, u32[]{:S(2)}) copy-start(f32[256]{0:T(256)} %param.24) | copy-start | bytes 3076
  267.2 4.8 %copy-start.2 = (bf16[256,256]{1,0:T(8,128)(2,1)S(1)}, bf16[256,256]{1,0:T(8,128)(2,1)}, u32[]{:S(2)}) copy-start(bf16[256,256]{1,0:T(8,128)(2,1)} %param.25) | copy-start | bytes 393220
  268.4 11.2 %copy-start.11 = (bf16[1,128,256]{2,1,0:T(8,128)(2,1)S(1)}, bf16[1,128,256]{2,1,0:T(8,128)(2,1)}, u32[]{:S(2)}) copy-start(bf16[1,128,256]{2,1,0:T(8,128)(2,1)} %param.21) | copy-start | bytes 196612
  268.4 11.2 %copy-start.12 = (f32[256]{0:T(256)S(1)}, f32[256]{0:T(256)}, u32[]{:S(2)}) copy-start(f32[256]{0:T(256)} %param.27) | copy-start | bytes 3076
  268.4 11.0 %all-to-all-start.5 = ((f32[4,128,256]{2,1,0:T(8,128)}), f32[4,128,256]{2,1,0:T(8,128)S(1)}, u32[]{:S(2)}, u32[]{:S(2)}) async-start(f32[4,128,256]{2,1,0:T(8,128)} %bitcast.20), calls=%async_computation.5 | async-start | bytes 1048576 | tf_op jit(solution)/shard_map/all_to_all | solution.py:465
  281.5 12.9 %all-to-all-start.6 = ((bf16[4,3,128,256]{3,2,1,0:T(8,128)(2,1)}), bf16[4,3,128,256]{3,2,1,0:T(8,128)(2,1)S(1)}, u32[]{:S(2)}, u32[]{:S(2)}) async-start(bf16[4,3,128,256]{3,2,1,0:T(8,128)(2,1)} %broadcast_in_dim.43), calls=%async_computation.6 | async-start | bytes 1572864 | tf_op jit(solution)/shard_map/all_to_all | solution.py:341
  296.8 21.5 %all-to-all-start.9 = ((bf16[4,768,256]{2,1,0:T(8,128)(2,1)}), bf16[4,768,256]{2,1,0:T(8,128)(2,1)S(1)}, u32[]{:S(2)}, u32[]{:S(2)}) async-start(bf16[4,768,256]{2,1,0:T(8,128)(2,1)} %broadcast_in_dim.45), calls=%async_computation.9 | async-start | bytes 3145728 | tf_op jit(solution)/shard_map/all_to_all | solution.py:341
  318.3 15.2 %all-to-all-start.7 = ((bf16[8,64,256]{2,1,0:T(8,128)(2,1)}), bf16[8,64,256]{2,1,0:T(8,128)(2,1)S(1)}, u32[]{:S(2)}, u32[]{:S(2)}) async-start(bf16[8,64,256]{2,1,0:T(8,128)(2,1)} %bitcast.31), calls=%async_computation.7 | async-start | bytes 524288 | tf_op jit(solution)/shard_map/all_to_all | solution.py:350
  323.8 2.2 copy-start.13
  333.5 13.1 %all-to-all-start.10 = ((bf16[8,64,256]{2,1,0:T(8,128)(2,1)}), bf16[8,64,256]{2,1,0:T(8,128)(2,1)S(1)}, u32[]{:S(2)}, u32[]{:S(2)}) async-start(bf16[8,64,256]{2,1,0:T(8,128)(2,1)} %bitcast.37), calls=%async_computation.10 | async-start | bytes 524288 | tf_op jit(solution)/shard_map/all_to_all | solution.py:350
  347.4 18.8 %all-to-all-start.8 = ((f32[8,64,256]{2,1,0:T(8,128)}), f32[8,64,256]{2,1,0:T(8,128)S(1)}, u32[]{:S(2)}, u32[]{:S(2)}) async-start(f32[8,64,256]{2,1,0:T(8,128)} %broadcast_in_dim.44), calls=%async_computation.8 | async-start | bytes 1048576 | tf_op jit(solution)/shard_map/all_to_all | solution.py:341
  367.1 18.8 %all-to-all-start.11 = ((f32[8,64,256]{2,1,0:T(8,128)}), f32[8,64,256]{2,1,0:T(8,128)S(1)}, u32[]{:S(2)}, u32[]{:S(2)}) async-start(f32[8,64,256]{2,1,0:T(8,128)} %broadcast_in_dim.78), calls=%async_computation.11 | async-start | bytes 1048576 | tf_op jit(solution)/shard_map/all_to_all | solution.py:341
  (2 other events, 3.4 us)

commit v3 on v2

--- a/solution.py
+++ b/solution.py
@@ -16,6 +16,7 @@
 VMEM_BYTES = 56 * 1024 * 1024
 VMEM = pl.BlockSpec(memory_space=pltpu.VMEM)
 SMEM = pl.BlockSpec(memory_space=pltpu.SMEM)
+ANY = pl.BlockSpec(memory_space=pl.ANY)
 
 
 def silu_grad(values):
@@ -117,9 +118,10 @@
 
     @pl.loop(0, width // SLOTS)
     def _(j):
+        at = [want_ref[group, first + j * SLOTS + u] for u in range(SLOTS)]
+        rows = [table[a] for a in at]
         for u in range(SLOTS):
-            at = j * SLOTS + u
-            lines[at] = table[want_ref[group, first + at]]
+            lines[j * SLOTS + u] = rows[u]
 
     for h in range(halves):
         out_ref[0, :, lane(h)] = lines[:, h, :].astype(jnp.bfloat16)
@@ -193,18 +195,26 @@
     )(near, table)
 
 
-def collect(piece, counts_ref, starts_ref, answer_ref, packed):
+def collect(piece, counts_ref, starts_ref, answer_ref, landed, arrived, packed):
     batch_count = answer_ref.shape[0]
+
+    def bring(o):
+        return pltpu.make_async_copy(answer_ref.at[o], landed.at[o], arrived.at[o])
 
     @pl.loop(0, batch_count)
     def _(o):
+        bring(o).start()
+
+    @pl.loop(0, batch_count)
+    def _(o):
+        bring(o).wait()
         base = starts_ref[o]
 
         @pl.loop(0, pl.cdiv(counts_ref[o], piece))
         def _(c):
             source = pl.ds(pl.multiple_of(c * piece, piece), piece)
             target = pl.ds(pl.multiple_of(base + c * piece, SLOTS), piece)
-            packed[target, :] = answer_ref[o, source, :]
+            packed[target, :] = landed[o, source, :]
 
     end = starts_ref[batch_count]
     packed[pl.ds(pl.multiple_of(end, SLOTS), WIDE * TILE), :] = jnp.zeros(
@@ -217,9 +227,9 @@
 ):
     if last:
         (total_in, own_in, deg_ref, wself_ref, wneigh_ref, own_ref, mean_ref, share_ref) = refs[:8]
-        packed, tiles_ref, ready, found_ref, total_ref = refs[8:]
+        packed, tiles_ref, ready, found_ref, landed, arrived, total_ref = refs[8:]
     else:
-        total_ref, own_ref, packed, tiles_ref, ready, found_ref = refs
+        total_ref, own_ref, packed, tiles_ref, ready, found_ref, landed, arrived = refs
     nodes = own_ref.shape[0]
     rows = math.gcd(nodes, 3 * TILE)
     begin, count = spans_ref[0], spans_ref[1]
@@ -233,7 +243,7 @@
     def _():
         fetch(0, 0).start()
 
-    collect(piece, counts_ref, starts_ref, answer_ref, packed)
+    collect(piece, counts_ref, starts_ref, answer_ref, landed, arrived, packed)
 
     @pl.loop(0, nodes // TILE)
     def _(r):
@@ -295,13 +305,15 @@
     piece = LANES if width % LANES == 0 else SLOTS
     last = rest is not None
     room = min(batch_count * width, inputs) + SLOTS * batch_count + 2 * WIDE * TILE
-    in_specs = [SMEM, SMEM, SMEM, VMEM, VMEM, pl.BlockSpec(memory_space=pl.ANY)]
+    in_specs = [SMEM, SMEM, SMEM, ANY, VMEM, ANY]
     rows = lambda dtype: jax.ShapeDtypeStruct((nodes, features), dtype)
     scratch = [
         pltpu.VMEM((room, features), jnp.bfloat16),
         pltpu.VMEM((2, WIDE, nodes, TILE), adj.dtype),
         pltpu.SemaphoreType.DMA((2,)),
         pltpu.VMEM((nodes, features), jnp.float32),
+        pltpu.VMEM(answer.shape, answer.dtype),
+        pltpu.SemaphoreType.DMA((batch_count,)),
     ]
     operands = [answer, column, adj]
     if last:
@@ -331,16 +343,38 @@
     others = array.shape[0] - seeds
     own, rest = seeds // parts, others // parts
     tail = array.shape[1:]
-    return jnp.concatenate(
+    blocks = jnp.concatenate(
         [array[:seeds].reshape(parts, own, *tail), array[seeds:].reshape(parts, rest, *tail)],
         axis=1,
-    ).reshape(array.shape)
+    )
+    return ahead(blocks).reshape(array.shape)
 
 
 def spread(part, axis, count):
     return lax.all_to_all(
         jnp.broadcast_to(part[None], (count,) + part.shape), axis, 0, 0, tiled=True
     )
+
+
+def passed(part, shift):
+    parts = lax.axis_size("feat")
+    return lax.ppermute(part, "feat", [((i + shift) % parts, i) for i in range(parts)])
+
+
+def ahead(array):
+    parts = lax.axis_size("feat")
+    twice = jnp.concatenate([array, array], axis=0)
+    return lax.dynamic_slice_in_dim(twice, lax.axis_index("feat"), parts, 0)
+
+
+def spread_parts(part):
+    return [part] + [passed(part, j) for j in range(1, lax.axis_size("feat"))]
+
+
+def sum_parts(blocks):
+    parts = lax.axis_size("feat")
+    came = [blocks[0]] + [passed(blocks[j], -j) for j in range(1, parts)]
+    return sum(x.astype(jnp.float32) for x in came)
 
 
 def total_over_batch(one, two):
@@ -420,7 +454,7 @@
     fanout_two = nbr_two.shape[2]
     used_two = jnp.arange(fanout_two)[:, None] < deg_two
     lists = jnp.concatenate([jnp.where(used_two, nbr_two[0].T, -1), deg_two], axis=0)
-    lists = spread(lists, "feat", parts)
+    lists = jnp.stack(spread_parts(lists))
 
     fanout = nbr_one.shape[2]
     used = jnp.arange(fanout)[None, :] < deg_one[0][:, None]
@@ -457,16 +491,13 @@
         adj,
         (total, own, deg_first, w1_self, w1_neigh),
     )
-    z_parts = lax.all_to_all(z_part.reshape(parts, share, hidden_width), "feat", 0, 0, tiled=True)
-    z_share = jnp.sum(z_parts.astype(jnp.float32), axis=0) + bias_one
+    z_share = sum_parts(z_part.reshape(parts, share, hidden_width)) + bias_one
     hidden = jax.nn.silu(z_share).astype(jnp.bfloat16)
 
     agg_parts = jnp.dot(adj_two, hidden, preferred_element_type=jnp.float32)
-    agg_parts = lax.all_to_all(
-        agg_parts.reshape(parts, seed_rows, hidden_width), "feat", 0, 0, tiled=True
-    )
+    agg_total = sum_parts(agg_parts.reshape(parts, seed_rows, hidden_width))
     deg_second = deg_two[0].astype(jnp.float32)[:, None]
-    agg_two = (jnp.sum(agg_parts, axis=0) / deg_second).astype(jnp.bfloat16)
+    agg_two = (agg_total / deg_second).astype(jnp.bfloat16)
     self_two = hidden[:seed_rows]
     z_two = (
         jnp.dot(self_two, w2_self, preferred_element_type=jnp.float32)
@@ -475,8 +506,8 @@
     )
     activations = jax.nn.silu(z_two).astype(jnp.bfloat16)[None]
     dz_two = (cotangent[0].astype(jnp.float32) * silu_grad(z_two)).astype(jnp.bfloat16)
-    group = spread(jnp.stack([self_two, agg_two, dz_two]), "feat", parts)
-    self_all, agg_all, dz_two_all = (group[:, i].reshape(seeds, hidden_width) for i in range(3))
+    group = jnp.stack(spread_parts(jnp.stack([self_two, agg_two, dz_two])), axis=1)
+    self_all, agg_all, dz_two_all = (x.reshape(seeds, hidden_width) for x in group)
     gw2 = total_over_batch(contract_rows(self_all, dz_two_all), contract_rows(agg_all, dz_two_all))
 
     back = contract_cols(dz_two_all, w2_neigh) / deg_all.astype(jnp.float32)[:, None]
@@ -485,7 +516,7 @@
     dh_share = contract_rows(adj_two, back_high) + contract_rows(adj_two, back_low)
     dh_share = dh_share + jnp.pad(contract_cols(dz_two, w2_self), ((0, rest), (0, 0)))
     dz_share = (dh_share * silu_grad(z_share)).astype(jnp.bfloat16)
-    dz_one = spread(dz_share, "feat", parts).reshape(nodes, hidden_width)
+    dz_one = jnp.concatenate(spread_parts(dz_share))
     gw1 = total_over_batch(contract_rows(self_one, dz_one), contract_rows(agg_one, dz_one))
     return (activations, *gw2, *gw1)
 

time: 388 us -> 365 us (0.941)
  waiting for transfers between devices: 138 us -> 116 us
    ppermute x0 -> x15, waiting for transfers between devices: none -> 37.3 us  [passed(): lax.ppermute(part, 'feat', [((i + shift) % parts, i) for i in range(parts)])]
    all_to_all x5 -> x2, waiting for transfers between devices: 55.3 us -> 29.7 us  [spread(): lax.all_to_all(jnp.broadcast_to(part[None], (count,) + part.shape), axis,...]
    all_to_all x2 -> x0, waiting for transfers between devices: 24 us -> none  [the longest x1 16.7 us: local(): lax.all_to_all(z_part.reshape(parts, share, hidden_width), 'feat', 0, 0,...]
    ppermute x0 -> x15, starting transfers between devices: none -> 17.8 us  [passed(): lax.ppermute(part, 'feat', [((i + shift) % parts, i) for i in range(parts)])]
    all_to_all x5 -> x2, starting transfers between devices: 17.9 us -> 6.98 us  [spread(): lax.all_to_all(jnp.broadcast_to(part[None], (count,) + part.shape), axis,...]
    all_to_all x2 -> x0, starting transfers between devices: 7.81 us -> none  [the longest x1 4.2 us: local(): lax.all_to_all(z_part.reshape(parts, share, hidden_width), 'feat', 0, 0,...]
    all_to_all x2, waiting for transfers between devices: 15.8 us -> 9.71 us  [total_over_batch(): pieces = lax.all_to_all(pieces, 'batch', 0, 0, tiled=True)]
  transfers between devices with their start and end apart: 12 -> 22, of which waited for: 10 -> 15; matrix products, arithmetic and copies ran while one was open for 5% -> 5% of each run, Pallas kernels for 37% -> 31%
where the time goes in v3:
time: 365 us; the launch traced here: 364 us
  Pallas kernels  165 us (45%)
  waiting for transfers between devices  116 us (32%)
  starting transfers between devices  51.6 us (14%)
  local copies, waits for them, and re-layouts  15.5 us (4%)
  other arithmetic  7.67 us (2%)
  matrix products  4.72 us (1%)
    pallas_call x2, Pallas kernels, lookup(): pl.pallas_call(functools.partial(lookup_body, first, width), out_shape=ja...  66 us
    pallas_call x2, Pallas kernels, gather_sum(): pl.pallas_call(functools.partial(gather_sum_body, piece, last), out_shape...  48.5 us
    pallas_call x1, Pallas kernels, adjacency(): pl.pallas_call(functools.partial(adjacency_body, tiles), out_shape=jax.Sh...  48.2 us
    ppermute x15, waiting for transfers between devices, passed(): lax.ppermute(part, 'feat', [((i + shift) % parts, i) for i in range(parts)])  37.3 us
    all_to_all x1, waiting for transfers between devices, local(): lax.all_to_all(looked, 'batch', split_axis=0, concat_axis=0, tiled=True)  35 us
    all_to_all x2, waiting for transfers between devices, spread(): lax.all_to_all(jnp.broadcast_to(part[None], (count,) + part.shape), axis,...  29.7 us
    ppermute x15, starting transfers between devices, passed(): lax.ppermute(part, 'feat', [((i + shift) % parts, i) for i in range(parts)])  17.8 us
    all_to_all x2, starting transfers between devices, total_over_batch(): pieces = lax.all_to_all(pieces, 'batch', 0, 0, tiled=True)  10.9 us
  transfers between devices with their start and end apart: 22, of which 15 were waited for; matrix products, arithmetic and copies ran while one was open for 5% of the time, Pallas kernels for 31%

profile of v3, /device:TPU:0, one launch (start us, length us, event | category | flops | bytes accessed | tf_op | source)
XLA Modules:
  0.0 363.7 jit_solution(649203933477099358)
XLA Ops:
  3.3 6.3 %all-to-all-start = ((s32[8,1,1536]{2,1,0:T(1,128)}), s32[8,1,1536]{2,1,0:T(1,128)S(1)}, u32[]{:S(2)}, u32[]{:S(2)}) async-start(s32[8,1,1536]{2,1,0:T(1,128)} %bitcast.160), calls=%async_computation | async-start | bytes 98304 | tf_op jit(solution)/shard_map/all_to_all | solution.py:421
  10.5 4.9 %all-to-all-done = s32[8,1,1536]{2,1,0:T(1,128)S(1)} async-done(((s32[8,1,1536]{2,1,0:T(1,128)}), s32[8,1,1536]{2,1,0:T(1,128)S(1)}, u32[]{:S(2)}, u32[]{:S(2)}) %all-to-all-start) | async-done | bytes 49184 | tf_op jit(solution)/shard_map/all_to_all | solution.py:421
  16.0 32.9 %lookup.3 = bf16[8,768,256]{2,1,0:T(8,128)(2,1)} custom-call(s32[8,1536]{1,0:T(8,128)} %bitcast.141, bf16[8192,256]{1,0:T(8,128)(2,1)} %store_ref.3), custom_call_target="tpu_custom_call" | custom-call | flops 62914560 | bytes 4194304 | tf_op jit(solution)/shard_map/lookup/pallas_call | solution.py:134
  49.0 4.6 %all-to-all-start.1 = ((bf16[8,768,256]{2,1,0:T(8,128)(2,1)}), bf16[8,768,256]{2,1,0:T(8,128)(2,1)}, u32[]{:S(2)}, u32[]{:S(2)}) async-start(bf16[8,768,256]{2,1,0:T(8,128)(2,1)} %lookup.3), calls=%async_computation.1 | async-start | bytes 6291456 | tf_op jit(solution)/shard_map/all_to_all | solution.py:427
  63.4 33.1 %lookup.2 = bf16[8,768,256]{2,1,0:T(8,128)(2,1)} custom-call(s32[8,1536]{1,0:T(8,128)} %bitcast.142, bf16[8192,256]{1,0:T(8,128)(2,1)} %store_ref.3), custom_call_target="tpu_custom_call" | custom-call | flops 62914560 | bytes 4194304 | tf_op jit(solution)/shard_map/lookup/pallas_call | solution.py:134
  96.5 48.2 %adjacency.1.adj_ref = f8e4m3fn[28,3072,256]{2,1,0:T(32,128)(4,1)} custom-call(s32[192,256]{1,0:T(8,128)} %reshape.252.near_ref, bf16[256,128]{1,0:T(8,128)(2,1)} %pad_maximum_fusion.7.table_ref), custom_call_target="tpu_custom_call" | custom-call | flops 22548578304 | bytes 22020096 | tf_op jit(solution)/shard_map/adjacency/pallas_call | solution.py:183
  144.7 5.0 %all-to-all-start.2 = ((bf16[8,768,256]{2,1,0:T(8,128)(2,1)}), bf16[8,768,256]{2,1,0:T(8,128)(2,1)S(1)}, u32[]{:S(2)}, u32[]{:S(2)}) async-start(bf16[8,768,256]{2,1,0:T(8,128)(2,1)} %lookup.2), calls=%async_computation.2 | async-start | bytes 6291456 | tf_op jit(solution)/shard_map/all_to_all | solution.py:466
  156.2 30.0 %gather_sum.2 = (f32[3072,256]{1,0:T(8,128)}, bf16[3072,256]{1,0:T(8,128)(2,1)}) custom-call(s32[2]{0:T(128)} %pad_add_fusion.5.spans_ref, s32[8]{0:T(128)} %get-tuple-element.54.counts_ref, s32[9]{0:T(128)} %copy-done.11, bf16[8,768,256]{2,1,0:T(8,128)(2,1)} %all-to-all-done.1.answer_ref, s32[3072,1]{1,0:T(8,128)} %bitcast.137, ...), custom_call_target="tpu_custom_call" | custom-call | flops 11274289152 | bytes 11010048 | tf_op jit(solution)/shard_map/gather_sum/pallas_call | solution.py:330
  186.2 35.0 %all-to-all-done.2.answer_ref = bf16[8,768,256]{2,1,0:T(8,128)(2,1)S(1)} async-done(((bf16[8,768,256]{2,1,0:T(8,128)(2,1)}), bf16[8,768,256]{2,1,0:T(8,128)(2,1)S(1)}, u32[]{:S(2)}, u32[]{:S(2)}) %all-to-all-start.2) | async-done | bytes 3145760 | tf_op jit(solution)/shard_map/all_to_all | solution.py:466
  222.9 18.5 %gather_sum.3 = (bf16[3072,256]{1,0:T(8,128)(2,1)}, bf16[3072,256]{1,0:T(8,128)(2,1)}, bf16[3072,256]{1,0:T(8,128)(2,1)}) custom-call(s32[2]{0:T(128)} %pad_add_fusion.4.spans_ref, s32[8]{0:T(128)} %get-tuple-element.55.counts_ref, s32[9]{0:T(128)} %copy-done.10, bf16[8,768,256]{2,1,0:T(8,128)(2,1)} %copy-done.1, s32[3072,1]{1,0:T(8,128)} %bitcast.138, ...), custom_call_target="tpu_custom_call" | custom-call | flops 11274289152 | bytes 11010048 | tf_op jit(solution)/shard_map/gather_sum/pallas_call | solution.py:330
  244.5 2.8 collective-permute-start.5
  249.4 6.3 %collective-permute-done.3 = bf16[768,256]{1,0:T(8,128)(2,1)S(1)} collective-permute-done((bf16[768,256]{1,0:T(8,128)(2,1)S(1)}, bf16[768,256]{1,0:T(8,128)(2,1)S(1)}, u32[]{:S(2)}, u32[]{:S(2)}) %collective-permute-start.3) | collective-permute-done | bytes 393248 | tf_op jit(solution)/shard_map/ppermute | solution.py:361
  255.8 7.0 %collective-permute-done.4 = bf16[768,256]{1,0:T(8,128)(2,1)S(1)} collective-permute-done((bf16[768,256]{1,0:T(8,128)(2,1)S(1)}, bf16[768,256]{1,0:T(8,128)(2,1)S(1)}, u32[]{:S(2)}, u32[]{:S(2)}) %collective-permute-start.4) | collective-permute-done | bytes 393248 | tf_op jit(solution)/shard_map/ppermute | solution.py:361
  267.5 3.6 collective-permute-done.6
  276.7 4.2 %collective-permute-done.9 = bf16[3,128,256]{2,1,0:T(8,128)(2,1)S(1)} collective-permute-done((bf16[3,128,256]{2,1,0:T(8,128)(2,1)S(1)}, bf16[3,128,256]{2,1,0:T(8,128)(2,1)S(1)}, u32[]{:S(2)}, u32[]{:S(2)}) %collective-permute-start.9) | collective-permute-done | bytes 196640 | tf_op jit(solution)/shard_map/ppermute | solution.py:361
  280.9 4.0 %collective-permute-done.10 = bf16[3,128,256]{2,1,0:T(8,128)(2,1)S(1)} collective-permute-done((bf16[3,128,256]{2,1,0:T(8,128)(2,1)S(1)}, bf16[3,128,256]{2,1,0:T(8,128)(2,1)S(1)}, u32[]{:S(2)}, u32[]{:S(2)}) %collective-permute-start.10) | collective-permute-done | bytes 196640 | tf_op jit(solution)/shard_map/ppermute | solution.py:361
  290.3 5.5 %all-to-all-start.3 = ((bf16[8,64,256]{2,1,0:T(8,128)(2,1)}), bf16[8,64,256]{2,1,0:T(8,128)(2,1)S(1)}, u32[]{:S(2)}, u32[]{:S(2)}) async-start(bf16[8,64,256]{2,1,0:T(8,128)(2,1)} %bitcast.37), calls=%async_computation.3 | async-start | bytes 524288 | tf_op jit(solution)/shard_map/all_to_all | solution.py:384
  298.5 7.1 %collective-permute-done.13 = bf16[768,256]{1,0:T(8,128)(2,1)S(1)} collective-permute-done((bf16[768,256]{1,0:T(8,128)(2,1)S(1)}, bf16[768,256]{1,0:T(8,128)(2,1)S(1)}, u32[]{:S(2)}, u32[]{:S(2)}) %collective-permute-start.13) | collective-permute-done | bytes 393248 | tf_op jit(solution)/shard_map/ppermute | solution.py:361
  308.4 5.4 %all-to-all-start.5 = ((bf16[8,64,256]{2,1,0:T(8,128)(2,1)}), bf16[8,64,256]{2,1,0:T(8,128)(2,1)S(1)}, u32[]{:S(2)}, u32[]{:S(2)}) async-start(bf16[8,64,256]{2,1,0:T(8,128)(2,1)} %bitcast.42), calls=%async_computation.5 | async-start | bytes 524288 | tf_op jit(solution)/shard_map/all_to_all | solution.py:384
  313.9 9.7 %all-to-all-done.5 = bf16[8,64,256]{2,1,0:T(8,128)(2,1)S(1)} async-done(((bf16[8,64,256]{2,1,0:T(8,128)(2,1)}), bf16[8,64,256]{2,1,0:T(8,128)(2,1)S(1)}, u32[]{:S(2)}, u32[]{:S(2)}) %all-to-all-start.5) | async-done | bytes 262176 | tf_op jit(solution)/shard_map/all_to_all | solution.py:384
  324.4 3.5 all-to-all-start.4
  328.0 15.2 %all-to-all-done.4 = f32[8,64,256]{2,1,0:T(8,128)S(1)} async-done(((f32[8,64,256]{2,1,0:T(8,128)}), f32[8,64,256]{2,1,0:T(8,128)S(1)}, u32[]{:S(2)}, u32[]{:S(2)}) %all-to-all-start.4) | async-done | bytes 524320 | tf_op jit(solution)/shard_map/all_to_all | solution.py:354
  344.1 3.5 all-to-all-start.6
  348.4 14.4 %all-to-all-done.6 = f32[8,64,256]{2,1,0:T(8,128)S(1)} async-done(((f32[8,64,256]{2,1,0:T(8,128)}), f32[8,64,256]{2,1,0:T(8,128)S(1)}, u32[]{:S(2)}, u32[]{:S(2)}) %all-to-all-start.6) | async-done | bytes 524320 | tf_op jit(solution)/shard_map/all_to_all | solution.py:354
  (139 shorter events, 50.6 us)
Async XLA Ops:
  0.6 271.5 %copy-start = (bf16[256,256]{1,0:T(8,128)(2,1)S(1)}, bf16[256,256]{1,0:T(8,128)(2,1)}, u32[]{:S(2)}) copy-start(bf16[256,256]{1,0:T(8,128)(2,1)} %param.26) | copy-start | bytes 393220
  3.3 12.2 %all-to-all-start = ((s32[8,1,1536]{2,1,0:T(1,128)}), s32[8,1,1536]{2,1,0:T(1,128)S(1)}, u32[]{:S(2)}, u32[]{:S(2)}) async-start(s32[8,1,1536]{2,1,0:T(1,128)} %bitcast.160), calls=%async_computation | async-start | bytes 98304 | tf_op jit(solution)/shard_map/all_to_all | solution.py:421
  49.0 95.7 %all-to-all-start.1 = ((bf16[8,768,256]{2,1,0:T(8,128)(2,1)}), bf16[8,768,256]{2,1,0:T(8,128)(2,1)}, u32[]{:S(2)}, u32[]{:S(2)}) async-start(bf16[8,768,256]{2,1,0:T(8,128)(2,1)} %lookup.3), calls=%async_computation.1 | async-start | bytes 6291456 | tf_op jit(solution)/shard_map/all_to_all | solution.py:427
  53.6 6.3 %collective-permute-start = (s32[11,128]{1,0:T(8,128)S(1)}, s32[11,128]{1,0:T(8,128)S(1)}, u32[]{:S(2)}, u32[]{:S(2)}) collective-permute-start(s32[11,128]{1,0:T(8,128)S(1)} %pad_add_fusion.1), channel_id=1, source_target_pairs={{8,0},{16,8},{24,16},{0,24},{9,1},{17,9},{25,17},{1,25},{10,2},{18... | collective-permute-start | bytes 16904 | tf_op jit(solution)/shard_map/ppermute | solution.py:361
  56.1 3.8 %collective-permute-start.1 = (s32[11,128]{1,0:T(8,128)S(1)}, s32[11,128]{1,0:T(8,128)S(1)}, u32[]{:S(2)}, u32[]{:S(2)}) collective-permute-start(s32[11,128]{1,0:T(8,128)S(1)} %pad_add_fusion.1), channel_id=1, source_target_pairs={{16,0},{24,8},{0,16},{8,24},{17,1},{25,9},{1,17},{9,25},{18,2},{26... | collective-permute-start | bytes 16904 | tf_op jit(solution)/shard_map/ppermute | solution.py:361
  56.6 4.5 %collective-permute-start.2 = (s32[11,128]{1,0:T(8,128)S(1)}, s32[11,128]{1,0:T(8,128)S(1)}, u32[]{:S(2)}, u32[]{:S(2)}) collective-permute-start(s32[11,128]{1,0:T(8,128)S(1)} %pad_add_fusion.1), channel_id=1, source_target_pairs={{24,0},{0,8},{8,16},{16,24},{25,1},{1,9},{9,17},{17,25},{26,2},{2,... | collective-permute-start | bytes 16904 | tf_op jit(solution)/shard_map/ppermute | solution.py:361
  144.7 76.5 %all-to-all-start.2 = ((bf16[8,768,256]{2,1,0:T(8,128)(2,1)}), bf16[8,768,256]{2,1,0:T(8,128)(2,1)S(1)}, u32[]{:S(2)}, u32[]{:S(2)}) async-start(bf16[8,768,256]{2,1,0:T(8,128)(2,1)} %lookup.2), calls=%async_computation.2 | async-start | bytes 6291456 | tf_op jit(solution)/shard_map/all_to_all | solution.py:466
  241.3 21.6 %copy-start.2 = (bf16[3072,256]{1,0:T(8,128)(2,1)S(1)}, bf16[3072,256]{1,0:T(8,128)(2,1)}, u32[]{:S(2)}) copy-start(bf16[3072,256]{1,0:T(8,128)(2,1)} %get-tuple-element.31) | copy-start | bytes 4718596
  242.8 13.0 %collective-permute-start.3 = (bf16[768,256]{1,0:T(8,128)(2,1)S(1)}, bf16[768,256]{1,0:T(8,128)(2,1)S(1)}, u32[]{:S(2)}, u32[]{:S(2)}) collective-permute-start(bf16[768,256]{1,0:T(8,128)(2,1)S(1)} %get-tuple-element.35), channel_id=1, source_target_pairs={{24,0},{0,8},{8,16},{16,24},{25,1},{1,9},{9,17},{17,25},{26,2},{2,... | collective-permute-start | bytes 1179656 | tf_op jit(solution)/shard_map/ppermute | solution.py:361
  244.0 18.8 %collective-permute-start.4 = (bf16[768,256]{1,0:T(8,128)(2,1)S(1)}, bf16[768,256]{1,0:T(8,128)(2,1)S(1)}, u32[]{:S(2)}, u32[]{:S(2)}) collective-permute-start(bf16[768,256]{1,0:T(8,128)(2,1)S(1)} %get-tuple-element.37), channel_id=1, source_target_pairs={{16,0},{24,8},{0,16},{8,24},{17,1},{25,9},{1,17},{9,25},{18,2},{26... | collective-permute-start | bytes 1179656 | tf_op jit(solution)/shard_map/ppermute | solution.py:361
  244.5 18.4 %collective-permute-start.5 = (bf16[768,256]{1,0:T(8,128)(2,1)S(1)}, bf16[768,256]{1,0:T(8,128)(2,1)S(1)}, u32[]{:S(2)}, u32[]{:S(2)}) collective-permute-start(bf16[768,256]{1,0:T(8,128)(2,1)S(1)} %get-tuple-element.36), channel_id=1, source_target_pairs={{8,0},{16,8},{24,16},{0,24},{9,1},{17,9},{25,17},{1,25},{10,2},{18... | collective-permute-start | bytes 1179656 | tf_op jit(solution)/shard_map/ppermute | solution.py:361
  263.7 7.3 %collective-permute-start.6 = (f32[128,256]{1,0:T(8,128)S(1)}, f32[128,256]{1,0:T(8,128)S(1)}, u32[]{:S(2)}, u32[]{:S(2)}) collective-permute-start(f32[128,256]{1,0:T(8,128)S(1)} %get-tuple-element.42), channel_id=1, source_target_pairs={{24,0},{0,8},{8,16},{16,24},{25,1},{1,9},{9,17},{17,25},{26,2},{2,... | collective-permute-start | bytes 393224 | tf_op jit(solution)/shard_map/ppermute | solution.py:361
  265.5 6.5 %collective-permute-start.7 = (f32[128,256]{1,0:T(8,128)S(1)}, f32[128,256]{1,0:T(8,128)S(1)}, u32[]{:S(2)}, u32[]{:S(2)}) collective-permute-start(f32[128,256]{1,0:T(8,128)S(1)} %get-tuple-element.44), channel_id=1, source_target_pairs={{16,0},{24,8},{0,16},{8,24},{17,1},{25,9},{1,17},{9,25},{18,2},{26... | collective-permute-start | bytes 393224 | tf_op jit(solution)/shard_map/ppermute | solution.py:361
  266.0 6.0 %collective-permute-start.8 = (f32[128,256]{1,0:T(8,128)S(1)}, f32[128,256]{1,0:T(8,128)S(1)}, u32[]{:S(2)}, u32[]{:S(2)}) collective-permute-start(f32[128,256]{1,0:T(8,128)S(1)} %get-tuple-element.43), channel_id=1, source_target_pairs={{8,0},{16,8},{24,16},{0,24},{9,1},{17,9},{25,17},{1,25},{10,2},{18... | collective-permute-start | bytes 393224 | tf_op jit(solution)/shard_map/ppermute | solution.py:361
  273.0 7.9 %collective-permute-start.9 = (bf16[3,128,256]{2,1,0:T(8,128)(2,1)S(1)}, bf16[3,128,256]{2,1,0:T(8,128)(2,1)S(1)}, u32[]{:S(2)}, u32[]{:S(2)}) collective-permute-start(bf16[3,128,256]{2,1,0:T(8,128)(2,1)S(1)} %get-tuple-element.46), channel_id=1, source_target_pairs={{8,0},{16,8},{24,16},{0,24},{9,1},{17,9},{25,17},{1,25},{10,2},{18... | collective-permute-start | bytes 589832 | tf_op jit(solution)/shard_map/ppermute | solution.py:361
  275.6 9.2 %collective-permute-start.10 = (bf16[3,128,256]{2,1,0:T(8,128)(2,1)S(1)}, bf16[3,128,256]{2,1,0:T(8,128)(2,1)S(1)}, u32[]{:S(2)}, u32[]{:S(2)}) collective-permute-start(bf16[3,128,256]{2,1,0:T(8,128)(2,1)S(1)} %get-tuple-element.46), channel_id=1, source_target_pairs={{16,0},{24,8},{0,16},{8,24},{17,1},{25,9},{1,17},{9,25},{18,2},{26... | collective-permute-start | bytes 589832 | tf_op jit(solution)/shard_map/ppermute | solution.py:361
  276.2 8.7 %collective-permute-start.11 = (bf16[3,128,256]{2,1,0:T(8,128)(2,1)S(1)}, bf16[3,128,256]{2,1,0:T(8,128)(2,1)S(1)}, u32[]{:S(2)}, u32[]{:S(2)}) collective-permute-start(bf16[3,128,256]{2,1,0:T(8,128)(2,1)S(1)} %get-tuple-element.46), channel_id=1, source_target_pairs={{24,0},{0,8},{8,16},{16,24},{25,1},{1,9},{9,17},{17,25},{26,2},{2,... | collective-permute-start | bytes 589832 | tf_op jit(solution)/shard_map/ppermute | solution.py:361
  286.4 12.1 %collective-permute-start.12 = (bf16[768,256]{1,0:T(8,128)(2,1)S(1)}, bf16[768,256]{1,0:T(8,128)(2,1)S(1)}, u32[]{:S(2)}, u32[]{:S(2)}) collective-permute-start(bf16[768,256]{1,0:T(8,128)(2,1)S(1)} %fusion.2), channel_id=1, source_target_pairs={{8,0},{16,8},{24,16},{0,24},{9,1},{17,9},{25,17},{1,25},{10,2},{18... | collective-permute-start | bytes 1179656 | tf_op jit(solution)/shard_map/ppermute | solution.py:361
  286.9 18.7 %collective-permute-start.13 = (bf16[768,256]{1,0:T(8,128)(2,1)S(1)}, bf16[768,256]{1,0:T(8,128)(2,1)S(1)}, u32[]{:S(2)}, u32[]{:S(2)}) collective-permute-start(bf16[768,256]{1,0:T(8,128)(2,1)S(1)} %fusion.2), channel_id=1, source_target_pairs={{16,0},{24,8},{0,16},{8,24},{17,1},{25,9},{1,17},{9,25},{18,2},{26... | collective-permute-start | bytes 1179656 | tf_op jit(solution)/shard_map/ppermute | solution.py:361
  287.9 17.7 %collective-permute-start.14 = (bf16[768,256]{1,0:T(8,128)(2,1)S(1)}, bf16[768,256]{1,0:T(8,128)(2,1)S(1)}, u32[]{:S(2)}, u32[]{:S(2)}) collective-permute-start(bf16[768,256]{1,0:T(8,128)(2,1)S(1)} %fusion.2), channel_id=1, source_target_pairs={{24,0},{0,8},{8,16},{16,24},{25,1},{1,9},{9,17},{17,25},{26,2},{2,... | collective-permute-start | bytes 1179656 | tf_op jit(solution)/shard_map/ppermute | solution.py:361
  290.3 18.1 %all-to-all-start.3 = ((bf16[8,64,256]{2,1,0:T(8,128)(2,1)}), bf16[8,64,256]{2,1,0:T(8,128)(2,1)S(1)}, u32[]{:S(2)}, u32[]{:S(2)}) async-start(bf16[8,64,256]{2,1,0:T(8,128)(2,1)} %bitcast.37), calls=%async_computation.3 | async-start | bytes 524288 | tf_op jit(solution)/shard_map/all_to_all | solution.py:384
  308.4 15.2 %all-to-all-start.5 = ((bf16[8,64,256]{2,1,0:T(8,128)(2,1)}), bf16[8,64,256]{2,1,0:T(8,128)(2,1)S(1)}, u32[]{:S(2)}, u32[]{:S(2)}) async-start(bf16[8,64,256]{2,1,0:T(8,128)(2,1)} %bitcast.42), calls=%async_computation.5 | async-start | bytes 524288 | tf_op jit(solution)/shard_map/all_to_all | solution.py:384
  324.4 18.8 %all-to-all-start.4 = ((f32[8,64,256]{2,1,0:T(8,128)}), f32[8,64,256]{2,1,0:T(8,128)S(1)}, u32[]{:S(2)}, u32[]{:S(2)}) async-start(f32[8,64,256]{2,1,0:T(8,128)} %broadcast_in_dim.56), calls=%async_computation.4 | async-start | bytes 1048576 | tf_op jit(solution)/shard_map/all_to_all | solution.py:354
  344.1 18.8 %all-to-all-start.6 = ((f32[8,64,256]{2,1,0:T(8,128)}), f32[8,64,256]{2,1,0:T(8,128)S(1)}, u32[]{:S(2)}, u32[]{:S(2)}) async-start(f32[8,64,256]{2,1,0:T(8,128)} %broadcast_in_dim.57), calls=%async_computation.6 | async-start | bytes 1048576 | tf_op jit(solution)/shard_map/all_to_all | solution.py:354
  (15 other events, 121.5 us)

commit v4 on v3

--- a/solution.py
+++ b/solution.py
@@ -12,6 +12,7 @@
 LANES = 128
 SLOTS = 16
 WIDE = 2
+FEW = 16
 TILE_BITS, LANE_BITS, SLOT_BITS = 8, 7, 4
 VMEM_BYTES = 56 * 1024 * 1024
 VMEM = pl.BlockSpec(memory_space=pltpu.VMEM)
@@ -102,7 +103,25 @@
     )(owners, wanted)
 
 
-def lookup_body(first, width, want_ref, store_ref, out_ref, table, lines):
+def joined_body(first, width, want_ref, store_ref, out_ref, table):
+    group = pl.program_id(0)
+    rows_all = store_ref.shape[0]
+
+    @pl.when(group == 0)
+    def _():
+        @pl.loop(0, rows_all // TILE)
+        def _(j):
+            part = pl.ds(pl.multiple_of(j * TILE, TILE), TILE)
+            table[part, :] = store_ref[part, :].astype(jnp.float32)
+
+    @pl.loop(0, width // SLOTS, unroll=2)
+    def _(j):
+        at = [want_ref[group, first + j * SLOTS + u] for u in range(SLOTS)]
+        rows = jnp.concatenate([table[pl.ds(a, 1), :] for a in at], axis=0)
+        out_ref[0, pl.ds(pl.multiple_of(j * SLOTS, SLOTS), SLOTS), :] = rows.astype(jnp.bfloat16)
+
+
+def paired_body(first, width, want_ref, store_ref, out_ref, table, lines):
     group = pl.program_id(0)
     rows_all = store_ref.shape[0]
     halves = store_ref.shape[1] // LANES
@@ -114,30 +133,35 @@
         def _(j):
             part = pl.ds(pl.multiple_of(j * TILE, TILE), TILE)
             for h in range(halves):
-                table[part, h, :] = store_ref[part, lane(h)].astype(jnp.float32)
+                spot = pl.ds(pl.multiple_of(j * TILE * halves, TILE) + h, TILE, stride=halves)
+                table[spot, :] = store_ref[part, lane(h)].astype(jnp.float32)
 
     @pl.loop(0, width // SLOTS)
     def _(j):
         at = [want_ref[group, first + j * SLOTS + u] for u in range(SLOTS)]
-        rows = [table[a] for a in at]
+        spot = lambda a: pl.ds(pl.multiple_of(a * halves, halves), halves)
+        rows = [table[spot(a), :] for a in at]
         for u in range(SLOTS):
-            lines[j * SLOTS + u] = rows[u]
+            lines[spot(j * SLOTS + u), :] = rows[u]
 
     for h in range(halves):
-        out_ref[0, :, lane(h)] = lines[:, h, :].astype(jnp.bfloat16)
-
-
-def lookup(store, received, first, width):
+        out_ref[0, :, lane(h)] = lines[pl.ds(h, width, stride=halves), :].astype(jnp.bfloat16)
+
+
+def lookup(store, received, first, width, paired):
     groups = received.shape[0]
     rows_all, features = store.shape
-    apart = lambda rows: pltpu.VMEM((rows, features // LANES, LANES), jnp.float32)
+    halves = features // LANES
+    apart = lambda rows: pltpu.VMEM((rows * halves, LANES), jnp.float32)
     return pl.pallas_call(
-        functools.partial(lookup_body, first, width),
+        functools.partial(paired_body if paired else joined_body, first, width),
         out_shape=jax.ShapeDtypeStruct((groups, width, features), jnp.bfloat16),
         grid=(groups,),
         in_specs=[SMEM, pl.BlockSpec((rows_all, features), lambda g: (0, 0))],
         out_specs=pl.BlockSpec((1, width, features), lambda g: (g, 0, 0)),
-        scratch_shapes=[apart(rows_all), apart(width)],
+        scratch_shapes=[apart(rows_all), apart(width)]
+        if paired
+        else [pltpu.VMEM((rows_all, features), jnp.float32)],
         compiler_params=params(),
         cost_estimate=cost(groups * width * features * 40, 2 * rows_all * features),
         name="lookup",
@@ -356,24 +380,27 @@
     )
 
 
-def passed(part, shift):
-    parts = lax.axis_size("feat")
-    return lax.ppermute(part, "feat", [((i + shift) % parts, i) for i in range(parts)])
-
-
-def ahead(array):
-    parts = lax.axis_size("feat")
+def passed(part, shift, axis="feat"):
+    parts = lax.axis_size(axis)
+    return lax.ppermute(part, axis, [((i + shift) % parts, i) for i in range(parts)])
+
+
+def turned(array, by):
     twice = jnp.concatenate([array, array], axis=0)
-    return lax.dynamic_slice_in_dim(twice, lax.axis_index("feat"), parts, 0)
-
-
-def spread_parts(part):
-    return [part] + [passed(part, j) for j in range(1, lax.axis_size("feat"))]
-
-
-def sum_parts(blocks):
-    parts = lax.axis_size("feat")
-    came = [blocks[0]] + [passed(blocks[j], -j) for j in range(1, parts)]
+    return lax.dynamic_slice_in_dim(twice, by, array.shape[0], 0)
+
+
+def ahead(array, axis="feat"):
+    return turned(array, lax.axis_index(axis))
+
+
+def spread_parts(part, axis="feat"):
+    return [part] + [passed(part, j, axis) for j in range(1, lax.axis_size(axis))]
+
+
+def sum_parts(blocks, axis="feat"):
+    parts = lax.axis_size(axis)
+    came = [blocks[0]] + [passed(blocks[j], -j, axis) for j in range(1, parts)]
     return sum(x.astype(jnp.float32) for x in came)
 
 
@@ -383,6 +410,21 @@
     pieces = both.reshape(count, both.shape[0] // count, both.shape[1])
     pieces = lax.all_to_all(pieces, "batch", 0, 0, tiled=True)
     total = spread(jnp.sum(pieces.astype(jnp.float32), axis=0), "batch", count)
+    total = total.reshape(both.shape)
+    return total[: one.shape[0]], total[one.shape[0] :]
+
+
+def total_by_permutes(one, two):
+    count = lax.axis_size("batch")
+    if count > FEW:
+        return total_over_batch(one, two)
+    both = jnp.concatenate([one, two]).astype(jnp.bfloat16)
+    pieces = ahead(both.reshape(count, both.shape[0] // count, both.shape[1]), "batch")
+    came = spread_parts(sum_parts(pieces, "batch"), "batch")
+    total = jnp.zeros(pieces.shape, jnp.float32)
+    for j, piece in enumerate(came):
+        spot = (lax.axis_index("batch") + j) % count
+        total = lax.dynamic_update_index_in_dim(total, piece, spot, 0)
     total = total.reshape(both.shape)
     return total[: one.shape[0]], total[one.shape[0] :]
 
@@ -422,10 +464,10 @@
         requests.reshape(batch_count, capacity), "batch", split_axis=0, concat_axis=0, tiled=True
     )
     first = capacity // 2
-    looked_a = lookup(store, received, 0, first)
+    looked_a = lookup(store, received, 0, first, False)
     near_first, looked_a = lax.optimization_barrier((nbr_one[0], looked_a))
     answer_a = lax.all_to_all(looked_a, "batch", split_axis=0, concat_axis=0, tiled=True)
-    looked = lookup(store, received, first, capacity - first)
+    looked = lookup(store, received, first, capacity - first, True)
 
     depth = WIDE * TILE
     steps = -(-(input_count + 2 * (SLOTS - 1) * batch_count + depth - 1) // depth)
@@ -508,7 +550,7 @@
     dz_two = (cotangent[0].astype(jnp.float32) * silu_grad(z_two)).astype(jnp.bfloat16)
     group = jnp.stack(spread_parts(jnp.stack([self_two, agg_two, dz_two])), axis=1)
     self_all, agg_all, dz_two_all = (x.reshape(seeds, hidden_width) for x in group)
-    gw2 = total_over_batch(contract_rows(self_all, dz_two_all), contract_rows(agg_all, dz_two_all))
+    gw2 = total_by_permutes(contract_rows(self_all, dz_two_all), contract_rows(agg_all, dz_two_all))
 
     back = contract_cols(dz_two_all, w2_neigh) / deg_all.astype(jnp.float32)[:, None]
     back_high = back.astype(jnp.bfloat16)

time: 365 us -> 339 us (0.929)
  Pallas kernels: 165 us -> 149 us
  waiting for transfers between devices: 116 us -> 103 us
  starting transfers between devices: 51.6 us -> 56.7 us
    pallas_call x2, Pallas kernels: 66 us -> 49.5 us  [lookup(): pl.pallas_call(functools.partial(paired_body if paired else joined_body,...]
    all_to_all x2 -> x1, waiting for transfers between devices: 29.7 us -> 14.3 us  [spread(): lax.all_to_all(jnp.broadcast_to(part[None], (count,) + part.shape), axis,...]
    ppermute x15 -> x29, starting transfers between devices: 17.8 us -> 32.6 us  [passed(): lax.ppermute(part, axis, [((i + shift) % parts, i) for i in range(parts)])]
    all_to_all x2 -> x1, starting transfers between devices: 10.9 us -> 4.71 us  [total_over_batch(): pieces = lax.all_to_all(pieces, 'batch', 0, 0, tiled=True)]
    ppermute x15 -> x29, waiting for transfers between devices: 37.3 us -> 38.8 us  [passed(): lax.ppermute(part, axis, [((i + shift) % parts, i) for i in range(parts)])]
    unnamed x42 -> x40, local copies, waits for them, and re-layouts: 7.49 us -> 6.66 us
    all_to_all x2 -> x1, waiting for transfers between devices: 9.71 us -> 9.86 us  [total_over_batch(): pieces = lax.all_to_all(pieces, 'batch', 0, 0, tiled=True)]
  transfers between devices with their start and end apart: 22 -> 34, of which waited for: 15 -> 15; matrix products, arithmetic and copies ran while one was open for 5% -> 6% of each run, Pallas kernels for 31% -> 30%
where the time goes in v4:
time: 339 us; the launch traced here: 338 us
  Pallas kernels  149 us (44%)
  waiting for transfers between devices  103 us (30%)
  starting transfers between devices  56.7 us (17%)
  local copies, waits for them, and re-layouts  13.9 us (4%)
  other arithmetic  7.07 us (2%)
  matrix products  6.27 us (2%)
    pallas_call x2, Pallas kernels, lookup(): pl.pallas_call(functools.partial(paired_body if paired else joined_body,...  49.5 us
    pallas_call x2, Pallas kernels, gather_sum(): pl.pallas_call(functools.partial(gather_sum_body, piece, last), out_shape...  48.4 us
    pallas_call x1, Pallas kernels, adjacency(): pl.pallas_call(functools.partial(adjacency_body, tiles), out_shape=jax.Sh...  48.2 us
    ppermute x29, waiting for transfers between devices, passed(): lax.ppermute(part, axis, [((i + shift) % parts, i) for i in range(parts)])  38.8 us
    all_to_all x1, waiting for transfers between devices, local(): lax.all_to_all(looked, 'batch', split_axis=0, concat_axis=0, tiled=True)  35 us
    ppermute x29, starting transfers between devices, passed(): lax.ppermute(part, axis, [((i + shift) % parts, i) for i in range(parts)])  32.6 us
    all_to_all x1, waiting for transfers between devices, spread(): lax.all_to_all(jnp.broadcast_to(part[None], (count,) + part.shape), axis,...  14.3 us
    all_to_all x1, waiting for transfers between devices, total_over_batch(): pieces = lax.all_to_all(pieces, 'batch', 0, 0, tiled=True)  9.86 us
  transfers between devices with their start and end apart: 34, of which 15 were waited for; matrix products, arithmetic and copies ran while one was open for 6% of the time, Pallas kernels for 30%

profile of v4, /device:TPU:0, one launch (start us, length us, event | category | flops | bytes accessed | tf_op | source)
XLA Modules:
  0.0 338.3 jit_solution(5855642244328634609)
XLA Ops:
  3.3 6.3 %all-to-all-start = ((s32[8,1,1536]{2,1,0:T(1,128)}), s32[8,1,1536]{2,1,0:T(1,128)S(1)}, u32[]{:S(2)}, u32[]{:S(2)}) async-start(s32[8,1,1536]{2,1,0:T(1,128)} %bitcast.197), calls=%async_computation | async-start | bytes 98304 | tf_op jit(solution)/shard_map/all_to_all | solution.py:463
  10.5 4.9 %all-to-all-done = s32[8,1,1536]{2,1,0:T(1,128)S(1)} async-done(((s32[8,1,1536]{2,1,0:T(1,128)}), s32[8,1,1536]{2,1,0:T(1,128)S(1)}, u32[]{:S(2)}, u32[]{:S(2)}) %all-to-all-start) | async-done | bytes 49184 | tf_op jit(solution)/shard_map/all_to_all | solution.py:463
  16.0 26.3 %lookup.3 = bf16[8,768,256]{2,1,0:T(8,128)(2,1)} custom-call(s32[8,1536]{1,0:T(8,128)} %bitcast.178, bf16[8192,256]{1,0:T(8,128)(2,1)} %store_ref.3), custom_call_target="tpu_custom_call" | custom-call | flops 62914560 | bytes 4194304 | tf_op jit(solution)/shard_map/lookup/pallas_call | solution.py:156
  42.4 4.6 %all-to-all-start.1 = ((bf16[8,768,256]{2,1,0:T(8,128)(2,1)}), bf16[8,768,256]{2,1,0:T(8,128)(2,1)}, u32[]{:S(2)}, u32[]{:S(2)}) async-start(bf16[8,768,256]{2,1,0:T(8,128)(2,1)} %lookup.3), calls=%async_computation.1 | async-start | bytes 6291456 | tf_op jit(solution)/shard_map/all_to_all | solution.py:469
  56.8 23.2 %lookup.2 = bf16[8,768,256]{2,1,0:T(8,128)(2,1)} custom-call(s32[8,1536]{1,0:T(8,128)} %bitcast.179, bf16[8192,256]{1,0:T(8,128)(2,1)} %store_ref.3), custom_call_target="tpu_custom_call" | custom-call | flops 62914560 | bytes 4194304 | tf_op jit(solution)/shard_map/lookup/pallas_call | solution.py:156
  80.0 48.2 %adjacency.1.adj_ref = f8e4m3fn[28,3072,256]{2,1,0:T(32,128)(4,1)} custom-call(s32[192,256]{1,0:T(8,128)} %reshape.253.near_ref, bf16[256,128]{1,0:T(8,128)(2,1)} %pad_maximum_fusion.7.table_ref), custom_call_target="tpu_custom_call" | custom-call | flops 22548578304 | bytes 22020096 | tf_op jit(solution)/shard_map/adjacency/pallas_call | solution.py:207
  128.2 5.0 %all-to-all-start.2 = ((bf16[8,768,256]{2,1,0:T(8,128)(2,1)}), bf16[8,768,256]{2,1,0:T(8,128)(2,1)S(1)}, u32[]{:S(2)}, u32[]{:S(2)}) async-start(bf16[8,768,256]{2,1,0:T(8,128)(2,1)} %lookup.2), calls=%async_computation.2 | async-start | bytes 6291456 | tf_op jit(solution)/shard_map/all_to_all | solution.py:508
  139.8 30.0 %gather_sum.2 = (f32[3072,256]{1,0:T(8,128)}, bf16[3072,256]{1,0:T(8,128)(2,1)}) custom-call(s32[2]{0:T(128)} %pad_add_fusion.5.spans_ref, s32[8]{0:T(128)} %get-tuple-element.63.counts_ref, s32[9]{0:T(128)} %copy-done.11, bf16[8,768,256]{2,1,0:T(8,128)(2,1)} %all-to-all-done.1.answer_ref, s32[3072,1]{1,0:T(8,128)} %bitcast.173, ...), custom_call_target="tpu_custom_call" | custom-call | flops 11274289152 | bytes 11010048 | tf_op jit(solution)/shard_map/gather_sum/pallas_call | solution.py:354
  169.8 35.0 %all-to-all-done.2.answer_ref = bf16[8,768,256]{2,1,0:T(8,128)(2,1)S(1)} async-done(((bf16[8,768,256]{2,1,0:T(8,128)(2,1)}), bf16[8,768,256]{2,1,0:T(8,128)(2,1)S(1)}, u32[]{:S(2)}, u32[]{:S(2)}) %all-to-all-start.2) | async-done | bytes 3145760 | tf_op jit(solution)/shard_map/all_to_all | solution.py:508
  206.4 18.5 %gather_sum.3 = (bf16[3072,256]{1,0:T(8,128)(2,1)}, bf16[3072,256]{1,0:T(8,128)(2,1)}, bf16[3072,256]{1,0:T(8,128)(2,1)}) custom-call(s32[2]{0:T(128)} %pad_add_fusion.4.spans_ref, s32[8]{0:T(128)} %get-tuple-element.64.counts_ref, s32[9]{0:T(128)} %copy-done.10, bf16[8,768,256]{2,1,0:T(8,128)(2,1)} %copy-done.1, s32[3072,1]{1,0:T(8,128)} %bitcast.174, ...), custom_call_target="tpu_custom_call" | custom-call | flops 11274289152 | bytes 11010048 | tf_op jit(solution)/shard_map/gather_sum/pallas_call | solution.py:354
  228.1 2.8 collective-permute-start.5
  233.0 6.3 %collective-permute-done.3 = bf16[768,256]{1,0:T(8,128)(2,1)S(1)} collective-permute-done((bf16[768,256]{1,0:T(8,128)(2,1)S(1)}, bf16[768,256]{1,0:T(8,128)(2,1)S(1)}, u32[]{:S(2)}, u32[]{:S(2)}) %collective-permute-start.3) | collective-permute-done | bytes 393248 | tf_op jit(solution)/shard_map/ppermute | solution.py:385
  239.3 7.1 %collective-permute-done.4 = bf16[768,256]{1,0:T(8,128)(2,1)S(1)} collective-permute-done((bf16[768,256]{1,0:T(8,128)(2,1)S(1)}, bf16[768,256]{1,0:T(8,128)(2,1)S(1)}, u32[]{:S(2)}, u32[]{:S(2)}) %collective-permute-start.4) | collective-permute-done | bytes 393248 | tf_op jit(solution)/shard_map/ppermute | solution.py:385
  251.0 3.6 %collective-permute-done.6 = f32[128,256]{1,0:T(8,128)S(1)} collective-permute-done((f32[128,256]{1,0:T(8,128)S(1)}, f32[128,256]{1,0:T(8,128)S(1)}, u32[]{:S(2)}, u32[]{:S(2)}) %collective-permute-start.6) | collective-permute-done | bytes 131104 | tf_op jit(solution)/shard_map/ppermute | solution.py:385
  256.6 2.6 collective-permute-start.9
  260.3 4.2 %collective-permute-done.9 = bf16[3,128,256]{2,1,0:T(8,128)(2,1)S(1)} collective-permute-done((bf16[3,128,256]{2,1,0:T(8,128)(2,1)S(1)}, bf16[3,128,256]{2,1,0:T(8,128)(2,1)S(1)}, u32[]{:S(2)}, u32[]{:S(2)}) %collective-permute-start.9) | collective-permute-done | bytes 196640 | tf_op jit(solution)/shard_map/ppermute | solution.py:385
  264.5 4.0 %collective-permute-done.10 = bf16[3,128,256]{2,1,0:T(8,128)(2,1)S(1)} collective-permute-done((bf16[3,128,256]{2,1,0:T(8,128)(2,1)S(1)}, bf16[3,128,256]{2,1,0:T(8,128)(2,1)S(1)}, u32[]{:S(2)}, u32[]{:S(2)}) %collective-permute-start.10) | collective-permute-done | bytes 196640 | tf_op jit(solution)/shard_map/ppermute | solution.py:385
  285.4 4.3 %collective-permute-done.26 = bf16[768,256]{1,0:T(8,128)(2,1)S(1)} collective-permute-done((bf16[768,256]{1,0:T(8,128)(2,1)S(1)}, bf16[768,256]{1,0:T(8,128)(2,1)S(1)}, u32[]{:S(2)}, u32[]{:S(2)}) %collective-permute-start.26) | collective-permute-done | bytes 393248 | tf_op jit(solution)/shard_map/ppermute | solution.py:385
  289.7 2.9 collective-permute-start.22
  292.6 5.2 %collective-permute-done.27 = bf16[768,256]{1,0:T(8,128)(2,1)S(1)} collective-permute-done((bf16[768,256]{1,0:T(8,128)(2,1)S(1)}, bf16[768,256]{1,0:T(8,128)(2,1)S(1)}, u32[]{:S(2)}, u32[]{:S(2)}) %collective-permute-start.27) | collective-permute-done | bytes 393248 | tf_op jit(solution)/shard_map/ppermute | solution.py:385
  302.7 4.7 %all-to-all-start.3 = ((bf16[8,64,256]{2,1,0:T(8,128)(2,1)}), bf16[8,64,256]{2,1,0:T(8,128)(2,1)S(1)}, u32[]{:S(2)}, u32[]{:S(2)}) async-start(bf16[8,64,256]{2,1,0:T(8,128)(2,1)} %bitcast.58), calls=%async_computation.3 | async-start | bytes 524288 | tf_op jit(solution)/shard_map/all_to_all | solution.py:411
  307.9 9.9 %all-to-all-done.3 = bf16[8,64,256]{2,1,0:T(8,128)(2,1)S(1)} async-done(((bf16[8,64,256]{2,1,0:T(8,128)(2,1)}), bf16[8,64,256]{2,1,0:T(8,128)(2,1)S(1)}, u32[]{:S(2)}, u32[]{:S(2)}) %all-to-all-start.3) | async-done | bytes 262176 | tf_op jit(solution)/shard_map/all_to_all | solution.py:411
  318.7 3.5 %all-to-all-start.4 = ((f32[8,64,256]{2,1,0:T(8,128)}), f32[8,64,256]{2,1,0:T(8,128)S(1)}, u32[]{:S(2)}, u32[]{:S(2)}) async-start(f32[8,64,256]{2,1,0:T(8,128)} %broadcast_in_dim.87), calls=%async_computation.4 | async-start | bytes 1048576 | tf_op jit(solution)/shard_map/all_to_all | solution.py:378
  323.1 14.3 %all-to-all-done.4 = f32[8,64,256]{2,1,0:T(8,128)S(1)} async-done(((f32[8,64,256]{2,1,0:T(8,128)}), f32[8,64,256]{2,1,0:T(8,128)S(1)}, u32[]{:S(2)}, u32[]{:S(2)}) %all-to-all-start.4) | async-done | bytes 524320 | tf_op jit(solution)/shard_map/all_to_all | solution.py:378
  (170 shorter events, 58.3 us)
Async XLA Ops:
  3.3 12.2 %all-to-all-start = ((s32[8,1,1536]{2,1,0:T(1,128)}), s32[8,1,1536]{2,1,0:T(1,128)S(1)}, u32[]{:S(2)}, u32[]{:S(2)}) async-start(s32[8,1,1536]{2,1,0:T(1,128)} %bitcast.197), calls=%async_computation | async-start | bytes 98304 | tf_op jit(solution)/shard_map/all_to_all | solution.py:463
  42.4 85.9 %all-to-all-start.1 = ((bf16[8,768,256]{2,1,0:T(8,128)(2,1)}), bf16[8,768,256]{2,1,0:T(8,128)(2,1)}, u32[]{:S(2)}, u32[]{:S(2)}) async-start(bf16[8,768,256]{2,1,0:T(8,128)(2,1)} %lookup.3), calls=%async_computation.1 | async-start | bytes 6291456 | tf_op jit(solution)/shard_map/all_to_all | solution.py:469
  128.2 76.5 %all-to-all-start.2 = ((bf16[8,768,256]{2,1,0:T(8,128)(2,1)}), bf16[8,768,256]{2,1,0:T(8,128)(2,1)S(1)}, u32[]{:S(2)}, u32[]{:S(2)}) async-start(bf16[8,768,256]{2,1,0:T(8,128)(2,1)} %lookup.2), calls=%async_computation.2 | async-start | bytes 6291456 | tf_op jit(solution)/shard_map/all_to_all | solution.py:508
  226.3 13.0 %collective-permute-start.3 = (bf16[768,256]{1,0:T(8,128)(2,1)S(1)}, bf16[768,256]{1,0:T(8,128)(2,1)S(1)}, u32[]{:S(2)}, u32[]{:S(2)}) collective-permute-start(bf16[768,256]{1,0:T(8,128)(2,1)S(1)} %get-tuple-element.37), channel_id=1, source_target_pairs={{24,0},{0,8},{8,16},{16,24},{25,1},{1,9},{9,17},{17,25},{26,2},{2,... | collective-permute-start | bytes 1179656 | tf_op jit(solution)/shard_map/ppermute | solution.py:385
  227.5 18.8 %collective-permute-start.4 = (bf16[768,256]{1,0:T(8,128)(2,1)S(1)}, bf16[768,256]{1,0:T(8,128)(2,1)S(1)}, u32[]{:S(2)}, u32[]{:S(2)}) collective-permute-start(bf16[768,256]{1,0:T(8,128)(2,1)S(1)} %get-tuple-element.39), channel_id=1, source_target_pairs={{16,0},{24,8},{0,16},{8,24},{17,1},{25,9},{1,17},{9,25},{18,2},{26... | collective-permute-start | bytes 1179656 | tf_op jit(solution)/shard_map/ppermute | solution.py:385
  228.1 18.4 %collective-permute-start.5 = (bf16[768,256]{1,0:T(8,128)(2,1)S(1)}, bf16[768,256]{1,0:T(8,128)(2,1)S(1)}, u32[]{:S(2)}, u32[]{:S(2)}) collective-permute-start(bf16[768,256]{1,0:T(8,128)(2,1)S(1)} %get-tuple-element.38), channel_id=1, source_target_pairs={{8,0},{16,8},{24,16},{0,24},{9,1},{17,9},{25,17},{1,25},{10,2},{18... | collective-permute-start | bytes 1179656 | tf_op jit(solution)/shard_map/ppermute | solution.py:385
  247.3 7.3 %collective-permute-start.6 = (f32[128,256]{1,0:T(8,128)S(1)}, f32[128,256]{1,0:T(8,128)S(1)}, u32[]{:S(2)}, u32[]{:S(2)}) collective-permute-start(f32[128,256]{1,0:T(8,128)S(1)} %get-tuple-element.44), channel_id=1, source_target_pairs={{24,0},{0,8},{8,16},{16,24},{25,1},{1,9},{9,17},{17,25},{26,2},{2,... | collective-permute-start | bytes 393224 | tf_op jit(solution)/shard_map/ppermute | solution.py:385
  249.0 6.5 %collective-permute-start.7 = (f32[128,256]{1,0:T(8,128)S(1)}, f32[128,256]{1,0:T(8,128)S(1)}, u32[]{:S(2)}, u32[]{:S(2)}) collective-permute-start(f32[128,256]{1,0:T(8,128)S(1)} %get-tuple-element.46), channel_id=1, source_target_pairs={{16,0},{24,8},{0,16},{8,24},{17,1},{25,9},{1,17},{9,25},{18,2},{26... | collective-permute-start | bytes 393224 | tf_op jit(solution)/shard_map/ppermute | solution.py:385
  256.6 7.9 %collective-permute-start.9 = (bf16[3,128,256]{2,1,0:T(8,128)(2,1)S(1)}, bf16[3,128,256]{2,1,0:T(8,128)(2,1)S(1)}, u32[]{:S(2)}, u32[]{:S(2)}) collective-permute-start(bf16[3,128,256]{2,1,0:T(8,128)(2,1)S(1)} %get-tuple-element.55), channel_id=1, source_target_pairs={{8,0},{16,8},{24,16},{0,24},{9,1},{17,9},{25,17},{1,25},{10,2},{18... | collective-permute-start | bytes 589832 | tf_op jit(solution)/shard_map/ppermute | solution.py:385
  259.2 9.2 %collective-permute-start.10 = (bf16[3,128,256]{2,1,0:T(8,128)(2,1)S(1)}, bf16[3,128,256]{2,1,0:T(8,128)(2,1)S(1)}, u32[]{:S(2)}, u32[]{:S(2)}) collective-permute-start(bf16[3,128,256]{2,1,0:T(8,128)(2,1)S(1)} %get-tuple-element.55), channel_id=1, source_target_pairs={{16,0},{24,8},{0,16},{8,24},{17,1},{25,9},{1,17},{9,25},{18,2},{26... | collective-permute-start | bytes 589832 | tf_op jit(solution)/shard_map/ppermute | solution.py:385
  259.7 8.7 %collective-permute-start.11 = (bf16[3,128,256]{2,1,0:T(8,128)(2,1)S(1)}, bf16[3,128,256]{2,1,0:T(8,128)(2,1)S(1)}, u32[]{:S(2)}, u32[]{:S(2)}) collective-permute-start(bf16[3,128,256]{2,1,0:T(8,128)(2,1)S(1)} %get-tuple-element.55), channel_id=1, source_target_pairs={{24,0},{0,8},{8,16},{16,24},{25,1},{1,9},{9,17},{17,25},{26,2},{2,... | collective-permute-start | bytes 589832 | tf_op jit(solution)/shard_map/ppermute | solution.py:385
  269.3 7.5 %collective-permute-start.13 = (bf16[64,256]{1,0:T(8,128)(2,1)S(1)}, bf16[64,256]{1,0:T(8,128)(2,1)S(1)}, u32[]{:S(2)}, u32[]{:S(2)}) collective-permute-start(bf16[64,256]{1,0:T(8,128)(2,1)S(1)} %get-tuple-element.52), channel_id=1, source_target_pairs={{6,0},{7,1},{0,2},{1,3},{2,4},{3,5},{4,6},{5,7},{14,8},{15,9},{8,1... | collective-permute-start | bytes 98312 | tf_op jit(solution)/shard_map/ppermute | solution.py:385
  270.1 7.6 %collective-permute-start.14 = (bf16[64,256]{1,0:T(8,128)(2,1)S(1)}, bf16[64,256]{1,0:T(8,128)(2,1)S(1)}, u32[]{:S(2)}, u32[]{:S(2)}) collective-permute-start(bf16[64,256]{1,0:T(8,128)(2,1)S(1)} %get-tuple-element.51), channel_id=1, source_target_pairs={{5,0},{6,1},{7,2},{0,3},{1,4},{2,5},{3,6},{4,7},{13,8},{14,9},{15,... | collective-permute-start | bytes 98312 | tf_op jit(solution)/shard_map/ppermute | solution.py:385
  277.7 12.0 %collective-permute-start.26 = (bf16[768,256]{1,0:T(8,128)(2,1)S(1)}, bf16[768,256]{1,0:T(8,128)(2,1)S(1)}, u32[]{:S(2)}, u32[]{:S(2)}) collective-permute-start(bf16[768,256]{1,0:T(8,128)(2,1)S(1)} %fusion.2), channel_id=1, source_target_pairs={{8,0},{16,8},{24,16},{0,24},{9,1},{17,9},{25,17},{1,25},{10,2},{18... | collective-permute-start | bytes 1179656 | tf_op jit(solution)/shard_map/ppermute | solution.py:385
  278.2 19.6 %collective-permute-start.27 = (bf16[768,256]{1,0:T(8,128)(2,1)S(1)}, bf16[768,256]{1,0:T(8,128)(2,1)S(1)}, u32[]{:S(2)}, u32[]{:S(2)}) collective-permute-start(bf16[768,256]{1,0:T(8,128)(2,1)S(1)} %fusion.2), channel_id=1, source_target_pairs={{16,0},{24,8},{0,16},{8,24},{17,1},{25,9},{1,17},{9,25},{18,2},{26... | collective-permute-start | bytes 1179656 | tf_op jit(solution)/shard_map/ppermute | solution.py:385
  279.3 18.6 %collective-permute-start.28 = (bf16[768,256]{1,0:T(8,128)(2,1)S(1)}, bf16[768,256]{1,0:T(8,128)(2,1)S(1)}, u32[]{:S(2)}, u32[]{:S(2)}) collective-permute-start(bf16[768,256]{1,0:T(8,128)(2,1)S(1)} %fusion.2), channel_id=1, source_target_pairs={{24,0},{0,8},{8,16},{16,24},{25,1},{1,9},{9,17},{17,25},{26,2},{2,... | collective-permute-start | bytes 1179656 | tf_op jit(solution)/shard_map/ppermute | solution.py:385
  282.6 24.8 %collective-permute-start.20 = (f32[64,256]{1,0:T(8,128)S(1)}, f32[64,256]{1,0:T(8,128)S(1)}, u32[]{:S(2)}, u32[]{:S(2)}) collective-permute-start(f32[64,256]{1,0:T(8,128)S(1)} %get-tuple-element.36), channel_id=1, source_target_pairs={{2,0},{3,1},{4,2},{5,3},{6,4},{7,5},{0,6},{1,7},{10,8},{11,9},{12,... | collective-permute-start | bytes 196616 | tf_op jit(solution)/shard_map/ppermute | solution.py:385
  284.9 23.0 %collective-permute-start.21 = (f32[64,256]{1,0:T(8,128)S(1)}, f32[64,256]{1,0:T(8,128)S(1)}, u32[]{:S(2)}, u32[]{:S(2)}) collective-permute-start(f32[64,256]{1,0:T(8,128)S(1)} %get-tuple-element.36), channel_id=1, source_target_pairs={{3,0},{4,1},{5,2},{6,3},{7,4},{0,5},{1,6},{2,7},{11,8},{12,9},{13,... | collective-permute-start | bytes 196616 | tf_op jit(solution)/shard_map/ppermute | solution.py:385
  289.7 18.2 %collective-permute-start.22 = (f32[64,256]{1,0:T(8,128)S(1)}, f32[64,256]{1,0:T(8,128)S(1)}, u32[]{:S(2)}, u32[]{:S(2)}) collective-permute-start(f32[64,256]{1,0:T(8,128)S(1)} %get-tuple-element.36), channel_id=1, source_target_pairs={{4,0},{5,1},{6,2},{7,3},{0,4},{1,5},{2,6},{3,7},{12,8},{13,9},{14,... | collective-permute-start | bytes 196616 | tf_op jit(solution)/shard_map/ppermute | solution.py:385
  297.8 24.3 %collective-permute-start.23 = (f32[64,256]{1,0:T(8,128)S(1)}, f32[64,256]{1,0:T(8,128)S(1)}, u32[]{:S(2)}, u32[]{:S(2)}) collective-permute-start(f32[64,256]{1,0:T(8,128)S(1)} %get-tuple-element.36), channel_id=1, source_target_pairs={{5,0},{6,1},{7,2},{0,3},{1,4},{2,5},{3,6},{4,7},{13,8},{14,9},{15,... | collective-permute-start | bytes 196616 | tf_op jit(solution)/shard_map/ppermute | solution.py:385
  297.8 24.4 %collective-permute-start.24 = (f32[64,256]{1,0:T(8,128)S(1)}, f32[64,256]{1,0:T(8,128)S(1)}, u32[]{:S(2)}, u32[]{:S(2)}) collective-permute-start(f32[64,256]{1,0:T(8,128)S(1)} %get-tuple-element.36), channel_id=1, source_target_pairs={{6,0},{7,1},{0,2},{1,3},{2,4},{3,5},{4,6},{5,7},{14,8},{15,9},{8,1... | collective-permute-start | bytes 196616 | tf_op jit(solution)/shard_map/ppermute | solution.py:385
  302.7 15.2 %all-to-all-start.3 = ((bf16[8,64,256]{2,1,0:T(8,128)(2,1)}), bf16[8,64,256]{2,1,0:T(8,128)(2,1)S(1)}, u32[]{:S(2)}, u32[]{:S(2)}) async-start(bf16[8,64,256]{2,1,0:T(8,128)(2,1)} %bitcast.58), calls=%async_computation.3 | async-start | bytes 524288 | tf_op jit(solution)/shard_map/all_to_all | solution.py:411
  307.4 14.9 %collective-permute-start.25 = (f32[64,256]{1,0:T(8,128)S(1)}, f32[64,256]{1,0:T(8,128)S(1)}, u32[]{:S(2)}, u32[]{:S(2)}) collective-permute-start(f32[64,256]{1,0:T(8,128)S(1)} %get-tuple-element.36), channel_id=1, source_target_pairs={{7,0},{0,1},{1,2},{2,3},{3,4},{4,5},{5,6},{6,7},{15,8},{8,9},{9,10... | collective-permute-start | bytes 196616 | tf_op jit(solution)/shard_map/ppermute | solution.py:385
  318.7 18.8 %all-to-all-start.4 = ((f32[8,64,256]{2,1,0:T(8,128)}), f32[8,64,256]{2,1,0:T(8,128)S(1)}, u32[]{:S(2)}, u32[]{:S(2)}) async-start(f32[8,64,256]{2,1,0:T(8,128)} %broadcast_in_dim.87), calls=%async_computation.4 | async-start | bytes 1048576 | tf_op jit(solution)/shard_map/all_to_all | solution.py:378
  (26 other events, 430.4 us)

commit v5 on v3

--- a/solution.py
+++ b/solution.py
@@ -12,8 +12,9 @@
 LANES = 128
 SLOTS = 16
 WIDE = 2
+FEW = 16
 TILE_BITS, LANE_BITS, SLOT_BITS = 8, 7, 4
-VMEM_BYTES = 56 * 1024 * 1024
+MIB = 1024 * 1024
 VMEM = pl.BlockSpec(memory_space=pltpu.VMEM)
 SMEM = pl.BlockSpec(memory_space=pltpu.SMEM)
 ANY = pl.BlockSpec(memory_space=pl.ANY)
@@ -36,8 +37,8 @@
     )
 
 
-def params(**more):
-    return pltpu.CompilerParams(vmem_limit_bytes=VMEM_BYTES, **more)
+def params(mib):
+    return pltpu.CompilerParams(vmem_limit_bytes=mib * MIB)
 
 
 def cost(flops, moved):
@@ -96,52 +97,54 @@
         ),
         in_specs=[VMEM, VMEM],
         out_specs=(VMEM, VMEM, VMEM),
-        compiler_params=params(),
+        compiler_params=params(16),
         cost_estimate=cost(4 * total * places * LANES, 24 * total),
         name="requests",
     )(owners, wanted)
 
 
-def lookup_body(first, width, want_ref, store_ref, out_ref, table, lines):
-    group = pl.program_id(0)
+def lookup_body(stride, first, width, want_ref, store_ref, out_ref, table, lines):
     rows_all = store_ref.shape[0]
     halves = store_ref.shape[1] // LANES
     lane = lambda h: pl.ds(h * LANES, LANES)
-
-    @pl.when(group == 0)
+    begin = pl.program_id(0) * stride + first
+
+    @pl.when(pl.program_id(0) == 0)
     def _():
         @pl.loop(0, rows_all // TILE)
         def _(j):
             part = pl.ds(pl.multiple_of(j * TILE, TILE), TILE)
             for h in range(halves):
-                table[part, h, :] = store_ref[part, lane(h)].astype(jnp.float32)
-
-    @pl.loop(0, width // SLOTS)
+                spot = pl.ds(pl.multiple_of(j * TILE * halves, TILE) + h, TILE, stride=halves)
+                table[spot, :] = store_ref[part, lane(h)].astype(jnp.float32)
+
+    @pl.loop(0, width // SLOTS, unroll=2)
     def _(j):
-        at = [want_ref[group, first + j * SLOTS + u] for u in range(SLOTS)]
-        rows = [table[a] for a in at]
+        at = [want_ref[begin + j * SLOTS + u] for u in range(SLOTS)]
+        rows = [table[pl.ds(pl.multiple_of(a, halves), halves), :] for a in at]
+        block = lines.at[pl.ds(pl.multiple_of(j * SLOTS * halves, SLOTS * halves), SLOTS * halves)]
         for u in range(SLOTS):
-            lines[j * SLOTS + u] = rows[u]
+            block[pl.ds(u * halves, halves), :] = rows[u]
 
     for h in range(halves):
-        out_ref[0, :, lane(h)] = lines[:, h, :].astype(jnp.bfloat16)
-
-
-def lookup(store, received, first, width):
-    groups = received.shape[0]
+        out_ref[0, :, lane(h)] = lines[pl.ds(h, width, stride=halves), :].astype(jnp.bfloat16)
+
+
+def lookup(store, places, groups, first, width):
     rows_all, features = store.shape
-    apart = lambda rows: pltpu.VMEM((rows, features // LANES, LANES), jnp.float32)
+    halves = features // LANES
+    apart = lambda rows: pltpu.VMEM((rows * halves, LANES), jnp.float32)
     return pl.pallas_call(
-        functools.partial(lookup_body, first, width),
+        functools.partial(lookup_body, places.shape[0] // groups, first, width),
         out_shape=jax.ShapeDtypeStruct((groups, width, features), jnp.bfloat16),
         grid=(groups,),
         in_specs=[SMEM, pl.BlockSpec((rows_all, features), lambda g: (0, 0))],
         out_specs=pl.BlockSpec((1, width, features), lambda g: (g, 0, 0)),
         scratch_shapes=[apart(rows_all), apart(width)],
-        compiler_params=params(),
+        compiler_params=params(24),
         cost_estimate=cost(groups * width * features * 40, 2 * rows_all * features),
         name="lookup",
-    )(received, store)
+    )(places, store)
 
 
 def adjacency_body(tiles, near_ref, table_ref, out_ref):
@@ -189,7 +192,7 @@
             pl.BlockSpec(table.shape, lambda r: (0, 0)),
         ],
         out_specs=pl.BlockSpec((tiles, TILE, TILE), lambda r: (0, r, 0)),
-        compiler_params=params(),
+        compiler_params=params(16),
         cost_estimate=cost(2 * nodes * TILE * TILE * tiles * 2, nodes * TILE * tiles),
         name="adjacency",
     )(near, table)
@@ -226,11 +229,17 @@
     piece, last, spans_ref, counts_ref, starts_ref, answer_ref, column_ref, adj_ref, *refs
 ):
     if last:
-        (total_in, own_in, deg_ref, wself_ref, wneigh_ref, own_ref, mean_ref, share_ref) = refs[:8]
-        packed, tiles_ref, ready, found_ref, landed, arrived, total_ref = refs[8:]
+        (total_in, found_in, deg_ref, wself_ref, wneigh_ref, own_ref, mean_ref) = refs[:7]
+        share_refs = refs[7:-8]
+        packed, tiles_ref, ready, landed, arrived, total_ref, found_ref, carried = refs[-8:]
+        carry = [
+            pltpu.make_async_copy(total_in, total_ref, carried.at[0]),
+            pltpu.make_async_copy(found_in, found_ref, carried.at[1]),
+        ]
     else:
-        total_ref, own_ref, packed, tiles_ref, ready, found_ref, landed, arrived = refs
-    nodes = own_ref.shape[0]
+        total_ref, found_ref, packed, tiles_ref, ready, landed, arrived = refs
+        carry = []
+    nodes = total_ref.shape[0]
     rows = math.gcd(nodes, 3 * TILE)
     begin, count = spans_ref[0], spans_ref[1]
 
@@ -243,17 +252,14 @@
     def _():
         fetch(0, 0).start()
 
+    for copy in carry:
+        copy.start()
     collect(piece, counts_ref, starts_ref, answer_ref, landed, arrived, packed)
-
-    @pl.loop(0, nodes // TILE)
-    def _(r):
-        part = pl.ds(pl.multiple_of(r * TILE, TILE), TILE)
-        if last:
-            total_ref[part, :] = total_in[part, :]
-            found_ref[part, :] = own_in[part, :].astype(jnp.float32)
-        else:
-            total_ref[part, :] = jnp.zeros((TILE, total_ref.shape[1]), jnp.float32)
-            found_ref[part, :] = jnp.zeros((TILE, found_ref.shape[1]), jnp.float32)
+    for copy in carry:
+        copy.wait()
+    if not last:
+        total_ref[...] = jnp.zeros(total_ref.shape, jnp.float32)
+        found_ref[...] = jnp.zeros(found_ref.shape, jnp.float32)
 
     @pl.loop(0, count)
     def _(step):
@@ -281,25 +287,23 @@
             total_ref[part, :] += both[:rows]
             found_ref[part, :] += both[rows:]
 
-    @pl.loop(0, nodes // TILE)
-    def _(r):
-        part = pl.ds(pl.multiple_of(r * TILE, TILE), TILE)
-        own_ref[part, :] = found_ref[part, :].astype(jnp.bfloat16)
-
     if last:
-
-        @pl.loop(0, nodes // TILE)
-        def _(r):
-            part = pl.ds(pl.multiple_of(r * TILE, TILE), TILE)
-            mean = (total_ref[part, :] / deg_ref[part, :]).astype(jnp.bfloat16)
-            mean_ref[part, :] = mean
-            share_ref[part, :] = (
-                jnp.dot(own_ref[part, :], wself_ref[...], preferred_element_type=jnp.float32)
-                + jnp.dot(mean, wneigh_ref[...], preferred_element_type=jnp.float32)
-            ).astype(share_ref.dtype)
-
-
-def gather_sum(inputs, spans, counts, starts, answer, column, adj, rest, share_type=jnp.bfloat16):
+        share = share_refs[0].shape[0]
+        step_rows = math.gcd(share, 3 * TILE)
+        for p, share_ref in enumerate(share_refs):
+            for r in range(share // step_rows):
+                part = pl.ds(p * share + r * step_rows, step_rows)
+                own = found_ref[part, :].astype(jnp.bfloat16)
+                mean = (total_ref[part, :] / deg_ref[part, :]).astype(jnp.bfloat16)
+                own_ref[part, :] = own
+                mean_ref[part, :] = mean
+                share_ref[pl.ds(r * step_rows, step_rows), :] = (
+                    jnp.dot(own, wself_ref[...], preferred_element_type=jnp.float32)
+                    + jnp.dot(mean, wneigh_ref[...], preferred_element_type=jnp.float32)
+                ).astype(share_ref.dtype)
+
+
+def gather_sum(inputs, parts, spans, counts, starts, answer, column, adj, rest):
     batch_count, width, features = answer.shape
     tiles, nodes, _ = adj.shape
     piece = LANES if width % LANES == 0 else SLOTS
@@ -311,29 +315,26 @@
         pltpu.VMEM((room, features), jnp.bfloat16),
         pltpu.VMEM((2, WIDE, nodes, TILE), adj.dtype),
         pltpu.SemaphoreType.DMA((2,)),
-        pltpu.VMEM((nodes, features), jnp.float32),
         pltpu.VMEM(answer.shape, answer.dtype),
         pltpu.SemaphoreType.DMA((batch_count,)),
     ]
     operands = [answer, column, adj]
     if last:
         operands += list(rest)
-        in_specs += [VMEM] * len(rest)
-        out_shape = (
-            rows(jnp.bfloat16),
-            rows(jnp.bfloat16),
-            jax.ShapeDtypeStruct((nodes, rest[3].shape[1]), share_type),
-        )
-        scratch += [pltpu.VMEM((nodes, features), jnp.float32)]
+        in_specs += [ANY, ANY, VMEM, VMEM, VMEM]
+        share = jax.ShapeDtypeStruct((nodes // parts, rest[3].shape[1]), jnp.bfloat16)
+        out_shape = (rows(jnp.bfloat16), rows(jnp.bfloat16)) + (share,) * parts
+        scratch += [pltpu.VMEM((nodes, features), jnp.float32)] * 2
+        scratch += [pltpu.SemaphoreType.DMA((2,))]
     else:
-        out_shape = (rows(jnp.float32), rows(jnp.bfloat16))
+        out_shape = (rows(jnp.float32), rows(jnp.float32))
     return pl.pallas_call(
         functools.partial(gather_sum_body, piece, last),
         out_shape=out_shape,
         in_specs=in_specs,
         out_specs=(VMEM,) * len(out_shape),
         scratch_shapes=scratch,
-        compiler_params=params(),
+        compiler_params=params(40),
         cost_estimate=cost(2 * nodes * features * TILE * tiles, nodes * TILE * tiles // 2),
         name="gather_sum",
     )(spans, counts, starts, *operands)
@@ -356,35 +357,53 @@
     )
 
 
-def passed(part, shift):
-    parts = lax.axis_size("feat")
-    return lax.ppermute(part, "feat", [((i + shift) % parts, i) for i in range(parts)])
-
-
-def ahead(array):
-    parts = lax.axis_size("feat")
+def passed(part, shift, axis="feat"):
+    parts = lax.axis_size(axis)
+    return lax.ppermute(part, axis, [((i + shift) % parts, i) for i in range(parts)])
+
+
+def turned(array, by):
     twice = jnp.concatenate([array, array], axis=0)
-    return lax.dynamic_slice_in_dim(twice, lax.axis_index("feat"), parts, 0)
-
-
-def spread_parts(part):
-    return [part] + [passed(part, j) for j in range(1, lax.axis_size("feat"))]
-
-
-def sum_parts(blocks):
-    parts = lax.axis_size("feat")
-    came = [blocks[0]] + [passed(blocks[j], -j) for j in range(1, parts)]
+    return lax.dynamic_slice_in_dim(twice, by, array.shape[0], 0)
+
+
+def ahead(array, axis="feat"):
+    return turned(array, lax.axis_index(axis))
+
+
+def spread_parts(part, axis="feat"):
+    return [part] + [passed(part, j, axis) for j in range(1, lax.axis_size(axis))]
+
+
+def sum_parts(blocks, axis="feat"):
+    parts = lax.axis_size(axis)
+    came = [blocks[0]] + [passed(blocks[j], -j, axis) for j in range(1, parts)]
     return sum(x.astype(jnp.float32) for x in came)
 
 
-def total_over_batch(one, two):
+def batch_pieces(one, two):
+    both = jnp.concatenate([one, two]).astype(jnp.bfloat16)
     count = lax.axis_size("batch")
-    both = jnp.concatenate([one, two]).astype(jnp.bfloat16)
-    pieces = both.reshape(count, both.shape[0] // count, both.shape[1])
+    return both.reshape(count, both.shape[0] // count, both.shape[1])
+
+
+def halves_of(total):
+    total = total.reshape(-1, total.shape[-1])
+    return total[: total.shape[0] // 2], total[total.shape[0] // 2 :]
+
+
+def reduce_pieces(pieces):
     pieces = lax.all_to_all(pieces, "batch", 0, 0, tiled=True)
-    total = spread(jnp.sum(pieces.astype(jnp.float32), axis=0), "batch", count)
-    total = total.reshape(both.shape)
-    return total[: one.shape[0]], total[one.shape[0] :]
+    return jnp.sum(pieces.astype(jnp.float32), axis=0)
+
+
+def placed(blocks, axis):
+    count = lax.axis_size(axis)
+    total = jnp.zeros((count,) + blocks[0].shape, blocks[0].dtype)
+    for j, block in enumerate(blocks):
+        spot = (lax.axis_index(axis) + j) % count
+        total = lax.dynamic_update_index_in_dim(total, block, spot, 0)
+    return total
 
 
 def local(
@@ -422,10 +441,11 @@
         requests.reshape(batch_count, capacity), "batch", split_axis=0, concat_axis=0, tiled=True
     )
     first = capacity // 2
-    looked_a = lookup(store, received, 0, first)
+    places = received.reshape(batch_count * capacity) * (store.shape[1] // LANES)
+    looked_a = lookup(store, places, batch_count, 0, first)
     near_first, looked_a = lax.optimization_barrier((nbr_one[0], looked_a))
     answer_a = lax.all_to_all(looked_a, "batch", split_axis=0, concat_axis=0, tiled=True)
-    looked = lookup(store, received, first, capacity - first)
+    looked = lookup(store, places, batch_count, first, capacity - first)
 
     depth = WIDE * TILE
     steps = -(-(input_count + 2 * (SLOTS - 1) * batch_count + depth - 1) // depth)
@@ -480,18 +500,21 @@
         place[:, :, None] == jnp.arange(share)[None, None, :], axis=0, dtype=jnp.float32
     ).astype(jnp.bfloat16)
 
-    total, own = gather_sum(input_count, spans_a, tally_a, starts_a, answer_a, own_column, adj, None)
-    self_one, agg_one, z_part = gather_sum(
+    total, found = gather_sum(
+        input_count, parts, spans_a, tally_a, starts_a, answer_a, own_column, adj, None
+    )
+    self_one, agg_one, *z_blocks = gather_sum(
         input_count,
+        parts,
         spans_b,
         tally_b,
         starts_b,
         answer_b,
         own_column,
         adj,
-        (total, own, deg_first, w1_self, w1_neigh),
-    )
-    z_share = sum_parts(z_part.reshape(parts, share, hidden_width)) + bias_one
+        (total, found, deg_first, w1_self, w1_neigh),
+    )
+    z_share = sum_parts(z_blocks) + bias_one
     hidden = jax.nn.silu(z_share).astype(jnp.bfloat16)
 
     agg_parts = jnp.dot(adj_two, hidden, preferred_element_type=jnp.float32)
@@ -506,9 +529,7 @@
     )
     activations = jax.nn.silu(z_two).astype(jnp.bfloat16)[None]
     dz_two = (cotangent[0].astype(jnp.float32) * silu_grad(z_two)).astype(jnp.bfloat16)
-    group = jnp.stack(spread_parts(jnp.stack([self_two, agg_two, dz_two])), axis=1)
-    self_all, agg_all, dz_two_all = (x.reshape(seeds, hidden_width) for x in group)
-    gw2 = total_over_batch(contract_rows(self_all, dz_two_all), contract_rows(agg_all, dz_two_all))
+    dz_two_all = jnp.concatenate(spread_parts(dz_two))
 
     back = contract_cols(dz_two_all, w2_neigh) / deg_all.astype(jnp.float32)[:, None]
     back_high = back.astype(jnp.bfloat16)
@@ -516,9 +537,22 @@
     dh_share = contract_rows(adj_two, back_high) + contract_rows(adj_two, back_low)
     dh_share = dh_share + jnp.pad(contract_cols(dz_two, w2_self), ((0, rest), (0, 0)))
     dz_share = (dh_share * silu_grad(z_share)).astype(jnp.bfloat16)
-    dz_one = jnp.concatenate(spread_parts(dz_share))
-    gw1 = total_over_batch(contract_rows(self_one, dz_one), contract_rows(agg_one, dz_one))
-    return (activations, *gw2, *gw1)
+    dz_blocks = spread_parts(dz_share)
+
+    pair = jnp.stack(spread_parts(jnp.stack([self_two, agg_two])), axis=1)
+    pair = pair.reshape(2, seeds, hidden_width)
+    gw2 = batch_pieces(contract_rows(pair[0], dz_two_all), contract_rows(pair[1], dz_two_all))
+    few = batch_count <= FEW
+    gw2 = sum_parts(ahead(gw2, "batch"), "batch") if few else reduce_pieces(gw2)
+    dz_blocks[-1], gw2 = lax.optimization_barrier((dz_blocks[-1], gw2))
+    dz_one = jnp.concatenate(dz_blocks)
+    gw1 = batch_pieces(contract_rows(self_one, dz_one), contract_rows(agg_one, dz_one))
+    gw1 = reduce_pieces(gw1).astype(jnp.bfloat16)
+    gw2 = spread_parts(gw2, "batch") if few else spread(gw2, "batch", batch_count)
+    gw1, gw2 = lax.optimization_barrier((gw1, gw2))
+    gw1 = spread(gw1, "batch", batch_count).astype(jnp.float32)
+    gw2 = placed(gw2, "batch") if few else gw2
+    return (activations, *halves_of(gw2), *halves_of(gw1))
 
 
 def solution(mesh):

time: 365 us -> 317 us (0.87)
  Pallas kernels: 165 us -> 110 us
  waiting for transfers between devices: 116 us -> 86.1 us
  local copies, waits for them, and re-layouts: 15.5 us -> 41.2 us
  starting transfers between devices: 51.6 us -> 63 us
    pallas_call x2, Pallas kernels: 66 us -> 19.3 us  [lookup(): pl.pallas_call(functools.partial(lookup_body, places.shape[0] // groups,...]
    ppermute x15 -> x32, starting transfers between devices: 17.8 us -> 39.5 us  [passed(): lax.ppermute(part, axis, [((i + shift) % parts, i) for i in range(parts)])]
    unnamed x42 -> x63, local copies, waits for them, and re-layouts: 7.49 us -> 29.1 us
    all_to_all x2 -> x1, waiting for transfers between devices: 29.7 us -> 8.63 us  [spread(): lax.all_to_all(jnp.broadcast_to(part[None], (count,) + part.shape), axis,...]
    all_to_all x2 -> x1, waiting for transfers between devices: 9.71 us -> 0.01 us  [reduce_pieces(): pieces = lax.all_to_all(pieces, 'batch', 0, 0, tiled=True)]
    pallas_call x2, Pallas kernels: 48.5 us -> 41.1 us  [gather_sum(): pl.pallas_call(functools.partial(gather_sum_body, piece, last), out_shape...]
    all_to_all x2 -> x1, starting transfers between devices: 10.9 us -> 4.81 us  [reduce_pieces(): pieces = lax.all_to_all(pieces, 'batch', 0, 0, tiled=True)]
    ppermute x15 -> x32, waiting for transfers between devices: 37.3 us -> 38.8 us  [passed(): lax.ppermute(part, axis, [((i + shift) % parts, i) for i in range(parts)])]
  transfers between devices with their start and end apart: 22 -> 37, of which waited for: 15 -> 21; matrix products, arithmetic and copies ran while one was open for 5% -> 8% of each run, Pallas kernels for 31% -> 26%
where the time goes in v5:
time: 317 us; the launch traced here: 316 us
  Pallas kernels  110 us (35%)
  waiting for transfers between devices  86.1 us (27%)
  starting transfers between devices  63 us (20%)
  local copies, waits for them, and re-layouts  41.2 us (13%)
  other arithmetic  8.55 us (3%)
  matrix products  4.76 us (2%)
    pallas_call x1, Pallas kernels, adjacency(): pl.pallas_call(functools.partial(adjacency_body, tiles), out_shape=jax.Sh...  47.4 us
    pallas_call x2, Pallas kernels, gather_sum(): pl.pallas_call(functools.partial(gather_sum_body, piece, last), out_shape...  41.1 us
    ppermute x32, starting transfers between devices, passed(): lax.ppermute(part, axis, [((i + shift) % parts, i) for i in range(parts)])  39.5 us
    ppermute x32, waiting for transfers between devices, passed(): lax.ppermute(part, axis, [((i + shift) % parts, i) for i in range(parts)])  38.8 us
    all_to_all x1, waiting for transfers between devices, local(): lax.all_to_all(looked, 'batch', split_axis=0, concat_axis=0, tiled=True)  34.4 us
    unnamed x63, local copies, waits for them, and re-layouts  29.1 us
    pallas_call x2, Pallas kernels, lookup(): pl.pallas_call(functools.partial(lookup_body, places.shape[0] // groups,...  19.3 us
    all_to_all x1, waiting for transfers between devices, spread(): lax.all_to_all(jnp.broadcast_to(part[None], (count,) + part.shape), axis,...  8.63 us
  transfers between devices with their start and end apart: 37, of which 21 were waited for; matrix products, arithmetic and copies ran while one was open for 8% of the time, Pallas kernels for 26%

profile of v5, /device:TPU:0, one launch (start us, length us, event | category | flops | bytes accessed | tf_op | source)
XLA Modules:
  0.0 315.9 jit_solution(6744956764864699098)
XLA Ops:
  4.0 6.3 %all-to-all-start = ((s32[8,1,1536]{2,1,0:T(1,128)}), s32[8,1,1536]{2,1,0:T(1,128)S(1)}, u32[]{:S(2)}, u32[]{:S(2)}) async-start(s32[8,1,1536]{2,1,0:T(1,128)} %bitcast.6), calls=%async_computation | async-start | bytes 98304 | tf_op jit(solution)/shard_map/all_to_all | solution.py:440
  11.9 4.2 %all-to-all-done = s32[8,1,1536]{2,1,0:T(1,128)S(1)} async-done(((s32[8,1,1536]{2,1,0:T(1,128)}), s32[8,1,1536]{2,1,0:T(1,128)S(1)}, u32[]{:S(2)}, u32[]{:S(2)}) %all-to-all-start) | async-done | bytes 49184 | tf_op jit(solution)/shard_map/all_to_all | solution.py:440
  18.4 9.8 %lookup.3 = bf16[8,768,256]{2,1,0:T(8,128)(2,1)} custom-call(s32[12288]{0:T(1024)S(1)} %bitcast.154, bf16[8192,256]{1,0:T(8,128)(2,1)S(1)} %copy-done.1), custom_call_target="tpu_custom_call" | custom-call | flops 62914560 | bytes 4194304 | tf_op jit(solution)/shard_map/lookup/pallas_call | solution.py:137
  28.2 3.8 %all-to-all-start.1 = ((bf16[8,768,256]{2,1,0:T(8,128)(2,1)}), bf16[8,768,256]{2,1,0:T(8,128)(2,1)S(1)}, u32[]{:S(2)}, u32[]{:S(2)}) async-start(bf16[8,768,256]{2,1,0:T(8,128)(2,1)} %lookup.3), calls=%async_computation.1 | async-start | bytes 6291456 | tf_op jit(solution)/shard_map/all_to_all | solution.py:447
  45.4 2.7 pad.12
  52.2 9.5 %lookup.2 = bf16[8,768,256]{2,1,0:T(8,128)(2,1)} custom-call(s32[12288]{0:T(1024)S(1)} %bitcast.155, bf16[8192,256]{1,0:T(8,128)(2,1)S(1)} %copy-done.2), custom_call_target="tpu_custom_call" | custom-call | flops 62914560 | bytes 4194304 | tf_op jit(solution)/shard_map/lookup/pallas_call | solution.py:137
  61.7 47.4 %adjacency.1.adj_ref = f8e4m3fn[28,3072,256]{2,1,0:T(32,128)(4,1)S(1)} custom-call(s32[192,256]{1,0:T(8,128)S(1)} %reshape.243.near_ref, bf16[256,128]{1,0:T(8,128)(2,1)S(1)} %copy-done.6), custom_call_target="tpu_custom_call" | custom-call | flops 22548578304 | bytes 22020096 | tf_op jit(solution)/shard_map/adjacency/pallas_call | solution.py:186
  109.2 7.3 %copy-done.12 = f8e4m3fn[28,3072,256]{2,1,0:T(32,128)(4,1)} copy-done((f8e4m3fn[28,3072,256]{2,1,0:T(32,128)(4,1)}, f8e4m3fn[28,3072,256]{2,1,0:T(32,128)(4,1)S(1)}, u32[]{:S(2)}) %copy-start.12) | copy-done | bytes 22020120
  116.5 5.1 %all-to-all-start.2 = ((bf16[8,768,256]{2,1,0:T(8,128)(2,1)}), bf16[8,768,256]{2,1,0:T(8,128)(2,1)}, u32[]{:S(2)}, u32[]{:S(2)}) async-start(bf16[8,768,256]{2,1,0:T(8,128)(2,1)} %lookup.2), calls=%async_computation.2 | async-start | bytes 6291456 | tf_op jit(solution)/shard_map/all_to_all | solution.py:486
  128.8 26.7 %gather_sum.2 = (f32[3072,256]{1,0:T(8,128)S(1)}, f32[3072,256]{1,0:T(8,128)S(1)}) custom-call(s32[2]{0:T(128)S(1)} %pad_add_fusion.5.spans_ref, s32[8]{0:T(128)S(1)} %get-tuple-element.88.counts_ref, s32[9]{0:T(128)S(1)} %get-tuple-element.90.starts_ref, bf16[8,768,256]{2,1,0:T(8,128)(2,1)S(1)} %all-to-all-done.1.answer_ref, s32[3072,1]{1,0:T(8,128)S(1)} %bitcast.151, ...), custom_call_target="tpu_custom_call" | custom-call | flops 11274289152 | bytes 11010048 | tf_op jit(solution)/shard_map/gather_sum/pallas_call | solution.py:331
  158.8 34.4 %all-to-all-done.2.answer_ref = bf16[8,768,256]{2,1,0:T(8,128)(2,1)} async-done(((bf16[8,768,256]{2,1,0:T(8,128)(2,1)}), bf16[8,768,256]{2,1,0:T(8,128)(2,1)}, u32[]{:S(2)}, u32[]{:S(2)}) %all-to-all-start.2) | async-done | bytes 3145760 | tf_op jit(solution)/shard_map/all_to_all | solution.py:486
  198.9 14.4 %gather_sum.3 = (bf16[3072,256]{1,0:T(8,128)(2,1)S(1)}, bf16[3072,256]{1,0:T(8,128)(2,1)S(1)}, bf16[768,256]{1,0:T(8,128)(2,1)S(1)}, bf16[768,256]{1,0:T(8,128)(...) custom-call(s32[2]{0:T(128)S(1)} %pad_add_fusion.4.spans_ref, s32[8]{0:T(128)S(1)} %get-tuple-element.89.counts_ref, ...), custom_call_target="tpu_custom_call" | custom-call | flops 11274289152 | bytes 11010048 | tf_op jit(solution)/shard_map/gather_sum/pallas_call | solution.py:331
  220.0 6.3 %collective-permute-done.3 = bf16[768,256]{1,0:T(8,128)(2,1)S(1)} collective-permute-done((bf16[768,256]{1,0:T(8,128)(2,1)S(1)}, bf16[768,256]{1,0:T(8,128)(2,1)S(1)}, u32[]{:S(2)}, u32[]{:S(2)}) %collective-permute-start.3) | collective-permute-done | bytes 393248 | tf_op jit(solution)/shard_map/ppermute | solution.py:362
  226.3 4.7 %collective-permute-done.4 = bf16[768,256]{1,0:T(8,128)(2,1)S(1)} collective-permute-done((bf16[768,256]{1,0:T(8,128)(2,1)S(1)}, bf16[768,256]{1,0:T(8,128)(2,1)S(1)}, u32[]{:S(2)}, u32[]{:S(2)}) %collective-permute-start.4) | collective-permute-done | bytes 393248 | tf_op jit(solution)/shard_map/ppermute | solution.py:362
  236.4 2.8 collective-permute-done.6
  246.0 2.7 collective-permute-start.9
  249.4 2.8 collective-permute-start.17
  259.8 3.6 %collective-permute-done.18 = bf16[64,256]{1,0:T(8,128)(2,1)S(1)} collective-permute-done((bf16[64,256]{1,0:T(8,128)(2,1)S(1)}, bf16[64,256]{1,0:T(8,128)(2,1)S(1)}, u32[]{:S(2)}, u32[]{:S(2)}) %collective-permute-start.18) | collective-permute-done | bytes 32800 | tf_op jit(solution)/shard_map/ppermute | solution.py:362
  275.5 4.8 %all-to-all-start.3 = ((bf16[8,64,256]{2,1,0:T(8,128)(2,1)}), bf16[8,64,256]{2,1,0:T(8,128)(2,1)S(1)}, u32[]{:S(2)}, u32[]{:S(2)}) async-start(bf16[8,64,256]{2,1,0:T(8,128)(2,1)} %bitcast.44), calls=%async_computation.3 | async-start | bytes 524288 | tf_op jit(solution)/shard_map/all_to_all | solution.py:396
  280.3 3.6 %collective-permute-start.25 = (f32[64,256]{1,0:T(8,128)S(1)}, f32[64,256]{1,0:T(8,128)S(1)}, u32[]{:S(2)}, u32[]{:S(2)}) collective-permute-start(f32[64,256]{1,0:T(8,128)S(1)} %fusion.24), channel_id=1, source_target_pairs={{1,0},{2,1},{3,2},{4,3},{5,4},{6,5},{7,6},{0,7},{9,8},{10,9},{11,1... | collective-permute-start | bytes 196616 | tf_op jit(solution)/shard_map/ppermute | solution.py:362
  287.9 2.6 collective-permute-done.26
  292.4 8.9 %collective-permute-done.28 = f32[64,256]{1,0:T(8,128)S(1)} collective-permute-done((f32[64,256]{1,0:T(8,128)S(1)}, f32[64,256]{1,0:T(8,128)S(1)}, u32[]{:S(2)}, u32[]{:S(2)}) %collective-permute-start.28) | collective-permute-done | bytes 65568 | tf_op jit(solution)/shard_map/ppermute | solution.py:362
  302.0 3.4 %all-to-all-start.4 = ((bf16[8,64,256]{2,1,0:T(8,128)(2,1)}), bf16[8,64,256]{2,1,0:T(8,128)(2,1)S(1)}, u32[]{:S(2)}, u32[]{:S(2)}) async-start(bf16[8,64,256]{2,1,0:T(8,128)(2,1)} %broadcast_in_dim.87), calls=%async_computation.4 | async-start | bytes 524288 | tf_op jit(solution)/shard_map/all_to_all | solution.py:355
  306.4 8.6 %all-to-all-done.4 = bf16[8,64,256]{2,1,0:T(8,128)(2,1)S(1)} async-done(((bf16[8,64,256]{2,1,0:T(8,128)(2,1)}), bf16[8,64,256]{2,1,0:T(8,128)(2,1)S(1)}, u32[]{:S(2)}, u32[]{:S(2)}) %all-to-all-start.4) | async-done | bytes 262176 | tf_op jit(solution)/shard_map/all_to_all | solution.py:355
  (200 shorter events, 86.6 us)
Async XLA Ops:
  4.0 12.2 %all-to-all-start = ((s32[8,1,1536]{2,1,0:T(1,128)}), s32[8,1,1536]{2,1,0:T(1,128)S(1)}, u32[]{:S(2)}, u32[]{:S(2)}) async-start(s32[8,1,1536]{2,1,0:T(1,128)} %bitcast.6), calls=%async_computation | async-start | bytes 98304 | tf_op jit(solution)/shard_map/all_to_all | solution.py:440
  28.2 88.3 %all-to-all-start.1 = ((bf16[8,768,256]{2,1,0:T(8,128)(2,1)}), bf16[8,768,256]{2,1,0:T(8,128)(2,1)S(1)}, u32[]{:S(2)}, u32[]{:S(2)}) async-start(bf16[8,768,256]{2,1,0:T(8,128)(2,1)} %lookup.3), calls=%async_computation.1 | async-start | bytes 6291456 | tf_op jit(solution)/shard_map/all_to_all | solution.py:447
  32.0 7.3 %collective-permute-start = (s32[11,128]{1,0:T(8,128)S(1)}, s32[11,128]{1,0:T(8,128)S(1)}, u32[]{:S(2)}, u32[]{:S(2)}) collective-permute-start(s32[11,128]{1,0:T(8,128)S(1)} %pad_add_fusion.1), channel_id=1, source_target_pairs={{8,0},{16,8},{24,16},{0,24},{9,1},{17,9},{25,17},{1,25},{10,2},{18... | collective-permute-start | bytes 16904 | tf_op jit(solution)/shard_map/ppermute | solution.py:362
  116.5 76.8 %all-to-all-start.2 = ((bf16[8,768,256]{2,1,0:T(8,128)(2,1)}), bf16[8,768,256]{2,1,0:T(8,128)(2,1)}, u32[]{:S(2)}, u32[]{:S(2)}) async-start(bf16[8,768,256]{2,1,0:T(8,128)(2,1)} %lookup.2), calls=%async_computation.2 | async-start | bytes 6291456 | tf_op jit(solution)/shard_map/all_to_all | solution.py:486
  213.3 13.0 %collective-permute-start.3 = (bf16[768,256]{1,0:T(8,128)(2,1)S(1)}, bf16[768,256]{1,0:T(8,128)(2,1)S(1)}, u32[]{:S(2)}, u32[]{:S(2)}) collective-permute-start(bf16[768,256]{1,0:T(8,128)(2,1)S(1)} %get-tuple-element.46), channel_id=1, source_target_pairs={{24,0},{0,8},{8,16},{16,24},{25,1},{1,9},{9,17},{17,25},{26,2},{2,... | collective-permute-start | bytes 1179656 | tf_op jit(solution)/shard_map/ppermute | solution.py:362
  215.5 15.6 %collective-permute-start.4 = (bf16[768,256]{1,0:T(8,128)(2,1)S(1)}, bf16[768,256]{1,0:T(8,128)(2,1)S(1)}, u32[]{:S(2)}, u32[]{:S(2)}) collective-permute-start(bf16[768,256]{1,0:T(8,128)(2,1)S(1)} %get-tuple-element.47), channel_id=1, source_target_pairs={{16,0},{24,8},{0,16},{8,24},{17,1},{25,9},{1,17},{9,25},{18,2},{26... | collective-permute-start | bytes 1179656 | tf_op jit(solution)/shard_map/ppermute | solution.py:362
  216.0 15.2 %collective-permute-start.5 = (bf16[768,256]{1,0:T(8,128)(2,1)S(1)}, bf16[768,256]{1,0:T(8,128)(2,1)S(1)}, u32[]{:S(2)}, u32[]{:S(2)}) collective-permute-start(bf16[768,256]{1,0:T(8,128)(2,1)S(1)} %get-tuple-element.48), channel_id=1, source_target_pairs={{8,0},{16,8},{24,16},{0,24},{9,1},{17,9},{25,17},{1,25},{10,2},{18... | collective-permute-start | bytes 1179656 | tf_op jit(solution)/shard_map/ppermute | solution.py:362
  231.9 7.3 %collective-permute-start.6 = (f32[128,256]{1,0:T(8,128)S(1)}, f32[128,256]{1,0:T(8,128)S(1)}, u32[]{:S(2)}, u32[]{:S(2)}) collective-permute-start(f32[128,256]{1,0:T(8,128)S(1)} %get-tuple-element.67), channel_id=1, source_target_pairs={{24,0},{0,8},{8,16},{16,24},{25,1},{1,9},{9,17},{17,25},{26,2},{2,... | collective-permute-start | bytes 393224 | tf_op jit(solution)/shard_map/ppermute | solution.py:362
  233.7 6.5 %collective-permute-start.7 = (f32[128,256]{1,0:T(8,128)S(1)}, f32[128,256]{1,0:T(8,128)S(1)}, u32[]{:S(2)}, u32[]{:S(2)}) collective-permute-start(f32[128,256]{1,0:T(8,128)S(1)} %get-tuple-element.69), channel_id=1, source_target_pairs={{16,0},{24,8},{0,16},{8,24},{17,1},{25,9},{1,17},{9,25},{18,2},{26... | collective-permute-start | bytes 393224 | tf_op jit(solution)/shard_map/ppermute | solution.py:362
  241.0 15.5 %collective-permute-start.15 = (bf16[2,128,256]{2,1,0:T(8,128)(2,1)S(1)}, bf16[2,128,256]{2,1,0:T(8,128)(2,1)S(1)}, u32[]{:S(2)}, u32[]{:S(2)}) collective-permute-start(bf16[2,128,256]{2,1,0:T(8,128)(2,1)S(1)} %get-tuple-element.80), channel_id=1, source_target_pairs={{8,0},{16,8},{24,16},{0,24},{9,1},{17,9},{25,17},{1,25},{10,2},{18... | collective-permute-start | bytes 393224 | tf_op jit(solution)/shard_map/ppermute | solution.py:362
  242.9 14.4 %collective-permute-start.16 = (bf16[2,128,256]{2,1,0:T(8,128)(2,1)S(1)}, bf16[2,128,256]{2,1,0:T(8,128)(2,1)S(1)}, u32[]{:S(2)}, u32[]{:S(2)}) collective-permute-start(bf16[2,128,256]{2,1,0:T(8,128)(2,1)S(1)} %get-tuple-element.80), channel_id=1, source_target_pairs={{16,0},{24,8},{0,16},{8,24},{17,1},{25,9},{1,17},{9,25},{18,2},{26... | collective-permute-start | bytes 393224 | tf_op jit(solution)/shard_map/ppermute | solution.py:362
  249.4 8.0 %collective-permute-start.17 = (bf16[2,128,256]{2,1,0:T(8,128)(2,1)S(1)}, bf16[2,128,256]{2,1,0:T(8,128)(2,1)S(1)}, u32[]{:S(2)}, u32[]{:S(2)}) collective-permute-start(bf16[2,128,256]{2,1,0:T(8,128)(2,1)S(1)} %get-tuple-element.80), channel_id=1, source_target_pairs={{24,0},{0,8},{8,16},{16,24},{25,1},{1,9},{9,17},{17,25},{26,2},{2,... | collective-permute-start | bytes 393224 | tf_op jit(solution)/shard_map/ppermute | solution.py:362
  253.6 19.9 %collective-permute-start.14 = (bf16[768,256]{1,0:T(8,128)(2,1)S(1)}, bf16[768,256]{1,0:T(8,128)(2,1)S(1)}, u32[]{:S(2)}, u32[]{:S(2)}) collective-permute-start(bf16[768,256]{1,0:T(8,128)(2,1)S(1)} %fusion.2), channel_id=1, source_target_pairs={{24,0},{0,8},{8,16},{16,24},{25,1},{1,9},{9,17},{17,25},{26,2},{2,... | collective-permute-start | bytes 1179656 | tf_op jit(solution)/shard_map/ppermute | solution.py:362
  255.2 18.2 %collective-permute-start.12 = (bf16[768,256]{1,0:T(8,128)(2,1)S(1)}, bf16[768,256]{1,0:T(8,128)(2,1)S(1)}, u32[]{:S(2)}, u32[]{:S(2)}) collective-permute-start(bf16[768,256]{1,0:T(8,128)(2,1)S(1)} %fusion.2), channel_id=1, source_target_pairs={{8,0},{16,8},{24,16},{0,24},{9,1},{17,9},{25,17},{1,25},{10,2},{18... | collective-permute-start | bytes 1179656 | tf_op jit(solution)/shard_map/ppermute | solution.py:362
  256.6 16.9 %collective-permute-start.13 = (bf16[768,256]{1,0:T(8,128)(2,1)S(1)}, bf16[768,256]{1,0:T(8,128)(2,1)S(1)}, u32[]{:S(2)}, u32[]{:S(2)}) collective-permute-start(bf16[768,256]{1,0:T(8,128)(2,1)S(1)} %fusion.2), channel_id=1, source_target_pairs={{16,0},{24,8},{0,16},{8,24},{17,1},{25,9},{1,17},{9,25},{18,2},{26... | collective-permute-start | bytes 1179656 | tf_op jit(solution)/shard_map/ppermute | solution.py:362
  275.5 16.8 %all-to-all-start.3 = ((bf16[8,64,256]{2,1,0:T(8,128)(2,1)}), bf16[8,64,256]{2,1,0:T(8,128)(2,1)S(1)}, u32[]{:S(2)}, u32[]{:S(2)}) async-start(bf16[8,64,256]{2,1,0:T(8,128)(2,1)} %bitcast.44), calls=%async_computation.3 | async-start | bytes 524288 | tf_op jit(solution)/shard_map/all_to_all | solution.py:396
  280.3 6.9 %collective-permute-start.25 = (f32[64,256]{1,0:T(8,128)S(1)}, f32[64,256]{1,0:T(8,128)S(1)}, u32[]{:S(2)}, u32[]{:S(2)}) collective-permute-start(f32[64,256]{1,0:T(8,128)S(1)} %fusion.24), channel_id=1, source_target_pairs={{1,0},{2,1},{3,2},{4,3},{5,4},{6,5},{7,6},{0,7},{9,8},{10,9},{11,1... | collective-permute-start | bytes 196616 | tf_op jit(solution)/shard_map/ppermute | solution.py:362
  283.9 6.7 %collective-permute-start.26 = (f32[64,256]{1,0:T(8,128)S(1)}, f32[64,256]{1,0:T(8,128)S(1)}, u32[]{:S(2)}, u32[]{:S(2)}) collective-permute-start(f32[64,256]{1,0:T(8,128)S(1)} %fusion.24), channel_id=1, source_target_pairs={{2,0},{3,1},{4,2},{5,3},{6,4},{7,5},{0,6},{1,7},{10,8},{11,9},{12,... | collective-permute-start | bytes 196616 | tf_op jit(solution)/shard_map/ppermute | solution.py:362
  284.4 7.9 %collective-permute-start.27 = (f32[64,256]{1,0:T(8,128)S(1)}, f32[64,256]{1,0:T(8,128)S(1)}, u32[]{:S(2)}, u32[]{:S(2)}) collective-permute-start(f32[64,256]{1,0:T(8,128)S(1)} %fusion.24), channel_id=1, source_target_pairs={{3,0},{4,1},{5,2},{6,3},{7,4},{0,5},{1,6},{2,7},{11,8},{12,9},{13,... | collective-permute-start | bytes 196616 | tf_op jit(solution)/shard_map/ppermute | solution.py:362
  284.4 16.8 %collective-permute-start.28 = (f32[64,256]{1,0:T(8,128)S(1)}, f32[64,256]{1,0:T(8,128)S(1)}, u32[]{:S(2)}, u32[]{:S(2)}) collective-permute-start(f32[64,256]{1,0:T(8,128)S(1)} %fusion.24), channel_id=1, source_target_pairs={{4,0},{5,1},{6,2},{7,3},{0,4},{1,5},{2,6},{3,7},{12,8},{13,9},{14,... | collective-permute-start | bytes 196616 | tf_op jit(solution)/shard_map/ppermute | solution.py:362
  286.9 14.4 %collective-permute-start.29 = (f32[64,256]{1,0:T(8,128)S(1)}, f32[64,256]{1,0:T(8,128)S(1)}, u32[]{:S(2)}, u32[]{:S(2)}) collective-permute-start(f32[64,256]{1,0:T(8,128)S(1)} %fusion.24), channel_id=1, source_target_pairs={{5,0},{6,1},{7,2},{0,3},{1,4},{2,5},{3,6},{4,7},{13,8},{14,9},{15,... | collective-permute-start | bytes 196616 | tf_op jit(solution)/shard_map/ppermute | solution.py:362
  287.2 14.1 %collective-permute-start.30 = (f32[64,256]{1,0:T(8,128)S(1)}, f32[64,256]{1,0:T(8,128)S(1)}, u32[]{:S(2)}, u32[]{:S(2)}) collective-permute-start(f32[64,256]{1,0:T(8,128)S(1)} %fusion.24), channel_id=1, source_target_pairs={{6,0},{7,1},{0,2},{1,3},{2,4},{3,5},{4,6},{5,7},{14,8},{15,9},{8,1... | collective-permute-start | bytes 196616 | tf_op jit(solution)/shard_map/ppermute | solution.py:362
  290.5 10.7 %collective-permute-start.31 = (f32[64,256]{1,0:T(8,128)S(1)}, f32[64,256]{1,0:T(8,128)S(1)}, u32[]{:S(2)}, u32[]{:S(2)}) collective-permute-start(f32[64,256]{1,0:T(8,128)S(1)} %fusion.24), channel_id=1, source_target_pairs={{7,0},{0,1},{1,2},{2,3},{3,4},{4,5},{5,6},{6,7},{15,8},{8,9},{9,10... | collective-permute-start | bytes 196616 | tf_op jit(solution)/shard_map/ppermute | solution.py:362
  302.0 13.1 %all-to-all-start.4 = ((bf16[8,64,256]{2,1,0:T(8,128)(2,1)}), bf16[8,64,256]{2,1,0:T(8,128)(2,1)S(1)}, u32[]{:S(2)}, u32[]{:S(2)}) async-start(bf16[8,64,256]{2,1,0:T(8,128)(2,1)} %broadcast_in_dim.87), calls=%async_computation.4 | async-start | bytes 524288 | tf_op jit(solution)/shard_map/all_to_all | solution.py:355
  (41 other events, 561.6 us)

commit v6 on v5

--- a/solution.py
+++ b/solution.py
@@ -18,6 +18,7 @@
 VMEM = pl.BlockSpec(memory_space=pltpu.VMEM)
 SMEM = pl.BlockSpec(memory_space=pltpu.SMEM)
 ANY = pl.BlockSpec(memory_space=pl.ANY)
+HBM = pl.BlockSpec(memory_space=pltpu.HBM)
 
 
 def silu_grad(values):
@@ -147,7 +148,7 @@
     )(places, store)
 
 
-def adjacency_body(tiles, near_ref, table_ref, out_ref):
+def adjacency_body(tiles, me_ref, near_ref, table_ref, out_ref):
     groups = near_ref.shape[0]
     node_high = lax.broadcasted_iota(jnp.int32, (LANES, TILE), 0)
     own_row = (
@@ -179,23 +180,35 @@
         )
 
 
-def adjacency(near, table, tiles):
+def adjacency(me, near, table, tiles, parts, seeds):
     groups = near.shape[0]
     nodes = groups * SLOTS
-    step = TILE // SLOTS
+    step = LANES // SLOTS
+    own, rest, share = (n // parts // LANES for n in (seeds, nodes - seeds, nodes))
+
+    def place(block, me_ref):
+        after = block - own * parts
+        is_own = after < 0
+        part = jnp.where(is_own, lax.div(block, own), lax.div(after, rest))
+        at = jnp.where(is_own, lax.rem(block, own), own + lax.rem(after, rest))
+        return (0, lax.rem(part - me_ref[0] + parts, parts) * share + at, 0)
+
     return pl.pallas_call(
         functools.partial(adjacency_body, tiles),
         out_shape=jax.ShapeDtypeStruct((tiles, nodes, TILE), jnp.float8_e4m3fn),
-        grid=(groups // step,),
-        in_specs=[
-            pl.BlockSpec((step, TILE), lambda r: (r, 0)),
-            pl.BlockSpec(table.shape, lambda r: (0, 0)),
-        ],
-        out_specs=pl.BlockSpec((tiles, TILE, TILE), lambda r: (0, r, 0)),
-        compiler_params=params(16),
+        grid_spec=pltpu.PrefetchScalarGridSpec(
+            num_scalar_prefetch=1,
+            grid=(groups // step,),
+            in_specs=[
+                pl.BlockSpec((step, TILE), lambda r, me: (r, 0)),
+                pl.BlockSpec(table.shape, lambda r, me: (0, 0)),
+            ],
+            out_specs=pl.BlockSpec((tiles, LANES, TILE), place),
+        ),
+        compiler_params=params(48),
         cost_estimate=cost(2 * nodes * TILE * TILE * tiles * 2, nodes * TILE * tiles),
         name="adjacency",
-    )(near, table)
+    )(me, near, table)
 
 
 def collect(piece, counts_ref, starts_ref, answer_ref, landed, arrived, packed):
@@ -226,19 +239,19 @@
 
 
 def gather_sum_body(
-    piece, last, spans_ref, counts_ref, starts_ref, answer_ref, column_ref, adj_ref, *refs
+    piece, last, spans_ref, counts_ref, starts_ref, answer_ref, notes_in, adj_ref, *refs
 ):
     if last:
-        (total_in, found_in, deg_ref, wself_ref, wneigh_ref, own_ref, mean_ref) = refs[:7]
-        share_refs = refs[7:-8]
-        packed, tiles_ref, ready, landed, arrived, total_ref, found_ref, carried = refs[-8:]
-        carry = [
-            pltpu.make_async_copy(total_in, total_ref, carried.at[0]),
-            pltpu.make_async_copy(found_in, found_ref, carried.at[1]),
-        ]
+        (total_in, found_in, wself_in, wneigh_in, own_ref, mean_ref) = refs[:6]
+        share_refs = refs[6:-11]
+        packed, tiles_ref, ready, landed, arrived, notes_ref, carried = refs[-11:-4]
+        total_ref, found_ref, wself_ref, wneigh_ref = refs[-4:]
+        pairs = ((notes_in, notes_ref), (total_in, total_ref), (found_in, found_ref))
+        pairs += ((wself_in, wself_ref), (wneigh_in, wneigh_ref))
     else:
-        total_ref, found_ref, packed, tiles_ref, ready, landed, arrived = refs
-        carry = []
+        total_ref, found_ref, packed, tiles_ref, ready, landed, arrived, notes_ref, carried = refs
+        pairs = ((notes_in, notes_ref),)
+    carry = [pltpu.make_async_copy(*pair, carried.at[n]) for n, pair in enumerate(pairs)]
     nodes = total_ref.shape[0]
     rows = math.gcd(nodes, 3 * TILE)
     begin, count = spans_ref[0], spans_ref[1]
@@ -273,6 +286,7 @@
         depth = WIDE * TILE
         block = packed[pl.ds(pl.multiple_of(step * depth, depth), depth), :]
         lane = lax.broadcasted_iota(jnp.int32, (rows, depth), 1) + (begin * TILE + step * depth)
+        lane = lane.astype(jnp.float32)
 
         @pl.loop(0, nodes // rows)
         def _(r):
@@ -280,7 +294,7 @@
             near = jnp.concatenate(
                 [tiles_ref[slot, w, part, :].astype(jnp.bfloat16) for w in range(WIDE)], axis=1
             )
-            own = jnp.where(column_ref[part, :] == lane, 1.0, 0.0).astype(jnp.bfloat16)
+            own = jnp.where(notes_ref[part, 0:1] == lane, 1.0, 0.0).astype(jnp.bfloat16)
             both = jnp.dot(
                 jnp.concatenate([near, own], axis=0), block, preferred_element_type=jnp.float32
             )
@@ -294,7 +308,7 @@
             for r in range(share // step_rows):
                 part = pl.ds(p * share + r * step_rows, step_rows)
                 own = found_ref[part, :].astype(jnp.bfloat16)
-                mean = (total_ref[part, :] / deg_ref[part, :]).astype(jnp.bfloat16)
+                mean = (total_ref[part, :] / notes_ref[part, 1:2]).astype(jnp.bfloat16)
                 own_ref[part, :] = own
                 mean_ref[part, :] = mean
                 share_ref[pl.ds(r * step_rows, step_rows), :] = (
@@ -303,13 +317,13 @@
                 ).astype(share_ref.dtype)
 
 
-def gather_sum(inputs, parts, spans, counts, starts, answer, column, adj, rest):
+def gather_sum(inputs, parts, spans, counts, starts, answer, notes, adj, rest):
     batch_count, width, features = answer.shape
     tiles, nodes, _ = adj.shape
     piece = LANES if width % LANES == 0 else SLOTS
     last = rest is not None
     room = min(batch_count * width, inputs) + SLOTS * batch_count + 2 * WIDE * TILE
-    in_specs = [SMEM, SMEM, SMEM, ANY, VMEM, ANY]
+    in_specs = [SMEM, SMEM, SMEM, ANY, HBM, HBM]
     rows = lambda dtype: jax.ShapeDtypeStruct((nodes, features), dtype)
     scratch = [
         pltpu.VMEM((room, features), jnp.bfloat16),
@@ -317,15 +331,16 @@
         pltpu.SemaphoreType.DMA((2,)),
         pltpu.VMEM(answer.shape, answer.dtype),
         pltpu.SemaphoreType.DMA((batch_count,)),
+        pltpu.VMEM(notes.shape, notes.dtype),
+        pltpu.SemaphoreType.DMA((5,)),
     ]
-    operands = [answer, column, adj]
+    operands = [answer, notes, adj]
     if last:
         operands += list(rest)
-        in_specs += [ANY, ANY, VMEM, VMEM, VMEM]
+        in_specs += [HBM] * len(rest)
         share = jax.ShapeDtypeStruct((nodes // parts, rest[3].shape[1]), jnp.bfloat16)
         out_shape = (rows(jnp.bfloat16), rows(jnp.bfloat16)) + (share,) * parts
-        scratch += [pltpu.VMEM((nodes, features), jnp.float32)] * 2
-        scratch += [pltpu.SemaphoreType.DMA((2,))]
+        scratch += [pltpu.VMEM(x.shape, x.dtype) for x in rest]
     else:
         out_shape = (rows(jnp.float32), rows(jnp.float32))
     return pl.pallas_call(
@@ -334,7 +349,7 @@
         in_specs=in_specs,
         out_specs=(VMEM,) * len(out_shape),
         scratch_shapes=scratch,
-        compiler_params=params(40),
+        compiler_params=params(50),
         cost_estimate=cost(2 * nodes * features * TILE * tiles, nodes * TILE * tiles // 2),
         name="gather_sum",
     )(spans, counts, starts, *operands)
@@ -381,29 +396,33 @@
     return sum(x.astype(jnp.float32) for x in came)
 
 
-def batch_pieces(one, two):
-    both = jnp.concatenate([one, two]).astype(jnp.bfloat16)
+def swapped(part):
+    return lax.ppermute(part, "batch", [(i, i ^ 1) for i in range(lax.axis_size("batch"))])
+
+
+def total_over_batch(terms):
     count = lax.axis_size("batch")
-    return both.reshape(count, both.shape[0] // count, both.shape[1])
-
-
-def halves_of(total):
-    total = total.reshape(-1, total.shape[-1])
-    return total[: total.shape[0] // 2], total[total.shape[0] // 2 :]
-
-
-def reduce_pieces(pieces):
-    pieces = lax.all_to_all(pieces, "batch", 0, 0, tiled=True)
-    return jnp.sum(pieces.astype(jnp.float32), axis=0)
-
-
-def placed(blocks, axis):
-    count = lax.axis_size(axis)
-    total = jnp.zeros((count,) + blocks[0].shape, blocks[0].dtype)
-    for j, block in enumerate(blocks):
-        spot = (lax.axis_index(axis) + j) % count
-        total = lax.dynamic_update_index_in_dim(total, block, spot, 0)
-    return total
+    rows, width = terms.shape
+    if count > FEW:
+        pieces = terms.astype(jnp.bfloat16).reshape(count, rows // count, width)
+        pieces = lax.all_to_all(pieces, "batch", 0, 0, tiled=True)
+        total = jnp.sum(pieces.astype(jnp.float32), axis=0).astype(jnp.bfloat16)
+        return spread(total, "batch", count).reshape(rows, width)
+    chips = count // 2
+    index = lax.axis_index("batch")
+    first, chip = index % 2 == 0, index // 2
+    upper, lower = terms[: rows // 2], terms[rows // 2 :]
+    came = swapped(jnp.where(first, lower, upper).astype(jnp.bfloat16))
+    mine = jnp.where(first, upper, lower) + came.astype(jnp.float32)
+    pieces = turned(mine.reshape(chips, rows // count, width), chip)
+    total = pieces[0]
+    for j in range(1, chips):
+        total = total + passed(pieces[j].astype(jnp.bfloat16), -2 * j, "batch").astype(jnp.float32)
+    total = total.astype(jnp.bfloat16)
+    mine = jnp.stack([total] + [passed(total, 2 * j, "batch") for j in range(1, chips)])
+    other = swapped(mine)
+    both = jnp.stack([jnp.where(first, mine, other), jnp.where(first, other, mine)], axis=1)
+    return turned(both, (chips - chip) % chips).transpose(1, 0, 2, 3).reshape(rows, width)
 
 
 def local(
@@ -469,7 +488,8 @@
     column = jnp.sum(jnp.where(mine, shifted, 0), axis=0)
     grid = jnp.pad(column.reshape(-1, LANES), ((0, LANES - input_count // LANES), (0, 0))).T
     table = jnp.concatenate([grid // TILE, grid % TILE], axis=0).astype(jnp.bfloat16)
-    own_column = share_order(column[:nodes], parts, seeds).reshape(nodes, 1)
+    notes = jnp.stack([column[:nodes], deg_one[0]], axis=1).astype(jnp.float32)
+    notes = share_order(notes, parts, seeds)
 
     fanout_two = nbr_two.shape[2]
     used_two = jnp.arange(fanout_two)[:, None] < deg_two
@@ -478,13 +498,13 @@
 
     fanout = nbr_one.shape[2]
     used = jnp.arange(fanout)[None, :] < deg_one[0][:, None]
-    near = share_order(jnp.where(used, near_first, -1), parts, seeds)
-    near = jnp.pad(near, ((0, 0), (0, SLOTS - fanout)), constant_values=-1)
+    near = jnp.pad(jnp.where(used, near_first, -1), ((0, 0), (0, SLOTS - fanout)), constant_values=-1)
     near, lists = lax.optimization_barrier((near, lists))
-    adj = adjacency(near.reshape(nodes // SLOTS, TILE), table, steps * WIDE)
+    me = feat_index.astype(jnp.int32).reshape(1)
+    near = near.reshape(nodes // SLOTS, TILE)
+    adj = adjacency(me, near, table, steps * WIDE, parts, seeds)
     looked, answer_a, adj = lax.optimization_barrier((looked, answer_a, adj))
     answer_b = lax.all_to_all(looked, "batch", split_axis=0, concat_axis=0, tiled=True)
-    deg_first = share_order(deg_one[0], parts, seeds).astype(jnp.float32).reshape(nodes, 1)
 
     near_two = lists[:, :fanout_two].transpose(1, 0, 2).reshape(fanout_two, seeds)
     deg_all = lists[:, fanout_two].reshape(seeds)
@@ -501,7 +521,7 @@
     ).astype(jnp.bfloat16)
 
     total, found = gather_sum(
-        input_count, parts, spans_a, tally_a, starts_a, answer_a, own_column, adj, None
+        input_count, parts, spans_a, tally_a, starts_a, answer_a, notes, adj, None
     )
     self_one, agg_one, *z_blocks = gather_sum(
         input_count,
@@ -510,9 +530,9 @@
         tally_b,
         starts_b,
         answer_b,
-        own_column,
+        notes,
         adj,
-        (total, found, deg_first, w1_self, w1_neigh),
+        (total, found, w1_self, w1_neigh),
     )
     z_share = sum_parts(z_blocks) + bias_one
     hidden = jax.nn.silu(z_share).astype(jnp.bfloat16)
@@ -529,7 +549,8 @@
     )
     activations = jax.nn.silu(z_two).astype(jnp.bfloat16)[None]
     dz_two = (cotangent[0].astype(jnp.float32) * silu_grad(z_two)).astype(jnp.bfloat16)
-    dz_two_all = jnp.concatenate(spread_parts(dz_two))
+    group = jnp.stack(spread_parts(jnp.stack([self_two, agg_two, dz_two])))
+    dz_two_all = group[:, 2].reshape(seeds, hidden_width)
 
     back = contract_cols(dz_two_all, w2_neigh) / deg_all.astype(jnp.float32)[:, None]
     back_high = back.astype(jnp.bfloat16)
@@ -537,22 +558,13 @@
     dh_share = contract_rows(adj_two, back_high) + contract_rows(adj_two, back_low)
     dh_share = dh_share + jnp.pad(contract_cols(dz_two, w2_self), ((0, rest), (0, 0)))
     dz_share = (dh_share * silu_grad(z_share)).astype(jnp.bfloat16)
-    dz_blocks = spread_parts(dz_share)
-
-    pair = jnp.stack(spread_parts(jnp.stack([self_two, agg_two])), axis=1)
-    pair = pair.reshape(2, seeds, hidden_width)
-    gw2 = batch_pieces(contract_rows(pair[0], dz_two_all), contract_rows(pair[1], dz_two_all))
-    few = batch_count <= FEW
-    gw2 = sum_parts(ahead(gw2, "batch"), "batch") if few else reduce_pieces(gw2)
-    dz_blocks[-1], gw2 = lax.optimization_barrier((dz_blocks[-1], gw2))
-    dz_one = jnp.concatenate(dz_blocks)
-    gw1 = batch_pieces(contract_rows(self_one, dz_one), contract_rows(agg_one, dz_one))
-    gw1 = reduce_pieces(gw1).astype(jnp.bfloat16)
-    gw2 = spread_parts(gw2, "batch") if few else spread(gw2, "batch", batch_count)
-    gw1, gw2 = lax.optimization_barrier((gw1, gw2))
-    gw1 = spread(gw1, "batch", batch_count).astype(jnp.float32)
-    gw2 = placed(gw2, "batch") if few else gw2
-    return (activations, *halves_of(gw2), *halves_of(gw1))
+    dz_one = jnp.concatenate(spread_parts(dz_share))
+    group = turned(group, (parts - feat_index) % parts).transpose(1, 0, 2, 3)
+    self_all, agg_all, dz_all = (x.reshape(seeds, hidden_width) for x in group)
+    grads = [contract_rows(self_all, dz_all), contract_rows(agg_all, dz_all)]
+    grads += [contract_rows(self_one, dz_one), contract_rows(agg_one, dz_one)]
+    total = total_over_batch(jnp.concatenate(grads)).astype(jnp.float32)
+    return (activations, *total.reshape(len(grads), -1, hidden_width))
 
 
 def solution(mesh):

time: 317 us -> 284 us (0.90)
  local copies, waits for them, and re-layouts: 41.2 us -> 11.7 us
  starting transfers between devices: 63 us -> 41.5 us
  waiting for transfers between devices: 86.1 us -> 103 us
  Pallas kernels: 110 us -> 115 us
  other arithmetic: 8.55 us -> 4.57 us
    unnamed x63 -> x42, local copies, waits for them, and re-layouts: 29.1 us -> 7.78 us
    ppermute x32 -> x21, waiting for transfers between devices: 38.8 us -> 54.5 us  [passed(): lax.ppermute(part, axis, [((i + shift) % parts, i) for i in range(parts)])]
    ppermute x32 -> x21, starting transfers between devices: 39.5 us -> 25.9 us  [passed(): lax.ppermute(part, axis, [((i + shift) % parts, i) for i in range(parts)])]
    all_to_all x2 -> x0, waiting for transfers between devices: 8.63 us -> none  [the longest x1 8.63 us: spread(): lax.all_to_all(jnp.broadcast_to(part[None], (count,) + part.shape), axis,...]
    all_to_all x2 -> x0, starting transfers between devices: 8.23 us -> none  [the longest x1 4.81 us: reduce_pieces(): pieces = lax.all_to_all(pieces, 'batch', 0, 0, tiled=True)]
    pallas_call x2, Pallas kernels: 41.1 us -> 46 us  [gather_sum(): pl.pallas_call(functools.partial(gather_sum_body, piece, last), out_shape...]
  transfers between devices with their start and end apart: 37 -> 26, of which waited for: 21 -> 21; matrix products, arithmetic and copies ran while one was open for 8% -> 3% of each run, Pallas kernels for 26% -> 32%
where the time goes in v6:
time: 284 us; the launch traced here: 283 us
  Pallas kernels  115 us (40%)
  waiting for transfers between devices  103 us (36%)
  starting transfers between devices  41.5 us (15%)
  local copies, waits for them, and re-layouts  11.7 us (4%)
  matrix products  4.66 us (2%)
  other arithmetic  4.57 us (2%)
    ppermute x21, waiting for transfers between devices, passed(): lax.ppermute(part, axis, [((i + shift) % parts, i) for i in range(parts)])  54.5 us
    pallas_call x1, Pallas kernels, adjacency(): pl.pallas_call(functools.partial(adjacency_body, tiles), out_shape=jax.Sh...  47.8 us
    pallas_call x2, Pallas kernels, gather_sum(): pl.pallas_call(functools.partial(gather_sum_body, piece, last), out_shape...  46 us
    all_to_all x1, waiting for transfers between devices, local(): lax.all_to_all(looked, 'batch', split_axis=0, concat_axis=0, tiled=True)  37.4 us
    ppermute x21, starting transfers between devices, passed(): lax.ppermute(part, axis, [((i + shift) % parts, i) for i in range(parts)])  25.9 us
    pallas_call x2, Pallas kernels, lookup(): pl.pallas_call(functools.partial(lookup_body, places.shape[0] // groups,...  19.3 us
    unnamed x42, local copies, waits for them, and re-layouts  7.78 us
    all_to_all x1, starting transfers between devices, local(): lax.all_to_all(requests.reshape(batch_count, capacity), 'batch', split_ax...  6.33 us
  transfers between devices with their start and end apart: 26, of which 21 were waited for; matrix products, arithmetic and copies ran while one was open for 3% of the time, Pallas kernels for 32%

profile of v6, /device:TPU:0, one launch (start us, length us, event | category | flops | bytes accessed | tf_op | source)
XLA Modules:
  0.0 282.9 jit_solution(17442679685718123962)
XLA Ops:
  4.0 6.3 %all-to-all-start = ((s32[8,1,1536]{2,1,0:T(1,128)}), s32[8,1,1536]{2,1,0:T(1,128)S(1)}, u32[]{:S(2)}, u32[]{:S(2)}) async-start(s32[8,1,1536]{2,1,0:T(1,128)} %bitcast.6), calls=%async_computation | async-start | bytes 98304 | tf_op jit(solution)/shard_map/all_to_all | solution.py:459
  11.3 4.9 %all-to-all-done = s32[8,1,1536]{2,1,0:T(1,128)S(1)} async-done(((s32[8,1,1536]{2,1,0:T(1,128)}), s32[8,1,1536]{2,1,0:T(1,128)S(1)}, u32[]{:S(2)}, u32[]{:S(2)}) %all-to-all-start) | async-done | bytes 49184 | tf_op jit(solution)/shard_map/all_to_all | solution.py:459
  16.2 2.2 copy-done.1
  18.4 9.7 %lookup.3 = bf16[8,768,256]{2,1,0:T(8,128)(2,1)} custom-call(s32[12288]{0:T(1024)S(1)} %bitcast.153, bf16[8192,256]{1,0:T(8,128)(2,1)S(1)} %copy-done.1), custom_call_target="tpu_custom_call" | custom-call | flops 62914560 | bytes 4194304 | tf_op jit(solution)/shard_map/lookup/pallas_call | solution.py:138
  28.1 4.6 %all-to-all-start.1 = ((bf16[8,768,256]{2,1,0:T(8,128)(2,1)}), bf16[8,768,256]{2,1,0:T(8,128)(2,1)}, u32[]{:S(2)}, u32[]{:S(2)}) async-start(bf16[8,768,256]{2,1,0:T(8,128)(2,1)} %lookup.3), calls=%async_computation.1 | async-start | bytes 6291456 | tf_op jit(solution)/shard_map/all_to_all | solution.py:466
  32.8 2.5 collective-permute-start
  41.6 2.2 copy-done.2
  43.7 9.5 %lookup.2 = bf16[8,768,256]{2,1,0:T(8,128)(2,1)} custom-call(s32[12288]{0:T(1024)S(1)} %bitcast.154, bf16[8192,256]{1,0:T(8,128)(2,1)S(1)} %copy-done.2), custom_call_target="tpu_custom_call" | custom-call | flops 62914560 | bytes 4194304 | tf_op jit(solution)/shard_map/lookup/pallas_call | solution.py:138
  53.3 47.8 %adjacency.1.adj_ref = f8e4m3fn[28,3072,256]{2,1,0:T(32,128)(4,1)} custom-call(s32[1]{0:T(128)} %bitcast.8.me_ref, s32[192,256]{1,0:T(8,128)S(1)} %reshape.217.near_ref, bf16[256,128]{1,0:T(8,128)(2,1)S(1)} %pad_maximum_fusion.10.table_ref), custom_call_target="tpu_custom_call" | custom-call | flops 22548578304 | bytes 22020096 | tf_op jit(solution)/shard_map/adjacency/pallas_call | solution.py:196
  101.1 3.2 %all-to-all-done.1.answer_ref = bf16[8,768,256]{2,1,0:T(8,128)(2,1)} async-done(((bf16[8,768,256]{2,1,0:T(8,128)(2,1)}), bf16[8,768,256]{2,1,0:T(8,128)(2,1)}, u32[]{:S(2)}, u32[]{:S(2)}) %all-to-all-start.1) | async-done | bytes 3145760 | tf_op jit(solution)/shard_map/all_to_all | solution.py:466
  104.3 4.5 %all-to-all-start.2 = ((bf16[8,768,256]{2,1,0:T(8,128)(2,1)}), bf16[8,768,256]{2,1,0:T(8,128)(2,1)}, u32[]{:S(2)}, u32[]{:S(2)}) async-start(bf16[8,768,256]{2,1,0:T(8,128)(2,1)} %lookup.2), calls=%async_computation.2 | async-start | bytes 6291456 | tf_op jit(solution)/shard_map/all_to_all | solution.py:507
  111.0 31.9 %gather_sum.2 = (f32[3072,256]{1,0:T(8,128)}, f32[3072,256]{1,0:T(8,128)}) custom-call(s32[2]{0:T(128)S(1)} %pad_add_fusion.6.spans_ref, s32[8]{0:T(128)S(1)} %get-tuple-element.64.counts_ref, s32[9]{0:T(128)S(1)} %get-tuple-element.66.starts_ref, bf16[8,768,256]{2,1,0:T(8,128)(2,1)} %all-to-all-done.1.answer_ref, f32[3072,2]{1,0:T(8,128)S(1)} %bitcast.151, ...), custom_call_target="tpu_custom_call" | custom-call | flops 11274289152 | bytes 11010048 | tf_op jit(solution)/shard_map/gather_sum/pallas_call | solution.py:346
  142.9 37.4 %all-to-all-done.2.answer_ref = bf16[8,768,256]{2,1,0:T(8,128)(2,1)} async-done(((bf16[8,768,256]{2,1,0:T(8,128)(2,1)}), bf16[8,768,256]{2,1,0:T(8,128)(2,1)}, u32[]{:S(2)}, u32[]{:S(2)}) %all-to-all-start.2) | async-done | bytes 3145760 | tf_op jit(solution)/shard_map/all_to_all | solution.py:507
  180.3 14.1 %gather_sum.3 = (bf16[3072,256]{1,0:T(8,128)(2,1)S(1)}, bf16[3072,256]{1,0:T(8,128)(2,1)}, bf16[768,256]{1,0:T(8,128)(2,1)S(1)}, bf16[768,256]{1,0:T(8,128)(2,1)...) custom-call(s32[2]{0:T(128)S(1)} %pad_add_fusion.5.spans_ref, s32[8]{0:T(128)S(1)} %get-tuple-element.65.counts_ref, ...), custom_call_target="tpu_custom_call" | custom-call | flops 11274289152 | bytes 11010048 | tf_op jit(solution)/shard_map/gather_sum/pallas_call | solution.py:346
  201.1 6.4 %collective-permute-done.3 = bf16[768,256]{1,0:T(8,128)(2,1)S(1)} collective-permute-done((bf16[768,256]{1,0:T(8,128)(2,1)S(1)}, bf16[768,256]{1,0:T(8,128)(2,1)S(1)}, u32[]{:S(2)}, u32[]{:S(2)}) %collective-permute-start.3) | collective-permute-done | bytes 393248 | tf_op jit(solution)/shard_map/ppermute | solution.py:377
  207.4 7.0 %collective-permute-done.4 = bf16[768,256]{1,0:T(8,128)(2,1)S(1)} collective-permute-done((bf16[768,256]{1,0:T(8,128)(2,1)S(1)}, bf16[768,256]{1,0:T(8,128)(2,1)S(1)}, u32[]{:S(2)}, u32[]{:S(2)}) %collective-permute-start.4) | collective-permute-done | bytes 393248 | tf_op jit(solution)/shard_map/ppermute | solution.py:377
  219.9 2.7 collective-permute-done.6
  229.0 4.5 %collective-permute-done.9 = bf16[3,128,256]{2,1,0:T(8,128)(2,1)S(1)} collective-permute-done((bf16[3,128,256]{2,1,0:T(8,128)(2,1)S(1)}, bf16[3,128,256]{2,1,0:T(8,128)(2,1)S(1)}, u32[]{:S(2)}, u32[]{:S(2)}) %collective-permute-start.9) | collective-permute-done | bytes 196640 | tf_op jit(solution)/shard_map/ppermute | solution.py:377
  233.5 3.6 %collective-permute-done.10 = bf16[3,128,256]{2,1,0:T(8,128)(2,1)S(1)} collective-permute-done((bf16[3,128,256]{2,1,0:T(8,128)(2,1)S(1)}, bf16[3,128,256]{2,1,0:T(8,128)(2,1)S(1)}, u32[]{:S(2)}, u32[]{:S(2)}) %collective-permute-start.10) | collective-permute-done | bytes 196640 | tf_op jit(solution)/shard_map/ppermute | solution.py:377
  242.7 7.9 %collective-permute-done.12 = bf16[768,256]{1,0:T(8,128)(2,1)S(1)} collective-permute-done((bf16[768,256]{1,0:T(8,128)(2,1)S(1)}, bf16[768,256]{1,0:T(8,128)(2,1)S(1)}, u32[]{:S(2)}, u32[]{:S(2)}) %collective-permute-start.12) | collective-permute-done | bytes 393248 | tf_op jit(solution)/shard_map/ppermute | solution.py:377
  250.6 7.5 %collective-permute-done.13 = bf16[768,256]{1,0:T(8,128)(2,1)S(1)} collective-permute-done((bf16[768,256]{1,0:T(8,128)(2,1)S(1)}, bf16[768,256]{1,0:T(8,128)(2,1)S(1)}, u32[]{:S(2)}, u32[]{:S(2)}) %collective-permute-start.13) | collective-permute-done | bytes 393248 | tf_op jit(solution)/shard_map/ppermute | solution.py:377
  262.1 2.2 collective-permute-start.17
  265.9 2.9 %collective-permute-done.16 = bf16[128,256]{1,0:T(8,128)(2,1)S(1)} collective-permute-done((bf16[128,256]{1,0:T(8,128)(2,1)S(1)}, bf16[128,256]{1,0:T(8,128)(2,1)S(1)}, u32[]{:S(2)}, u32[]{:S(2)}) %collective-permute-start.16) | collective-permute-done | bytes 65568 | tf_op jit(solution)/shard_map/ppermute | solution.py:377
  275.4 4.5 %collective-permute-done.20 = bf16[128,256]{1,0:T(8,128)(2,1)S(1)} collective-permute-done((bf16[128,256]{1,0:T(8,128)(2,1)S(1)}, bf16[128,256]{1,0:T(8,128)(2,1)S(1)}, u32[]{:S(2)}, u32[]{:S(2)}) %collective-permute-start.20) | collective-permute-done | bytes 65568 | tf_op jit(solution)/shard_map/ppermute | solution.py:377
  (145 shorter events, 50.2 us)
Async XLA Ops:
  4.0 12.2 %all-to-all-start = ((s32[8,1,1536]{2,1,0:T(1,128)}), s32[8,1,1536]{2,1,0:T(1,128)S(1)}, u32[]{:S(2)}, u32[]{:S(2)}) async-start(s32[8,1,1536]{2,1,0:T(1,128)} %bitcast.6), calls=%async_computation | async-start | bytes 98304 | tf_op jit(solution)/shard_map/all_to_all | solution.py:459
  28.1 76.1 %all-to-all-start.1 = ((bf16[8,768,256]{2,1,0:T(8,128)(2,1)}), bf16[8,768,256]{2,1,0:T(8,128)(2,1)}, u32[]{:S(2)}, u32[]{:S(2)}) async-start(bf16[8,768,256]{2,1,0:T(8,128)(2,1)} %lookup.3), calls=%async_computation.1 | async-start | bytes 6291456 | tf_op jit(solution)/shard_map/all_to_all | solution.py:466
  32.8 5.7 %collective-permute-start = (s32[11,128]{1,0:T(8,128)S(1)}, s32[11,128]{1,0:T(8,128)S(1)}, u32[]{:S(2)}, u32[]{:S(2)}) collective-permute-start(s32[11,128]{1,0:T(8,128)S(1)} %pad_add_fusion.2), channel_id=1, source_target_pairs={{8,0},{16,8},{24,16},{0,24},{9,1},{17,9},{25,17},{1,25},{10,2},{18... | collective-permute-start | bytes 16904 | tf_op jit(solution)/shard_map/ppermute | solution.py:377
  35.3 3.7 %collective-permute-start.1 = (s32[11,128]{1,0:T(8,128)S(1)}, s32[11,128]{1,0:T(8,128)S(1)}, u32[]{:S(2)}, u32[]{:S(2)}) collective-permute-start(s32[11,128]{1,0:T(8,128)S(1)} %pad_add_fusion.2), channel_id=1, source_target_pairs={{16,0},{24,8},{0,16},{8,24},{17,1},{25,9},{1,17},{9,25},{18,2},{26... | collective-permute-start | bytes 16904 | tf_op jit(solution)/shard_map/ppermute | solution.py:377
  35.8 4.5 %collective-permute-start.2 = (s32[11,128]{1,0:T(8,128)S(1)}, s32[11,128]{1,0:T(8,128)S(1)}, u32[]{:S(2)}, u32[]{:S(2)}) collective-permute-start(s32[11,128]{1,0:T(8,128)S(1)} %pad_add_fusion.2), channel_id=1, source_target_pairs={{24,0},{0,8},{8,16},{16,24},{25,1},{1,9},{9,17},{17,25},{26,2},{2,... | collective-permute-start | bytes 16904 | tf_op jit(solution)/shard_map/ppermute | solution.py:377
  104.3 76.0 %all-to-all-start.2 = ((bf16[8,768,256]{2,1,0:T(8,128)(2,1)}), bf16[8,768,256]{2,1,0:T(8,128)(2,1)}, u32[]{:S(2)}, u32[]{:S(2)}) async-start(bf16[8,768,256]{2,1,0:T(8,128)(2,1)} %lookup.2), calls=%async_computation.2 | async-start | bytes 6291456 | tf_op jit(solution)/shard_map/all_to_all | solution.py:507
  194.4 13.0 %collective-permute-start.3 = (bf16[768,256]{1,0:T(8,128)(2,1)S(1)}, bf16[768,256]{1,0:T(8,128)(2,1)S(1)}, u32[]{:S(2)}, u32[]{:S(2)}) collective-permute-start(bf16[768,256]{1,0:T(8,128)(2,1)S(1)} %get-tuple-element.35), channel_id=1, source_target_pairs={{24,0},{0,8},{8,16},{16,24},{25,1},{1,9},{9,17},{17,25},{26,2},{2,... | collective-permute-start | bytes 1179656 | tf_op jit(solution)/shard_map/ppermute | solution.py:377
  195.9 18.5 %collective-permute-start.4 = (bf16[768,256]{1,0:T(8,128)(2,1)S(1)}, bf16[768,256]{1,0:T(8,128)(2,1)S(1)}, u32[]{:S(2)}, u32[]{:S(2)}) collective-permute-start(bf16[768,256]{1,0:T(8,128)(2,1)S(1)} %get-tuple-element.36), channel_id=1, source_target_pairs={{16,0},{24,8},{0,16},{8,24},{17,1},{25,9},{1,17},{9,25},{18,2},{26... | collective-permute-start | bytes 1179656 | tf_op jit(solution)/shard_map/ppermute | solution.py:377
  197.5 17.1 %collective-permute-start.5 = (bf16[768,256]{1,0:T(8,128)(2,1)S(1)}, bf16[768,256]{1,0:T(8,128)(2,1)S(1)}, u32[]{:S(2)}, u32[]{:S(2)}) collective-permute-start(bf16[768,256]{1,0:T(8,128)(2,1)S(1)} %get-tuple-element.37), channel_id=1, source_target_pairs={{8,0},{16,8},{24,16},{0,24},{9,1},{17,9},{25,17},{1,25},{10,2},{18... | collective-permute-start | bytes 1179656 | tf_op jit(solution)/shard_map/ppermute | solution.py:377
  215.3 7.3 %collective-permute-start.6 = (f32[128,256]{1,0:T(8,128)S(1)}, f32[128,256]{1,0:T(8,128)S(1)}, u32[]{:S(2)}, u32[]{:S(2)}) collective-permute-start(f32[128,256]{1,0:T(8,128)S(1)} %get-tuple-element.49), channel_id=1, source_target_pairs={{24,0},{0,8},{8,16},{16,24},{25,1},{1,9},{9,17},{17,25},{26,2},{2,... | collective-permute-start | bytes 393224 | tf_op jit(solution)/shard_map/ppermute | solution.py:377
  217.1 6.5 %collective-permute-start.7 = (f32[128,256]{1,0:T(8,128)S(1)}, f32[128,256]{1,0:T(8,128)S(1)}, u32[]{:S(2)}, u32[]{:S(2)}) collective-permute-start(f32[128,256]{1,0:T(8,128)S(1)} %get-tuple-element.51), channel_id=1, source_target_pairs={{16,0},{24,8},{0,16},{8,24},{17,1},{25,9},{1,17},{9,25},{18,2},{26... | collective-permute-start | bytes 393224 | tf_op jit(solution)/shard_map/ppermute | solution.py:377
  217.6 6.9 %collective-permute-start.8 = (f32[128,256]{1,0:T(8,128)S(1)}, f32[128,256]{1,0:T(8,128)S(1)}, u32[]{:S(2)}, u32[]{:S(2)}) collective-permute-start(f32[128,256]{1,0:T(8,128)S(1)} %get-tuple-element.50), channel_id=1, source_target_pairs={{8,0},{16,8},{24,16},{0,24},{9,1},{17,9},{25,17},{1,25},{10,2},{18... | collective-permute-start | bytes 393224 | tf_op jit(solution)/shard_map/ppermute | solution.py:377
  225.6 7.9 %collective-permute-start.9 = (bf16[3,128,256]{2,1,0:T(8,128)(2,1)S(1)}, bf16[3,128,256]{2,1,0:T(8,128)(2,1)S(1)}, u32[]{:S(2)}, u32[]{:S(2)}) collective-permute-start(bf16[3,128,256]{2,1,0:T(8,128)(2,1)S(1)} %get-tuple-element.56), channel_id=1, source_target_pairs={{8,0},{16,8},{24,16},{0,24},{9,1},{17,9},{25,17},{1,25},{10,2},{18... | collective-permute-start | bytes 589832 | tf_op jit(solution)/shard_map/ppermute | solution.py:377
  227.3 9.8 %collective-permute-start.10 = (bf16[3,128,256]{2,1,0:T(8,128)(2,1)S(1)}, bf16[3,128,256]{2,1,0:T(8,128)(2,1)S(1)}, u32[]{:S(2)}, u32[]{:S(2)}) collective-permute-start(bf16[3,128,256]{2,1,0:T(8,128)(2,1)S(1)} %get-tuple-element.56), channel_id=1, source_target_pairs={{16,0},{24,8},{0,16},{8,24},{17,1},{25,9},{1,17},{9,25},{18,2},{26... | collective-permute-start | bytes 589832 | tf_op jit(solution)/shard_map/ppermute | solution.py:377
  228.8 8.3 %collective-permute-start.11 = (bf16[3,128,256]{2,1,0:T(8,128)(2,1)S(1)}, bf16[3,128,256]{2,1,0:T(8,128)(2,1)S(1)}, u32[]{:S(2)}, u32[]{:S(2)}) collective-permute-start(bf16[3,128,256]{2,1,0:T(8,128)(2,1)S(1)} %get-tuple-element.56), channel_id=1, source_target_pairs={{24,0},{0,8},{8,16},{16,24},{25,1},{1,9},{9,17},{17,25},{26,2},{2,... | collective-permute-start | bytes 589832 | tf_op jit(solution)/shard_map/ppermute | solution.py:377
  238.5 12.1 %collective-permute-start.12 = (bf16[768,256]{1,0:T(8,128)(2,1)S(1)}, bf16[768,256]{1,0:T(8,128)(2,1)S(1)}, u32[]{:S(2)}, u32[]{:S(2)}) collective-permute-start(bf16[768,256]{1,0:T(8,128)(2,1)S(1)} %fusion.2), channel_id=1, source_target_pairs={{8,0},{16,8},{24,16},{0,24},{9,1},{17,9},{25,17},{1,25},{10,2},{18... | collective-permute-start | bytes 1179656 | tf_op jit(solution)/shard_map/ppermute | solution.py:377
  239.7 18.4 %collective-permute-start.13 = (bf16[768,256]{1,0:T(8,128)(2,1)S(1)}, bf16[768,256]{1,0:T(8,128)(2,1)S(1)}, u32[]{:S(2)}, u32[]{:S(2)}) collective-permute-start(bf16[768,256]{1,0:T(8,128)(2,1)S(1)} %fusion.2), channel_id=1, source_target_pairs={{16,0},{24,8},{0,16},{8,24},{17,1},{25,9},{1,17},{9,25},{18,2},{26... | collective-permute-start | bytes 1179656 | tf_op jit(solution)/shard_map/ppermute | solution.py:377
  240.5 17.6 %collective-permute-start.14 = (bf16[768,256]{1,0:T(8,128)(2,1)S(1)}, bf16[768,256]{1,0:T(8,128)(2,1)S(1)}, u32[]{:S(2)}, u32[]{:S(2)}) collective-permute-start(bf16[768,256]{1,0:T(8,128)(2,1)S(1)} %fusion.2), channel_id=1, source_target_pairs={{24,0},{0,8},{8,16},{16,24},{25,1},{1,9},{9,17},{17,25},{26,2},{2,... | collective-permute-start | bytes 1179656 | tf_op jit(solution)/shard_map/ppermute | solution.py:377
  262.0 6.8 %collective-permute-start.16 = (bf16[128,256]{1,0:T(8,128)(2,1)S(1)}, bf16[128,256]{1,0:T(8,128)(2,1)S(1)}, u32[]{:S(2)}, u32[]{:S(2)}) collective-permute-start(bf16[128,256]{1,0:T(8,128)(2,1)S(1)} %get-tuple-element.52), channel_id=1, source_target_pairs={{6,0},{7,1},{0,2},{1,3},{2,4},{3,5},{4,6},{5,7},{14,8},{15,9},{8,1... | collective-permute-start | bytes 196616 | tf_op jit(solution)/shard_map/ppermute | solution.py:377
  262.1 8.6 %collective-permute-start.17 = (bf16[128,256]{1,0:T(8,128)(2,1)S(1)}, bf16[128,256]{1,0:T(8,128)(2,1)S(1)}, u32[]{:S(2)}, u32[]{:S(2)}) collective-permute-start(bf16[128,256]{1,0:T(8,128)(2,1)S(1)} %get-tuple-element.54), channel_id=1, source_target_pairs={{4,0},{5,1},{6,2},{7,3},{0,4},{1,5},{2,6},{3,7},{12,8},{13,9},{14,... | collective-permute-start | bytes 196616 | tf_op jit(solution)/shard_map/ppermute | solution.py:377
  264.3 6.4 %collective-permute-start.18 = (bf16[128,256]{1,0:T(8,128)(2,1)S(1)}, bf16[128,256]{1,0:T(8,128)(2,1)S(1)}, u32[]{:S(2)}, u32[]{:S(2)}) collective-permute-start(bf16[128,256]{1,0:T(8,128)(2,1)S(1)} %get-tuple-element.53), channel_id=1, source_target_pairs={{2,0},{3,1},{4,2},{5,3},{6,4},{7,5},{0,6},{1,7},{10,8},{11,9},{12,... | collective-permute-start | bytes 196616 | tf_op jit(solution)/shard_map/ppermute | solution.py:377
  270.8 4.6 %collective-permute-start.19 = (bf16[128,256]{1,0:T(8,128)(2,1)S(1)}, bf16[128,256]{1,0:T(8,128)(2,1)S(1)}, u32[]{:S(2)}, u32[]{:S(2)}) collective-permute-start(bf16[128,256]{1,0:T(8,128)(2,1)S(1)} %fusion.15), channel_id=1, source_target_pairs={{2,0},{3,1},{4,2},{5,3},{6,4},{7,5},{0,6},{1,7},{10,8},{11,9},{12,... | collective-permute-start | bytes 196616 | tf_op jit(solution)/shard_map/ppermute | solution.py:377
  272.9 7.0 %collective-permute-start.20 = (bf16[128,256]{1,0:T(8,128)(2,1)S(1)}, bf16[128,256]{1,0:T(8,128)(2,1)S(1)}, u32[]{:S(2)}, u32[]{:S(2)}) collective-permute-start(bf16[128,256]{1,0:T(8,128)(2,1)S(1)} %fusion.15), channel_id=1, source_target_pairs={{4,0},{5,1},{6,2},{7,3},{0,4},{1,5},{2,6},{3,7},{12,8},{13,9},{14,... | collective-permute-start | bytes 196616 | tf_op jit(solution)/shard_map/ppermute | solution.py:377
  273.7 6.2 %collective-permute-start.21 = (bf16[128,256]{1,0:T(8,128)(2,1)S(1)}, bf16[128,256]{1,0:T(8,128)(2,1)S(1)}, u32[]{:S(2)}, u32[]{:S(2)}) collective-permute-start(bf16[128,256]{1,0:T(8,128)(2,1)S(1)} %fusion.15), channel_id=1, source_target_pairs={{6,0},{7,1},{0,2},{1,3},{2,4},{3,5},{4,6},{5,7},{14,8},{15,9},{8,1... | collective-permute-start | bytes 196616 | tf_op jit(solution)/shard_map/ppermute | solution.py:377
  (19 other events, 495.5 us)

commit v7 on v6

--- a/solution.py
+++ b/solution.py
@@ -104,46 +104,55 @@
     )(owners, wanted)
 
 
-def lookup_body(stride, first, width, want_ref, store_ref, out_ref, table, lines):
+def lookup_body(stride, first, width, want_ref, store_ref, *refs):
+    *out_refs, table, lines = refs
     rows_all = store_ref.shape[0]
     halves = store_ref.shape[1] // LANES
     lane = lambda h: pl.ds(h * LANES, LANES)
-    begin = pl.program_id(0) * stride + first
-
-    @pl.when(pl.program_id(0) == 0)
-    def _():
-        @pl.loop(0, rows_all // TILE)
-        def _(j):
-            part = pl.ds(pl.multiple_of(j * TILE, TILE), TILE)
+
+    @pl.loop(0, rows_all // TILE)
+    def _(j):
+        part = pl.ds(pl.multiple_of(j * TILE, TILE), TILE)
+        for h in range(halves):
+            spot = pl.ds(pl.multiple_of(j * TILE * halves, TILE) + h, TILE, stride=halves)
+            table[spot, :] = store_ref[part, lane(h)].astype(jnp.float32)
+
+    group = 0
+    for out_ref in out_refs:
+
+        @pl.loop(0, out_ref.shape[0])
+        def _(k, out_ref=out_ref, group=group):
+            begin = (group + k) * stride + first
+
+            @pl.loop(0, width // SLOTS, unroll=2)
+            def _(j):
+                at = [want_ref[begin + j * SLOTS + u] for u in range(SLOTS)]
+                rows = [table[pl.ds(pl.multiple_of(a, halves), halves), :] for a in at]
+                depth = SLOTS * halves
+                block = lines.at[pl.ds(pl.multiple_of(j * depth, depth), depth)]
+                for u in range(SLOTS):
+                    block[pl.ds(u * halves, halves), :] = rows[u]
+
             for h in range(halves):
-                spot = pl.ds(pl.multiple_of(j * TILE * halves, TILE) + h, TILE, stride=halves)
-                table[spot, :] = store_ref[part, lane(h)].astype(jnp.float32)
-
-    @pl.loop(0, width // SLOTS, unroll=2)
-    def _(j):
-        at = [want_ref[begin + j * SLOTS + u] for u in range(SLOTS)]
-        rows = [table[pl.ds(pl.multiple_of(a, halves), halves), :] for a in at]
-        block = lines.at[pl.ds(pl.multiple_of(j * SLOTS * halves, SLOTS * halves), SLOTS * halves)]
-        for u in range(SLOTS):
-            block[pl.ds(u * halves, halves), :] = rows[u]
-
-    for h in range(halves):
-        out_ref[0, :, lane(h)] = lines[pl.ds(h, width, stride=halves), :].astype(jnp.bfloat16)
-
-
-def lookup(store, places, groups, first, width):
+                out_ref[k, :, lane(h)] = lines[pl.ds(h, width, stride=halves), :].astype(
+                    jnp.bfloat16
+                )
+
+        group += out_ref.shape[0]
+
+
+def lookup(store, places, sizes, first, width):
     rows_all, features = store.shape
     halves = features // LANES
     apart = lambda rows: pltpu.VMEM((rows * halves, LANES), jnp.float32)
     return pl.pallas_call(
-        functools.partial(lookup_body, places.shape[0] // groups, first, width),
-        out_shape=jax.ShapeDtypeStruct((groups, width, features), jnp.bfloat16),
-        grid=(groups,),
-        in_specs=[SMEM, pl.BlockSpec((rows_all, features), lambda g: (0, 0))],
-        out_specs=pl.BlockSpec((1, width, features), lambda g: (g, 0, 0)),
+        functools.partial(lookup_body, places.shape[0] // sum(sizes), first, width),
+        out_shape=[jax.ShapeDtypeStruct((n, width, features), jnp.bfloat16) for n in sizes],
+        in_specs=[SMEM, VMEM],
+        out_specs=[VMEM] * len(sizes),
         scratch_shapes=[apart(rows_all), apart(width)],
         compiler_params=params(24),
-        cost_estimate=cost(groups * width * features * 40, 2 * rows_all * features),
+        cost_estimate=cost(sum(sizes) * width * features * 40, 2 * rows_all * features),
         name="lookup",
     )(places, store)
 
@@ -211,19 +220,22 @@
     )(me, near, table)
 
 
-def collect(piece, counts_ref, starts_ref, answer_ref, landed, arrived, packed):
-    batch_count = answer_ref.shape[0]
-
-    def bring(o):
-        return pltpu.make_async_copy(answer_ref.at[o], landed.at[o], arrived.at[o])
+def collect(piece, counts_ref, starts_ref, answer_refs, landed, arrived, packed):
+    batch_count = landed.shape[0]
+    each = batch_count // len(answer_refs)
+
+    def bring(n):
+        return pltpu.make_async_copy(
+            answer_refs[n], landed.at[pl.ds(n * each, each)], arrived.at[n]
+        )
+
+    for n in range(len(answer_refs)):
+        bring(n).start()
+    for n in range(len(answer_refs)):
+        bring(n).wait()
 
     @pl.loop(0, batch_count)
     def _(o):
-        bring(o).start()
-
-    @pl.loop(0, batch_count)
-    def _(o):
-        bring(o).wait()
         base = starts_ref[o]
 
         @pl.loop(0, pl.cdiv(counts_ref[o], piece))
@@ -239,8 +251,9 @@
 
 
 def gather_sum_body(
-    piece, last, spans_ref, counts_ref, starts_ref, answer_ref, notes_in, adj_ref, *refs
+    piece, last, answers, spans_ref, counts_ref, starts_ref, notes_in, adj_ref, *refs
 ):
+    answer_refs, refs = refs[:answers], refs[answers:]
     if last:
         (total_in, found_in, wself_in, wneigh_in, own_ref, mean_ref) = refs[:6]
         share_refs = refs[6:-11]
@@ -267,7 +280,7 @@
 
     for copy in carry:
         copy.start()
-    collect(piece, counts_ref, starts_ref, answer_ref, landed, arrived, packed)
+    collect(piece, counts_ref, starts_ref, answer_refs, landed, arrived, packed)
     for copy in carry:
         copy.wait()
     if not last:
@@ -317,24 +330,25 @@
                 ).astype(share_ref.dtype)
 
 
-def gather_sum(inputs, parts, spans, counts, starts, answer, notes, adj, rest):
-    batch_count, width, features = answer.shape
+def gather_sum(inputs, parts, spans, counts, starts, answers, notes, adj, rest):
+    batch_count = sum(a.shape[0] for a in answers)
+    _, width, features = answers[0].shape
     tiles, nodes, _ = adj.shape
     piece = LANES if width % LANES == 0 else SLOTS
     last = rest is not None
     room = min(batch_count * width, inputs) + SLOTS * batch_count + 2 * WIDE * TILE
-    in_specs = [SMEM, SMEM, SMEM, ANY, HBM, HBM]
+    in_specs = [SMEM, SMEM, SMEM, HBM, HBM] + [ANY] * len(answers)
     rows = lambda dtype: jax.ShapeDtypeStruct((nodes, features), dtype)
     scratch = [
         pltpu.VMEM((room, features), jnp.bfloat16),
         pltpu.VMEM((2, WIDE, nodes, TILE), adj.dtype),
         pltpu.SemaphoreType.DMA((2,)),
-        pltpu.VMEM(answer.shape, answer.dtype),
-        pltpu.SemaphoreType.DMA((batch_count,)),
+        pltpu.VMEM((batch_count, width, features), jnp.bfloat16),
+        pltpu.SemaphoreType.DMA((len(answers),)),
         pltpu.VMEM(notes.shape, notes.dtype),
         pltpu.SemaphoreType.DMA((5,)),
     ]
-    operands = [answer, notes, adj]
+    operands = [notes, adj, *answers]
     if last:
         operands += list(rest)
         in_specs += [HBM] * len(rest)
@@ -344,7 +358,7 @@
     else:
         out_shape = (rows(jnp.float32), rows(jnp.float32))
     return pl.pallas_call(
-        functools.partial(gather_sum_body, piece, last),
+        functools.partial(gather_sum_body, piece, last, len(answers)),
         out_shape=out_shape,
         in_specs=in_specs,
         out_specs=(VMEM,) * len(out_shape),
@@ -390,10 +404,12 @@
     return [part] + [passed(part, j, axis) for j in range(1, lax.axis_size(axis))]
 
 
+def pushed(blocks, axis):
+    return [blocks[0]] + [passed(x, -j, axis) for j, x in enumerate(blocks) if j]
+
+
 def sum_parts(blocks, axis="feat"):
-    parts = lax.axis_size(axis)
-    came = [blocks[0]] + [passed(blocks[j], -j, axis) for j in range(1, parts)]
-    return sum(x.astype(jnp.float32) for x in came)
+    return sum(x.astype(jnp.float32) for x in pushed(blocks, axis))
 
 
 def swapped(part):
@@ -456,19 +472,35 @@
     wanted = input_row.reshape(input_count // LANES, LANES)
     slots, counts, requests = make_requests(batch_count, capacity, owners, wanted)
     owners = owners.reshape(1, input_count)
-    received = lax.all_to_all(
-        requests.reshape(batch_count, capacity), "batch", split_axis=0, concat_axis=0, tiled=True
-    )
+    requests = requests.reshape(batch_count, capacity)
+    few = batch_count <= FEW
+    if few:
+        blocks = ahead(requests.reshape(batch_count, -1, LANES), "batch")
+        received = jnp.stack(pushed(list(blocks), "batch"))
+        sizes = (1,) * batch_count
+    else:
+        received = lax.all_to_all(requests, "batch", split_axis=0, concat_axis=0, tiled=True)
+        sizes = (batch_count,)
+
+    def answers(looked):
+        if few:
+            return [looked[0]] + [passed(x, j, "batch") for j, x in enumerate(looked) if j]
+        return [lax.all_to_all(looked[0], "batch", split_axis=0, concat_axis=0, tiled=True)]
+
     first = capacity // 2
     places = received.reshape(batch_count * capacity) * (store.shape[1] // LANES)
-    looked_a = lookup(store, places, batch_count, 0, first)
+    looked_a = lookup(store, places, sizes, 0, first)
     near_first, looked_a = lax.optimization_barrier((nbr_one[0], looked_a))
-    answer_a = lax.all_to_all(looked_a, "batch", split_axis=0, concat_axis=0, tiled=True)
-    looked = lookup(store, places, batch_count, first, capacity - first)
+    answer_a = answers(looked_a)
+    looked = lookup(store, places, sizes, first, capacity - first)
 
     depth = WIDE * TILE
     steps = -(-(input_count + 2 * (SLOTS - 1) * batch_count + depth - 1) // depth)
     tally = counts[:, 0]
+    near_owner = owners
+    if few:
+        tally = ahead(tally, "batch")
+        near_owner = (owners - lax.axis_index("batch")) & (batch_count - 1)
     tally_a = jnp.minimum(tally, first)
     tally_b = tally - tally_a
     padded = lambda n: (n + SLOTS - 1) // SLOTS * SLOTS
@@ -484,7 +516,7 @@
         slot + starts_a[:batch_count, None],
         slot - first + steps_a * depth + starts_b[:batch_count, None],
     )
-    mine = owners == jnp.arange(batch_count)[:, None]
+    mine = near_owner == jnp.arange(batch_count)[:, None]
     column = jnp.sum(jnp.where(mine, shifted, 0), axis=0)
     grid = jnp.pad(column.reshape(-1, LANES), ((0, LANES - input_count // LANES), (0, 0))).T
     table = jnp.concatenate([grid // TILE, grid % TILE], axis=0).astype(jnp.bfloat16)
@@ -504,7 +536,7 @@
     near = near.reshape(nodes // SLOTS, TILE)
     adj = adjacency(me, near, table, steps * WIDE, parts, seeds)
     looked, answer_a, adj = lax.optimization_barrier((looked, answer_a, adj))
-    answer_b = lax.all_to_all(looked, "batch", split_axis=0, concat_axis=0, tiled=True)
+    answer_b = answers(looked)
 
     near_two = lists[:, :fanout_two].transpose(1, 0, 2).reshape(fanout_two, seeds)
     deg_all = lists[:, fanout_two].reshape(seeds)

time: 284 us -> 334 us (1.18)
  starting transfers between devices: 41.5 us -> 69 us
  waiting for transfers between devices: 103 us -> 126 us
  Pallas kernels: 115 us -> 110 us
    ppermute x21 -> x42, waiting for transfers between devices: 54.5 us -> 123 us  [passed(): lax.ppermute(part, axis, [((i + shift) % parts, i) for i in range(parts)])]
    all_to_all x3 -> x0, waiting for transfers between devices: 45.4 us -> none  [the longest x1 37.4 us: local(): lax.all_to_all(looked, 'batch', split_axis=0, concat_axis=0, tiled=True)]
    ppermute x21 -> x42, starting transfers between devices: 25.9 us -> 61.3 us  [passed(): lax.ppermute(part, axis, [((i + shift) % parts, i) for i in range(parts)])]
    all_to_all x3 -> x0, starting transfers between devices: 15.4 us -> none  [the longest x1 6.33 us: local(): lax.all_to_all(requests.reshape(batch_count, capacity), 'batch', split_ax...]
    ppermute x2, starting transfers between devices: 0.14 us -> 7.71 us  [swapped(): lax.ppermute(part, 'batch', [(i, i ^ 1) for i in range(lax.axis_size('bat...]
    pallas_call x4, Pallas kernels: 65.3 us -> 61.4 us  [the longest x2 43.8 us: gather_sum(): pl.pallas_call(functools.partial(gather_sum_body, piece, last, len(answer...]
    unnamed x42 -> x56, local copies, waits for them, and re-layouts: 7.78 us -> 6.39 us
  transfers between devices with their start and end apart: 26 -> 44, of which waited for: 21 -> 22; matrix products, arithmetic and copies ran while one was open for 3% -> 4% of each run, Pallas kernels for 32% -> 25%
where the time goes in v7:
time: 334 us
  waiting for transfers between devices  126 us (38%)
  Pallas kernels  110 us (33%)
  starting transfers between devices  69 us (21%)
  local copies, waits for them, and re-layouts  14.3 us (4%)
  other arithmetic  6.83 us (2%)
  matrix products  4.66 us (1%)
    ppermute x42, waiting for transfers between devices, passed(): lax.ppermute(part, axis, [((i + shift) % parts, i) for i in range(parts)])  123 us
    ppermute x42, starting transfers between devices, passed(): lax.ppermute(part, axis, [((i + shift) % parts, i) for i in range(parts)])  61.3 us
    pallas_call x1, Pallas kernels, adjacency(): pl.pallas_call(functools.partial(adjacency_body, tiles), out_shape=jax.Sh...  47.8 us
    pallas_call x2, Pallas kernels, gather_sum(): pl.pallas_call(functools.partial(gather_sum_body, piece, last, len(answer...  43.8 us
    pallas_call x2, Pallas kernels, lookup(): pl.pallas_call(functools.partial(lookup_body, places.shape[0] // sum(size...  17.7 us
    ppermute x2, starting transfers between devices, swapped(): lax.ppermute(part, 'batch', [(i, i ^ 1) for i in range(lax.axis_size('bat...  7.71 us
  transfers between devices with their start and end apart: 44, of which 22 were waited for; matrix products, arithmetic and copies ran while one was open for 4% of the time, Pallas kernels for 25%

profile of v7, /device:TPU:0, one launch (start us, length us, event | category | flops | bytes accessed | tf_op | source)
XLA Modules:
  0.0 333.6 jit_solution(14047813128239087190)
XLA Ops:
  2.1 3.9 %collective-permute-start.14 = (s32[11,128]{1,0:T(8,128)S(1)}, s32[11,128]{1,0:T(8,128)S(1)}, u32[]{:S(2)}, u32[]{:S(2)}) collective-permute-start(s32[11,128]{1,0:T(8,128)S(1)} %pad_add_fusion.2), channel_id=1, source_target_pairs={{8,0},{16,8},{24,16},{0,24},{9,1},{17,9},{25,17},{1,25},{10,2},{18... | collective-permute-start | bytes 16904 | tf_op jit(solution)/shard_map/ppermute | solution.py:391
  29.4 9.2 %lookup.3 = (bf16[1,768,256]{2,1,0:T(8,128)(2,1)S(1)}, bf16[1,768,256]{2,1,0:T(8,128)(2,1)S(1)}, bf16[1,768,256]{2,1,0:T(8,128)(2,1)S(1)}, bf16[1,768,256]{2,1,0...) custom-call(s32[12288]{0:T(1024)S(1)} %mul.69.want_ref, ...), custom_call_target="tpu_custom_call" | custom-call | flops 62914560 | bytes 4194304 | tf_op jit(solution)/shard_map/lookup/pallas_call | solution.py:148
  39.8 3.4 %collective-permute-start.11 = (bf16[1,768,256]{2,1,0:T(8,128)(2,1)}, bf16[1,768,256]{2,1,0:T(8,128)(2,1)S(1)}, u32[]{:S(2)}, u32[]{:S(2)}) collective-permute-start(bf16[1,768,256]{2,1,0:T(8,128)(2,1)} %get-tuple-element.84), channel_id=1, source_target_pairs={{5,0},{6,1},{7,2},{0,3},{1,4},{2,5},{3,6},{4,7},{13,8},{14,9},{15,... | collective-permute-start | bytes 1179656 | tf_op jit(solution)/shard_map/ppermute | solution.py:391
  47.0 3.5 %collective-permute-start.7 = (bf16[1,768,256]{2,1,0:T(8,128)(2,1)S(1)}, bf16[1,768,256]{2,1,0:T(8,128)(2,1)S(1)}, u32[]{:S(2)}, u32[]{:S(2)}) collective-permute-start(bf16[1,768,256]{2,1,0:T(8,128)(2,1)S(1)} %get-tuple-element.80), channel_id=1, source_target_pairs={{1,0},{2,1},{3,2},{4,3},{5,4},{6,5},{7,6},{0,7},{9,8},{10,9},{11,1... | collective-permute-start | bytes 1179656 | tf_op jit(solution)/shard_map/ppermute | solution.py:391
  50.5 31.5 %collective-permute-done.10.refs_4_ = bf16[1,768,256]{2,1,0:T(8,128)(2,1)S(1)} collective-permute-done((bf16[1,768,256]{2,1,0:T(8,128)(2,1)}, bf16[1,768,256]{2,1,0:T(8,128)(2,1)S(1)}, u32[]{:S(2)}, u32[]{:S(2)}) %collective-permute-start.10) | collective-permute-done | bytes 393248 | tf_op jit(solution)/shard_map/ppermute | solution.py:391
  82.0 8.0 %collective-permute-done.11.refs_5_ = bf16[1,768,256]{2,1,0:T(8,128)(2,1)S(1)} collective-permute-done((bf16[1,768,256]{2,1,0:T(8,128)(2,1)}, bf16[1,768,256]{2,1,0:T(8,128)(2,1)S(1)}, u32[]{:S(2)}, u32[]{:S(2)}) %collective-permute-start.11) | collective-permute-done | bytes 393248 | tf_op jit(solution)/shard_map/ppermute | solution.py:391
  90.0 47.8 %adjacency.1.adj_ref = f8e4m3fn[28,3072,256]{2,1,0:T(32,128)(4,1)} custom-call(s32[1]{0:T(128)} %bitcast.29.me_ref, s32[192,256]{1,0:T(8,128)S(1)} %reshape.235.near_ref, bf16[256,128]{1,0:T(8,128)(2,1)S(1)} %pad_maximum_fusion.10.table_ref), custom_call_target="tpu_custom_call" | custom-call | flops 22548578304 | bytes 22020096 | tf_op jit(solution)/shard_map/adjacency/pallas_call | solution.py:205
  137.8 8.4 %lookup.2 = (bf16[1,768,256]{2,1,0:T(8,128)(2,1)S(1)}, bf16[1,768,256]{2,1,0:T(8,128)(2,1)S(1)}, bf16[1,768,256]{2,1,0:T(8,128)(2,1)S(1)}, bf16[1,768,256]{2,1,0...) custom-call(s32[12288]{0:T(1024)S(1)} %mul.69.want_ref, ...), custom_call_target="tpu_custom_call" | custom-call | flops 62914560 | bytes 4194304 | tf_op jit(solution)/shard_map/lookup/pallas_call | solution.py:148
  151.2 4.7 %collective-permute-done.17.refs_1_ = bf16[1,768,256]{2,1,0:T(8,128)(2,1)S(1)} collective-permute-done((bf16[1,768,256]{2,1,0:T(8,128)(2,1)S(1)}, bf16[1,768,256]{2,1,0:T(8,128)(2,1)S(1)}, u32[]{:S(2)}, u32[]{:S(2)}) %collective-permute-start.17) | collective-permute-done | bytes 393248 | tf_op jit(solution)/shard_map/ppermute | solution.py:391
  155.9 8.4 %collective-permute-done.18.refs_2_ = bf16[1,768,256]{2,1,0:T(8,128)(2,1)S(1)} collective-permute-done((bf16[1,768,256]{2,1,0:T(8,128)(2,1)S(1)}, bf16[1,768,256]{2,1,0:T(8,128)(2,1)S(1)}, u32[]{:S(2)}, u32[]{:S(2)}) %collective-permute-start.18) | collective-permute-done | bytes 393248 | tf_op jit(solution)/shard_map/ppermute | solution.py:391
  164.3 26.8 %gather_sum.2 = (f32[3072,256]{1,0:T(8,128)}, f32[3072,256]{1,0:T(8,128)}) custom-call(s32[2]{0:T(128)S(1)} %pad_add_fusion.7.spans_ref, s32[8]{0:T(128)S(1)} %get-tuple-element.118.counts_ref, s32[9]{0:T(128)S(1)} %get-tuple-element.147.starts_ref, f32[3072,2]{1,0:T(8,128)} %bitcast.193, f8e4m3fn[28,3072,256]{2,1,0:T(32,128)(4,1)} %adjacency.1.adj_ref, ...), custom_call_target="tpu_custom_call" | custom-call | flops 11274289152 | bytes 11010048 | tf_op jit(solution)/shard_map/gather_sum/pallas_call | solution.py:360
  191.1 26.8 %collective-permute-done.20.refs_4_ = bf16[1,768,256]{2,1,0:T(8,128)(2,1)S(1)} collective-permute-done((bf16[1,768,256]{2,1,0:T(8,128)(2,1)S(1)}, bf16[1,768,256]{2,1,0:T(8,128)(2,1)S(1)}, u32[]{:S(2)}, u32[]{:S(2)}) %collective-permute-start.20) | collective-permute-done | bytes 393248 | tf_op jit(solution)/shard_map/ppermute | solution.py:391
  219.0 17.0 %gather_sum.3 = (bf16[3072,256]{1,0:T(8,128)(2,1)}, bf16[3072,256]{1,0:T(8,128)(2,1)}, bf16[768,256]{1,0:T(8,128)(2,1)S(1)}, bf16[768,256]{1,0:T(8,128)(2,1)S(1)...) custom-call(s32[2]{0:T(128)S(1)} %pad_add_fusion.6.spans_ref, s32[8]{0:T(128)S(1)} %get-tuple-element.120.counts_ref, ...), custom_call_target="tpu_custom_call" | custom-call | flops 11274289152 | bytes 11010048 | tf_op jit(solution)/shard_map/gather_sum/pallas_call | solution.py:360
  244.8 4.1 %collective-permute-done.25 = bf16[768,256]{1,0:T(8,128)(2,1)S(1)} collective-permute-done((bf16[768,256]{1,0:T(8,128)(2,1)S(1)}, bf16[768,256]{1,0:T(8,128)(2,1)S(1)}, u32[]{:S(2)}, u32[]{:S(2)}) %collective-permute-start.25) | collective-permute-done | bytes 393248 | tf_op jit(solution)/shard_map/ppermute | solution.py:391
  253.9 3.3 collective-permute-done.27
  262.6 3.3 collective-permute-start.31
  266.2 4.1 %collective-permute-done.30 = bf16[3,128,256]{2,1,0:T(8,128)(2,1)S(1)} collective-permute-done((bf16[3,128,256]{2,1,0:T(8,128)(2,1)S(1)}, bf16[3,128,256]{2,1,0:T(8,128)(2,1)S(1)}, u32[]{:S(2)}, u32[]{:S(2)}) %collective-permute-start.30) | collective-permute-done | bytes 196640 | tf_op jit(solution)/shard_map/ppermute | solution.py:391
  278.6 5.9 %collective-permute-done.33 = bf16[768,256]{1,0:T(8,128)(2,1)S(1)} collective-permute-done((bf16[768,256]{1,0:T(8,128)(2,1)S(1)}, bf16[768,256]{1,0:T(8,128)(2,1)S(1)}, u32[]{:S(2)}, u32[]{:S(2)}) %collective-permute-start.33) | collective-permute-done | bytes 393248 | tf_op jit(solution)/shard_map/ppermute | solution.py:391
  284.6 3.9 %collective-permute-done.34 = bf16[768,256]{1,0:T(8,128)(2,1)S(1)} collective-permute-done((bf16[768,256]{1,0:T(8,128)(2,1)S(1)}, bf16[768,256]{1,0:T(8,128)(2,1)S(1)}, u32[]{:S(2)}, u32[]{:S(2)}) %collective-permute-start.34) | collective-permute-done | bytes 393248 | tf_op jit(solution)/shard_map/ppermute | solution.py:391
  288.5 3.1 collective-permute-done.35
  293.6 7.6 %collective-permute-start.36 = (bf16[512,256]{1,0:T(8,128)(2,1)S(1)}, bf16[512,256]{1,0:T(8,128)(2,1)S(1)}, u32[]{:S(2)}, u32[]{:S(2)}) collective-permute-start(bf16[512,256]{1,0:T(8,128)(2,1)S(1)} %select_convert_fusion), channel_id=1, source_target_pairs={{0,1},{1,0},{2,3},{3,2},{4,5},{5,4},{6,7},{7,6},{8,9},{9,8},{10,11... | collective-permute-start | bytes 786440 | tf_op jit(solution)/shard_map/ppermute | solution.py:416
  302.7 12.0 %collective-permute-start.37 = (bf16[128,256]{1,0:T(8,128)(2,1)S(1)}, bf16[128,256]{1,0:T(8,128)(2,1)S(1)}, u32[]{:S(2)}, u32[]{:S(2)}) collective-permute-start(bf16[128,256]{1,0:T(8,128)(2,1)S(1)} %get-tuple-element.130), channel_id=1, source_target_pairs={{6,0},{7,1},{0,2},{1,3},{2,4},{3,5},{4,6},{5,7},{14,8},{15,9},{8,1... | collective-permute-start | bytes 196616 | tf_op jit(solution)/shard_map/ppermute | solution.py:391
  317.2 3.6 %collective-permute-done.38 = bf16[128,256]{1,0:T(8,128)(2,1)S(1)} collective-permute-done((bf16[128,256]{1,0:T(8,128)(2,1)S(1)}, bf16[128,256]{1,0:T(8,128)(2,1)S(1)}, u32[]{:S(2)}, u32[]{:S(2)}) %collective-permute-start.38) | collective-permute-done | bytes 65568 | tf_op jit(solution)/shard_map/ppermute | solution.py:391
  326.1 4.5 %collective-permute-done.41 = bf16[128,256]{1,0:T(8,128)(2,1)S(1)} collective-permute-done((bf16[128,256]{1,0:T(8,128)(2,1)S(1)}, bf16[128,256]{1,0:T(8,128)(2,1)S(1)}, u32[]{:S(2)}, u32[]{:S(2)}) %collective-permute-start.41) | collective-permute-done | bytes 65568 | tf_op jit(solution)/shard_map/ppermute | solution.py:391
  (201 shorter events, 75.9 us)
Async XLA Ops:
  2.1 15.9 %collective-permute-start.14 = (s32[11,128]{1,0:T(8,128)S(1)}, s32[11,128]{1,0:T(8,128)S(1)}, u32[]{:S(2)}, u32[]{:S(2)}) collective-permute-start(s32[11,128]{1,0:T(8,128)S(1)} %pad_add_fusion.2), channel_id=1, source_target_pairs={{8,0},{16,8},{24,16},{0,24},{9,1},{17,9},{25,17},{1,25},{10,2},{18... | collective-permute-start | bytes 16904 | tf_op jit(solution)/shard_map/ppermute | solution.py:391
  6.0 14.6 %collective-permute-start.15 = (s32[11,128]{1,0:T(8,128)S(1)}, s32[11,128]{1,0:T(8,128)S(1)}, u32[]{:S(2)}, u32[]{:S(2)}) collective-permute-start(s32[11,128]{1,0:T(8,128)S(1)} %pad_add_fusion.2), channel_id=1, source_target_pairs={{16,0},{24,8},{0,16},{8,24},{17,1},{25,9},{1,17},{9,25},{18,2},{26... | collective-permute-start | bytes 16904 | tf_op jit(solution)/shard_map/ppermute | solution.py:391
  6.5 15.3 %collective-permute-start.16 = (s32[11,128]{1,0:T(8,128)S(1)}, s32[11,128]{1,0:T(8,128)S(1)}, u32[]{:S(2)}, u32[]{:S(2)}) collective-permute-start(s32[11,128]{1,0:T(8,128)S(1)} %pad_add_fusion.2), channel_id=1, source_target_pairs={{24,0},{0,8},{8,16},{16,24},{25,1},{1,9},{9,17},{17,25},{26,2},{2,... | collective-permute-start | bytes 16904 | tf_op jit(solution)/shard_map/ppermute | solution.py:391
  9.8 13.2 %collective-permute-start = (s32[12,128]{1,0:T(8,128)S(1)}, s32[12,128]{1,0:T(8,128)S(1)}, u32[]{:S(2)}, u32[]{:S(2)}) collective-permute-start(s32[12,128]{1,0:T(8,128)S(1)} %get-tuple-element.145), channel_id=1, source_target_pairs={{7,0},{0,1},{1,2},{2,3},{3,4},{4,5},{5,6},{6,7},{15,8},{8,9},{9,10... | collective-permute-start | bytes 18440 | tf_op jit(solution)/shard_map/ppermute | solution.py:391
  9.9 14.5 %collective-permute-start.1 = (s32[12,128]{1,0:T(8,128)S(1)}, s32[12,128]{1,0:T(8,128)S(1)}, u32[]{:S(2)}, u32[]{:S(2)}) collective-permute-start(s32[12,128]{1,0:T(8,128)S(1)} %get-tuple-element.144), channel_id=1, source_target_pairs={{6,0},{7,1},{0,2},{1,3},{2,4},{3,5},{4,6},{5,7},{14,8},{15,9},{8,1... | collective-permute-start | bytes 18440 | tf_op jit(solution)/shard_map/ppermute | solution.py:391
  39.4 42.6 %collective-permute-start.10 = (bf16[1,768,256]{2,1,0:T(8,128)(2,1)}, bf16[1,768,256]{2,1,0:T(8,128)(2,1)S(1)}, u32[]{:S(2)}, u32[]{:S(2)}) collective-permute-start(bf16[1,768,256]{2,1,0:T(8,128)(2,1)} %get-tuple-element.83), channel_id=1, source_target_pairs={{4,0},{5,1},{6,2},{7,3},{0,4},{1,5},{2,6},{3,7},{12,8},{13,9},{14,... | collective-permute-start | bytes 1179656 | tf_op jit(solution)/shard_map/ppermute | solution.py:391
  39.8 50.2 %collective-permute-start.11 = (bf16[1,768,256]{2,1,0:T(8,128)(2,1)}, bf16[1,768,256]{2,1,0:T(8,128)(2,1)S(1)}, u32[]{:S(2)}, u32[]{:S(2)}) collective-permute-start(bf16[1,768,256]{2,1,0:T(8,128)(2,1)} %get-tuple-element.84), channel_id=1, source_target_pairs={{5,0},{6,1},{7,2},{0,3},{1,4},{2,5},{3,6},{4,7},{13,8},{14,9},{15,... | collective-permute-start | bytes 1179656 | tf_op jit(solution)/shard_map/ppermute | solution.py:391
  46.8 99.4 %collective-permute-start.12 = (bf16[1,768,256]{2,1,0:T(8,128)(2,1)}, bf16[1,768,256]{2,1,0:T(8,128)(2,1)S(1)}, u32[]{:S(2)}, u32[]{:S(2)}) collective-permute-start(bf16[1,768,256]{2,1,0:T(8,128)(2,1)} %copy-done.5), channel_id=1, source_target_pairs={{6,0},{7,1},{0,2},{1,3},{2,4},{3,5},{4,6},{5,7},{14,8},{15,9},{8,1... | collective-permute-start | bytes 1179656 | tf_op jit(solution)/shard_map/ppermute | solution.py:391
  46.9 99.3 %collective-permute-start.13 = (bf16[1,768,256]{2,1,0:T(8,128)(2,1)S(1)}, bf16[1,768,256]{2,1,0:T(8,128)(2,1)S(1)}, u32[]{:S(2)}, u32[]{:S(2)}) collective-permute-start(bf16[1,768,256]{2,1,0:T(8,128)(2,1)S(1)} %get-tuple-element.86), channel_id=1, source_target_pairs={{7,0},{0,1},{1,2},{2,3},{3,4},{4,5},{5,6},{6,7},{15,8},{8,9},{9,10... | collective-permute-start | bytes 1179656 | tf_op jit(solution)/shard_map/ppermute | solution.py:391
  47.0 99.2 %collective-permute-start.7 = (bf16[1,768,256]{2,1,0:T(8,128)(2,1)S(1)}, bf16[1,768,256]{2,1,0:T(8,128)(2,1)S(1)}, u32[]{:S(2)}, u32[]{:S(2)}) collective-permute-start(bf16[1,768,256]{2,1,0:T(8,128)(2,1)S(1)} %get-tuple-element.80), channel_id=1, source_target_pairs={{1,0},{2,1},{3,2},{4,3},{5,4},{6,5},{7,6},{0,7},{9,8},{10,9},{11,1... | collective-permute-start | bytes 1179656 | tf_op jit(solution)/shard_map/ppermute | solution.py:391
  82.0 64.3 %collective-permute-start.8 = (bf16[1,768,256]{2,1,0:T(8,128)(2,1)S(1)}, bf16[1,768,256]{2,1,0:T(8,128)(2,1)S(1)}, u32[]{:S(2)}, u32[]{:S(2)}) collective-permute-start(bf16[1,768,256]{2,1,0:T(8,128)(2,1)S(1)} %get-tuple-element.81), channel_id=1, source_target_pairs={{2,0},{3,1},{4,2},{5,3},{6,4},{7,5},{0,6},{1,7},{10,8},{11,9},{12,... | collective-permute-start | bytes 1179656 | tf_op jit(solution)/shard_map/ppermute | solution.py:391
  90.0 56.3 %collective-permute-start.9 = (bf16[1,768,256]{2,1,0:T(8,128)(2,1)S(1)}, bf16[1,768,256]{2,1,0:T(8,128)(2,1)S(1)}, u32[]{:S(2)}, u32[]{:S(2)}) collective-permute-start(bf16[1,768,256]{2,1,0:T(8,128)(2,1)S(1)} %get-tuple-element.82), channel_id=1, source_target_pairs={{3,0},{4,1},{5,2},{6,3},{7,4},{0,5},{1,6},{2,7},{11,8},{12,9},{13,... | collective-permute-start | bytes 1179656 | tf_op jit(solution)/shard_map/ppermute | solution.py:391
  146.3 18.0 %collective-permute-start.18 = (bf16[1,768,256]{2,1,0:T(8,128)(2,1)S(1)}, bf16[1,768,256]{2,1,0:T(8,128)(2,1)S(1)}, u32[]{:S(2)}, u32[]{:S(2)}) collective-permute-start(bf16[1,768,256]{2,1,0:T(8,128)(2,1)S(1)} %get-tuple-element.92), channel_id=1, source_target_pairs={{2,0},{3,1},{4,2},{5,3},{6,4},{7,5},{0,6},{1,7},{10,8},{11,9},{12,... | collective-permute-start | bytes 1179656 | tf_op jit(solution)/shard_map/ppermute | solution.py:391
  147.3 43.8 %collective-permute-start.19 = (bf16[1,768,256]{2,1,0:T(8,128)(2,1)S(1)}, bf16[1,768,256]{2,1,0:T(8,128)(2,1)S(1)}, u32[]{:S(2)}, u32[]{:S(2)}) collective-permute-start(bf16[1,768,256]{2,1,0:T(8,128)(2,1)S(1)} %get-tuple-element.93), channel_id=1, source_target_pairs={{3,0},{4,1},{5,2},{6,3},{7,4},{0,5},{1,6},{2,7},{11,8},{12,9},{13,... | collective-permute-start | bytes 1179656 | tf_op jit(solution)/shard_map/ppermute | solution.py:391
  149.5 68.5 %collective-permute-start.20 = (bf16[1,768,256]{2,1,0:T(8,128)(2,1)S(1)}, bf16[1,768,256]{2,1,0:T(8,128)(2,1)S(1)}, u32[]{:S(2)}, u32[]{:S(2)}) collective-permute-start(bf16[1,768,256]{2,1,0:T(8,128)(2,1)S(1)} %get-tuple-element.94), channel_id=1, source_target_pairs={{4,0},{5,1},{6,2},{7,3},{0,4},{1,5},{2,6},{3,7},{12,8},{13,9},{14,... | collective-permute-start | bytes 1179656 | tf_op jit(solution)/shard_map/ppermute | solution.py:391
  149.8 68.2 %collective-permute-start.21 = (bf16[1,768,256]{2,1,0:T(8,128)(2,1)S(1)}, bf16[1,768,256]{2,1,0:T(8,128)(2,1)S(1)}, u32[]{:S(2)}, u32[]{:S(2)}) collective-permute-start(bf16[1,768,256]{2,1,0:T(8,128)(2,1)S(1)} %get-tuple-element.95), channel_id=1, source_target_pairs={{5,0},{6,1},{7,2},{0,3},{1,4},{2,5},{3,6},{4,7},{13,8},{14,9},{15,... | collective-permute-start | bytes 1179656 | tf_op jit(solution)/shard_map/ppermute | solution.py:391
  155.9 62.1 %collective-permute-start.22 = (bf16[1,768,256]{2,1,0:T(8,128)(2,1)S(1)}, bf16[1,768,256]{2,1,0:T(8,128)(2,1)S(1)}, u32[]{:S(2)}, u32[]{:S(2)}) collective-permute-start(bf16[1,768,256]{2,1,0:T(8,128)(2,1)S(1)} %get-tuple-element.96), channel_id=1, source_target_pairs={{6,0},{7,1},{0,2},{1,3},{2,4},{3,5},{4,6},{5,7},{14,8},{15,9},{8,1... | collective-permute-start | bytes 1179656 | tf_op jit(solution)/shard_map/ppermute | solution.py:391
  164.3 53.6 %collective-permute-start.23 = (bf16[1,768,256]{2,1,0:T(8,128)(2,1)S(1)}, bf16[1,768,256]{2,1,0:T(8,128)(2,1)S(1)}, u32[]{:S(2)}, u32[]{:S(2)}) collective-permute-start(bf16[1,768,256]{2,1,0:T(8,128)(2,1)S(1)} %get-tuple-element.97), channel_id=1, source_target_pairs={{7,0},{0,1},{1,2},{2,3},{3,4},{4,5},{5,6},{6,7},{15,8},{8,9},{9,10... | collective-permute-start | bytes 1179656 | tf_op jit(solution)/shard_map/ppermute | solution.py:391
  238.4 10.5 %collective-permute-start.25 = (bf16[768,256]{1,0:T(8,128)(2,1)S(1)}, bf16[768,256]{1,0:T(8,128)(2,1)S(1)}, u32[]{:S(2)}, u32[]{:S(2)}) collective-permute-start(bf16[768,256]{1,0:T(8,128)(2,1)S(1)} %get-tuple-element.110), channel_id=1, source_target_pairs={{16,0},{24,8},{0,16},{8,24},{17,1},{25,9},{1,17},{9,25},{18,2},{26... | collective-permute-start | bytes 1179656 | tf_op jit(solution)/shard_map/ppermute | solution.py:391
  239.0 10.0 %collective-permute-start.26 = (bf16[768,256]{1,0:T(8,128)(2,1)S(1)}, bf16[768,256]{1,0:T(8,128)(2,1)S(1)}, u32[]{:S(2)}, u32[]{:S(2)}) collective-permute-start(bf16[768,256]{1,0:T(8,128)(2,1)S(1)} %get-tuple-element.111), channel_id=1, source_target_pairs={{8,0},{16,8},{24,16},{0,24},{9,1},{17,9},{25,17},{1,25},{10,2},{18... | collective-permute-start | bytes 1179656 | tf_op jit(solution)/shard_map/ppermute | solution.py:391
  262.6 10.6 %collective-permute-start.31 = (bf16[3,128,256]{2,1,0:T(8,128)(2,1)S(1)}, bf16[3,128,256]{2,1,0:T(8,128)(2,1)S(1)}, u32[]{:S(2)}, u32[]{:S(2)}) collective-permute-start(bf16[3,128,256]{2,1,0:T(8,128)(2,1)S(1)} %get-tuple-element.134), channel_id=1, source_target_pairs={{16,0},{24,8},{0,16},{8,24},{17,1},{25,9},{1,17},{9,25},{18,2},{26... | collective-permute-start | bytes 589832 | tf_op jit(solution)/shard_map/ppermute | solution.py:391
  276.0 12.4 %collective-permute-start.34 = (bf16[768,256]{1,0:T(8,128)(2,1)S(1)}, bf16[768,256]{1,0:T(8,128)(2,1)S(1)}, u32[]{:S(2)}, u32[]{:S(2)}) collective-permute-start(bf16[768,256]{1,0:T(8,128)(2,1)S(1)} %fusion.2), channel_id=1, source_target_pairs={{16,0},{24,8},{0,16},{8,24},{17,1},{25,9},{1,17},{9,25},{18,2},{26... | collective-permute-start | bytes 1179656 | tf_op jit(solution)/shard_map/ppermute | solution.py:391
  277.4 14.1 %collective-permute-start.35 = (bf16[768,256]{1,0:T(8,128)(2,1)S(1)}, bf16[768,256]{1,0:T(8,128)(2,1)S(1)}, u32[]{:S(2)}, u32[]{:S(2)}) collective-permute-start(bf16[768,256]{1,0:T(8,128)(2,1)S(1)} %fusion.2), channel_id=1, source_target_pairs={{24,0},{0,8},{8,16},{16,24},{25,1},{1,9},{9,17},{17,25},{26,2},{2,... | collective-permute-start | bytes 1179656 | tf_op jit(solution)/shard_map/ppermute | solution.py:391
  302.7 14.5 %collective-permute-start.37 = (bf16[128,256]{1,0:T(8,128)(2,1)S(1)}, bf16[128,256]{1,0:T(8,128)(2,1)S(1)}, u32[]{:S(2)}, u32[]{:S(2)}) collective-permute-start(bf16[128,256]{1,0:T(8,128)(2,1)S(1)} %get-tuple-element.130), channel_id=1, source_target_pairs={{6,0},{7,1},{0,2},{1,3},{2,4},{3,5},{4,6},{5,7},{14,8},{15,9},{8,1... | collective-permute-start | bytes 196616 | tf_op jit(solution)/shard_map/ppermute | solution.py:391
  (41 other events, 674.7 us)

commit v8 on v6

--- a/solution.py
+++ b/solution.py
@@ -104,7 +104,7 @@
     )(owners, wanted)
 
 
-def lookup_body(stride, first, width, want_ref, store_ref, out_ref, table, lines):
+def lookup_body(stride, first, width, want_ref, store_in, out_ref, table, lines, store_ref, came):
     rows_all = store_ref.shape[0]
     halves = store_ref.shape[1] // LANES
     lane = lambda h: pl.ds(h * LANES, LANES)
@@ -112,12 +112,25 @@
 
     @pl.when(pl.program_id(0) == 0)
     def _():
-        @pl.loop(0, rows_all // TILE)
-        def _(j):
-            part = pl.ds(pl.multiple_of(j * TILE, TILE), TILE)
-            for h in range(halves):
-                spot = pl.ds(pl.multiple_of(j * TILE * halves, TILE) + h, TILE, stride=halves)
-                table[spot, :] = store_ref[part, lane(h)].astype(jnp.float32)
+        pieces = came.shape[0]
+        depth = rows_all // pieces
+        copies = [
+            pltpu.make_async_copy(
+                store_in.at[pl.ds(n * depth, depth)], store_ref.at[pl.ds(n * depth, depth)], came.at[n]
+            )
+            for n in range(pieces)
+        ]
+        for copy in copies:
+            copy.start()
+        for n, copy in enumerate(copies):
+            copy.wait()
+
+            @pl.loop(n * depth // TILE, (n + 1) * depth // TILE)
+            def _(j):
+                part = pl.ds(pl.multiple_of(j * TILE, TILE), TILE)
+                for h in range(halves):
+                    spot = pl.ds(pl.multiple_of(j * TILE * halves, TILE) + h, TILE, stride=halves)
+                    table[spot, :] = store_ref[part, lane(h)].astype(jnp.float32)
 
     @pl.loop(0, width // SLOTS, unroll=2)
     def _(j):
@@ -139,9 +152,14 @@
         functools.partial(lookup_body, places.shape[0] // groups, first, width),
         out_shape=jax.ShapeDtypeStruct((groups, width, features), jnp.bfloat16),
         grid=(groups,),
-        in_specs=[SMEM, pl.BlockSpec((rows_all, features), lambda g: (0, 0))],
+        in_specs=[SMEM, HBM],
         out_specs=pl.BlockSpec((1, width, features), lambda g: (g, 0, 0)),
-        scratch_shapes=[apart(rows_all), apart(width)],
+        scratch_shapes=[
+            apart(rows_all),
+            apart(width),
+            pltpu.VMEM((rows_all, features), store.dtype),
+            pltpu.SemaphoreType.DMA((4,)),
+        ],
         compiler_params=params(24),
         cost_estimate=cost(groups * width * features * 40, 2 * rows_all * features),
         name="lookup",
@@ -212,26 +230,32 @@
 
 
 def collect(piece, counts_ref, starts_ref, answer_ref, landed, arrived, packed):
-    batch_count = answer_ref.shape[0]
-
-    def bring(o):
-        return pltpu.make_async_copy(answer_ref.at[o], landed.at[o], arrived.at[o])
-
-    @pl.loop(0, batch_count)
-    def _(o):
-        bring(o).start()
-
-    @pl.loop(0, batch_count)
-    def _(o):
-        bring(o).wait()
-        base = starts_ref[o]
-
-        @pl.loop(0, pl.cdiv(counts_ref[o], piece))
-        def _(c):
-            source = pl.ds(pl.multiple_of(c * piece, piece), piece)
-            target = pl.ds(pl.multiple_of(base + c * piece, SLOTS), piece)
-            packed[target, :] = landed[o, source, :]
-
+    batch_count, width, _ = answer_ref.shape
+    pieces = width // piece
+
+    def each_used(what):
+        @pl.loop(0, batch_count)
+        def _(o):
+            for c in range(pieces):
+
+                @pl.when(c * piece < counts_ref[o])
+                def _(c=c):
+                    part = pl.ds(c * piece, piece)
+                    what(
+                        o,
+                        c,
+                        part,
+                        pltpu.make_async_copy(
+                            answer_ref.at[o, part], landed.at[o, part], arrived.at[o, c]
+                        ),
+                    )
+
+    def lay(o, c, part, copy):
+        copy.wait()
+        packed[pl.ds(pl.multiple_of(starts_ref[o] + c * piece, SLOTS), piece), :] = landed[o, part]
+
+    each_used(lambda o, c, part, copy: copy.start())
+    each_used(lay)
     end = starts_ref[batch_count]
     packed[pl.ds(pl.multiple_of(end, SLOTS), WIDE * TILE), :] = jnp.zeros(
         (WIDE * TILE, packed.shape[1]), packed.dtype
@@ -239,14 +263,16 @@
 
 
 def gather_sum_body(
-    piece, last, spans_ref, counts_ref, starts_ref, answer_ref, notes_in, adj_ref, *refs
+    piece, last, row0, spans_ref, counts_ref, starts_ref, answer_ref, notes_in, adj_ref, *refs
 ):
     if last:
         (total_in, found_in, wself_in, wneigh_in, own_ref, mean_ref) = refs[:6]
         share_refs = refs[6:-11]
         packed, tiles_ref, ready, landed, arrived, notes_ref, carried = refs[-11:-4]
         total_ref, found_ref, wself_ref, wneigh_ref = refs[-4:]
-        pairs = ((notes_in, notes_ref), (total_in, total_ref), (found_in, found_ref))
+        mine = pl.ds(row0, total_ref.shape[0])
+        pairs = ((notes_in.at[mine], notes_ref), (total_in.at[mine], total_ref))
+        pairs += ((found_in.at[mine], found_ref),)
         pairs += ((wself_in, wself_ref), (wneigh_in, wneigh_ref))
     else:
         total_ref, found_ref, packed, tiles_ref, ready, landed, arrived, notes_ref, carried = refs
@@ -258,7 +284,9 @@
 
     def fetch(step, slot):
         return pltpu.make_async_copy(
-            adj_ref.at[pl.ds(begin + step * WIDE, WIDE)], tiles_ref.at[slot], ready.at[slot]
+            adj_ref.at[pl.ds(begin + step * WIDE, WIDE), pl.ds(row0, nodes)],
+            tiles_ref.at[slot],
+            ready.at[slot],
         )
 
     @pl.when(count > 0)
@@ -317,9 +345,10 @@
                 ).astype(share_ref.dtype)
 
 
-def gather_sum(inputs, parts, spans, counts, starts, answer, notes, adj, rest):
+def gather_sum(inputs, spans, counts, starts, answer, notes, adj, rest=None, row0=0, shares=()):
     batch_count, width, features = answer.shape
     tiles, nodes, _ = adj.shape
+    nodes = sum(shares) or nodes
     piece = LANES if width % LANES == 0 else SLOTS
     last = rest is not None
     room = min(batch_count * width, inputs) + SLOTS * batch_count + 2 * WIDE * TILE
@@ -330,21 +359,24 @@
         pltpu.VMEM((2, WIDE, nodes, TILE), adj.dtype),
         pltpu.SemaphoreType.DMA((2,)),
         pltpu.VMEM(answer.shape, answer.dtype),
-        pltpu.SemaphoreType.DMA((batch_count,)),
-        pltpu.VMEM(notes.shape, notes.dtype),
+        pltpu.SemaphoreType.DMA((batch_count, width // piece)),
+        pltpu.VMEM((nodes, notes.shape[1]), notes.dtype),
         pltpu.SemaphoreType.DMA((5,)),
     ]
     operands = [answer, notes, adj]
     if last:
         operands += list(rest)
         in_specs += [HBM] * len(rest)
-        share = jax.ShapeDtypeStruct((nodes // parts, rest[3].shape[1]), jnp.bfloat16)
-        out_shape = (rows(jnp.bfloat16), rows(jnp.bfloat16)) + (share,) * parts
-        scratch += [pltpu.VMEM(x.shape, x.dtype) for x in rest]
+        out_shape = (rows(jnp.bfloat16), rows(jnp.bfloat16))
+        out_shape += tuple(
+            jax.ShapeDtypeStruct((n, rest[3].shape[1]), jnp.bfloat16) for n in shares
+        )
+        scratch += [pltpu.VMEM((nodes, features), jnp.float32)] * 2
+        scratch += [pltpu.VMEM(x.shape, x.dtype) for x in rest[2:]]
     else:
         out_shape = (rows(jnp.float32), rows(jnp.float32))
     return pl.pallas_call(
-        functools.partial(gather_sum_body, piece, last),
+        functools.partial(gather_sum_body, piece, last, row0),
         out_shape=out_shape,
         in_specs=in_specs,
         out_specs=(VMEM,) * len(out_shape),
@@ -520,21 +552,26 @@
         place[:, :, None] == jnp.arange(share)[None, None, :], axis=0, dtype=jnp.float32
     ).astype(jnp.bfloat16)
 
-    total, found = gather_sum(
-        input_count, parts, spans_a, tally_a, starts_a, answer_a, notes, adj, None
-    )
-    self_one, agg_one, *z_blocks = gather_sum(
-        input_count,
-        parts,
-        spans_b,
-        tally_b,
-        starts_b,
-        answer_b,
-        notes,
-        adj,
-        (total, found, w1_self, w1_neigh),
-    )
-    z_share = sum_parts(z_blocks) + bias_one
+    total, found = gather_sum(input_count, spans_a, tally_a, starts_a, answer_a, notes, adj)
+
+    def finish(begin, end):
+        return gather_sum(
+            input_count,
+            spans_b,
+            tally_b,
+            starts_b,
+            answer_b,
+            notes,
+            adj,
+            (total, found, w1_self, w1_neigh),
+            begin * share,
+            (share,) * (end - begin),
+        )
+
+    self_far, agg_far, *z_far = finish(1, parts)
+    total, z_far = lax.optimization_barrier((total, z_far))
+    self_near, agg_near, *z_near = finish(0, 1)
+    z_share = sum_parts(z_near + z_far) + bias_one
     hidden = jax.nn.silu(z_share).astype(jnp.bfloat16)
 
     agg_parts = jnp.dot(adj_two, hidden, preferred_element_type=jnp.float32)
@@ -558,11 +595,13 @@
     dh_share = contract_rows(adj_two, back_high) + contract_rows(adj_two, back_low)
     dh_share = dh_share + jnp.pad(contract_cols(dz_two, w2_self), ((0, rest), (0, 0)))
     dz_share = (dh_share * silu_grad(z_share)).astype(jnp.bfloat16)
-    dz_one = jnp.concatenate(spread_parts(dz_share))
+    dz_blocks = spread_parts(dz_share)
+    dz_near, dz_far = dz_blocks[0], jnp.concatenate(dz_blocks[1:])
     group = turned(group, (parts - feat_index) % parts).transpose(1, 0, 2, 3)
     self_all, agg_all, dz_all = (x.reshape(seeds, hidden_width) for x in group)
     grads = [contract_rows(self_all, dz_all), contract_rows(agg_all, dz_all)]
-    grads += [contract_rows(self_one, dz_one), contract_rows(agg_one, dz_one)]
+    grads.append(contract_rows(self_near, dz_near) + contract_rows(self_far, dz_far))
+    grads.append(contract_rows(agg_near, dz_near) + contract_rows(agg_far, dz_far))
     total = total_over_batch(jnp.concatenate(grads)).astype(jnp.float32)
     return (activations, *total.reshape(len(grads), -1, hidden_width))
 

time: 284 us -> 278 us (0.979)
  waiting for transfers between devices: 103 us -> 94.9 us
    ppermute x21, waiting for transfers between devices: 54.5 us -> 45.9 us  [passed(): lax.ppermute(part, axis, [((i + shift) % parts, i) for i in range(parts)])]
    unnamed x42 -> x46, local copies, waits for them, and re-layouts: 7.78 us -> 7.06 us
    pallas_call x2 -> x3, Pallas kernels: 46 us -> 45.9 us  [gather_sum(): pl.pallas_call(functools.partial(gather_sum_body, piece, last, row0), out...]
  transfers between devices with their start and end apart: 26 -> 26, of which waited for: 21 -> 19; matrix products, arithmetic and copies ran while one was open for 3% -> 3% of each run, Pallas kernels for 32% -> 34%
where the time goes in v8:
time: 278 us; the launch traced here: 276 us
  Pallas kernels  115 us (41%)
  waiting for transfers between devices  94.9 us (34%)
  starting transfers between devices  41.1 us (15%)
  local copies, waits for them, and re-layouts  11 us (4%)
  other arithmetic  5.27 us (2%)
  matrix products  5.12 us (2%)
  between operations  2.81 us (1%)
    pallas_call x1, Pallas kernels, adjacency(): pl.pallas_call(functools.partial(adjacency_body, tiles), out_shape=jax.Sh...  47.9 us
    ppermute x21, waiting for transfers between devices, passed(): lax.ppermute(part, axis, [((i + shift) % parts, i) for i in range(parts)])  45.9 us
    pallas_call x3, Pallas kernels, gather_sum(): pl.pallas_call(functools.partial(gather_sum_body, piece, last, row0), out...  45.9 us
    all_to_all x1, waiting for transfers between devices, local(): lax.all_to_all(looked, 'batch', split_axis=0, concat_axis=0, tiled=True)  37.4 us
    ppermute x21, starting transfers between devices, passed(): lax.ppermute(part, axis, [((i + shift) % parts, i) for i in range(parts)])  25.6 us
    pallas_call x2, Pallas kernels, lookup(): pl.pallas_call(functools.partial(lookup_body, places.shape[0] // groups,...  19.8 us
    unnamed x46, local copies, waits for them, and re-layouts  7.06 us
    all_to_all x1, starting transfers between devices, local(): lax.all_to_all(requests.reshape(batch_count, capacity), 'batch', split_ax...  6.33 us
  transfers between devices with their start and end apart: 26, of which 19 were waited for; matrix products, arithmetic and copies ran while one was open for 3% of the time, Pallas kernels for 34%

profile of v8, /device:TPU:0, one launch (start us, length us, event | category | flops | bytes accessed | tf_op | source)
XLA Modules:
  0.0 275.6 jit_solution(4987088458744341013)
XLA Ops:
  4.0 6.3 %all-to-all-start = ((s32[8,1,1536]{2,1,0:T(1,128)}), s32[8,1,1536]{2,1,0:T(1,128)S(1)}, u32[]{:S(2)}, u32[]{:S(2)}) async-start(s32[8,1,1536]{2,1,0:T(1,128)} %bitcast.6), calls=%async_computation | async-start | bytes 98304 | tf_op jit(solution)/shard_map/all_to_all | solution.py:491
  11.3 4.9 %all-to-all-done = s32[8,1,1536]{2,1,0:T(1,128)S(1)} async-done(((s32[8,1,1536]{2,1,0:T(1,128)}), s32[8,1,1536]{2,1,0:T(1,128)S(1)}, u32[]{:S(2)}, u32[]{:S(2)}) %all-to-all-start) | async-done | bytes 49184 | tf_op jit(solution)/shard_map/all_to_all | solution.py:491
  18.4 10.0 %lookup.3 = bf16[8,768,256]{2,1,0:T(8,128)(2,1)} custom-call(s32[12288]{0:T(1024)S(1)} %bitcast.160, bf16[8192,256]{1,0:T(8,128)(2,1)S(1)} %copy-done.1), custom_call_target="tpu_custom_call" | custom-call | flops 62914560 | bytes 4194304 | tf_op jit(solution)/shard_map/lookup/pallas_call | solution.py:151
  28.4 4.6 %all-to-all-start.1 = ((bf16[8,768,256]{2,1,0:T(8,128)(2,1)}), bf16[8,768,256]{2,1,0:T(8,128)(2,1)}, u32[]{:S(2)}, u32[]{:S(2)}) async-start(bf16[8,768,256]{2,1,0:T(8,128)(2,1)} %lookup.3), calls=%async_computation.1 | async-start | bytes 6291456 | tf_op jit(solution)/shard_map/all_to_all | solution.py:498
  43.2 9.8 %lookup.2 = bf16[8,768,256]{2,1,0:T(8,128)(2,1)} custom-call(s32[12288]{0:T(1024)S(1)} %bitcast.161, bf16[8192,256]{1,0:T(8,128)(2,1)S(1)} %copy-done.2), custom_call_target="tpu_custom_call" | custom-call | flops 62914560 | bytes 4194304 | tf_op jit(solution)/shard_map/lookup/pallas_call | solution.py:151
  53.0 47.9 %adjacency.1.adj_ref = f8e4m3fn[28,3072,256]{2,1,0:T(32,128)(4,1)} custom-call(s32[1]{0:T(128)} %bitcast.8.me_ref, s32[192,256]{1,0:T(8,128)S(1)} %reshape.217.near_ref, bf16[256,128]{1,0:T(8,128)(2,1)S(1)} %pad_maximum_fusion.7.table_ref), custom_call_target="tpu_custom_call" | custom-call | flops 22548578304 | bytes 22020096 | tf_op jit(solution)/shard_map/adjacency/pallas_call | solution.py:214
  100.9 3.7 %all-to-all-done.1.answer_ref = bf16[8,768,256]{2,1,0:T(8,128)(2,1)} async-done(((bf16[8,768,256]{2,1,0:T(8,128)(2,1)}), bf16[8,768,256]{2,1,0:T(8,128)(2,1)}, u32[]{:S(2)}, u32[]{:S(2)}) %all-to-all-start.1) | async-done | bytes 3145760 | tf_op jit(solution)/shard_map/all_to_all | solution.py:498
  104.6 4.5 %all-to-all-start.2 = ((bf16[8,768,256]{2,1,0:T(8,128)(2,1)}), bf16[8,768,256]{2,1,0:T(8,128)(2,1)}, u32[]{:S(2)}, u32[]{:S(2)}) async-start(bf16[8,768,256]{2,1,0:T(8,128)(2,1)} %lookup.2), calls=%async_computation.2 | async-start | bytes 6291456 | tf_op jit(solution)/shard_map/all_to_all | solution.py:539
  113.5 29.7 %gather_sum.3 = (f32[3072,256]{1,0:T(8,128)}, f32[3072,256]{1,0:T(8,128)}) custom-call(s32[2]{0:T(128)S(1)} %pad_add_fusion.6.spans_ref, s32[8]{0:T(128)S(1)} %get-tuple-element.77.counts_ref, s32[9]{0:T(128)S(1)} %get-tuple-element.78.starts_ref, bf16[8,768,256]{2,1,0:T(8,128)(2,1)} %all-to-all-done.1.answer_ref, f32[3072,2]{1,0:T(8,128)S(1)} %bitcast.157, ...), custom_call_target="tpu_custom_call" | custom-call | flops 11274289152 | bytes 11010048 | tf_op jit(solution)/shard_map/gather_sum/pallas_call | solution.py:378
  143.2 37.4 %all-to-all-done.2.answer_ref = bf16[8,768,256]{2,1,0:T(8,128)(2,1)} async-done(((bf16[8,768,256]{2,1,0:T(8,128)(2,1)}), bf16[8,768,256]{2,1,0:T(8,128)(2,1)}, u32[]{:S(2)}, u32[]{:S(2)}) %all-to-all-start.2) | async-done | bytes 3145760 | tf_op jit(solution)/shard_map/all_to_all | solution.py:539
  180.6 10.5 %gather_sum.4 = (bf16[2304,256]{1,0:T(8,128)(2,1)S(1)}, bf16[2304,256]{1,0:T(8,128)(2,1)S(1)}, bf16[768,256]{1,0:T(8,128)(2,1)S(1)}, bf16[768,256]{1,0:T(8,128)(2,1)S(1)}, bf16[768,256]{1,0:T(8,128)(2,1)S(1)}) custom-call(s32[2]{0:T(128)S(1)} %pad_add_fusion.5.spans_ref, s32[8]{0:T(128)S(1)} %get-tuple-element.76.counts_ref, ...), custom_call_target="tpu_custom_call" | custom-call | flops 8455716864 | bytes 8257536 | tf_op jit(solution)/shard_map/gather_sum/pallas_call | solution.py:378
  191.2 2.5 collective-permute-start.5
  195.5 5.6 %gather_sum.5 = (bf16[768,256]{1,0:T(8,128)(2,1)S(1)}, bf16[768,256]{1,0:T(8,128)(2,1)S(1)}, bf16[768,256]{1,0:T(8,128)(2,1)S(1)}) custom-call(s32[2]{0:T(128)S(1)} %pad_add_fusion.5.spans_ref, s32[8]{0:T(128)S(1)} %get-tuple-element.76.counts_ref, s32[9]{0:T(128)S(1)} %get-tuple-element.79.starts_ref, bf16[8,768,256]{2,1,0:T(8,128)(2,1)} %all-to-all-done.2.answer_ref, ...), custom_call_target="tpu_custom_call" | custom-call | flops 2818572288 | bytes 2752512 | tf_op jit(solution)/shard_map/gather_sum/pallas_call | solution.py:378
  203.3 9.1 %collective-permute-done.4 = bf16[768,256]{1,0:T(8,128)(2,1)S(1)} collective-permute-done((bf16[768,256]{1,0:T(8,128)(2,1)S(1)}, bf16[768,256]{1,0:T(8,128)(2,1)S(1)}, u32[]{:S(2)}, u32[]{:S(2)}) %collective-permute-start.4) | collective-permute-done | bytes 393248 | tf_op jit(solution)/shard_map/ppermute | solution.py:409
  215.9 3.6 %collective-permute-done.8 = f32[128,256]{1,0:T(8,128)S(1)} collective-permute-done((f32[128,256]{1,0:T(8,128)S(1)}, f32[128,256]{1,0:T(8,128)S(1)}, u32[]{:S(2)}, u32[]{:S(2)}) %collective-permute-start.8) | collective-permute-done | bytes 131104 | tf_op jit(solution)/shard_map/ppermute | solution.py:409
  223.7 2.8 %collective-permute-start.9 = (bf16[3,128,256]{2,1,0:T(8,128)(2,1)S(1)}, bf16[3,128,256]{2,1,0:T(8,128)(2,1)S(1)}, u32[]{:S(2)}, u32[]{:S(2)}) collective-permute-start(bf16[3,128,256]{2,1,0:T(8,128)(2,1)S(1)} %get-tuple-element.68), channel_id=1, source_target_pairs={{8,0},{16,8},{24,16},{0,24},{9,1},{17,9},{25,17},{1,25},{10,2},{18... | collective-permute-start | bytes 589832 | tf_op jit(solution)/shard_map/ppermute | solution.py:409
  226.8 3.5 %collective-permute-done.11 = bf16[3,128,256]{2,1,0:T(8,128)(2,1)S(1)} collective-permute-done((bf16[3,128,256]{2,1,0:T(8,128)(2,1)S(1)}, bf16[3,128,256]{2,1,0:T(8,128)(2,1)S(1)}, u32[]{:S(2)}, u32[]{:S(2)}) %collective-permute-start.11) | collective-permute-done | bytes 196640 | tf_op jit(solution)/shard_map/ppermute | solution.py:409
  233.6 2.3 collective-permute-start.12
  238.4 7.4 %collective-permute-done.12 = bf16[768,256]{1,0:T(8,128)(2,1)S(1)} collective-permute-done((bf16[768,256]{1,0:T(8,128)(2,1)S(1)}, bf16[768,256]{1,0:T(8,128)(2,1)S(1)}, u32[]{:S(2)}, u32[]{:S(2)}) %collective-permute-start.12) | collective-permute-done | bytes 393248 | tf_op jit(solution)/shard_map/ppermute | solution.py:409
  245.8 6.5 %collective-permute-done.14 = bf16[768,256]{1,0:T(8,128)(2,1)S(1)} collective-permute-done((bf16[768,256]{1,0:T(8,128)(2,1)S(1)}, bf16[768,256]{1,0:T(8,128)(2,1)S(1)}, u32[]{:S(2)}, u32[]{:S(2)}) %collective-permute-start.14) | collective-permute-done | bytes 393248 | tf_op jit(solution)/shard_map/ppermute | solution.py:409
  259.9 4.5 %collective-permute-done.17 = bf16[128,256]{1,0:T(8,128)(2,1)S(1)} collective-permute-done((bf16[128,256]{1,0:T(8,128)(2,1)S(1)}, bf16[128,256]{1,0:T(8,128)(2,1)S(1)}, u32[]{:S(2)}, u32[]{:S(2)}) %collective-permute-start.17) | collective-permute-done | bytes 65568 | tf_op jit(solution)/shard_map/ppermute | solution.py:409
  264.5 2.2 collective-permute-start.20
  266.7 2.3 collective-permute-start.19
  268.9 2.3 collective-permute-done.21
  (153 shorter events, 49.0 us)
Async XLA Ops:
  4.0 12.2 %all-to-all-start = ((s32[8,1,1536]{2,1,0:T(1,128)}), s32[8,1,1536]{2,1,0:T(1,128)S(1)}, u32[]{:S(2)}, u32[]{:S(2)}) async-start(s32[8,1,1536]{2,1,0:T(1,128)} %bitcast.6), calls=%async_computation | async-start | bytes 98304 | tf_op jit(solution)/shard_map/all_to_all | solution.py:491
  28.4 76.1 %all-to-all-start.1 = ((bf16[8,768,256]{2,1,0:T(8,128)(2,1)}), bf16[8,768,256]{2,1,0:T(8,128)(2,1)}, u32[]{:S(2)}, u32[]{:S(2)}) async-start(bf16[8,768,256]{2,1,0:T(8,128)(2,1)} %lookup.3), calls=%async_computation.1 | async-start | bytes 6291456 | tf_op jit(solution)/shard_map/all_to_all | solution.py:498
  33.1 6.6 %collective-permute-start.2 = (s32[11,128]{1,0:T(8,128)S(1)}, s32[11,128]{1,0:T(8,128)S(1)}, u32[]{:S(2)}, u32[]{:S(2)}) collective-permute-start(s32[11,128]{1,0:T(8,128)S(1)} %pad_add_fusion.2), channel_id=1, source_target_pairs={{24,0},{0,8},{8,16},{16,24},{25,1},{1,9},{9,17},{17,25},{26,2},{2,... | collective-permute-start | bytes 16904 | tf_op jit(solution)/shard_map/ppermute | solution.py:409
  34.6 5.1 %collective-permute-start.1 = (s32[11,128]{1,0:T(8,128)S(1)}, s32[11,128]{1,0:T(8,128)S(1)}, u32[]{:S(2)}, u32[]{:S(2)}) collective-permute-start(s32[11,128]{1,0:T(8,128)S(1)} %pad_add_fusion.2), channel_id=1, source_target_pairs={{16,0},{24,8},{0,16},{8,24},{17,1},{25,9},{1,17},{9,25},{18,2},{26... | collective-permute-start | bytes 16904 | tf_op jit(solution)/shard_map/ppermute | solution.py:409
  36.2 3.7 %collective-permute-start = (s32[11,128]{1,0:T(8,128)S(1)}, s32[11,128]{1,0:T(8,128)S(1)}, u32[]{:S(2)}, u32[]{:S(2)}) collective-permute-start(s32[11,128]{1,0:T(8,128)S(1)} %pad_add_fusion.2), channel_id=1, source_target_pairs={{8,0},{16,8},{24,16},{0,24},{9,1},{17,9},{25,17},{1,25},{10,2},{18... | collective-permute-start | bytes 16904 | tf_op jit(solution)/shard_map/ppermute | solution.py:409
  104.6 76.0 %all-to-all-start.2 = ((bf16[8,768,256]{2,1,0:T(8,128)(2,1)}), bf16[8,768,256]{2,1,0:T(8,128)(2,1)}, u32[]{:S(2)}, u32[]{:S(2)}) async-start(bf16[8,768,256]{2,1,0:T(8,128)(2,1)} %lookup.2), calls=%async_computation.2 | async-start | bytes 6291456 | tf_op jit(solution)/shard_map/all_to_all | solution.py:539
  191.2 12.1 %collective-permute-start.5 = (bf16[768,256]{1,0:T(8,128)(2,1)S(1)}, bf16[768,256]{1,0:T(8,128)(2,1)S(1)}, u32[]{:S(2)}, u32[]{:S(2)}) collective-permute-start(bf16[768,256]{1,0:T(8,128)(2,1)S(1)} %get-tuple-element.47), channel_id=1, source_target_pairs={{8,0},{16,8},{24,16},{0,24},{9,1},{17,9},{25,17},{1,25},{10,2},{18... | collective-permute-start | bytes 1179656 | tf_op jit(solution)/shard_map/ppermute | solution.py:409
  193.7 18.7 %collective-permute-start.4 = (bf16[768,256]{1,0:T(8,128)(2,1)S(1)}, bf16[768,256]{1,0:T(8,128)(2,1)S(1)}, u32[]{:S(2)}, u32[]{:S(2)}) collective-permute-start(bf16[768,256]{1,0:T(8,128)(2,1)S(1)} %get-tuple-element.46), channel_id=1, source_target_pairs={{16,0},{24,8},{0,16},{8,24},{17,1},{25,9},{1,17},{9,25},{18,2},{26... | collective-permute-start | bytes 1179656 | tf_op jit(solution)/shard_map/ppermute | solution.py:409
  194.2 18.2 %collective-permute-start.3 = (bf16[768,256]{1,0:T(8,128)(2,1)S(1)}, bf16[768,256]{1,0:T(8,128)(2,1)S(1)}, u32[]{:S(2)}, u32[]{:S(2)}) collective-permute-start(bf16[768,256]{1,0:T(8,128)(2,1)S(1)} %get-tuple-element.45), channel_id=1, source_target_pairs={{24,0},{0,8},{8,16},{16,24},{25,1},{1,9},{9,17},{17,25},{26,2},{2,... | collective-permute-start | bytes 1179656 | tf_op jit(solution)/shard_map/ppermute | solution.py:409
  213.3 6.2 %collective-permute-start.8 = (f32[128,256]{1,0:T(8,128)S(1)}, f32[128,256]{1,0:T(8,128)S(1)}, u32[]{:S(2)}, u32[]{:S(2)}) collective-permute-start(f32[128,256]{1,0:T(8,128)S(1)} %get-tuple-element.62), channel_id=1, source_target_pairs={{8,0},{16,8},{24,16},{0,24},{9,1},{17,9},{25,17},{1,25},{10,2},{18... | collective-permute-start | bytes 393224 | tf_op jit(solution)/shard_map/ppermute | solution.py:409
  213.9 7.3 %collective-permute-start.7 = (f32[128,256]{1,0:T(8,128)S(1)}, f32[128,256]{1,0:T(8,128)S(1)}, u32[]{:S(2)}, u32[]{:S(2)}) collective-permute-start(f32[128,256]{1,0:T(8,128)S(1)} %get-tuple-element.63), channel_id=1, source_target_pairs={{16,0},{24,8},{0,16},{8,24},{17,1},{25,9},{1,17},{9,25},{18,2},{26... | collective-permute-start | bytes 393224 | tf_op jit(solution)/shard_map/ppermute | solution.py:409
  215.2 6.1 %collective-permute-start.6 = (f32[128,256]{1,0:T(8,128)S(1)}, f32[128,256]{1,0:T(8,128)S(1)}, u32[]{:S(2)}, u32[]{:S(2)}) collective-permute-start(f32[128,256]{1,0:T(8,128)S(1)} %get-tuple-element.61), channel_id=1, source_target_pairs={{24,0},{0,8},{8,16},{16,24},{25,1},{1,9},{9,17},{17,25},{26,2},{2,... | collective-permute-start | bytes 393224 | tf_op jit(solution)/shard_map/ppermute | solution.py:409
  222.3 8.0 %collective-permute-start.11 = (bf16[3,128,256]{2,1,0:T(8,128)(2,1)S(1)}, bf16[3,128,256]{2,1,0:T(8,128)(2,1)S(1)}, u32[]{:S(2)}, u32[]{:S(2)}) collective-permute-start(bf16[3,128,256]{2,1,0:T(8,128)(2,1)S(1)} %get-tuple-element.68), channel_id=1, source_target_pairs={{24,0},{0,8},{8,16},{16,24},{25,1},{1,9},{9,17},{17,25},{26,2},{2,... | collective-permute-start | bytes 589832 | tf_op jit(solution)/shard_map/ppermute | solution.py:409
  222.6 9.2 %collective-permute-start.10 = (bf16[3,128,256]{2,1,0:T(8,128)(2,1)S(1)}, bf16[3,128,256]{2,1,0:T(8,128)(2,1)S(1)}, u32[]{:S(2)}, u32[]{:S(2)}) collective-permute-start(bf16[3,128,256]{2,1,0:T(8,128)(2,1)S(1)} %get-tuple-element.68), channel_id=1, source_target_pairs={{16,0},{24,8},{0,16},{8,24},{17,1},{25,9},{1,17},{9,25},{18,2},{26... | collective-permute-start | bytes 589832 | tf_op jit(solution)/shard_map/ppermute | solution.py:409
  223.7 8.5 %collective-permute-start.9 = (bf16[3,128,256]{2,1,0:T(8,128)(2,1)S(1)}, bf16[3,128,256]{2,1,0:T(8,128)(2,1)S(1)}, u32[]{:S(2)}, u32[]{:S(2)}) collective-permute-start(bf16[3,128,256]{2,1,0:T(8,128)(2,1)S(1)} %get-tuple-element.68), channel_id=1, source_target_pairs={{8,0},{16,8},{24,16},{0,24},{9,1},{17,9},{25,17},{1,25},{10,2},{18... | collective-permute-start | bytes 589832 | tf_op jit(solution)/shard_map/ppermute | solution.py:409
  233.6 12.1 %collective-permute-start.12 = (bf16[768,256]{1,0:T(8,128)(2,1)S(1)}, bf16[768,256]{1,0:T(8,128)(2,1)S(1)}, u32[]{:S(2)}, u32[]{:S(2)}) collective-permute-start(bf16[768,256]{1,0:T(8,128)(2,1)S(1)} %fusion.2), channel_id=1, source_target_pairs={{8,0},{16,8},{24,16},{0,24},{9,1},{17,9},{25,17},{1,25},{10,2},{18... | collective-permute-start | bytes 1179656 | tf_op jit(solution)/shard_map/ppermute | solution.py:409
  236.0 9.8 %collective-permute-start.13 = (bf16[768,256]{1,0:T(8,128)(2,1)S(1)}, bf16[768,256]{1,0:T(8,128)(2,1)S(1)}, u32[]{:S(2)}, u32[]{:S(2)}) collective-permute-start(bf16[768,256]{1,0:T(8,128)(2,1)S(1)} %fusion.2), channel_id=1, source_target_pairs={{16,0},{24,8},{0,16},{8,24},{17,1},{25,9},{1,17},{9,25},{18,2},{26... | collective-permute-start | bytes 1179656 | tf_op jit(solution)/shard_map/ppermute | solution.py:409
  237.0 15.3 %collective-permute-start.14 = (bf16[768,256]{1,0:T(8,128)(2,1)S(1)}, bf16[768,256]{1,0:T(8,128)(2,1)S(1)}, u32[]{:S(2)}, u32[]{:S(2)}) collective-permute-start(bf16[768,256]{1,0:T(8,128)(2,1)S(1)} %fusion.2), channel_id=1, source_target_pairs={{24,0},{0,8},{8,16},{16,24},{25,1},{1,9},{9,17},{17,25},{26,2},{2,... | collective-permute-start | bytes 1179656 | tf_op jit(solution)/shard_map/ppermute | solution.py:409
  255.3 4.6 %collective-permute-start.18 = (bf16[128,256]{1,0:T(8,128)(2,1)S(1)}, bf16[128,256]{1,0:T(8,128)(2,1)S(1)}, u32[]{:S(2)}, u32[]{:S(2)}) collective-permute-start(bf16[128,256]{1,0:T(8,128)(2,1)S(1)} %get-tuple-element.65), channel_id=1, source_target_pairs={{2,0},{3,1},{4,2},{5,3},{6,4},{7,5},{0,6},{1,7},{10,8},{11,9},{12,... | collective-permute-start | bytes 196616 | tf_op jit(solution)/shard_map/ppermute | solution.py:409
  257.4 7.0 %collective-permute-start.17 = (bf16[128,256]{1,0:T(8,128)(2,1)S(1)}, bf16[128,256]{1,0:T(8,128)(2,1)S(1)}, u32[]{:S(2)}, u32[]{:S(2)}) collective-permute-start(bf16[128,256]{1,0:T(8,128)(2,1)S(1)} %get-tuple-element.66), channel_id=1, source_target_pairs={{4,0},{5,1},{6,2},{7,3},{0,4},{1,5},{2,6},{3,7},{12,8},{13,9},{14,... | collective-permute-start | bytes 196616 | tf_op jit(solution)/shard_map/ppermute | solution.py:409
  257.4 7.0 %collective-permute-start.16 = (bf16[128,256]{1,0:T(8,128)(2,1)S(1)}, bf16[128,256]{1,0:T(8,128)(2,1)S(1)}, u32[]{:S(2)}, u32[]{:S(2)}) collective-permute-start(bf16[128,256]{1,0:T(8,128)(2,1)S(1)} %get-tuple-element.64), channel_id=1, source_target_pairs={{6,0},{7,1},{0,2},{1,3},{2,4},{3,5},{4,6},{5,7},{14,8},{15,9},{8,1... | collective-permute-start | bytes 196616 | tf_op jit(solution)/shard_map/ppermute | solution.py:409
  264.4 6.9 %collective-permute-start.21 = (bf16[128,256]{1,0:T(8,128)(2,1)S(1)}, bf16[128,256]{1,0:T(8,128)(2,1)S(1)}, u32[]{:S(2)}, u32[]{:S(2)}) collective-permute-start(bf16[128,256]{1,0:T(8,128)(2,1)S(1)} %fusion.13), channel_id=1, source_target_pairs={{6,0},{7,1},{0,2},{1,3},{2,4},{3,5},{4,6},{5,7},{14,8},{15,9},{8,1... | collective-permute-start | bytes 196616 | tf_op jit(solution)/shard_map/ppermute | solution.py:409
  264.5 8.2 %collective-permute-start.20 = (bf16[128,256]{1,0:T(8,128)(2,1)S(1)}, bf16[128,256]{1,0:T(8,128)(2,1)S(1)}, u32[]{:S(2)}, u32[]{:S(2)}) collective-permute-start(bf16[128,256]{1,0:T(8,128)(2,1)S(1)} %fusion.13), channel_id=1, source_target_pairs={{4,0},{5,1},{6,2},{7,3},{0,4},{1,5},{2,6},{3,7},{12,8},{13,9},{14,... | collective-permute-start | bytes 196616 | tf_op jit(solution)/shard_map/ppermute | solution.py:409
  266.7 6.0 %collective-permute-start.19 = (bf16[128,256]{1,0:T(8,128)(2,1)S(1)}, bf16[128,256]{1,0:T(8,128)(2,1)S(1)}, u32[]{:S(2)}, u32[]{:S(2)}) collective-permute-start(bf16[128,256]{1,0:T(8,128)(2,1)S(1)} %fusion.13), channel_id=1, source_target_pairs={{2,0},{3,1},{4,2},{5,3},{6,4},{7,5},{0,6},{1,7},{10,8},{11,9},{12,... | collective-permute-start | bytes 196616 | tf_op jit(solution)/shard_map/ppermute | solution.py:409
  (20 other events, 559.6 us)

commit v9 on v8

--- a/solution.py
+++ b/solution.py
@@ -144,7 +144,7 @@
         out_ref[0, :, lane(h)] = lines[pl.ds(h, width, stride=halves), :].astype(jnp.bfloat16)
 
 
-def lookup(store, places, groups, first, width):
+def lookup(store, places, groups, first, width, mib):
     rows_all, features = store.shape
     halves = features // LANES
     apart = lambda rows: pltpu.VMEM((rows * halves, LANES), jnp.float32)
@@ -160,7 +160,7 @@
             pltpu.VMEM((rows_all, features), store.dtype),
             pltpu.SemaphoreType.DMA((4,)),
         ],
-        compiler_params=params(24),
+        compiler_params=params(mib),
         cost_estimate=cost(groups * width * features * 40, 2 * rows_all * features),
         name="lookup",
     )(places, store)
@@ -263,7 +263,17 @@
 
 
 def gather_sum_body(
-    piece, last, row0, spans_ref, counts_ref, starts_ref, answer_ref, notes_in, adj_ref, *refs
+    piece,
+    last,
+    row0,
+    spans_ref,
+    counts_ref,
+    starts_ref,
+    own_here_ref,
+    answer_ref,
+    notes_in,
+    adj_ref,
+    *refs,
 ):
     if last:
         (total_in, found_in, wself_in, wneigh_in, own_ref, mean_ref) = refs[:6]
@@ -279,7 +289,7 @@
         pairs = ((notes_in, notes_ref),)
     carry = [pltpu.make_async_copy(*pair, carried.at[n]) for n, pair in enumerate(pairs)]
     nodes = total_ref.shape[0]
-    rows = math.gcd(nodes, 3 * TILE)
+    rows = math.gcd(adj_ref.shape[1], 3 * TILE)
     begin, count = spans_ref[0], spans_ref[1]
 
     def fetch(step, slot):
@@ -322,12 +332,20 @@
             near = jnp.concatenate(
                 [tiles_ref[slot, w, part, :].astype(jnp.bfloat16) for w in range(WIDE)], axis=1
             )
-            own = jnp.where(notes_ref[part, 0:1] == lane, 1.0, 0.0).astype(jnp.bfloat16)
-            both = jnp.dot(
-                jnp.concatenate([near, own], axis=0), block, preferred_element_type=jnp.float32
-            )
-            total_ref[part, :] += both[:rows]
-            found_ref[part, :] += both[rows:]
+            flag = (lax.div(begin, WIDE) + step) * (adj_ref.shape[1] // rows) + row0 // rows + r
+
+            @pl.when(own_here_ref[flag] == 0)
+            def _():
+                total_ref[part, :] += jnp.dot(near, block, preferred_element_type=jnp.float32)
+
+            @pl.when(own_here_ref[flag] != 0)
+            def _():
+                own = jnp.where(notes_ref[part, 0:1] == lane, 1.0, 0.0).astype(jnp.bfloat16)
+                both = jnp.dot(
+                    jnp.concatenate([near, own], axis=0), block, preferred_element_type=jnp.float32
+                )
+                total_ref[part, :] += both[:rows]
+                found_ref[part, :] += both[rows:]
 
     if last:
         share = share_refs[0].shape[0]
@@ -345,14 +363,14 @@
                 ).astype(share_ref.dtype)
 
 
-def gather_sum(inputs, spans, counts, starts, answer, notes, adj, rest=None, row0=0, shares=()):
+def gather_sum(inputs, scalars, answer, notes, adj, rest=None, row0=0, shares=()):
     batch_count, width, features = answer.shape
     tiles, nodes, _ = adj.shape
     nodes = sum(shares) or nodes
     piece = LANES if width % LANES == 0 else SLOTS
     last = rest is not None
     room = min(batch_count * width, inputs) + SLOTS * batch_count + 2 * WIDE * TILE
-    in_specs = [SMEM, SMEM, SMEM, ANY, HBM, HBM]
+    in_specs = [SMEM, SMEM, SMEM, SMEM, ANY, HBM, HBM]
     rows = lambda dtype: jax.ShapeDtypeStruct((nodes, features), dtype)
     scratch = [
         pltpu.VMEM((room, features), jnp.bfloat16),
@@ -384,7 +402,7 @@
         compiler_params=params(50),
         cost_estimate=cost(2 * nodes * features * TILE * tiles, nodes * TILE * tiles // 2),
         name="gather_sum",
-    )(spans, counts, starts, *operands)
+    )(*scalars, *operands)
 
 
 def share_order(array, parts, seeds):
@@ -493,10 +511,10 @@
     )
     first = capacity // 2
     places = received.reshape(batch_count * capacity) * (store.shape[1] // LANES)
-    looked_a = lookup(store, places, batch_count, 0, first)
+    looked_a = lookup(store, places, batch_count, 0, first, 60)
     near_first, looked_a = lax.optimization_barrier((nbr_one[0], looked_a))
     answer_a = lax.all_to_all(looked_a, "batch", split_axis=0, concat_axis=0, tiled=True)
-    looked = lookup(store, places, batch_count, first, capacity - first)
+    looked = lookup(store, places, batch_count, first, capacity - first, 24)
 
     depth = WIDE * TILE
     steps = -(-(input_count + 2 * (SLOTS - 1) * batch_count + depth - 1) // depth)
@@ -522,6 +540,10 @@
     table = jnp.concatenate([grid // TILE, grid % TILE], axis=0).astype(jnp.bfloat16)
     notes = jnp.stack([column[:nodes], deg_one[0]], axis=1).astype(jnp.float32)
     notes = share_order(notes, parts, seeds)
+    block = math.gcd(nodes, 3 * TILE)
+    met = notes[:, 0].reshape(1, nodes // block, block) // depth
+    met = met.astype(jnp.int32) == jnp.arange(steps)[:, None, None]
+    own_here = jnp.any(met, axis=2).astype(jnp.int32).reshape(-1)
 
     fanout_two = nbr_two.shape[2]
     used_two = jnp.arange(fanout_two)[:, None] < deg_two
@@ -552,14 +574,13 @@
         place[:, :, None] == jnp.arange(share)[None, None, :], axis=0, dtype=jnp.float32
     ).astype(jnp.bfloat16)
 
-    total, found = gather_sum(input_count, spans_a, tally_a, starts_a, answer_a, notes, adj)
+    scalars = (spans_a, tally_a, starts_a, own_here)
+    total, found = gather_sum(input_count, scalars, answer_a, notes, adj)
 
     def finish(begin, end):
         return gather_sum(
             input_count,
-            spans_b,
-            tally_b,
-            starts_b,
+            (spans_b, tally_b, starts_b, own_here),
             answer_b,
             notes,
             adj,

time: 278 us -> 277 us (level)
  Pallas kernels: 115 us -> 118 us
    unnamed x46 -> x44, local copies, waits for them, and re-layouts: 7.06 us -> 4.88 us
where the time goes in v9:
time: 277 us; the launch traced here: 274 us
  Pallas kernels  118 us (43%)
  waiting for transfers between devices  92.7 us (33%)
  starting transfers between devices  40.4 us (15%)
  local copies, waits for them, and re-layouts  9.43 us (3%)
  other arithmetic  5.54 us (2%)
  matrix products  5.1 us (2%)
  between operations  2.82 us (1%)
    pallas_call x1, Pallas kernels, adjacency(): pl.pallas_call(functools.partial(adjacency_body, tiles), out_shape=jax.Sh...  47.9 us
    pallas_call x3, Pallas kernels, gather_sum(): pl.pallas_call(functools.partial(gather_sum_body, piece, last, row0), out...  46.7 us
    ppermute x21, waiting for transfers between devices, passed(): lax.ppermute(part, axis, [((i + shift) % parts, i) for i in range(parts)])  44.5 us
    all_to_all x1, waiting for transfers between devices, local(): lax.all_to_all(looked, 'batch', split_axis=0, concat_axis=0, tiled=True)  36.7 us
    ppermute x21, starting transfers between devices, passed(): lax.ppermute(part, axis, [((i + shift) % parts, i) for i in range(parts)])  24.9 us
    pallas_call x2, Pallas kernels, lookup(): pl.pallas_call(functools.partial(lookup_body, places.shape[0] // groups,...  21.3 us
    all_to_all x1, starting transfers between devices, local(): lax.all_to_all(requests.reshape(batch_count, capacity), 'batch', split_ax...  6.33 us
  transfers between devices with their start and end apart: 26, of which 19 were waited for; matrix products, arithmetic and copies ran while one was open for 3% of the time, Pallas kernels for 34%

profile of v9, /device:TPU:0, one launch (start us, length us, event | category | flops | bytes accessed | tf_op | source)
XLA Modules:
  0.0 273.8 jit_solution(3152232968507265170)
XLA Ops:
  4.0 6.3 %all-to-all-start = ((s32[8,1,1536]{2,1,0:T(1,128)}), s32[8,1,1536]{2,1,0:T(1,128)S(1)}, u32[]{:S(2)}, u32[]{:S(2)}) async-start(s32[8,1,1536]{2,1,0:T(1,128)} %bitcast.11), calls=%async_computation | async-start | bytes 98304 | tf_op jit(solution)/shard_map/all_to_all | solution.py:509
  11.3 4.9 %all-to-all-done = s32[8,1,1536]{2,1,0:T(1,128)S(1)} async-done(((s32[8,1,1536]{2,1,0:T(1,128)}), s32[8,1,1536]{2,1,0:T(1,128)S(1)}, u32[]{:S(2)}, u32[]{:S(2)}) %all-to-all-start) | async-done | bytes 49184 | tf_op jit(solution)/shard_map/all_to_all | solution.py:509
  16.8 11.5 %lookup.3 = bf16[8,768,256]{2,1,0:T(8,128)(2,1)} custom-call(s32[12288]{0:T(1024)} %bitcast.161, bf16[8192,256]{1,0:T(8,128)(2,1)} %store_in.3), custom_call_target="tpu_custom_call" | custom-call | flops 62914560 | bytes 4194304 | tf_op jit(solution)/shard_map/lookup/pallas_call | solution.py:151
  28.4 4.6 %all-to-all-start.1 = ((bf16[8,768,256]{2,1,0:T(8,128)(2,1)}), bf16[8,768,256]{2,1,0:T(8,128)(2,1)}, u32[]{:S(2)}, u32[]{:S(2)}) async-start(bf16[8,768,256]{2,1,0:T(8,128)(2,1)} %lookup.3), calls=%async_computation.1 | async-start | bytes 6291456 | tf_op jit(solution)/shard_map/all_to_all | solution.py:516
  41.0 2.2 copy-done.3
  43.2 9.8 %lookup.2 = bf16[8,768,256]{2,1,0:T(8,128)(2,1)} custom-call(s32[12288]{0:T(1024)S(1)} %bitcast.162, bf16[8192,256]{1,0:T(8,128)(2,1)S(1)} %copy-done.3), custom_call_target="tpu_custom_call" | custom-call | flops 62914560 | bytes 4194304 | tf_op jit(solution)/shard_map/lookup/pallas_call | solution.py:151
  53.0 47.9 %adjacency.1.adj_ref = f8e4m3fn[28,3072,256]{2,1,0:T(32,128)(4,1)} custom-call(s32[1]{0:T(128)} %bitcast.13.me_ref, s32[192,256]{1,0:T(8,128)S(1)} %reshape.261.near_ref, bf16[256,128]{1,0:T(8,128)(2,1)S(1)} %pad_maximum_fusion.7.table_ref), custom_call_target="tpu_custom_call" | custom-call | flops 22548578304 | bytes 22020096 | tf_op jit(solution)/shard_map/adjacency/pallas_call | solution.py:214
  100.9 3.6 %all-to-all-done.1.answer_ref = bf16[8,768,256]{2,1,0:T(8,128)(2,1)} async-done(((bf16[8,768,256]{2,1,0:T(8,128)(2,1)}), bf16[8,768,256]{2,1,0:T(8,128)(2,1)}, u32[]{:S(2)}, u32[]{:S(2)}) %all-to-all-start.1) | async-done | bytes 3145760 | tf_op jit(solution)/shard_map/all_to_all | solution.py:516
  104.5 4.5 %all-to-all-start.2 = ((bf16[8,768,256]{2,1,0:T(8,128)(2,1)}), bf16[8,768,256]{2,1,0:T(8,128)(2,1)}, u32[]{:S(2)}, u32[]{:S(2)}) async-start(bf16[8,768,256]{2,1,0:T(8,128)(2,1)} %lookup.2), calls=%async_computation.2 | async-start | bytes 6291456 | tf_op jit(solution)/shard_map/all_to_all | solution.py:561
  114.3 29.5 %gather_sum.3 = (f32[3072,256]{1,0:T(8,128)}, f32[3072,256]{1,0:T(8,128)}) custom-call(s32[2]{0:T(128)S(1)} %pad_add_fusion.6.spans_ref, s32[8]{0:T(128)S(1)} %get-tuple-element.77.counts_ref, s32[9]{0:T(128)S(1)} %get-tuple-element.78.starts_ref, s32[56]{0:T(128)S(1)} %reshape.268.own_here_ref, bf16[8,768,256]{2,1,0:T(8,128)(2,1)} %all-to-all-done.1.answer_ref, ...), custom_call_target="tpu_custom_call" | custom-call | flops 11274289152 | bytes 11010048 | tf_op jit(solution)/shard_map/gather_sum/pallas_call | solution.py:396
  143.8 36.7 %all-to-all-done.2.answer_ref = bf16[8,768,256]{2,1,0:T(8,128)(2,1)} async-done(((bf16[8,768,256]{2,1,0:T(8,128)(2,1)}), bf16[8,768,256]{2,1,0:T(8,128)(2,1)}, u32[]{:S(2)}, u32[]{:S(2)}) %all-to-all-start.2) | async-done | bytes 3145760 | tf_op jit(solution)/shard_map/all_to_all | solution.py:561
  180.5 10.7 %gather_sum.4 = (bf16[2304,256]{1,0:T(8,128)(2,1)S(1)}, bf16[2304,256]{1,0:T(8,128)(2,1)S(1)}, bf16[768,256]{1,0:T(8,128)(2,1)S(1)}, bf16[768,256]{1,0:T(8,128)(2,1)S(1)}, bf16[768,256]{1,0:T(8,128)(2,1)S(1)}) custom-call(s32[2]{0:T(128)S(1)} %pad_add_fusion.5.spans_ref, s32[8]{0:T(128)S(1)} %get-tuple-element.76.counts_ref, ...), custom_call_target="tpu_custom_call" | custom-call | flops 8455716864 | bytes 8257536 | tf_op jit(solution)/shard_map/gather_sum/pallas_call | solution.py:396
  191.3 2.3 collective-permute-start.5
  194.9 6.5 %gather_sum.5 = (bf16[768,256]{1,0:T(8,128)(2,1)S(1)}, bf16[768,256]{1,0:T(8,128)(2,1)S(1)}, bf16[768,256]{1,0:T(8,128)(2,1)S(1)}) custom-call(s32[2]{0:T(128)S(1)} %pad_add_fusion.5.spans_ref, s32[8]{0:T(128)S(1)} %get-tuple-element.76.counts_ref, s32[9]{0:T(128)S(1)} %get-tuple-element.79.starts_ref, s32[56]{0:T(128)S(1)} %reshape.268.own_here_ref, ...), custom_call_target="tpu_custom_call" | custom-call | flops 2818572288 | bytes 2752512 | tf_op jit(solution)/shard_map/gather_sum/pallas_call | solution.py:396
  203.4 7.6 %collective-permute-done.4 = bf16[768,256]{1,0:T(8,128)(2,1)S(1)} collective-permute-done((bf16[768,256]{1,0:T(8,128)(2,1)S(1)}, bf16[768,256]{1,0:T(8,128)(2,1)S(1)}, u32[]{:S(2)}, u32[]{:S(2)}) %collective-permute-start.4) | collective-permute-done | bytes 393248 | tf_op jit(solution)/shard_map/ppermute | solution.py:427
  214.8 3.4 %collective-permute-done.8 = f32[128,256]{1,0:T(8,128)S(1)} collective-permute-done((f32[128,256]{1,0:T(8,128)S(1)}, f32[128,256]{1,0:T(8,128)S(1)}, u32[]{:S(2)}, u32[]{:S(2)}) %collective-permute-start.8) | collective-permute-done | bytes 131104 | tf_op jit(solution)/shard_map/ppermute | solution.py:427
  222.7 2.8 %collective-permute-start.9 = (bf16[3,128,256]{2,1,0:T(8,128)(2,1)S(1)}, bf16[3,128,256]{2,1,0:T(8,128)(2,1)S(1)}, u32[]{:S(2)}, u32[]{:S(2)}) collective-permute-start(bf16[3,128,256]{2,1,0:T(8,128)(2,1)S(1)} %get-tuple-element.68), channel_id=1, source_target_pairs={{8,0},{16,8},{24,16},{0,24},{9,1},{17,9},{25,17},{1,25},{10,2},{18... | collective-permute-start | bytes 589832 | tf_op jit(solution)/shard_map/ppermute | solution.py:427
  225.8 3.2 %collective-permute-done.11 = bf16[3,128,256]{2,1,0:T(8,128)(2,1)S(1)} collective-permute-done((bf16[3,128,256]{2,1,0:T(8,128)(2,1)S(1)}, bf16[3,128,256]{2,1,0:T(8,128)(2,1)S(1)}, u32[]{:S(2)}, u32[]{:S(2)}) %collective-permute-start.11) | collective-permute-done | bytes 196640 | tf_op jit(solution)/shard_map/ppermute | solution.py:427
  237.8 7.5 %collective-permute-done.12 = bf16[768,256]{1,0:T(8,128)(2,1)S(1)} collective-permute-done((bf16[768,256]{1,0:T(8,128)(2,1)S(1)}, bf16[768,256]{1,0:T(8,128)(2,1)S(1)}, u32[]{:S(2)}, u32[]{:S(2)}) %collective-permute-start.12) | collective-permute-done | bytes 393248 | tf_op jit(solution)/shard_map/ppermute | solution.py:427
  245.4 6.5 %collective-permute-done.14 = bf16[768,256]{1,0:T(8,128)(2,1)S(1)} collective-permute-done((bf16[768,256]{1,0:T(8,128)(2,1)S(1)}, bf16[768,256]{1,0:T(8,128)(2,1)S(1)}, u32[]{:S(2)}, u32[]{:S(2)}) %collective-permute-start.14) | collective-permute-done | bytes 393248 | tf_op jit(solution)/shard_map/ppermute | solution.py:427
  257.0 2.2 collective-permute-done.18
  259.2 4.1 %collective-permute-done.17 = bf16[128,256]{1,0:T(8,128)(2,1)S(1)} collective-permute-done((bf16[128,256]{1,0:T(8,128)(2,1)S(1)}, bf16[128,256]{1,0:T(8,128)(2,1)S(1)}, u32[]{:S(2)}, u32[]{:S(2)}) %collective-permute-start.17) | collective-permute-done | bytes 65568 | tf_op jit(solution)/shard_map/ppermute | solution.py:427
  265.2 2.5 collective-permute-start.19
  267.8 2.3 collective-permute-done.21
  (157 shorter events, 47.8 us)
Async XLA Ops:
  4.0 12.2 %all-to-all-start = ((s32[8,1,1536]{2,1,0:T(1,128)}), s32[8,1,1536]{2,1,0:T(1,128)S(1)}, u32[]{:S(2)}, u32[]{:S(2)}) async-start(s32[8,1,1536]{2,1,0:T(1,128)} %bitcast.11), calls=%async_computation | async-start | bytes 98304 | tf_op jit(solution)/shard_map/all_to_all | solution.py:509
  28.4 76.1 %all-to-all-start.1 = ((bf16[8,768,256]{2,1,0:T(8,128)(2,1)}), bf16[8,768,256]{2,1,0:T(8,128)(2,1)}, u32[]{:S(2)}, u32[]{:S(2)}) async-start(bf16[8,768,256]{2,1,0:T(8,128)(2,1)} %lookup.3), calls=%async_computation.1 | async-start | bytes 6291456 | tf_op jit(solution)/shard_map/all_to_all | solution.py:516
  33.0 6.6 %collective-permute-start.2 = (s32[11,128]{1,0:T(8,128)S(1)}, s32[11,128]{1,0:T(8,128)S(1)}, u32[]{:S(2)}, u32[]{:S(2)}) collective-permute-start(s32[11,128]{1,0:T(8,128)S(1)} %pad_add_fusion.2), channel_id=1, source_target_pairs={{24,0},{0,8},{8,16},{16,24},{25,1},{1,9},{9,17},{17,25},{26,2},{2,... | collective-permute-start | bytes 16904 | tf_op jit(solution)/shard_map/ppermute | solution.py:427
  34.6 5.1 %collective-permute-start.1 = (s32[11,128]{1,0:T(8,128)S(1)}, s32[11,128]{1,0:T(8,128)S(1)}, u32[]{:S(2)}, u32[]{:S(2)}) collective-permute-start(s32[11,128]{1,0:T(8,128)S(1)} %pad_add_fusion.2), channel_id=1, source_target_pairs={{16,0},{24,8},{0,16},{8,24},{17,1},{25,9},{1,17},{9,25},{18,2},{26... | collective-permute-start | bytes 16904 | tf_op jit(solution)/shard_map/ppermute | solution.py:427
  36.1 3.7 %collective-permute-start = (s32[11,128]{1,0:T(8,128)S(1)}, s32[11,128]{1,0:T(8,128)S(1)}, u32[]{:S(2)}, u32[]{:S(2)}) collective-permute-start(s32[11,128]{1,0:T(8,128)S(1)} %pad_add_fusion.2), channel_id=1, source_target_pairs={{8,0},{16,8},{24,16},{0,24},{9,1},{17,9},{25,17},{1,25},{10,2},{18... | collective-permute-start | bytes 16904 | tf_op jit(solution)/shard_map/ppermute | solution.py:427
  104.5 76.0 %all-to-all-start.2 = ((bf16[8,768,256]{2,1,0:T(8,128)(2,1)}), bf16[8,768,256]{2,1,0:T(8,128)(2,1)}, u32[]{:S(2)}, u32[]{:S(2)}) async-start(bf16[8,768,256]{2,1,0:T(8,128)(2,1)} %lookup.2), calls=%async_computation.2 | async-start | bytes 6291456 | tf_op jit(solution)/shard_map/all_to_all | solution.py:561
  191.3 12.1 %collective-permute-start.5 = (bf16[768,256]{1,0:T(8,128)(2,1)S(1)}, bf16[768,256]{1,0:T(8,128)(2,1)S(1)}, u32[]{:S(2)}, u32[]{:S(2)}) collective-permute-start(bf16[768,256]{1,0:T(8,128)(2,1)S(1)} %get-tuple-element.47), channel_id=1, source_target_pairs={{8,0},{16,8},{24,16},{0,24},{9,1},{17,9},{25,17},{1,25},{10,2},{18... | collective-permute-start | bytes 1179656 | tf_op jit(solution)/shard_map/ppermute | solution.py:427
  193.6 17.5 %collective-permute-start.4 = (bf16[768,256]{1,0:T(8,128)(2,1)S(1)}, bf16[768,256]{1,0:T(8,128)(2,1)S(1)}, u32[]{:S(2)}, u32[]{:S(2)}) collective-permute-start(bf16[768,256]{1,0:T(8,128)(2,1)S(1)} %get-tuple-element.46), channel_id=1, source_target_pairs={{16,0},{24,8},{0,16},{8,24},{17,1},{25,9},{1,17},{9,25},{18,2},{26... | collective-permute-start | bytes 1179656 | tf_op jit(solution)/shard_map/ppermute | solution.py:427
  194.3 16.7 %collective-permute-start.3 = (bf16[768,256]{1,0:T(8,128)(2,1)S(1)}, bf16[768,256]{1,0:T(8,128)(2,1)S(1)}, u32[]{:S(2)}, u32[]{:S(2)}) collective-permute-start(bf16[768,256]{1,0:T(8,128)(2,1)S(1)} %get-tuple-element.45), channel_id=1, source_target_pairs={{24,0},{0,8},{8,16},{16,24},{25,1},{1,9},{9,17},{17,25},{26,2},{2,... | collective-permute-start | bytes 1179656 | tf_op jit(solution)/shard_map/ppermute | solution.py:427
  212.0 6.2 %collective-permute-start.8 = (f32[128,256]{1,0:T(8,128)S(1)}, f32[128,256]{1,0:T(8,128)S(1)}, u32[]{:S(2)}, u32[]{:S(2)}) collective-permute-start(f32[128,256]{1,0:T(8,128)S(1)} %get-tuple-element.62), channel_id=1, source_target_pairs={{8,0},{16,8},{24,16},{0,24},{9,1},{17,9},{25,17},{1,25},{10,2},{18... | collective-permute-start | bytes 393224 | tf_op jit(solution)/shard_map/ppermute | solution.py:427
  212.8 7.5 %collective-permute-start.7 = (f32[128,256]{1,0:T(8,128)S(1)}, f32[128,256]{1,0:T(8,128)S(1)}, u32[]{:S(2)}, u32[]{:S(2)}) collective-permute-start(f32[128,256]{1,0:T(8,128)S(1)} %get-tuple-element.63), channel_id=1, source_target_pairs={{16,0},{24,8},{0,16},{8,24},{17,1},{25,9},{1,17},{9,25},{18,2},{26... | collective-permute-start | bytes 393224 | tf_op jit(solution)/shard_map/ppermute | solution.py:427
  213.8 6.5 %collective-permute-start.6 = (f32[128,256]{1,0:T(8,128)S(1)}, f32[128,256]{1,0:T(8,128)S(1)}, u32[]{:S(2)}, u32[]{:S(2)}) collective-permute-start(f32[128,256]{1,0:T(8,128)S(1)} %get-tuple-element.61), channel_id=1, source_target_pairs={{24,0},{0,8},{8,16},{16,24},{25,1},{1,9},{9,17},{17,25},{26,2},{2,... | collective-permute-start | bytes 393224 | tf_op jit(solution)/shard_map/ppermute | solution.py:427
  221.3 7.7 %collective-permute-start.11 = (bf16[3,128,256]{2,1,0:T(8,128)(2,1)S(1)}, bf16[3,128,256]{2,1,0:T(8,128)(2,1)S(1)}, u32[]{:S(2)}, u32[]{:S(2)}) collective-permute-start(bf16[3,128,256]{2,1,0:T(8,128)(2,1)S(1)} %get-tuple-element.68), channel_id=1, source_target_pairs={{24,0},{0,8},{8,16},{16,24},{25,1},{1,9},{9,17},{17,25},{26,2},{2,... | collective-permute-start | bytes 589832 | tf_op jit(solution)/shard_map/ppermute | solution.py:427
  221.7 9.3 %collective-permute-start.10 = (bf16[3,128,256]{2,1,0:T(8,128)(2,1)S(1)}, bf16[3,128,256]{2,1,0:T(8,128)(2,1)S(1)}, u32[]{:S(2)}, u32[]{:S(2)}) collective-permute-start(bf16[3,128,256]{2,1,0:T(8,128)(2,1)S(1)} %get-tuple-element.68), channel_id=1, source_target_pairs={{16,0},{24,8},{0,16},{8,24},{17,1},{25,9},{1,17},{9,25},{18,2},{26... | collective-permute-start | bytes 589832 | tf_op jit(solution)/shard_map/ppermute | solution.py:427
  222.7 9.1 %collective-permute-start.9 = (bf16[3,128,256]{2,1,0:T(8,128)(2,1)S(1)}, bf16[3,128,256]{2,1,0:T(8,128)(2,1)S(1)}, u32[]{:S(2)}, u32[]{:S(2)}) collective-permute-start(bf16[3,128,256]{2,1,0:T(8,128)(2,1)S(1)} %get-tuple-element.68), channel_id=1, source_target_pairs={{8,0},{16,8},{24,16},{0,24},{9,1},{17,9},{25,17},{1,25},{10,2},{18... | collective-permute-start | bytes 589832 | tf_op jit(solution)/shard_map/ppermute | solution.py:427
  233.2 12.1 %collective-permute-start.12 = (bf16[768,256]{1,0:T(8,128)(2,1)S(1)}, bf16[768,256]{1,0:T(8,128)(2,1)S(1)}, u32[]{:S(2)}, u32[]{:S(2)}) collective-permute-start(bf16[768,256]{1,0:T(8,128)(2,1)S(1)} %fusion.2), channel_id=1, source_target_pairs={{8,0},{16,8},{24,16},{0,24},{9,1},{17,9},{25,17},{1,25},{10,2},{18... | collective-permute-start | bytes 1179656 | tf_op jit(solution)/shard_map/ppermute | solution.py:427
  235.3 10.1 %collective-permute-start.13 = (bf16[768,256]{1,0:T(8,128)(2,1)S(1)}, bf16[768,256]{1,0:T(8,128)(2,1)S(1)}, u32[]{:S(2)}, u32[]{:S(2)}) collective-permute-start(bf16[768,256]{1,0:T(8,128)(2,1)S(1)} %fusion.2), channel_id=1, source_target_pairs={{16,0},{24,8},{0,16},{8,24},{17,1},{25,9},{1,17},{9,25},{18,2},{26... | collective-permute-start | bytes 1179656 | tf_op jit(solution)/shard_map/ppermute | solution.py:427
  236.5 15.4 %collective-permute-start.14 = (bf16[768,256]{1,0:T(8,128)(2,1)S(1)}, bf16[768,256]{1,0:T(8,128)(2,1)S(1)}, u32[]{:S(2)}, u32[]{:S(2)}) collective-permute-start(bf16[768,256]{1,0:T(8,128)(2,1)S(1)} %fusion.2), channel_id=1, source_target_pairs={{24,0},{0,8},{8,16},{16,24},{25,1},{1,9},{9,17},{17,25},{26,2},{2,... | collective-permute-start | bytes 1179656 | tf_op jit(solution)/shard_map/ppermute | solution.py:427
  254.9 4.3 %collective-permute-start.18 = (bf16[128,256]{1,0:T(8,128)(2,1)S(1)}, bf16[128,256]{1,0:T(8,128)(2,1)S(1)}, u32[]{:S(2)}, u32[]{:S(2)}) collective-permute-start(bf16[128,256]{1,0:T(8,128)(2,1)S(1)} %get-tuple-element.65), channel_id=1, source_target_pairs={{2,0},{3,1},{4,2},{5,3},{6,4},{7,5},{0,6},{1,7},{10,8},{11,9},{12,... | collective-permute-start | bytes 196616 | tf_op jit(solution)/shard_map/ppermute | solution.py:427
  255.7 7.6 %collective-permute-start.17 = (bf16[128,256]{1,0:T(8,128)(2,1)S(1)}, bf16[128,256]{1,0:T(8,128)(2,1)S(1)}, u32[]{:S(2)}, u32[]{:S(2)}) collective-permute-start(bf16[128,256]{1,0:T(8,128)(2,1)S(1)} %get-tuple-element.66), channel_id=1, source_target_pairs={{4,0},{5,1},{6,2},{7,3},{0,4},{1,5},{2,6},{3,7},{12,8},{13,9},{14,... | collective-permute-start | bytes 196616 | tf_op jit(solution)/shard_map/ppermute | solution.py:427
  255.7 7.6 %collective-permute-start.16 = (bf16[128,256]{1,0:T(8,128)(2,1)S(1)}, bf16[128,256]{1,0:T(8,128)(2,1)S(1)}, u32[]{:S(2)}, u32[]{:S(2)}) collective-permute-start(bf16[128,256]{1,0:T(8,128)(2,1)S(1)} %get-tuple-element.64), channel_id=1, source_target_pairs={{6,0},{7,1},{0,2},{1,3},{2,4},{3,5},{4,6},{5,7},{14,8},{15,9},{8,1... | collective-permute-start | bytes 196616 | tf_op jit(solution)/shard_map/ppermute | solution.py:427
  263.4 6.7 %collective-permute-start.21 = (bf16[128,256]{1,0:T(8,128)(2,1)S(1)}, bf16[128,256]{1,0:T(8,128)(2,1)S(1)}, u32[]{:S(2)}, u32[]{:S(2)}) collective-permute-start(bf16[128,256]{1,0:T(8,128)(2,1)S(1)} %fusion.14), channel_id=1, source_target_pairs={{6,0},{7,1},{0,2},{1,3},{2,4},{3,5},{4,6},{5,7},{14,8},{15,9},{8,1... | collective-permute-start | bytes 196616 | tf_op jit(solution)/shard_map/ppermute | solution.py:427
  263.4 7.4 %collective-permute-start.20 = (bf16[128,256]{1,0:T(8,128)(2,1)S(1)}, bf16[128,256]{1,0:T(8,128)(2,1)S(1)}, u32[]{:S(2)}, u32[]{:S(2)}) collective-permute-start(bf16[128,256]{1,0:T(8,128)(2,1)S(1)} %fusion.14), channel_id=1, source_target_pairs={{4,0},{5,1},{6,2},{7,3},{0,4},{1,5},{2,6},{3,7},{12,8},{13,9},{14,... | collective-permute-start | bytes 196616 | tf_op jit(solution)/shard_map/ppermute | solution.py:427
  265.2 5.6 %collective-permute-start.19 = (bf16[128,256]{1,0:T(8,128)(2,1)S(1)}, bf16[128,256]{1,0:T(8,128)(2,1)S(1)}, u32[]{:S(2)}, u32[]{:S(2)}) collective-permute-start(bf16[128,256]{1,0:T(8,128)(2,1)S(1)} %fusion.14), channel_id=1, source_target_pairs={{2,0},{3,1},{4,2},{5,3},{6,4},{7,5},{0,6},{1,7},{10,8},{11,9},{12,... | collective-permute-start | bytes 196616 | tf_op jit(solution)/shard_map/ppermute | solution.py:427
  (19 other events, 483.0 us)

commit v10 on v9

--- a/solution.py
+++ b/solution.py
@@ -46,7 +46,7 @@
     return pl.CostEstimate(flops=int(flops), bytes_accessed=int(moved), transcendentals=0)
 
 
-def requests_body(batch_count, capacity, owner_ref, row_ref, slot_ref, count_ref, request_ref):
+def requests_body(batch_count, capacity, scale, owner_ref, row_ref, slot_ref, count_ref, request_ref):
     blocks, width = owner_ref.shape[0] // 2, TILE
     places = request_ref.shape[0]
     line = lambda ref, b: jnp.concatenate([ref[2 * b : 2 * b + 1], ref[2 * b + 1 : 2 * b + 2]], axis=1)
@@ -83,14 +83,14 @@
         right = jnp.where((bucket & (LANES - 1)) == low_id, 1.0, 0.0).astype(jnp.bfloat16)
         total = total + contract_cols(left, right)
     count_ref[...] = jnp.broadcast_to(running, count_ref.shape).astype(jnp.int32)
-    request_ref[...] = (total[:places] * TILE + total[places:]).astype(jnp.int32)
-
-
-def make_requests(batch_count, capacity, owners, wanted):
+    request_ref[...] = (total[:places] * TILE + total[places:]).astype(jnp.int32) * scale
+
+
+def make_requests(batch_count, capacity, scale, owners, wanted):
     total = owners.shape[0] * LANES
     places = batch_count * capacity // LANES
     return pl.pallas_call(
-        functools.partial(requests_body, batch_count, capacity),
+        functools.partial(requests_body, batch_count, capacity, scale),
         out_shape=(
             jax.ShapeDtypeStruct(owners.shape, jnp.int32),
             jax.ShapeDtypeStruct((batch_count, LANES), jnp.int32),
@@ -104,66 +104,64 @@
     )(owners, wanted)
 
 
-def lookup_body(stride, first, width, want_ref, store_in, out_ref, table, lines, store_ref, came):
-    rows_all = store_ref.shape[0]
+def table_body(store_ref, table_ref):
     halves = store_ref.shape[1] // LANES
-    lane = lambda h: pl.ds(h * LANES, LANES)
-    begin = pl.program_id(0) * stride + first
-
-    @pl.when(pl.program_id(0) == 0)
-    def _():
-        pieces = came.shape[0]
-        depth = rows_all // pieces
-        copies = [
-            pltpu.make_async_copy(
-                store_in.at[pl.ds(n * depth, depth)], store_ref.at[pl.ds(n * depth, depth)], came.at[n]
-            )
-            for n in range(pieces)
-        ]
-        for copy in copies:
-            copy.start()
-        for n, copy in enumerate(copies):
-            copy.wait()
-
-            @pl.loop(n * depth // TILE, (n + 1) * depth // TILE)
-            def _(j):
-                part = pl.ds(pl.multiple_of(j * TILE, TILE), TILE)
-                for h in range(halves):
-                    spot = pl.ds(pl.multiple_of(j * TILE * halves, TILE) + h, TILE, stride=halves)
-                    table[spot, :] = store_ref[part, lane(h)].astype(jnp.float32)
-
-    @pl.loop(0, width // SLOTS, unroll=2)
+
+    @pl.loop(0, store_ref.shape[0] // TILE)
     def _(j):
-        at = [want_ref[begin + j * SLOTS + u] for u in range(SLOTS)]
-        rows = [table[pl.ds(pl.multiple_of(a, halves), halves), :] for a in at]
-        block = lines.at[pl.ds(pl.multiple_of(j * SLOTS * halves, SLOTS * halves), SLOTS * halves)]
-        for u in range(SLOTS):
-            block[pl.ds(u * halves, halves), :] = rows[u]
-
-    for h in range(halves):
-        out_ref[0, :, lane(h)] = lines[pl.ds(h, width, stride=halves), :].astype(jnp.bfloat16)
-
-
-def lookup(store, places, groups, first, width, mib):
+        part = pl.ds(pl.multiple_of(j * TILE, TILE), TILE)
+        for h in range(halves):
+            spot = pl.ds(pl.multiple_of(j * TILE * halves, TILE) + h, TILE, stride=halves)
+            table_ref[spot, :] = store_ref[part, pl.ds(h * LANES, LANES)].astype(jnp.float32)
+
+
+def make_table(store):
     rows_all, features = store.shape
+    return pl.pallas_call(
+        table_body,
+        out_shape=jax.ShapeDtypeStruct((rows_all * features // LANES, LANES), jnp.float32),
+        in_specs=[VMEM],
+        out_specs=VMEM,
+        compiler_params=params(24),
+        cost_estimate=cost(rows_all * features, 6 * rows_all * features),
+        name="table",
+    )(store)
+
+
+def lookup_body(stride, first, want_ref, table_ref, out_ref, lines):
+    groups, width, features = out_ref.shape
     halves = features // LANES
-    apart = lambda rows: pltpu.VMEM((rows * halves, LANES), jnp.float32)
+
+    @pl.loop(0, groups)
+    def _(g):
+        begin = g * stride + first
+
+        @pl.loop(0, width // SLOTS, unroll=2)
+        def _(j):
+            at = [want_ref[begin + j * SLOTS + u] for u in range(SLOTS)]
+            rows = [table_ref[pl.ds(pl.multiple_of(a, halves), halves), :] for a in at]
+            depth = SLOTS * halves
+            block = lines.at[pl.ds(pl.multiple_of(j * depth, depth), depth)]
+            for u in range(SLOTS):
+                block[pl.ds(u * halves, halves), :] = rows[u]
+
+        for h in range(halves):
+            out_ref[g, :, pl.ds(h * LANES, LANES)] = lines[
+                pl.ds(h, width, stride=halves), :
+            ].astype(jnp.bfloat16)
+
+
+def lookup(table, places, groups, features, first, width):
     return pl.pallas_call(
-        functools.partial(lookup_body, places.shape[0] // groups, first, width),
+        functools.partial(lookup_body, places.shape[0] // groups, first),
         out_shape=jax.ShapeDtypeStruct((groups, width, features), jnp.bfloat16),
-        grid=(groups,),
-        in_specs=[SMEM, HBM],
-        out_specs=pl.BlockSpec((1, width, features), lambda g: (g, 0, 0)),
-        scratch_shapes=[
-            apart(rows_all),
-            apart(width),
-            pltpu.VMEM((rows_all, features), store.dtype),
-            pltpu.SemaphoreType.DMA((4,)),
-        ],
-        compiler_params=params(mib),
-        cost_estimate=cost(groups * width * features * 40, 2 * rows_all * features),
+        in_specs=[SMEM, VMEM],
+        out_specs=VMEM,
+        scratch_shapes=[pltpu.VMEM((width * features // LANES, LANES), jnp.float32)],
+        compiler_params=params(24),
+        cost_estimate=cost(groups * width * features * 40, 4 * table.size),
         name="lookup",
-    )(places, store)
+    )(places, table)
 
 
 def adjacency_body(tiles, me_ref, near_ref, table_ref, out_ref):
@@ -230,25 +228,22 @@
 
 
 def collect(piece, counts_ref, starts_ref, answer_ref, landed, arrived, packed):
-    batch_count, width, _ = answer_ref.shape
-    pieces = width // piece
+    batch_count = answer_ref.shape[0]
 
     def each_used(what):
         @pl.loop(0, batch_count)
         def _(o):
-            for c in range(pieces):
-
-                @pl.when(c * piece < counts_ref[o])
-                def _(c=c):
-                    part = pl.ds(c * piece, piece)
-                    what(
-                        o,
-                        c,
-                        part,
-                        pltpu.make_async_copy(
-                            answer_ref.at[o, part], landed.at[o, part], arrived.at[o, c]
-                        ),
-                    )
+            @pl.loop(0, pl.cdiv(counts_ref[o], piece))
+            def _(c):
+                part = pl.ds(pl.multiple_of(c * piece, piece), piece)
+                what(
+                    o,
+                    c,
+                    part,
+                    pltpu.make_async_copy(
+                        answer_ref.at[o, part], landed.at[o, part], arrived.at[o, c]
+                    ),
+                )
 
     def lay(o, c, part, copy):
         copy.wait()
@@ -504,17 +499,21 @@
 
     owners = input_owner.reshape(input_count // LANES, LANES)
     wanted = input_row.reshape(input_count // LANES, LANES)
-    slots, counts, requests = make_requests(batch_count, capacity, owners, wanted)
+    slots, counts, requests = make_requests(
+        batch_count, capacity, store.shape[1] // LANES, owners, wanted
+    )
     owners = owners.reshape(1, input_count)
     received = lax.all_to_all(
         requests.reshape(batch_count, capacity), "batch", split_axis=0, concat_axis=0, tiled=True
     )
     first = capacity // 2
-    places = received.reshape(batch_count * capacity) * (store.shape[1] // LANES)
-    looked_a = lookup(store, places, batch_count, 0, first, 60)
+    places = received.reshape(batch_count * capacity)
+    table = make_table(store)
+    features = store.shape[1]
+    looked_a = lookup(table, places, batch_count, features, 0, first)
     near_first, looked_a = lax.optimization_barrier((nbr_one[0], looked_a))
     answer_a = lax.all_to_all(looked_a, "batch", split_axis=0, concat_axis=0, tiled=True)
-    looked = lookup(store, places, batch_count, first, capacity - first, 24)
+    looked = lookup(table, places, batch_count, features, first, capacity - first)
 
     depth = WIDE * TILE
     steps = -(-(input_count + 2 * (SLOTS - 1) * batch_count + depth - 1) // depth)
@@ -537,7 +536,7 @@
     mine = owners == jnp.arange(batch_count)[:, None]
     column = jnp.sum(jnp.where(mine, shifted, 0), axis=0)
     grid = jnp.pad(column.reshape(-1, LANES), ((0, LANES - input_count // LANES), (0, 0))).T
-    table = jnp.concatenate([grid // TILE, grid % TILE], axis=0).astype(jnp.bfloat16)
+    finder = jnp.concatenate([grid // TILE, grid % TILE], axis=0).astype(jnp.bfloat16)
     notes = jnp.stack([column[:nodes], deg_one[0]], axis=1).astype(jnp.float32)
     notes = share_order(notes, parts, seeds)
     block = math.gcd(nodes, 3 * TILE)
@@ -556,7 +555,7 @@
     near, lists = lax.optimization_barrier((near, lists))
     me = feat_index.astype(jnp.int32).reshape(1)
     near = near.reshape(nodes // SLOTS, TILE)
-    adj = adjacency(me, near, table, steps * WIDE, parts, seeds)
+    adj = adjacency(me, near, finder, steps * WIDE, parts, seeds)
     looked, answer_a, adj = lax.optimization_barrier((looked, answer_a, adj))
     answer_b = lax.all_to_all(looked, "batch", split_axis=0, concat_axis=0, tiled=True)
 

time: 277 us -> 280 us (1.011)
  local copies, waits for them, and re-layouts: 9.43 us -> 19.4 us
  waiting for transfers between devices: 92.7 us -> 86.9 us
  starting transfers between devices: 40.4 us -> 43.5 us
  Pallas kernels: 118 us -> 115 us
    unnamed x44 -> x48, local copies, waits for them, and re-layouts: 4.88 us -> 14.9 us
    all_to_all x1, waiting for transfers between devices: 4.87 us -> 0.01 us  [local(): lax.all_to_all(requests.reshape(batch_count, capacity), 'batch', split_ax...]
where the time goes in v10:
time: 280 us; the launch traced here: 278 us
  Pallas kernels  115 us (41%)
  waiting for transfers between devices  86.9 us (31%)
  starting transfers between devices  43.5 us (16%)
  local copies, waits for them, and re-layouts  19.4 us (7%)
  matrix products  5.11 us (2%)
  other arithmetic  4.89 us (2%)
    pallas_call x1, Pallas kernels, adjacency(): pl.pallas_call(functools.partial(adjacency_body, tiles), out_shape=jax.Sh...  47.8 us
    ppermute x21, waiting for transfers between devices, passed(): lax.ppermute(part, axis, [((i + shift) % parts, i) for i in range(parts)])  46.3 us
    pallas_call x3, Pallas kernels, gather_sum(): pl.pallas_call(functools.partial(gather_sum_body, piece, last, row0), out...  46 us
    all_to_all x1, waiting for transfers between devices, local(): lax.all_to_all(looked, 'batch', split_axis=0, concat_axis=0, tiled=True)  34.7 us
    ppermute x21, starting transfers between devices, passed(): lax.ppermute(part, axis, [((i + shift) % parts, i) for i in range(parts)])  27.3 us
    pallas_call x2, Pallas kernels, lookup(): pl.pallas_call(functools.partial(lookup_body, places.shape[0] // groups,...  19.1 us
    unnamed x48, local copies, waits for them, and re-layouts  14.9 us
    all_to_all x1, starting transfers between devices, local(): lax.all_to_all(requests.reshape(batch_count, capacity), 'batch', split_ax...  6.33 us
  transfers between devices with their start and end apart: 26, of which 19 were waited for; matrix products, arithmetic and copies ran while one was open for 3% of the time, Pallas kernels for 34%

profile of v10, /device:TPU:0, one launch (start us, length us, event | category | flops | bytes accessed | tf_op | source)
XLA Modules:
  0.0 277.9 jit_solution(2613335155408580547)
XLA Ops:
  4.0 6.3 %all-to-all-start = ((s32[8,1,1536]{2,1,0:T(1,128)}), s32[8,1,1536]{2,1,0:T(1,128)S(1)}, u32[]{:S(2)}, u32[]{:S(2)}) async-start(s32[8,1,1536]{2,1,0:T(1,128)} %bitcast.11), calls=%async_computation | async-start | bytes 98304 | tf_op jit(solution)/shard_map/all_to_all | solution.py:506
  14.1 3.3 %copy-done.1 = f32[16384,128]{1,0:T(8,128)} copy-done((f32[16384,128]{1,0:T(8,128)}, f32[16384,128]{1,0:T(8,128)S(1)}, u32[]{:S(2)}) %copy-start.1) | copy-done | bytes 8388632
  17.4 3.4 %copy-done.2 = f32[16384,128]{1,0:T(8,128)S(1)} copy-done((f32[16384,128]{1,0:T(8,128)S(1)}, f32[16384,128]{1,0:T(8,128)}, u32[]{:S(2)}) %copy-start.2) | copy-done | bytes 8388632
  20.8 9.5 %lookup.3 = bf16[8,768,256]{2,1,0:T(8,128)(2,1)} custom-call(s32[12288]{0:T(1024)S(1)} %bitcast.161, f32[16384,128]{1,0:T(8,128)S(1)} %copy-done.2), custom_call_target="tpu_custom_call" | custom-call | flops 62914560 | bytes 8388608 | tf_op jit(solution)/shard_map/lookup/pallas_call | solution.py:155
  30.3 5.2 %all-to-all-start.1 = ((bf16[8,768,256]{2,1,0:T(8,128)(2,1)}), bf16[8,768,256]{2,1,0:T(8,128)(2,1)}, u32[]{:S(2)}, u32[]{:S(2)}) async-start(bf16[8,768,256]{2,1,0:T(8,128)(2,1)} %lookup.3), calls=%async_computation.1 | async-start | bytes 6291456 | tf_op jit(solution)/shard_map/all_to_all | solution.py:515
  43.5 3.4 %copy-done.3 = f32[16384,128]{1,0:T(8,128)S(1)} copy-done((f32[16384,128]{1,0:T(8,128)S(1)}, f32[16384,128]{1,0:T(8,128)}, u32[]{:S(2)}) %copy-start.3) | copy-done | bytes 8388632
  46.9 9.6 %lookup.2 = bf16[8,768,256]{2,1,0:T(8,128)(2,1)} custom-call(s32[12288]{0:T(1024)S(1)} %bitcast.162, f32[16384,128]{1,0:T(8,128)S(1)} %copy-done.3), custom_call_target="tpu_custom_call" | custom-call | flops 62914560 | bytes 8388608 | tf_op jit(solution)/shard_map/lookup/pallas_call | solution.py:155
  56.4 47.8 %adjacency.1.adj_ref = f8e4m3fn[28,3072,256]{2,1,0:T(32,128)(4,1)} custom-call(s32[1]{0:T(128)} %bitcast.13.me_ref, s32[192,256]{1,0:T(8,128)S(1)} %reshape.262.near_ref, bf16[256,128]{1,0:T(8,128)(2,1)S(1)} %pad_maximum_fusion.7.table_ref), custom_call_target="tpu_custom_call" | custom-call | flops 22548578304 | bytes 22020096 | tf_op jit(solution)/shard_map/adjacency/pallas_call | solution.py:212
  104.2 2.9 %all-to-all-done.1.answer_ref = bf16[8,768,256]{2,1,0:T(8,128)(2,1)} async-done(((bf16[8,768,256]{2,1,0:T(8,128)(2,1)}), bf16[8,768,256]{2,1,0:T(8,128)(2,1)}, u32[]{:S(2)}, u32[]{:S(2)}) %all-to-all-start.1) | async-done | bytes 3145760 | tf_op jit(solution)/shard_map/all_to_all | solution.py:515
  107.2 4.5 %all-to-all-start.2 = ((bf16[8,768,256]{2,1,0:T(8,128)(2,1)}), bf16[8,768,256]{2,1,0:T(8,128)(2,1)}, u32[]{:S(2)}, u32[]{:S(2)}) async-start(bf16[8,768,256]{2,1,0:T(8,128)(2,1)} %lookup.2), calls=%async_computation.2 | async-start | bytes 6291456 | tf_op jit(solution)/shard_map/all_to_all | solution.py:560
  117.0 31.5 %gather_sum.3 = (f32[3072,256]{1,0:T(8,128)}, f32[3072,256]{1,0:T(8,128)}) custom-call(s32[2]{0:T(128)S(1)} %pad_add_fusion.6.spans_ref, s32[8]{0:T(128)S(1)} %get-tuple-element.77.counts_ref, s32[9]{0:T(128)S(1)} %get-tuple-element.78.starts_ref, s32[56]{0:T(128)S(1)} %reshape.269.own_here_ref, bf16[8,768,256]{2,1,0:T(8,128)(2,1)} %all-to-all-done.1.answer_ref, ...), custom_call_target="tpu_custom_call" | custom-call | flops 11274289152 | bytes 11010048 | tf_op jit(solution)/shard_map/gather_sum/pallas_call | solution.py:391
  148.5 34.7 %all-to-all-done.2.answer_ref = bf16[8,768,256]{2,1,0:T(8,128)(2,1)} async-done(((bf16[8,768,256]{2,1,0:T(8,128)(2,1)}), bf16[8,768,256]{2,1,0:T(8,128)(2,1)}, u32[]{:S(2)}, u32[]{:S(2)}) %all-to-all-start.2) | async-done | bytes 3145760 | tf_op jit(solution)/shard_map/all_to_all | solution.py:560
  183.2 9.1 %gather_sum.4 = (bf16[2304,256]{1,0:T(8,128)(2,1)S(1)}, bf16[2304,256]{1,0:T(8,128)(2,1)S(1)}, bf16[768,256]{1,0:T(8,128)(2,1)S(1)}, bf16[768,256]{1,0:T(8,128)(2,1)S(1)}, bf16[768,256]{1,0:T(8,128)(2,1)S(1)}) custom-call(s32[2]{0:T(128)S(1)} %pad_add_fusion.5.spans_ref, s32[8]{0:T(128)S(1)} %get-tuple-element.76.counts_ref, ...), custom_call_target="tpu_custom_call" | custom-call | flops 8455716864 | bytes 8257536 | tf_op jit(solution)/shard_map/gather_sum/pallas_call | solution.py:391
  195.9 5.4 %gather_sum.5 = (bf16[768,256]{1,0:T(8,128)(2,1)S(1)}, bf16[768,256]{1,0:T(8,128)(2,1)S(1)}, bf16[768,256]{1,0:T(8,128)(2,1)S(1)}) custom-call(s32[2]{0:T(128)S(1)} %pad_add_fusion.5.spans_ref, s32[8]{0:T(128)S(1)} %get-tuple-element.76.counts_ref, s32[9]{0:T(128)S(1)} %get-tuple-element.79.starts_ref, s32[56]{0:T(128)S(1)} %reshape.269.own_here_ref, ...), custom_call_target="tpu_custom_call" | custom-call | flops 2818572288 | bytes 2752512 | tf_op jit(solution)/shard_map/gather_sum/pallas_call | solution.py:391
  201.3 3.0 %collective-permute-done.5 = bf16[768,256]{1,0:T(8,128)(2,1)S(1)} collective-permute-done((bf16[768,256]{1,0:T(8,128)(2,1)S(1)}, bf16[768,256]{1,0:T(8,128)(2,1)S(1)}, u32[]{:S(2)}, u32[]{:S(2)}) %collective-permute-start.5) | collective-permute-done | bytes 393248 | tf_op jit(solution)/shard_map/ppermute | solution.py:422
  204.4 9.1 %collective-permute-done.4 = bf16[768,256]{1,0:T(8,128)(2,1)S(1)} collective-permute-done((bf16[768,256]{1,0:T(8,128)(2,1)S(1)}, bf16[768,256]{1,0:T(8,128)(2,1)S(1)}, u32[]{:S(2)}, u32[]{:S(2)}) %collective-permute-start.4) | collective-permute-done | bytes 393248 | tf_op jit(solution)/shard_map/ppermute | solution.py:422
  217.1 3.6 %collective-permute-done.8 = f32[128,256]{1,0:T(8,128)S(1)} collective-permute-done((f32[128,256]{1,0:T(8,128)S(1)}, f32[128,256]{1,0:T(8,128)S(1)}, u32[]{:S(2)}, u32[]{:S(2)}) %collective-permute-start.8) | collective-permute-done | bytes 131104 | tf_op jit(solution)/shard_map/ppermute | solution.py:422
  224.9 2.8 %collective-permute-start.9 = (bf16[3,128,256]{2,1,0:T(8,128)(2,1)S(1)}, bf16[3,128,256]{2,1,0:T(8,128)(2,1)S(1)}, u32[]{:S(2)}, u32[]{:S(2)}) collective-permute-start(bf16[3,128,256]{2,1,0:T(8,128)(2,1)S(1)} %get-tuple-element.68), channel_id=1, source_target_pairs={{8,0},{16,8},{24,16},{0,24},{9,1},{17,9},{25,17},{1,25},{10,2},{18... | collective-permute-start | bytes 589832 | tf_op jit(solution)/shard_map/ppermute | solution.py:422
  227.9 3.6 %collective-permute-done.11 = bf16[3,128,256]{2,1,0:T(8,128)(2,1)S(1)} collective-permute-done((bf16[3,128,256]{2,1,0:T(8,128)(2,1)S(1)}, bf16[3,128,256]{2,1,0:T(8,128)(2,1)S(1)}, u32[]{:S(2)}, u32[]{:S(2)}) %collective-permute-start.11) | collective-permute-done | bytes 196640 | tf_op jit(solution)/shard_map/ppermute | solution.py:422
  239.6 7.3 %collective-permute-done.12 = bf16[768,256]{1,0:T(8,128)(2,1)S(1)} collective-permute-done((bf16[768,256]{1,0:T(8,128)(2,1)S(1)}, bf16[768,256]{1,0:T(8,128)(2,1)S(1)}, u32[]{:S(2)}, u32[]{:S(2)}) %collective-permute-start.12) | collective-permute-done | bytes 393248 | tf_op jit(solution)/shard_map/ppermute | solution.py:422
  247.0 6.4 %collective-permute-done.14 = bf16[768,256]{1,0:T(8,128)(2,1)S(1)} collective-permute-done((bf16[768,256]{1,0:T(8,128)(2,1)S(1)}, bf16[768,256]{1,0:T(8,128)(2,1)S(1)}, u32[]{:S(2)}, u32[]{:S(2)}) %collective-permute-start.14) | collective-permute-done | bytes 393248 | tf_op jit(solution)/shard_map/ppermute | solution.py:422
  256.4 2.8 collective-permute-start.18
  262.5 5.4 %collective-permute-done.17 = bf16[128,256]{1,0:T(8,128)(2,1)S(1)} collective-permute-done((bf16[128,256]{1,0:T(8,128)(2,1)S(1)}, bf16[128,256]{1,0:T(8,128)(2,1)S(1)}, u32[]{:S(2)}, u32[]{:S(2)}) %collective-permute-start.17) | collective-permute-done | bytes 65568 | tf_op jit(solution)/shard_map/ppermute | solution.py:422
  268.7 3.1 %collective-permute-start.19 = (bf16[128,256]{1,0:T(8,128)(2,1)S(1)}, bf16[128,256]{1,0:T(8,128)(2,1)S(1)}, u32[]{:S(2)}, u32[]{:S(2)}) collective-permute-start(bf16[128,256]{1,0:T(8,128)(2,1)S(1)} %fusion.14), channel_id=1, source_target_pairs={{2,0},{3,1},{4,2},{5,3},{6,4},{7,5},{0,6},{1,7},{10,8},{11,9},{12,... | collective-permute-start | bytes 196616 | tf_op jit(solution)/shard_map/ppermute | solution.py:422
  (161 shorter events, 51.5 us)
Async XLA Ops:
  4.0 13.4 %all-to-all-start = ((s32[8,1,1536]{2,1,0:T(1,128)}), s32[8,1,1536]{2,1,0:T(1,128)S(1)}, u32[]{:S(2)}, u32[]{:S(2)}) async-start(s32[8,1,1536]{2,1,0:T(1,128)} %bitcast.11), calls=%async_computation | async-start | bytes 98304 | tf_op jit(solution)/shard_map/all_to_all | solution.py:506
  30.3 76.9 %all-to-all-start.1 = ((bf16[8,768,256]{2,1,0:T(8,128)(2,1)}), bf16[8,768,256]{2,1,0:T(8,128)(2,1)}, u32[]{:S(2)}, u32[]{:S(2)}) async-start(bf16[8,768,256]{2,1,0:T(8,128)(2,1)} %lookup.3), calls=%async_computation.1 | async-start | bytes 6291456 | tf_op jit(solution)/shard_map/all_to_all | solution.py:515
  35.6 6.6 %collective-permute-start.2 = (s32[11,128]{1,0:T(8,128)S(1)}, s32[11,128]{1,0:T(8,128)S(1)}, u32[]{:S(2)}, u32[]{:S(2)}) collective-permute-start(s32[11,128]{1,0:T(8,128)S(1)} %pad_add_fusion.2), channel_id=1, source_target_pairs={{24,0},{0,8},{8,16},{16,24},{25,1},{1,9},{9,17},{17,25},{26,2},{2,... | collective-permute-start | bytes 16904 | tf_op jit(solution)/shard_map/ppermute | solution.py:422
  37.1 5.1 %collective-permute-start.1 = (s32[11,128]{1,0:T(8,128)S(1)}, s32[11,128]{1,0:T(8,128)S(1)}, u32[]{:S(2)}, u32[]{:S(2)}) collective-permute-start(s32[11,128]{1,0:T(8,128)S(1)} %pad_add_fusion.2), channel_id=1, source_target_pairs={{16,0},{24,8},{0,16},{8,24},{17,1},{25,9},{1,17},{9,25},{18,2},{26... | collective-permute-start | bytes 16904 | tf_op jit(solution)/shard_map/ppermute | solution.py:422
  38.6 3.7 %collective-permute-start = (s32[11,128]{1,0:T(8,128)S(1)}, s32[11,128]{1,0:T(8,128)S(1)}, u32[]{:S(2)}, u32[]{:S(2)}) collective-permute-start(s32[11,128]{1,0:T(8,128)S(1)} %pad_add_fusion.2), channel_id=1, source_target_pairs={{8,0},{16,8},{24,16},{0,24},{9,1},{17,9},{25,17},{1,25},{10,2},{18... | collective-permute-start | bytes 16904 | tf_op jit(solution)/shard_map/ppermute | solution.py:422
  107.2 76.0 %all-to-all-start.2 = ((bf16[8,768,256]{2,1,0:T(8,128)(2,1)}), bf16[8,768,256]{2,1,0:T(8,128)(2,1)}, u32[]{:S(2)}, u32[]{:S(2)}) async-start(bf16[8,768,256]{2,1,0:T(8,128)(2,1)} %lookup.2), calls=%async_computation.2 | async-start | bytes 6291456 | tf_op jit(solution)/shard_map/all_to_all | solution.py:560
  192.3 12.1 %collective-permute-start.5 = (bf16[768,256]{1,0:T(8,128)(2,1)S(1)}, bf16[768,256]{1,0:T(8,128)(2,1)S(1)}, u32[]{:S(2)}, u32[]{:S(2)}) collective-permute-start(bf16[768,256]{1,0:T(8,128)(2,1)S(1)} %get-tuple-element.47), channel_id=1, source_target_pairs={{8,0},{16,8},{24,16},{0,24},{9,1},{17,9},{25,17},{1,25},{10,2},{18... | collective-permute-start | bytes 1179656 | tf_op jit(solution)/shard_map/ppermute | solution.py:422
  194.8 18.7 %collective-permute-start.4 = (bf16[768,256]{1,0:T(8,128)(2,1)S(1)}, bf16[768,256]{1,0:T(8,128)(2,1)S(1)}, u32[]{:S(2)}, u32[]{:S(2)}) collective-permute-start(bf16[768,256]{1,0:T(8,128)(2,1)S(1)} %get-tuple-element.46), channel_id=1, source_target_pairs={{16,0},{24,8},{0,16},{8,24},{17,1},{25,9},{1,17},{9,25},{18,2},{26... | collective-permute-start | bytes 1179656 | tf_op jit(solution)/shard_map/ppermute | solution.py:422
  195.3 18.2 %collective-permute-start.3 = (bf16[768,256]{1,0:T(8,128)(2,1)S(1)}, bf16[768,256]{1,0:T(8,128)(2,1)S(1)}, u32[]{:S(2)}, u32[]{:S(2)}) collective-permute-start(bf16[768,256]{1,0:T(8,128)(2,1)S(1)} %get-tuple-element.45), channel_id=1, source_target_pairs={{24,0},{0,8},{8,16},{16,24},{25,1},{1,9},{9,17},{17,25},{26,2},{2,... | collective-permute-start | bytes 1179656 | tf_op jit(solution)/shard_map/ppermute | solution.py:422
  214.5 6.2 %collective-permute-start.8 = (f32[128,256]{1,0:T(8,128)S(1)}, f32[128,256]{1,0:T(8,128)S(1)}, u32[]{:S(2)}, u32[]{:S(2)}) collective-permute-start(f32[128,256]{1,0:T(8,128)S(1)} %get-tuple-element.62), channel_id=1, source_target_pairs={{8,0},{16,8},{24,16},{0,24},{9,1},{17,9},{25,17},{1,25},{10,2},{18... | collective-permute-start | bytes 393224 | tf_op jit(solution)/shard_map/ppermute | solution.py:422
  215.1 7.4 %collective-permute-start.7 = (f32[128,256]{1,0:T(8,128)S(1)}, f32[128,256]{1,0:T(8,128)S(1)}, u32[]{:S(2)}, u32[]{:S(2)}) collective-permute-start(f32[128,256]{1,0:T(8,128)S(1)} %get-tuple-element.63), channel_id=1, source_target_pairs={{16,0},{24,8},{0,16},{8,24},{17,1},{25,9},{1,17},{9,25},{18,2},{26... | collective-permute-start | bytes 393224 | tf_op jit(solution)/shard_map/ppermute | solution.py:422
  216.3 6.2 %collective-permute-start.6 = (f32[128,256]{1,0:T(8,128)S(1)}, f32[128,256]{1,0:T(8,128)S(1)}, u32[]{:S(2)}, u32[]{:S(2)}) collective-permute-start(f32[128,256]{1,0:T(8,128)S(1)} %get-tuple-element.61), channel_id=1, source_target_pairs={{24,0},{0,8},{8,16},{16,24},{25,1},{1,9},{9,17},{17,25},{26,2},{2,... | collective-permute-start | bytes 393224 | tf_op jit(solution)/shard_map/ppermute | solution.py:422
  223.5 8.0 %collective-permute-start.11 = (bf16[3,128,256]{2,1,0:T(8,128)(2,1)S(1)}, bf16[3,128,256]{2,1,0:T(8,128)(2,1)S(1)}, u32[]{:S(2)}, u32[]{:S(2)}) collective-permute-start(bf16[3,128,256]{2,1,0:T(8,128)(2,1)S(1)} %get-tuple-element.68), channel_id=1, source_target_pairs={{24,0},{0,8},{8,16},{16,24},{25,1},{1,9},{9,17},{17,25},{26,2},{2,... | collective-permute-start | bytes 589832 | tf_op jit(solution)/shard_map/ppermute | solution.py:422
  223.7 9.2 %collective-permute-start.10 = (bf16[3,128,256]{2,1,0:T(8,128)(2,1)S(1)}, bf16[3,128,256]{2,1,0:T(8,128)(2,1)S(1)}, u32[]{:S(2)}, u32[]{:S(2)}) collective-permute-start(bf16[3,128,256]{2,1,0:T(8,128)(2,1)S(1)} %get-tuple-element.68), channel_id=1, source_target_pairs={{16,0},{24,8},{0,16},{8,24},{17,1},{25,9},{1,17},{9,25},{18,2},{26... | collective-permute-start | bytes 589832 | tf_op jit(solution)/shard_map/ppermute | solution.py:422
  224.9 8.5 %collective-permute-start.9 = (bf16[3,128,256]{2,1,0:T(8,128)(2,1)S(1)}, bf16[3,128,256]{2,1,0:T(8,128)(2,1)S(1)}, u32[]{:S(2)}, u32[]{:S(2)}) collective-permute-start(bf16[3,128,256]{2,1,0:T(8,128)(2,1)S(1)} %get-tuple-element.68), channel_id=1, source_target_pairs={{8,0},{16,8},{24,16},{0,24},{9,1},{17,9},{25,17},{1,25},{10,2},{18... | collective-permute-start | bytes 589832 | tf_op jit(solution)/shard_map/ppermute | solution.py:422
  234.8 12.1 %collective-permute-start.12 = (bf16[768,256]{1,0:T(8,128)(2,1)S(1)}, bf16[768,256]{1,0:T(8,128)(2,1)S(1)}, u32[]{:S(2)}, u32[]{:S(2)}) collective-permute-start(bf16[768,256]{1,0:T(8,128)(2,1)S(1)} %fusion.2), channel_id=1, source_target_pairs={{8,0},{16,8},{24,16},{0,24},{9,1},{17,9},{25,17},{1,25},{10,2},{18... | collective-permute-start | bytes 1179656 | tf_op jit(solution)/shard_map/ppermute | solution.py:422
  237.1 9.9 %collective-permute-start.13 = (bf16[768,256]{1,0:T(8,128)(2,1)S(1)}, bf16[768,256]{1,0:T(8,128)(2,1)S(1)}, u32[]{:S(2)}, u32[]{:S(2)}) collective-permute-start(bf16[768,256]{1,0:T(8,128)(2,1)S(1)} %fusion.2), channel_id=1, source_target_pairs={{16,0},{24,8},{0,16},{8,24},{17,1},{25,9},{1,17},{9,25},{18,2},{26... | collective-permute-start | bytes 1179656 | tf_op jit(solution)/shard_map/ppermute | solution.py:422
  238.2 15.2 %collective-permute-start.14 = (bf16[768,256]{1,0:T(8,128)(2,1)S(1)}, bf16[768,256]{1,0:T(8,128)(2,1)S(1)}, u32[]{:S(2)}, u32[]{:S(2)}) collective-permute-start(bf16[768,256]{1,0:T(8,128)(2,1)S(1)} %fusion.2), channel_id=1, source_target_pairs={{24,0},{0,8},{8,16},{16,24},{25,1},{1,9},{9,17},{17,25},{26,2},{2,... | collective-permute-start | bytes 1179656 | tf_op jit(solution)/shard_map/ppermute | solution.py:422
  256.4 6.0 %collective-permute-start.18 = (bf16[128,256]{1,0:T(8,128)(2,1)S(1)}, bf16[128,256]{1,0:T(8,128)(2,1)S(1)}, u32[]{:S(2)}, u32[]{:S(2)}) collective-permute-start(bf16[128,256]{1,0:T(8,128)(2,1)S(1)} %get-tuple-element.65), channel_id=1, source_target_pairs={{2,0},{3,1},{4,2},{5,3},{6,4},{7,5},{0,6},{1,7},{10,8},{11,9},{12,... | collective-permute-start | bytes 196616 | tf_op jit(solution)/shard_map/ppermute | solution.py:422
  259.2 8.7 %collective-permute-start.17 = (bf16[128,256]{1,0:T(8,128)(2,1)S(1)}, bf16[128,256]{1,0:T(8,128)(2,1)S(1)}, u32[]{:S(2)}, u32[]{:S(2)}) collective-permute-start(bf16[128,256]{1,0:T(8,128)(2,1)S(1)} %get-tuple-element.66), channel_id=1, source_target_pairs={{4,0},{5,1},{6,2},{7,3},{0,4},{1,5},{2,6},{3,7},{12,8},{13,9},{14,... | collective-permute-start | bytes 196616 | tf_op jit(solution)/shard_map/ppermute | solution.py:422
  261.5 6.3 %collective-permute-start.16 = (bf16[128,256]{1,0:T(8,128)(2,1)S(1)}, bf16[128,256]{1,0:T(8,128)(2,1)S(1)}, u32[]{:S(2)}, u32[]{:S(2)}) collective-permute-start(bf16[128,256]{1,0:T(8,128)(2,1)S(1)} %get-tuple-element.64), channel_id=1, source_target_pairs={{6,0},{7,1},{0,2},{1,3},{2,4},{3,5},{4,6},{5,7},{14,8},{15,9},{8,1... | collective-permute-start | bytes 196616 | tf_op jit(solution)/shard_map/ppermute | solution.py:422
  267.9 6.2 %collective-permute-start.21 = (bf16[128,256]{1,0:T(8,128)(2,1)S(1)}, bf16[128,256]{1,0:T(8,128)(2,1)S(1)}, u32[]{:S(2)}, u32[]{:S(2)}) collective-permute-start(bf16[128,256]{1,0:T(8,128)(2,1)S(1)} %fusion.14), channel_id=1, source_target_pairs={{6,0},{7,1},{0,2},{1,3},{2,4},{3,5},{4,6},{5,7},{14,8},{15,9},{8,1... | collective-permute-start | bytes 196616 | tf_op jit(solution)/shard_map/ppermute | solution.py:422
  268.0 7.0 %collective-permute-start.20 = (bf16[128,256]{1,0:T(8,128)(2,1)S(1)}, bf16[128,256]{1,0:T(8,128)(2,1)S(1)}, u32[]{:S(2)}, u32[]{:S(2)}) collective-permute-start(bf16[128,256]{1,0:T(8,128)(2,1)S(1)} %fusion.14), channel_id=1, source_target_pairs={{4,0},{5,1},{6,2},{7,3},{0,4},{1,5},{2,6},{3,7},{12,8},{13,9},{14,... | collective-permute-start | bytes 196616 | tf_op jit(solution)/shard_map/ppermute | solution.py:422
  268.7 6.3 %collective-permute-start.19 = (bf16[128,256]{1,0:T(8,128)(2,1)S(1)}, bf16[128,256]{1,0:T(8,128)(2,1)S(1)}, u32[]{:S(2)}, u32[]{:S(2)}) collective-permute-start(bf16[128,256]{1,0:T(8,128)(2,1)S(1)} %fusion.14), channel_id=1, source_target_pairs={{2,0},{3,1},{4,2},{5,3},{6,4},{7,5},{0,6},{1,7},{10,8},{11,9},{12,... | collective-permute-start | bytes 196616 | tf_op jit(solution)/shard_map/ppermute | solution.py:422
  (21 other events, 500.3 us)

commit v11 on v9

--- a/solution.py
+++ b/solution.py
@@ -46,7 +46,7 @@
     return pl.CostEstimate(flops=int(flops), bytes_accessed=int(moved), transcendentals=0)
 
 
-def requests_body(batch_count, capacity, owner_ref, row_ref, slot_ref, count_ref, request_ref):
+def requests_body(batch_count, capacity, scale, owner_ref, row_ref, slot_ref, count_ref, request_ref):
     blocks, width = owner_ref.shape[0] // 2, TILE
     places = request_ref.shape[0]
     line = lambda ref, b: jnp.concatenate([ref[2 * b : 2 * b + 1], ref[2 * b + 1 : 2 * b + 2]], axis=1)
@@ -83,14 +83,14 @@
         right = jnp.where((bucket & (LANES - 1)) == low_id, 1.0, 0.0).astype(jnp.bfloat16)
         total = total + contract_cols(left, right)
     count_ref[...] = jnp.broadcast_to(running, count_ref.shape).astype(jnp.int32)
-    request_ref[...] = (total[:places] * TILE + total[places:]).astype(jnp.int32)
-
-
-def make_requests(batch_count, capacity, owners, wanted):
+    request_ref[...] = (total[:places] * TILE + total[places:]).astype(jnp.int32) * scale
+
+
+def make_requests(batch_count, capacity, scale, owners, wanted):
     total = owners.shape[0] * LANES
     places = batch_count * capacity // LANES
     return pl.pallas_call(
-        functools.partial(requests_body, batch_count, capacity),
+        functools.partial(requests_body, batch_count, capacity, scale),
         out_shape=(
             jax.ShapeDtypeStruct(owners.shape, jnp.int32),
             jax.ShapeDtypeStruct((batch_count, LANES), jnp.int32),
@@ -230,25 +230,22 @@
 
 
 def collect(piece, counts_ref, starts_ref, answer_ref, landed, arrived, packed):
-    batch_count, width, _ = answer_ref.shape
-    pieces = width // piece
+    batch_count = answer_ref.shape[0]
 
     def each_used(what):
         @pl.loop(0, batch_count)
         def _(o):
-            for c in range(pieces):
-
-                @pl.when(c * piece < counts_ref[o])
-                def _(c=c):
-                    part = pl.ds(c * piece, piece)
-                    what(
-                        o,
-                        c,
-                        part,
-                        pltpu.make_async_copy(
-                            answer_ref.at[o, part], landed.at[o, part], arrived.at[o, c]
-                        ),
-                    )
+            @pl.loop(0, pl.cdiv(counts_ref[o], piece))
+            def _(c):
+                part = pl.ds(pl.multiple_of(c * piece, piece), piece)
+                what(
+                    o,
+                    c,
+                    part,
+                    pltpu.make_async_copy(
+                        answer_ref.at[o, part], landed.at[o, part], arrived.at[o, c]
+                    ),
+                )
 
     def lay(o, c, part, copy):
         copy.wait()
@@ -400,7 +397,7 @@
         out_specs=(VMEM,) * len(out_shape),
         scratch_shapes=scratch,
         compiler_params=params(50),
-        cost_estimate=cost(2 * nodes * features * TILE * tiles, nodes * TILE * tiles // 2),
+        cost_estimate=cost(2 * nodes * features * TILE * tiles // (4 if last else 1), nodes * TILE),
         name="gather_sum",
     )(*scalars, *operands)
 
@@ -504,13 +501,15 @@
 
     owners = input_owner.reshape(input_count // LANES, LANES)
     wanted = input_row.reshape(input_count // LANES, LANES)
-    slots, counts, requests = make_requests(batch_count, capacity, owners, wanted)
+    slots, counts, requests = make_requests(
+        batch_count, capacity, store.shape[1] // LANES, owners, wanted
+    )
     owners = owners.reshape(1, input_count)
     received = lax.all_to_all(
         requests.reshape(batch_count, capacity), "batch", split_axis=0, concat_axis=0, tiled=True
     )
     first = capacity // 2
-    places = received.reshape(batch_count * capacity) * (store.shape[1] // LANES)
+    places = received.reshape(batch_count * capacity)
     looked_a = lookup(store, places, batch_count, 0, first, 60)
     near_first, looked_a = lax.optimization_barrier((nbr_one[0], looked_a))
     answer_a = lax.all_to_all(looked_a, "batch", split_axis=0, concat_axis=0, tiled=True)
@@ -537,7 +536,7 @@
     mine = owners == jnp.arange(batch_count)[:, None]
     column = jnp.sum(jnp.where(mine, shifted, 0), axis=0)
     grid = jnp.pad(column.reshape(-1, LANES), ((0, LANES - input_count // LANES), (0, 0))).T
-    table = jnp.concatenate([grid // TILE, grid % TILE], axis=0).astype(jnp.bfloat16)
+    finder = jnp.concatenate([grid // TILE, grid % TILE], axis=0).astype(jnp.bfloat16)
     notes = jnp.stack([column[:nodes], deg_one[0]], axis=1).astype(jnp.float32)
     notes = share_order(notes, parts, seeds)
     block = math.gcd(nodes, 3 * TILE)
@@ -556,7 +555,7 @@
     near, lists = lax.optimization_barrier((near, lists))
     me = feat_index.astype(jnp.int32).reshape(1)
     near = near.reshape(nodes // SLOTS, TILE)
-    adj = adjacency(me, near, table, steps * WIDE, parts, seeds)
+    adj = adjacency(me, near, finder, steps * WIDE, parts, seeds)
     looked, answer_a, adj = lax.optimization_barrier((looked, answer_a, adj))
     answer_b = lax.all_to_all(looked, "batch", split_axis=0, concat_axis=0, tiled=True)
 
@@ -589,10 +588,16 @@
             (share,) * (end - begin),
         )
 
-    self_far, agg_far, *z_far = finish(1, parts)
-    total, z_far = lax.optimization_barrier((total, z_far))
-    self_near, agg_near, *z_near = finish(0, 1)
-    z_share = sum_parts(z_near + z_far) + bias_one
+    half = parts // 2
+    cuts = [(half, parts), (1, half), (0, 1)]
+    own_rows, mean_rows, z_blocks = [], [], []
+    for begin, end in cuts:
+        own, mean, *blocks = finish(begin, end)
+        total, blocks = lax.optimization_barrier((total, blocks))
+        own_rows.append(own)
+        mean_rows.append(mean)
+        z_blocks = blocks + z_blocks
+    z_share = sum_parts(z_blocks) + bias_one
     hidden = jax.nn.silu(z_share).astype(jnp.bfloat16)
 
     agg_parts = jnp.dot(adj_two, hidden, preferred_element_type=jnp.float32)
@@ -617,12 +622,12 @@
     dh_share = dh_share + jnp.pad(contract_cols(dz_two, w2_self), ((0, rest), (0, 0)))
     dz_share = (dh_share * silu_grad(z_share)).astype(jnp.bfloat16)
     dz_blocks = spread_parts(dz_share)
-    dz_near, dz_far = dz_blocks[0], jnp.concatenate(dz_blocks[1:])
+    dz_rows = [jnp.concatenate(dz_blocks[begin:end]) for begin, end in cuts]
     group = turned(group, (parts - feat_index) % parts).transpose(1, 0, 2, 3)
     self_all, agg_all, dz_all = (x.reshape(seeds, hidden_width) for x in group)
     grads = [contract_rows(self_all, dz_all), contract_rows(agg_all, dz_all)]
-    grads.append(contract_rows(self_near, dz_near) + contract_rows(self_far, dz_far))
-    grads.append(contract_rows(agg_near, dz_near) + contract_rows(agg_far, dz_far))
+    for rows in (own_rows, mean_rows):
+        grads.append(sum(contract_rows(x, y) for x, y in zip(rows, dz_rows)))
     total = total_over_batch(jnp.concatenate(grads)).astype(jnp.float32)
     return (activations, *total.reshape(len(grads), -1, hidden_width))
 

time: 277 us -> 277 us (level)
  waiting for transfers between devices: 92.7 us -> 86.6 us
  starting transfers between devices: 40.4 us -> 45.9 us
  Pallas kernels: 118 us -> 121 us
    ppermute x21, waiting for transfers between devices: 44.5 us -> 38.3 us  [passed(): lax.ppermute(part, axis, [((i + shift) % parts, i) for i in range(parts)])]
    ppermute x21, starting transfers between devices: 24.9 us -> 30.3 us  [passed(): lax.ppermute(part, axis, [((i + shift) % parts, i) for i in range(parts)])]
    pallas_call x3 -> x4, Pallas kernels: 46.7 us -> 49.5 us  [gather_sum(): pl.pallas_call(functools.partial(gather_sum_body, piece, last, row0), out...]
  transfers between devices with their start and end apart: 26 -> 26, of which waited for: 19 -> 18; matrix products, arithmetic and copies ran while one was open for 3% -> 4% of each run, Pallas kernels for 34% -> 36%
where the time goes in v11:
time: 277 us; the launch traced here: 276 us
  Pallas kernels  121 us (44%)
  waiting for transfers between devices  86.6 us (31%)
  starting transfers between devices  45.9 us (17%)
  local copies, waits for them, and re-layouts  10 us (4%)
  matrix products  5.47 us (2%)
  other arithmetic  4.87 us (2%)
  between operations  2.83 us (1%)
    pallas_call x4, Pallas kernels, gather_sum(): pl.pallas_call(functools.partial(gather_sum_body, piece, last, row0), out...  49.5 us
    pallas_call x1, Pallas kernels, adjacency(): pl.pallas_call(functools.partial(adjacency_body, tiles), out_shape=jax.Sh...  47.9 us
    ppermute x21, waiting for transfers between devices, passed(): lax.ppermute(part, axis, [((i + shift) % parts, i) for i in range(parts)])  38.3 us
    all_to_all x1, waiting for transfers between devices, local(): lax.all_to_all(looked, 'batch', split_axis=0, concat_axis=0, tiled=True)  36.8 us
    ppermute x21, starting transfers between devices, passed(): lax.ppermute(part, axis, [((i + shift) % parts, i) for i in range(parts)])  30.3 us
    pallas_call x2, Pallas kernels, lookup(): pl.pallas_call(functools.partial(lookup_body, places.shape[0] // groups,...  21.3 us
    all_to_all x1, starting transfers between devices, local(): lax.all_to_all(requests.reshape(batch_count, capacity), 'batch', split_ax...  6.33 us
  transfers between devices with their start and end apart: 26, of which 18 were waited for; matrix products, arithmetic and copies ran while one was open for 4% of the time, Pallas kernels for 36%

profile of v11, /device:TPU:0, one launch (start us, length us, event | category | flops | bytes accessed | tf_op | source)
XLA Modules:
  0.0 276.2 jit_solution(16195198321998545307)
XLA Ops:
  4.0 6.3 %all-to-all-start = ((s32[8,1,1536]{2,1,0:T(1,128)}), s32[8,1,1536]{2,1,0:T(1,128)S(1)}, u32[]{:S(2)}, u32[]{:S(2)}) async-start(s32[8,1,1536]{2,1,0:T(1,128)} %bitcast.9), calls=%async_computation | async-start | bytes 98304 | tf_op jit(solution)/shard_map/all_to_all | solution.py:508
  11.3 4.9 %all-to-all-done = s32[8,1,1536]{2,1,0:T(1,128)S(1)} async-done(((s32[8,1,1536]{2,1,0:T(1,128)}), s32[8,1,1536]{2,1,0:T(1,128)S(1)}, u32[]{:S(2)}, u32[]{:S(2)}) %all-to-all-start) | async-done | bytes 49184 | tf_op jit(solution)/shard_map/all_to_all | solution.py:508
  16.8 11.5 %lookup.3 = bf16[8,768,256]{2,1,0:T(8,128)(2,1)} custom-call(s32[12288]{0:T(1024)} %bitcast.166, bf16[8192,256]{1,0:T(8,128)(2,1)} %store_in.3), custom_call_target="tpu_custom_call" | custom-call | flops 62914560 | bytes 4194304 | tf_op jit(solution)/shard_map/lookup/pallas_call | solution.py:151
  28.3 4.6 %all-to-all-start.1 = ((bf16[8,768,256]{2,1,0:T(8,128)(2,1)}), bf16[8,768,256]{2,1,0:T(8,128)(2,1)}, u32[]{:S(2)}, u32[]{:S(2)}) async-start(bf16[8,768,256]{2,1,0:T(8,128)(2,1)} %lookup.3), calls=%async_computation.1 | async-start | bytes 6291456 | tf_op jit(solution)/shard_map/all_to_all | solution.py:515
  43.1 9.8 %lookup.2 = bf16[8,768,256]{2,1,0:T(8,128)(2,1)} custom-call(s32[12288]{0:T(1024)S(1)} %bitcast.167, bf16[8192,256]{1,0:T(8,128)(2,1)S(1)} %copy-done.3), custom_call_target="tpu_custom_call" | custom-call | flops 62914560 | bytes 4194304 | tf_op jit(solution)/shard_map/lookup/pallas_call | solution.py:151
  53.0 47.9 %adjacency.1.adj_ref = f8e4m3fn[28,3072,256]{2,1,0:T(32,128)(4,1)} custom-call(s32[1]{0:T(128)} %bitcast.11.me_ref, s32[192,256]{1,0:T(8,128)S(1)} %reshape.262.near_ref, bf16[256,128]{1,0:T(8,128)(2,1)S(1)} %pad_maximum_fusion.7.table_ref), custom_call_target="tpu_custom_call" | custom-call | flops 22548578304 | bytes 22020096 | tf_op jit(solution)/shard_map/adjacency/pallas_call | solution.py:214
  100.8 3.6 %all-to-all-done.1.answer_ref = bf16[8,768,256]{2,1,0:T(8,128)(2,1)} async-done(((bf16[8,768,256]{2,1,0:T(8,128)(2,1)}), bf16[8,768,256]{2,1,0:T(8,128)(2,1)}, u32[]{:S(2)}, u32[]{:S(2)}) %all-to-all-start.1) | async-done | bytes 3145760 | tf_op jit(solution)/shard_map/all_to_all | solution.py:515
  104.5 4.5 %all-to-all-start.2 = ((bf16[8,768,256]{2,1,0:T(8,128)(2,1)}), bf16[8,768,256]{2,1,0:T(8,128)(2,1)}, u32[]{:S(2)}, u32[]{:S(2)}) async-start(bf16[8,768,256]{2,1,0:T(8,128)(2,1)} %lookup.2), calls=%async_computation.2 | async-start | bytes 6291456 | tf_op jit(solution)/shard_map/all_to_all | solution.py:560
  112.1 31.5 %gather_sum.4 = (f32[3072,256]{1,0:T(8,128)}, f32[3072,256]{1,0:T(8,128)}) custom-call(s32[2]{0:T(128)S(1)} %pad_add_fusion.5.spans_ref, s32[8]{0:T(128)S(1)} %get-tuple-element.85.counts_ref, s32[9]{0:T(128)S(1)} %get-tuple-element.87.starts_ref, s32[56]{0:T(128)S(1)} %reshape.269.own_here_ref, bf16[8,768,256]{2,1,0:T(8,128)(2,1)} %all-to-all-done.1.answer_ref, ...), custom_call_target="tpu_custom_call" | custom-call | flops 11274289152 | bytes 786432 | tf_op jit(solution)/shard_map/gather_sum/pallas_call | solution.py:393
  143.7 36.8 %all-to-all-done.2.answer_ref = bf16[8,768,256]{2,1,0:T(8,128)(2,1)} async-done(((bf16[8,768,256]{2,1,0:T(8,128)(2,1)}), bf16[8,768,256]{2,1,0:T(8,128)(2,1)}, u32[]{:S(2)}, u32[]{:S(2)}) %all-to-all-start.2) | async-done | bytes 3145760 | tf_op jit(solution)/shard_map/all_to_all | solution.py:560
  180.5 7.4 %gather_sum.5 = (bf16[1536,256]{1,0:T(8,128)(2,1)S(1)}, bf16[1536,256]{1,0:T(8,128)(2,1)S(1)}, bf16[768,256]{1,0:T(8,128)(2,1)S(1)}, bf16[768,256]{1,0:T(8,128)(2,1)S(1)}) custom-call(s32[2]{0:T(128)S(1)} %pad_add_fusion.6.spans_ref, s32[8]{0:T(128)S(1)} %get-tuple-element.84.counts_ref, s32[9]{0:T(128)S(1)} %get-tuple-element.86.starts_ref, ...), custom_call_target="tpu_custom_call" | custom-call | flops 1409286144 | bytes 393216 | tf_op jit(solution)/shard_map/gather_sum/pallas_call | solution.py:393
  187.9 2.3 collective-permute-start.5
  190.9 5.3 %gather_sum.6 = (bf16[768,256]{1,0:T(8,128)(2,1)S(1)}, bf16[768,256]{1,0:T(8,128)(2,1)S(1)}, bf16[768,256]{1,0:T(8,128)(2,1)S(1)}) custom-call(s32[2]{0:T(128)S(1)} %pad_add_fusion.6.spans_ref, s32[8]{0:T(128)S(1)} %get-tuple-element.84.counts_ref, s32[9]{0:T(128)S(1)} %get-tuple-element.86.starts_ref, s32[56]{0:T(128)S(1)} %reshape.269.own_here_ref, ...), custom_call_target="tpu_custom_call" | custom-call | flops 704643072 | bytes 196608 | tf_op jit(solution)/shard_map/gather_sum/pallas_call | solution.py:393
  199.1 5.3 %gather_sum.7 = (bf16[768,256]{1,0:T(8,128)(2,1)S(1)}, bf16[768,256]{1,0:T(8,128)(2,1)S(1)}, bf16[768,256]{1,0:T(8,128)(2,1)S(1)}) custom-call(s32[2]{0:T(128)S(1)} %pad_add_fusion.6.spans_ref, s32[8]{0:T(128)S(1)} %get-tuple-element.84.counts_ref, s32[9]{0:T(128)S(1)} %get-tuple-element.86.starts_ref, s32[56]{0:T(128)S(1)} %reshape.269.own_here_ref, ...), custom_call_target="tpu_custom_call" | custom-call | flops 704643072 | bytes 196608 | tf_op jit(solution)/shard_map/gather_sum/pallas_call | solution.py:393
  204.4 4.7 %collective-permute-done.4 = bf16[768,256]{1,0:T(8,128)(2,1)S(1)} collective-permute-done((bf16[768,256]{1,0:T(8,128)(2,1)S(1)}, bf16[768,256]{1,0:T(8,128)(2,1)S(1)}, u32[]{:S(2)}, u32[]{:S(2)}) %collective-permute-start.4) | collective-permute-done | bytes 393248 | tf_op jit(solution)/shard_map/ppermute | solution.py:424
  212.6 3.6 %collective-permute-done.8 = f32[128,256]{1,0:T(8,128)S(1)} collective-permute-done((f32[128,256]{1,0:T(8,128)S(1)}, f32[128,256]{1,0:T(8,128)S(1)}, u32[]{:S(2)}, u32[]{:S(2)}) %collective-permute-start.8) | collective-permute-done | bytes 131104 | tf_op jit(solution)/shard_map/ppermute | solution.py:424
  220.4 2.8 %collective-permute-start.9 = (bf16[3,128,256]{2,1,0:T(8,128)(2,1)S(1)}, bf16[3,128,256]{2,1,0:T(8,128)(2,1)S(1)}, u32[]{:S(2)}, u32[]{:S(2)}) collective-permute-start(bf16[3,128,256]{2,1,0:T(8,128)(2,1)S(1)} %get-tuple-element.76), channel_id=1, source_target_pairs={{8,0},{16,8},{24,16},{0,24},{9,1},{17,9},{25,17},{1,25},{10,2},{18... | collective-permute-start | bytes 589832 | tf_op jit(solution)/shard_map/ppermute | solution.py:424
  223.5 4.1 %collective-permute-done.11 = bf16[3,128,256]{2,1,0:T(8,128)(2,1)S(1)} collective-permute-done((bf16[3,128,256]{2,1,0:T(8,128)(2,1)S(1)}, bf16[3,128,256]{2,1,0:T(8,128)(2,1)S(1)}, u32[]{:S(2)}, u32[]{:S(2)}) %collective-permute-start.11) | collective-permute-done | bytes 196640 | tf_op jit(solution)/shard_map/ppermute | solution.py:424
  230.2 2.5 collective-permute-start.14
  235.3 7.9 %collective-permute-done.12 = bf16[768,256]{1,0:T(8,128)(2,1)S(1)} collective-permute-done((bf16[768,256]{1,0:T(8,128)(2,1)S(1)}, bf16[768,256]{1,0:T(8,128)(2,1)S(1)}, u32[]{:S(2)}, u32[]{:S(2)}) %collective-permute-start.12) | collective-permute-done | bytes 393248 | tf_op jit(solution)/shard_map/ppermute | solution.py:424
  243.5 5.4 %collective-permute-done.13 = bf16[768,256]{1,0:T(8,128)(2,1)S(1)} collective-permute-done((bf16[768,256]{1,0:T(8,128)(2,1)S(1)}, bf16[768,256]{1,0:T(8,128)(2,1)S(1)}, u32[]{:S(2)}, u32[]{:S(2)}) %collective-permute-start.13) | collective-permute-done | bytes 393248 | tf_op jit(solution)/shard_map/ppermute | solution.py:424
  252.0 6.3 %collective-permute-start.18 = (bf16[128,256]{1,0:T(8,128)(2,1)S(1)}, bf16[128,256]{1,0:T(8,128)(2,1)S(1)}, u32[]{:S(2)}, u32[]{:S(2)}) collective-permute-start(bf16[128,256]{1,0:T(8,128)(2,1)S(1)} %get-tuple-element.73), channel_id=1, source_target_pairs={{2,0},{3,1},{4,2},{5,3},{6,4},{7,5},{0,6},{1,7},{10,8},{11,9},{12,... | collective-permute-start | bytes 196616 | tf_op jit(solution)/shard_map/ppermute | solution.py:424
  260.8 4.1 %collective-permute-done.17 = bf16[128,256]{1,0:T(8,128)(2,1)S(1)} collective-permute-done((bf16[128,256]{1,0:T(8,128)(2,1)S(1)}, bf16[128,256]{1,0:T(8,128)(2,1)S(1)}, u32[]{:S(2)}, u32[]{:S(2)}) %collective-permute-start.17) | collective-permute-done | bytes 65568 | tf_op jit(solution)/shard_map/ppermute | solution.py:424
  267.6 2.3 collective-permute-start.19
  (160 shorter events, 48.0 us)
Async XLA Ops:
  4.0 12.2 %all-to-all-start = ((s32[8,1,1536]{2,1,0:T(1,128)}), s32[8,1,1536]{2,1,0:T(1,128)S(1)}, u32[]{:S(2)}, u32[]{:S(2)}) async-start(s32[8,1,1536]{2,1,0:T(1,128)} %bitcast.9), calls=%async_computation | async-start | bytes 98304 | tf_op jit(solution)/shard_map/all_to_all | solution.py:508
  28.3 76.1 %all-to-all-start.1 = ((bf16[8,768,256]{2,1,0:T(8,128)(2,1)}), bf16[8,768,256]{2,1,0:T(8,128)(2,1)}, u32[]{:S(2)}, u32[]{:S(2)}) async-start(bf16[8,768,256]{2,1,0:T(8,128)(2,1)} %lookup.3), calls=%async_computation.1 | async-start | bytes 6291456 | tf_op jit(solution)/shard_map/all_to_all | solution.py:515
  33.0 6.6 %collective-permute-start.2 = (s32[11,128]{1,0:T(8,128)S(1)}, s32[11,128]{1,0:T(8,128)S(1)}, u32[]{:S(2)}, u32[]{:S(2)}) collective-permute-start(s32[11,128]{1,0:T(8,128)S(1)} %pad_add_fusion.2), channel_id=1, source_target_pairs={{24,0},{0,8},{8,16},{16,24},{25,1},{1,9},{9,17},{17,25},{26,2},{2,... | collective-permute-start | bytes 16904 | tf_op jit(solution)/shard_map/ppermute | solution.py:424
  34.5 5.1 %collective-permute-start.1 = (s32[11,128]{1,0:T(8,128)S(1)}, s32[11,128]{1,0:T(8,128)S(1)}, u32[]{:S(2)}, u32[]{:S(2)}) collective-permute-start(s32[11,128]{1,0:T(8,128)S(1)} %pad_add_fusion.2), channel_id=1, source_target_pairs={{16,0},{24,8},{0,16},{8,24},{17,1},{25,9},{1,17},{9,25},{18,2},{26... | collective-permute-start | bytes 16904 | tf_op jit(solution)/shard_map/ppermute | solution.py:424
  36.0 3.7 %collective-permute-start = (s32[11,128]{1,0:T(8,128)S(1)}, s32[11,128]{1,0:T(8,128)S(1)}, u32[]{:S(2)}, u32[]{:S(2)}) collective-permute-start(s32[11,128]{1,0:T(8,128)S(1)} %pad_add_fusion.2), channel_id=1, source_target_pairs={{8,0},{16,8},{24,16},{0,24},{9,1},{17,9},{25,17},{1,25},{10,2},{18... | collective-permute-start | bytes 16904 | tf_op jit(solution)/shard_map/ppermute | solution.py:424
  104.5 76.0 %all-to-all-start.2 = ((bf16[8,768,256]{2,1,0:T(8,128)(2,1)}), bf16[8,768,256]{2,1,0:T(8,128)(2,1)}, u32[]{:S(2)}, u32[]{:S(2)}) async-start(bf16[8,768,256]{2,1,0:T(8,128)(2,1)} %lookup.2), calls=%async_computation.2 | async-start | bytes 6291456 | tf_op jit(solution)/shard_map/all_to_all | solution.py:560
  187.9 16.4 %collective-permute-start.5 = (bf16[768,256]{1,0:T(8,128)(2,1)S(1)}, bf16[768,256]{1,0:T(8,128)(2,1)S(1)}, u32[]{:S(2)}, u32[]{:S(2)}) collective-permute-start(bf16[768,256]{1,0:T(8,128)(2,1)S(1)} %get-tuple-element.53), channel_id=1, source_target_pairs={{8,0},{16,8},{24,16},{0,24},{9,1},{17,9},{25,17},{1,25},{10,2},{18... | collective-permute-start | bytes 1179656 | tf_op jit(solution)/shard_map/ppermute | solution.py:424
  190.2 18.8 %collective-permute-start.4 = (bf16[768,256]{1,0:T(8,128)(2,1)S(1)}, bf16[768,256]{1,0:T(8,128)(2,1)S(1)}, u32[]{:S(2)}, u32[]{:S(2)}) collective-permute-start(bf16[768,256]{1,0:T(8,128)(2,1)S(1)} %get-tuple-element.52), channel_id=1, source_target_pairs={{16,0},{24,8},{0,16},{8,24},{17,1},{25,9},{1,17},{9,25},{18,2},{26... | collective-permute-start | bytes 1179656 | tf_op jit(solution)/shard_map/ppermute | solution.py:424
  196.2 12.9 %collective-permute-start.3 = (bf16[768,256]{1,0:T(8,128)(2,1)S(1)}, bf16[768,256]{1,0:T(8,128)(2,1)S(1)}, u32[]{:S(2)}, u32[]{:S(2)}) collective-permute-start(bf16[768,256]{1,0:T(8,128)(2,1)S(1)} %get-tuple-element.51), channel_id=1, source_target_pairs={{24,0},{0,8},{8,16},{16,24},{25,1},{1,9},{9,17},{17,25},{26,2},{2,... | collective-permute-start | bytes 1179656 | tf_op jit(solution)/shard_map/ppermute | solution.py:424
  210.1 6.2 %collective-permute-start.8 = (f32[128,256]{1,0:T(8,128)S(1)}, f32[128,256]{1,0:T(8,128)S(1)}, u32[]{:S(2)}, u32[]{:S(2)}) collective-permute-start(f32[128,256]{1,0:T(8,128)S(1)} %get-tuple-element.70), channel_id=1, source_target_pairs={{8,0},{16,8},{24,16},{0,24},{9,1},{17,9},{25,17},{1,25},{10,2},{18... | collective-permute-start | bytes 393224 | tf_op jit(solution)/shard_map/ppermute | solution.py:424
  210.6 7.5 %collective-permute-start.7 = (f32[128,256]{1,0:T(8,128)S(1)}, f32[128,256]{1,0:T(8,128)S(1)}, u32[]{:S(2)}, u32[]{:S(2)}) collective-permute-start(f32[128,256]{1,0:T(8,128)S(1)} %get-tuple-element.71), channel_id=1, source_target_pairs={{16,0},{24,8},{0,16},{8,24},{17,1},{25,9},{1,17},{9,25},{18,2},{26... | collective-permute-start | bytes 393224 | tf_op jit(solution)/shard_map/ppermute | solution.py:424
  211.9 6.2 %collective-permute-start.6 = (f32[128,256]{1,0:T(8,128)S(1)}, f32[128,256]{1,0:T(8,128)S(1)}, u32[]{:S(2)}, u32[]{:S(2)}) collective-permute-start(f32[128,256]{1,0:T(8,128)S(1)} %get-tuple-element.69), channel_id=1, source_target_pairs={{24,0},{0,8},{8,16},{16,24},{25,1},{1,9},{9,17},{17,25},{26,2},{2,... | collective-permute-start | bytes 393224 | tf_op jit(solution)/shard_map/ppermute | solution.py:424
  219.2 8.4 %collective-permute-start.11 = (bf16[3,128,256]{2,1,0:T(8,128)(2,1)S(1)}, bf16[3,128,256]{2,1,0:T(8,128)(2,1)S(1)}, u32[]{:S(2)}, u32[]{:S(2)}) collective-permute-start(bf16[3,128,256]{2,1,0:T(8,128)(2,1)S(1)} %get-tuple-element.76), channel_id=1, source_target_pairs={{24,0},{0,8},{8,16},{16,24},{25,1},{1,9},{9,17},{17,25},{26,2},{2,... | collective-permute-start | bytes 589832 | tf_op jit(solution)/shard_map/ppermute | solution.py:424
  219.2 9.5 %collective-permute-start.10 = (bf16[3,128,256]{2,1,0:T(8,128)(2,1)S(1)}, bf16[3,128,256]{2,1,0:T(8,128)(2,1)S(1)}, u32[]{:S(2)}, u32[]{:S(2)}) collective-permute-start(bf16[3,128,256]{2,1,0:T(8,128)(2,1)S(1)} %get-tuple-element.76), channel_id=1, source_target_pairs={{16,0},{24,8},{0,16},{8,24},{17,1},{25,9},{1,17},{9,25},{18,2},{26... | collective-permute-start | bytes 589832 | tf_op jit(solution)/shard_map/ppermute | solution.py:424
  220.4 8.4 %collective-permute-start.9 = (bf16[3,128,256]{2,1,0:T(8,128)(2,1)S(1)}, bf16[3,128,256]{2,1,0:T(8,128)(2,1)S(1)}, u32[]{:S(2)}, u32[]{:S(2)}) collective-permute-start(bf16[3,128,256]{2,1,0:T(8,128)(2,1)S(1)} %get-tuple-element.76), channel_id=1, source_target_pairs={{8,0},{16,8},{24,16},{0,24},{9,1},{17,9},{25,17},{1,25},{10,2},{18... | collective-permute-start | bytes 589832 | tf_op jit(solution)/shard_map/ppermute | solution.py:424
  230.2 13.0 %collective-permute-start.14 = (bf16[768,256]{1,0:T(8,128)(2,1)S(1)}, bf16[768,256]{1,0:T(8,128)(2,1)S(1)}, u32[]{:S(2)}, u32[]{:S(2)}) collective-permute-start(bf16[768,256]{1,0:T(8,128)(2,1)S(1)} %fusion.2), channel_id=1, source_target_pairs={{8,0},{16,8},{24,16},{0,24},{9,1},{17,9},{25,17},{1,25},{10,2},{18... | collective-permute-start | bytes 1179656 | tf_op jit(solution)/shard_map/ppermute | solution.py:424
  232.8 10.4 %collective-permute-start.12 = (bf16[768,256]{1,0:T(8,128)(2,1)S(1)}, bf16[768,256]{1,0:T(8,128)(2,1)S(1)}, u32[]{:S(2)}, u32[]{:S(2)}) collective-permute-start(bf16[768,256]{1,0:T(8,128)(2,1)S(1)} %fusion.2), channel_id=1, source_target_pairs={{16,0},{24,8},{0,16},{8,24},{17,1},{25,9},{1,17},{9,25},{18,2},{26... | collective-permute-start | bytes 1179656 | tf_op jit(solution)/shard_map/ppermute | solution.py:424
  233.9 15.0 %collective-permute-start.13 = (bf16[768,256]{1,0:T(8,128)(2,1)S(1)}, bf16[768,256]{1,0:T(8,128)(2,1)S(1)}, u32[]{:S(2)}, u32[]{:S(2)}) collective-permute-start(bf16[768,256]{1,0:T(8,128)(2,1)S(1)} %fusion.2), channel_id=1, source_target_pairs={{24,0},{0,8},{8,16},{16,24},{25,1},{1,9},{9,17},{17,25},{26,2},{2,... | collective-permute-start | bytes 1179656 | tf_op jit(solution)/shard_map/ppermute | solution.py:424
  252.0 8.7 %collective-permute-start.18 = (bf16[128,256]{1,0:T(8,128)(2,1)S(1)}, bf16[128,256]{1,0:T(8,128)(2,1)S(1)}, u32[]{:S(2)}, u32[]{:S(2)}) collective-permute-start(bf16[128,256]{1,0:T(8,128)(2,1)S(1)} %get-tuple-element.73), channel_id=1, source_target_pairs={{2,0},{3,1},{4,2},{5,3},{6,4},{7,5},{0,6},{1,7},{10,8},{11,9},{12,... | collective-permute-start | bytes 196616 | tf_op jit(solution)/shard_map/ppermute | solution.py:424
  258.3 6.6 %collective-permute-start.17 = (bf16[128,256]{1,0:T(8,128)(2,1)S(1)}, bf16[128,256]{1,0:T(8,128)(2,1)S(1)}, u32[]{:S(2)}, u32[]{:S(2)}) collective-permute-start(bf16[128,256]{1,0:T(8,128)(2,1)S(1)} %get-tuple-element.74), channel_id=1, source_target_pairs={{4,0},{5,1},{6,2},{7,3},{0,4},{1,5},{2,6},{3,7},{12,8},{13,9},{14,... | collective-permute-start | bytes 196616 | tf_op jit(solution)/shard_map/ppermute | solution.py:424
  258.3 6.6 %collective-permute-start.16 = (bf16[128,256]{1,0:T(8,128)(2,1)S(1)}, bf16[128,256]{1,0:T(8,128)(2,1)S(1)}, u32[]{:S(2)}, u32[]{:S(2)}) collective-permute-start(bf16[128,256]{1,0:T(8,128)(2,1)S(1)} %get-tuple-element.72), channel_id=1, source_target_pairs={{6,0},{7,1},{0,2},{1,3},{2,4},{3,5},{4,6},{5,7},{14,8},{15,9},{8,1... | collective-permute-start | bytes 196616 | tf_op jit(solution)/shard_map/ppermute | solution.py:424
  265.0 6.9 %collective-permute-start.21 = (bf16[128,256]{1,0:T(8,128)(2,1)S(1)}, bf16[128,256]{1,0:T(8,128)(2,1)S(1)}, u32[]{:S(2)}, u32[]{:S(2)}) collective-permute-start(bf16[128,256]{1,0:T(8,128)(2,1)S(1)} %fusion.16), channel_id=1, source_target_pairs={{6,0},{7,1},{0,2},{1,3},{2,4},{3,5},{4,6},{5,7},{14,8},{15,9},{8,1... | collective-permute-start | bytes 196616 | tf_op jit(solution)/shard_map/ppermute | solution.py:424
  265.4 7.8 %collective-permute-start.20 = (bf16[128,256]{1,0:T(8,128)(2,1)S(1)}, bf16[128,256]{1,0:T(8,128)(2,1)S(1)}, u32[]{:S(2)}, u32[]{:S(2)}) collective-permute-start(bf16[128,256]{1,0:T(8,128)(2,1)S(1)} %fusion.16), channel_id=1, source_target_pairs={{4,0},{5,1},{6,2},{7,3},{0,4},{1,5},{2,6},{3,7},{12,8},{13,9},{14,... | collective-permute-start | bytes 196616 | tf_op jit(solution)/shard_map/ppermute | solution.py:424
  267.6 5.6 %collective-permute-start.19 = (bf16[128,256]{1,0:T(8,128)(2,1)S(1)}, bf16[128,256]{1,0:T(8,128)(2,1)S(1)}, u32[]{:S(2)}, u32[]{:S(2)}) collective-permute-start(bf16[128,256]{1,0:T(8,128)(2,1)S(1)} %fusion.16), channel_id=1, source_target_pairs={{2,0},{3,1},{4,2},{5,3},{6,4},{7,5},{0,6},{1,7},{10,8},{11,9},{12,... | collective-permute-start | bytes 196616 | tf_op jit(solution)/shard_map/ppermute | solution.py:424
  (20 other events, 470.4 us)

commit v12 on v11

--- a/solution.py
+++ b/solution.py
@@ -433,6 +433,15 @@
     return turned(array, lax.axis_index(axis))
 
 
+def in_order(blocks):
+    parts = lax.axis_size("feat")
+    total = jnp.zeros((parts,) + blocks[0].shape, blocks[0].dtype)
+    for j, block in enumerate(blocks):
+        spot = (lax.axis_index("feat") + j) % parts
+        total = lax.dynamic_update_index_in_dim(total, block, spot, 0)
+    return total
+
+
 def spread_parts(part, axis="feat"):
     return [part] + [passed(part, j, axis) for j in range(1, lax.axis_size(axis))]
 
@@ -547,12 +556,13 @@
     fanout_two = nbr_two.shape[2]
     used_two = jnp.arange(fanout_two)[:, None] < deg_two
     lists = jnp.concatenate([jnp.where(used_two, nbr_two[0].T, -1), deg_two], axis=0)
-    lists = jnp.stack(spread_parts(lists))
+    lists = in_order(spread_parts(lists))
+    upstream = in_order(spread_parts(cotangent[0])).reshape(seeds, hidden_width)
 
     fanout = nbr_one.shape[2]
     used = jnp.arange(fanout)[None, :] < deg_one[0][:, None]
     near = jnp.pad(jnp.where(used, near_first, -1), ((0, 0), (0, SLOTS - fanout)), constant_values=-1)
-    near, lists = lax.optimization_barrier((near, lists))
+    near, lists, upstream = lax.optimization_barrier((near, lists, upstream))
     me = feat_index.astype(jnp.int32).reshape(1)
     near = near.reshape(nodes // SLOTS, TILE)
     adj = adjacency(me, near, finder, steps * WIDE, parts, seeds)
@@ -600,32 +610,30 @@
     z_share = sum_parts(z_blocks) + bias_one
     hidden = jax.nn.silu(z_share).astype(jnp.bfloat16)
 
-    agg_parts = jnp.dot(adj_two, hidden, preferred_element_type=jnp.float32)
-    agg_total = sum_parts(agg_parts.reshape(parts, seed_rows, hidden_width))
-    deg_second = deg_two[0].astype(jnp.float32)[:, None]
-    agg_two = (agg_total / deg_second).astype(jnp.bfloat16)
-    self_two = hidden[:seed_rows]
+    agg_part = jnp.dot(adj_two, hidden, preferred_element_type=jnp.float32).astype(jnp.bfloat16)
+    blocks = spread_parts(jnp.concatenate([agg_part, hidden[:seed_rows]]))
+    deg_second = deg_all.astype(jnp.float32)[:, None]
+    agg_two = sum(x[:seeds].astype(jnp.float32) for x in blocks) / deg_second
+    agg_two = agg_two.astype(jnp.bfloat16)
+    self_two = in_order([x[seeds:] for x in blocks]).reshape(seeds, hidden_width)
     z_two = (
         jnp.dot(self_two, w2_self, preferred_element_type=jnp.float32)
         + jnp.dot(agg_two, w2_neigh, preferred_element_type=jnp.float32)
         + bias_two
     )
-    activations = jax.nn.silu(z_two).astype(jnp.bfloat16)[None]
-    dz_two = (cotangent[0].astype(jnp.float32) * silu_grad(z_two)).astype(jnp.bfloat16)
-    group = jnp.stack(spread_parts(jnp.stack([self_two, agg_two, dz_two])))
-    dz_two_all = group[:, 2].reshape(seeds, hidden_width)
-
-    back = contract_cols(dz_two_all, w2_neigh) / deg_all.astype(jnp.float32)[:, None]
+    dz_two = (upstream.astype(jnp.float32) * silu_grad(z_two)).astype(jnp.bfloat16)
+    mine = lambda x: lax.dynamic_slice_in_dim(x, feat_index * seed_rows, seed_rows, 0)
+    activations = jax.nn.silu(mine(z_two)).astype(jnp.bfloat16)[None]
+
+    back = contract_cols(dz_two, w2_neigh) / deg_second
     back_high = back.astype(jnp.bfloat16)
     back_low = (back - back_high.astype(jnp.float32)).astype(jnp.bfloat16)
     dh_share = contract_rows(adj_two, back_high) + contract_rows(adj_two, back_low)
-    dh_share = dh_share + jnp.pad(contract_cols(dz_two, w2_self), ((0, rest), (0, 0)))
+    dh_share = dh_share + jnp.pad(contract_cols(mine(dz_two), w2_self), ((0, rest), (0, 0)))
     dz_share = (dh_share * silu_grad(z_share)).astype(jnp.bfloat16)
     dz_blocks = spread_parts(dz_share)
     dz_rows = [jnp.concatenate(dz_blocks[begin:end]) for begin, end in cuts]
-    group = turned(group, (parts - feat_index) % parts).transpose(1, 0, 2, 3)
-    self_all, agg_all, dz_all = (x.reshape(seeds, hidden_width) for x in group)
-    grads = [contract_rows(self_all, dz_all), contract_rows(agg_all, dz_all)]
+    grads = [contract_rows(self_two, dz_two), contract_rows(agg_two, dz_two)]
     for rows in (own_rows, mean_rows):
         grads.append(sum(contract_rows(x, y) for x, y in zip(rows, dz_rows)))
     total = total_over_batch(jnp.concatenate(grads)).astype(jnp.float32)

time: 277 us -> 277 us (level)
  starting transfers between devices: 45.9 us -> 42.1 us
    ppermute x21, starting transfers between devices: 30.3 us -> 26.1 us  [passed(): lax.ppermute(part, axis, [((i + shift) % parts, i) for i in range(parts)])]
    all_to_all x1, waiting for transfers between devices: 3.62 us -> 0.01 us  [local(): lax.all_to_all(looked_a, 'batch', split_axis=0, concat_axis=0, tiled=True)]
    ppermute x21, waiting for transfers between devices: 38.3 us -> 41.8 us  [passed(): lax.ppermute(part, axis, [((i + shift) % parts, i) for i in range(parts)])]
  transfers between devices with their start and end apart: 26 -> 26, of which waited for: 18 -> 15; matrix products, arithmetic and copies ran while one was open for 4% -> 4% of each run, Pallas kernels for 36% -> 36%
where the time goes in v12:
time: 277 us; the launch traced here: 275 us
  Pallas kernels  121 us (44%)
  waiting for transfers between devices  88.2 us (32%)
  starting transfers between devices  42.1 us (15%)
  local copies, waits for them, and re-layouts  10.2 us (4%)
  other arithmetic  5.76 us (2%)
  matrix products  4.92 us (2%)
  between operations  2.93 us (1%)
    pallas_call x4, Pallas kernels, gather_sum(): pl.pallas_call(functools.partial(gather_sum_body, piece, last, row0), out...  50.3 us
    pallas_call x1, Pallas kernels, adjacency(): pl.pallas_call(functools.partial(adjacency_body, tiles), out_shape=jax.Sh...  47.8 us
    ppermute x21, waiting for transfers between devices, passed(): lax.ppermute(part, axis, [((i + shift) % parts, i) for i in range(parts)])  41.8 us
    all_to_all x1, waiting for transfers between devices, local(): lax.all_to_all(looked, 'batch', split_axis=0, concat_axis=0, tiled=True)  39.3 us
    ppermute x21, starting transfers between devices, passed(): lax.ppermute(part, axis, [((i + shift) % parts, i) for i in range(parts)])  26.1 us
    pallas_call x2, Pallas kernels, lookup(): pl.pallas_call(functools.partial(lookup_body, places.shape[0] // groups,...  21.3 us
    all_to_all x1, starting transfers between devices, local(): lax.all_to_all(requests.reshape(batch_count, capacity), 'batch', split_ax...  6.33 us
  transfers between devices with their start and end apart: 26, of which 15 were waited for; matrix products, arithmetic and copies ran while one was open for 4% of the time, Pallas kernels for 36%

profile of v12, /device:TPU:0, one launch (start us, length us, event | category | flops | bytes accessed | tf_op | source)
XLA Modules:
  0.0 275.4 jit_solution(6077802620336375269)
XLA Ops:
  4.0 6.3 %all-to-all-start = ((s32[8,1,1536]{2,1,0:T(1,128)}), s32[8,1,1536]{2,1,0:T(1,128)S(1)}, u32[]{:S(2)}, u32[]{:S(2)}) async-start(s32[8,1,1536]{2,1,0:T(1,128)} %bitcast.9), calls=%async_computation | async-start | bytes 98304 | tf_op jit(solution)/shard_map/all_to_all | solution.py:517
  11.3 4.9 %all-to-all-done = s32[8,1,1536]{2,1,0:T(1,128)S(1)} async-done(((s32[8,1,1536]{2,1,0:T(1,128)}), s32[8,1,1536]{2,1,0:T(1,128)S(1)}, u32[]{:S(2)}, u32[]{:S(2)}) %all-to-all-start) | async-done | bytes 49184 | tf_op jit(solution)/shard_map/all_to_all | solution.py:517
  16.8 11.5 %lookup.3 = bf16[8,768,256]{2,1,0:T(8,128)(2,1)} custom-call(s32[12288]{0:T(1024)} %bitcast.156, bf16[8192,256]{1,0:T(8,128)(2,1)} %store_in.3), custom_call_target="tpu_custom_call" | custom-call | flops 62914560 | bytes 4194304 | tf_op jit(solution)/shard_map/lookup/pallas_call | solution.py:151
  28.3 4.6 %all-to-all-start.1 = ((bf16[8,768,256]{2,1,0:T(8,128)(2,1)}), bf16[8,768,256]{2,1,0:T(8,128)(2,1)}, u32[]{:S(2)}, u32[]{:S(2)}) async-start(bf16[8,768,256]{2,1,0:T(8,128)(2,1)} %lookup.3), calls=%async_computation.1 | async-start | bytes 6291456 | tf_op jit(solution)/shard_map/all_to_all | solution.py:524
  33.0 2.5 collective-permute-start
  36.6 2.3 collective-permute-start.3
  43.2 4.8 %collective-permute-done.5 = bf16[128,256]{1,0:T(8,128)(2,1)S(1)} collective-permute-done((bf16[128,256]{1,0:T(8,128)(2,1)S(1)}, bf16[128,256]{1,0:T(8,128)(2,1)S(1)}, u32[]{:S(2)}, u32[]{:S(2)}) %collective-permute-start.5) | collective-permute-done | bytes 65568 | tf_op jit(solution)/shard_map/ppermute | solution.py:424
  49.2 2.2 copy-done.3
  51.4 9.8 %lookup.2 = bf16[8,768,256]{2,1,0:T(8,128)(2,1)} custom-call(s32[12288]{0:T(1024)S(1)} %bitcast.157, bf16[8192,256]{1,0:T(8,128)(2,1)S(1)} %copy-done.3), custom_call_target="tpu_custom_call" | custom-call | flops 62914560 | bytes 4194304 | tf_op jit(solution)/shard_map/lookup/pallas_call | solution.py:151
  61.2 47.8 %adjacency.1.adj_ref = f8e4m3fn[28,3072,256]{2,1,0:T(32,128)(4,1)} custom-call(s32[1]{0:T(128)} %bitcast.11.me_ref, s32[192,256]{1,0:T(8,128)S(1)} %reshape.243.near_ref, bf16[256,128]{1,0:T(8,128)(2,1)S(1)} %pad_maximum_fusion.4.table_ref), custom_call_target="tpu_custom_call" | custom-call | flops 22548578304 | bytes 22020096 | tf_op jit(solution)/shard_map/adjacency/pallas_call | solution.py:214
  109.1 5.0 %all-to-all-start.2 = ((bf16[8,768,256]{2,1,0:T(8,128)(2,1)}), bf16[8,768,256]{2,1,0:T(8,128)(2,1)}, u32[]{:S(2)}, u32[]{:S(2)}) async-start(bf16[8,768,256]{2,1,0:T(8,128)(2,1)} %lookup.2), calls=%async_computation.2 | async-start | bytes 6291456 | tf_op jit(solution)/shard_map/all_to_all | solution.py:570
  117.1 29.3 %gather_sum.4 = (f32[3072,256]{1,0:T(8,128)}, f32[3072,256]{1,0:T(8,128)}) custom-call(s32[2]{0:T(128)S(1)} %pad_add_fusion.4.spans_ref, s32[8]{0:T(128)S(1)} %get-tuple-element.80.counts_ref, s32[9]{0:T(128)S(1)} %get-tuple-element.82.starts_ref, s32[56]{0:T(128)S(1)} %reshape.248.own_here_ref, bf16[8,768,256]{2,1,0:T(8,128)(2,1)} %all-to-all-done.1.answer_ref, ...), custom_call_target="tpu_custom_call" | custom-call | flops 11274289152 | bytes 786432 | tf_op jit(solution)/shard_map/gather_sum/pallas_call | solution.py:393
  146.4 39.3 %all-to-all-done.2.answer_ref = bf16[8,768,256]{2,1,0:T(8,128)(2,1)} async-done(((bf16[8,768,256]{2,1,0:T(8,128)(2,1)}), bf16[8,768,256]{2,1,0:T(8,128)(2,1)}, u32[]{:S(2)}, u32[]{:S(2)}) %all-to-all-start.2) | async-done | bytes 3145760 | tf_op jit(solution)/shard_map/all_to_all | solution.py:570
  185.7 8.4 %gather_sum.5 = (bf16[1536,256]{1,0:T(8,128)(2,1)S(1)}, bf16[1536,256]{1,0:T(8,128)(2,1)S(1)}, bf16[768,256]{1,0:T(8,128)(2,1)S(1)}, bf16[768,256]{1,0:T(8,128)(2,1)S(1)}) custom-call(s32[2]{0:T(128)S(1)} %pad_add_fusion.5.spans_ref, s32[8]{0:T(128)S(1)} %get-tuple-element.79.counts_ref, s32[9]{0:T(128)S(1)} %get-tuple-element.81.starts_ref, ...), custom_call_target="tpu_custom_call" | custom-call | flops 1409286144 | bytes 393216 | tf_op jit(solution)/shard_map/gather_sum/pallas_call | solution.py:393
  194.8 6.3 %gather_sum.6 = (bf16[768,256]{1,0:T(8,128)(2,1)S(1)}, bf16[768,256]{1,0:T(8,128)(2,1)S(1)}, bf16[768,256]{1,0:T(8,128)(2,1)S(1)}) custom-call(s32[2]{0:T(128)S(1)} %pad_add_fusion.5.spans_ref, s32[8]{0:T(128)S(1)} %get-tuple-element.79.counts_ref, s32[9]{0:T(128)S(1)} %get-tuple-element.81.starts_ref, s32[56]{0:T(128)S(1)} %reshape.248.own_here_ref, ...), custom_call_target="tpu_custom_call" | custom-call | flops 704643072 | bytes 196608 | tf_op jit(solution)/shard_map/gather_sum/pallas_call | solution.py:393
  205.4 6.3 %gather_sum.7 = (bf16[768,256]{1,0:T(8,128)(2,1)S(1)}, bf16[768,256]{1,0:T(8,128)(2,1)S(1)}, bf16[768,256]{1,0:T(8,128)(2,1)S(1)}) custom-call(s32[2]{0:T(128)S(1)} %pad_add_fusion.5.spans_ref, s32[8]{0:T(128)S(1)} %get-tuple-element.79.counts_ref, s32[9]{0:T(128)S(1)} %get-tuple-element.81.starts_ref, s32[56]{0:T(128)S(1)} %reshape.248.own_here_ref, ...), custom_call_target="tpu_custom_call" | custom-call | flops 704643072 | bytes 196608 | tf_op jit(solution)/shard_map/gather_sum/pallas_call | solution.py:393
  214.7 2.6 collective-permute-start.9
  217.3 7.2 %collective-permute-done.11 = bf16[640,256]{1,0:T(8,128)(2,1)S(1)} collective-permute-done((bf16[640,256]{1,0:T(8,128)(2,1)S(1)}, bf16[640,256]{1,0:T(8,128)(2,1)S(1)}, u32[]{:S(2)}, u32[]{:S(2)}) %collective-permute-start.11) | collective-permute-done | bytes 327712 | tf_op jit(solution)/shard_map/ppermute | solution.py:424
  224.5 4.5 %collective-permute-done.10 = bf16[640,256]{1,0:T(8,128)(2,1)S(1)} collective-permute-done((bf16[640,256]{1,0:T(8,128)(2,1)S(1)}, bf16[640,256]{1,0:T(8,128)(2,1)S(1)}, u32[]{:S(2)}, u32[]{:S(2)}) %collective-permute-start.10) | collective-permute-done | bytes 327712 | tf_op jit(solution)/shard_map/ppermute | solution.py:424
  235.9 14.7 %collective-permute-done.12 = bf16[768,256]{1,0:T(8,128)(2,1)S(1)} collective-permute-done((bf16[768,256]{1,0:T(8,128)(2,1)S(1)}, bf16[768,256]{1,0:T(8,128)(2,1)S(1)}, u32[]{:S(2)}, u32[]{:S(2)}) %collective-permute-start.12) | collective-permute-done | bytes 393248 | tf_op jit(solution)/shard_map/ppermute | solution.py:424
  254.4 2.7 collective-permute-start.18
  259.7 4.3 %collective-permute-done.17 = bf16[128,256]{1,0:T(8,128)(2,1)S(1)} collective-permute-done((bf16[128,256]{1,0:T(8,128)(2,1)S(1)}, bf16[128,256]{1,0:T(8,128)(2,1)S(1)}, u32[]{:S(2)}, u32[]{:S(2)}) %collective-permute-start.17) | collective-permute-done | bytes 65568 | tf_op jit(solution)/shard_map/ppermute | solution.py:424
  264.2 2.2 collective-permute-start.20
  266.5 2.3 collective-permute-start.19
  (167 shorter events, 40.7 us)
Async XLA Ops:
  4.0 12.2 %all-to-all-start = ((s32[8,1,1536]{2,1,0:T(1,128)}), s32[8,1,1536]{2,1,0:T(1,128)S(1)}, u32[]{:S(2)}, u32[]{:S(2)}) async-start(s32[8,1,1536]{2,1,0:T(1,128)} %bitcast.9), calls=%async_computation | async-start | bytes 98304 | tf_op jit(solution)/shard_map/all_to_all | solution.py:517
  28.3 80.7 %all-to-all-start.1 = ((bf16[8,768,256]{2,1,0:T(8,128)(2,1)}), bf16[8,768,256]{2,1,0:T(8,128)(2,1)}, u32[]{:S(2)}, u32[]{:S(2)}) async-start(bf16[8,768,256]{2,1,0:T(8,128)(2,1)} %lookup.3), calls=%async_computation.1 | async-start | bytes 6291456 | tf_op jit(solution)/shard_map/all_to_all | solution.py:524
  33.0 9.8 %collective-permute-start = (s32[11,128]{1,0:T(8,128)S(1)}, s32[11,128]{1,0:T(8,128)S(1)}, u32[]{:S(2)}, u32[]{:S(2)}) collective-permute-start(s32[11,128]{1,0:T(8,128)S(1)} %pad_add_fusion.1), channel_id=1, source_target_pairs={{8,0},{16,8},{24,16},{0,24},{9,1},{17,9},{25,17},{1,25},{10,2},{18... | collective-permute-start | bytes 16904 | tf_op jit(solution)/shard_map/ppermute | solution.py:424
  35.5 7.3 %collective-permute-start.1 = (s32[11,128]{1,0:T(8,128)S(1)}, s32[11,128]{1,0:T(8,128)S(1)}, u32[]{:S(2)}, u32[]{:S(2)}) collective-permute-start(s32[11,128]{1,0:T(8,128)S(1)} %pad_add_fusion.1), channel_id=1, source_target_pairs={{16,0},{24,8},{0,16},{8,24},{17,1},{25,9},{1,17},{9,25},{18,2},{26... | collective-permute-start | bytes 16904 | tf_op jit(solution)/shard_map/ppermute | solution.py:424
  36.0 6.9 %collective-permute-start.2 = (s32[11,128]{1,0:T(8,128)S(1)}, s32[11,128]{1,0:T(8,128)S(1)}, u32[]{:S(2)}, u32[]{:S(2)}) collective-permute-start(s32[11,128]{1,0:T(8,128)S(1)} %pad_add_fusion.1), channel_id=1, source_target_pairs={{24,0},{0,8},{8,16},{16,24},{25,1},{1,9},{9,17},{17,25},{26,2},{2,... | collective-permute-start | bytes 16904 | tf_op jit(solution)/shard_map/ppermute | solution.py:424
  36.6 6.4 %collective-permute-start.3 = (bf16[128,256]{1,0:T(8,128)(2,1)S(1)}, bf16[128,256]{1,0:T(8,128)(2,1)S(1)}, u32[]{:S(2)}, u32[]{:S(2)}) collective-permute-start(bf16[128,256]{1,0:T(8,128)(2,1)S(1)} %bitcast.186), channel_id=1, source_target_pairs={{8,0},{16,8},{24,16},{0,24},{9,1},{17,9},{25,17},{1,25},{10,2},{18... | collective-permute-start | bytes 196616 | tf_op jit(solution)/shard_map/ppermute | solution.py:424
  38.9 4.3 %collective-permute-start.4 = (bf16[128,256]{1,0:T(8,128)(2,1)S(1)}, bf16[128,256]{1,0:T(8,128)(2,1)S(1)}, u32[]{:S(2)}, u32[]{:S(2)}) collective-permute-start(bf16[128,256]{1,0:T(8,128)(2,1)S(1)} %bitcast.187), channel_id=1, source_target_pairs={{16,0},{24,8},{0,16},{8,24},{17,1},{25,9},{1,17},{9,25},{18,2},{26... | collective-permute-start | bytes 196616 | tf_op jit(solution)/shard_map/ppermute | solution.py:424
  42.7 5.2 %collective-permute-start.5 = (bf16[128,256]{1,0:T(8,128)(2,1)S(1)}, bf16[128,256]{1,0:T(8,128)(2,1)S(1)}, u32[]{:S(2)}, u32[]{:S(2)}) collective-permute-start(bf16[128,256]{1,0:T(8,128)(2,1)S(1)} %bitcast.188), channel_id=1, source_target_pairs={{24,0},{0,8},{8,16},{16,24},{25,1},{1,9},{9,17},{17,25},{26,2},{2,... | collective-permute-start | bytes 196616 | tf_op jit(solution)/shard_map/ppermute | solution.py:424
  109.1 76.6 %all-to-all-start.2 = ((bf16[8,768,256]{2,1,0:T(8,128)(2,1)}), bf16[8,768,256]{2,1,0:T(8,128)(2,1)}, u32[]{:S(2)}, u32[]{:S(2)}) async-start(bf16[8,768,256]{2,1,0:T(8,128)(2,1)} %lookup.2), calls=%async_computation.2 | async-start | bytes 6291456 | tf_op jit(solution)/shard_map/all_to_all | solution.py:570
  194.1 17.7 %collective-permute-start.8 = (bf16[768,256]{1,0:T(8,128)(2,1)S(1)}, bf16[768,256]{1,0:T(8,128)(2,1)S(1)}, u32[]{:S(2)}, u32[]{:S(2)}) collective-permute-start(bf16[768,256]{1,0:T(8,128)(2,1)S(1)} %get-tuple-element.54), channel_id=1, source_target_pairs={{8,0},{16,8},{24,16},{0,24},{9,1},{17,9},{25,17},{1,25},{10,2},{18... | collective-permute-start | bytes 1179656 | tf_op jit(solution)/shard_map/ppermute | solution.py:424
  194.1 18.0 %collective-permute-start.7 = (bf16[768,256]{1,0:T(8,128)(2,1)S(1)}, bf16[768,256]{1,0:T(8,128)(2,1)S(1)}, u32[]{:S(2)}, u32[]{:S(2)}) collective-permute-start(bf16[768,256]{1,0:T(8,128)(2,1)S(1)} %get-tuple-element.53), channel_id=1, source_target_pairs={{16,0},{24,8},{0,16},{8,24},{17,1},{25,9},{1,17},{9,25},{18,2},{26... | collective-permute-start | bytes 1179656 | tf_op jit(solution)/shard_map/ppermute | solution.py:424
  201.0 11.1 %collective-permute-start.6 = (bf16[768,256]{1,0:T(8,128)(2,1)S(1)}, bf16[768,256]{1,0:T(8,128)(2,1)S(1)}, u32[]{:S(2)}, u32[]{:S(2)}) collective-permute-start(bf16[768,256]{1,0:T(8,128)(2,1)S(1)} %get-tuple-element.52), channel_id=1, source_target_pairs={{24,0},{0,8},{8,16},{16,24},{25,1},{1,9},{9,17},{17,25},{26,2},{2,... | collective-permute-start | bytes 1179656 | tf_op jit(solution)/shard_map/ppermute | solution.py:424
  212.9 11.6 %collective-permute-start.11 = (bf16[640,256]{1,0:T(8,128)(2,1)S(1)}, bf16[640,256]{1,0:T(8,128)(2,1)S(1)}, u32[]{:S(2)}, u32[]{:S(2)}) collective-permute-start(bf16[640,256]{1,0:T(8,128)(2,1)S(1)} %pad_maximum_fusion.2), channel_id=1, source_target_pairs={{24,0},{0,8},{8,16},{16,24},{25,1},{1,9},{9,17},{17,25},{26,2},{2,... | collective-permute-start | bytes 983048 | tf_op jit(solution)/shard_map/ppermute | solution.py:424
  213.7 15.4 %collective-permute-start.10 = (bf16[640,256]{1,0:T(8,128)(2,1)S(1)}, bf16[640,256]{1,0:T(8,128)(2,1)S(1)}, u32[]{:S(2)}, u32[]{:S(2)}) collective-permute-start(bf16[640,256]{1,0:T(8,128)(2,1)S(1)} %pad_maximum_fusion.2), channel_id=1, source_target_pairs={{16,0},{24,8},{0,16},{8,24},{17,1},{25,9},{1,17},{9,25},{18,2},{26... | collective-permute-start | bytes 983048 | tf_op jit(solution)/shard_map/ppermute | solution.py:424
  214.7 14.4 %collective-permute-start.9 = (bf16[640,256]{1,0:T(8,128)(2,1)S(1)}, bf16[640,256]{1,0:T(8,128)(2,1)S(1)}, u32[]{:S(2)}, u32[]{:S(2)}) collective-permute-start(bf16[640,256]{1,0:T(8,128)(2,1)S(1)} %pad_maximum_fusion.2), channel_id=1, source_target_pairs={{8,0},{16,8},{24,16},{0,24},{9,1},{17,9},{25,17},{1,25},{10,2},{18... | collective-permute-start | bytes 983048 | tf_op jit(solution)/shard_map/ppermute | solution.py:424
  231.5 19.2 %collective-permute-start.14 = (bf16[768,256]{1,0:T(8,128)(2,1)S(1)}, bf16[768,256]{1,0:T(8,128)(2,1)S(1)}, u32[]{:S(2)}, u32[]{:S(2)}) collective-permute-start(bf16[768,256]{1,0:T(8,128)(2,1)S(1)} %fusion.2), channel_id=1, source_target_pairs={{8,0},{16,8},{24,16},{0,24},{9,1},{17,9},{25,17},{1,25},{10,2},{18... | collective-permute-start | bytes 1179656 | tf_op jit(solution)/shard_map/ppermute | solution.py:424
  233.4 17.3 %collective-permute-start.12 = (bf16[768,256]{1,0:T(8,128)(2,1)S(1)}, bf16[768,256]{1,0:T(8,128)(2,1)S(1)}, u32[]{:S(2)}, u32[]{:S(2)}) collective-permute-start(bf16[768,256]{1,0:T(8,128)(2,1)S(1)} %fusion.2), channel_id=1, source_target_pairs={{16,0},{24,8},{0,16},{8,24},{17,1},{25,9},{1,17},{9,25},{18,2},{26... | collective-permute-start | bytes 1179656 | tf_op jit(solution)/shard_map/ppermute | solution.py:424
  234.7 16.6 %collective-permute-start.13 = (bf16[768,256]{1,0:T(8,128)(2,1)S(1)}, bf16[768,256]{1,0:T(8,128)(2,1)S(1)}, u32[]{:S(2)}, u32[]{:S(2)}) collective-permute-start(bf16[768,256]{1,0:T(8,128)(2,1)S(1)} %fusion.2), channel_id=1, source_target_pairs={{24,0},{0,8},{8,16},{16,24},{25,1},{1,9},{9,17},{17,25},{26,2},{2,... | collective-permute-start | bytes 1179656 | tf_op jit(solution)/shard_map/ppermute | solution.py:424
  254.4 5.2 %collective-permute-start.18 = (bf16[128,256]{1,0:T(8,128)(2,1)S(1)}, bf16[128,256]{1,0:T(8,128)(2,1)S(1)}, u32[]{:S(2)}, u32[]{:S(2)}) collective-permute-start(bf16[128,256]{1,0:T(8,128)(2,1)S(1)} %get-tuple-element.72), channel_id=1, source_target_pairs={{2,0},{3,1},{4,2},{5,3},{6,4},{7,5},{0,6},{1,7},{10,8},{11,9},{12,... | collective-permute-start | bytes 196616 | tf_op jit(solution)/shard_map/ppermute | solution.py:424
  257.2 6.8 %collective-permute-start.17 = (bf16[128,256]{1,0:T(8,128)(2,1)S(1)}, bf16[128,256]{1,0:T(8,128)(2,1)S(1)}, u32[]{:S(2)}, u32[]{:S(2)}) collective-permute-start(bf16[128,256]{1,0:T(8,128)(2,1)S(1)} %get-tuple-element.73), channel_id=1, source_target_pairs={{4,0},{5,1},{6,2},{7,3},{0,4},{1,5},{2,6},{3,7},{12,8},{13,9},{14,... | collective-permute-start | bytes 196616 | tf_op jit(solution)/shard_map/ppermute | solution.py:424
  257.2 6.8 %collective-permute-start.16 = (bf16[128,256]{1,0:T(8,128)(2,1)S(1)}, bf16[128,256]{1,0:T(8,128)(2,1)S(1)}, u32[]{:S(2)}, u32[]{:S(2)}) collective-permute-start(bf16[128,256]{1,0:T(8,128)(2,1)S(1)} %get-tuple-element.71), channel_id=1, source_target_pairs={{6,0},{7,1},{0,2},{1,3},{2,4},{3,5},{4,6},{5,7},{14,8},{15,9},{8,1... | collective-permute-start | bytes 196616 | tf_op jit(solution)/shard_map/ppermute | solution.py:424
  264.0 6.8 %collective-permute-start.21 = (bf16[128,256]{1,0:T(8,128)(2,1)S(1)}, bf16[128,256]{1,0:T(8,128)(2,1)S(1)}, u32[]{:S(2)}, u32[]{:S(2)}) collective-permute-start(bf16[128,256]{1,0:T(8,128)(2,1)S(1)} %fusion.16), channel_id=1, source_target_pairs={{6,0},{7,1},{0,2},{1,3},{2,4},{3,5},{4,6},{5,7},{14,8},{15,9},{8,1... | collective-permute-start | bytes 196616 | tf_op jit(solution)/shard_map/ppermute | solution.py:424
  264.2 8.1 %collective-permute-start.20 = (bf16[128,256]{1,0:T(8,128)(2,1)S(1)}, bf16[128,256]{1,0:T(8,128)(2,1)S(1)}, u32[]{:S(2)}, u32[]{:S(2)}) collective-permute-start(bf16[128,256]{1,0:T(8,128)(2,1)S(1)} %fusion.16), channel_id=1, source_target_pairs={{4,0},{5,1},{6,2},{7,3},{0,4},{1,5},{2,6},{3,7},{12,8},{13,9},{14,... | collective-permute-start | bytes 196616 | tf_op jit(solution)/shard_map/ppermute | solution.py:424
  266.5 5.9 %collective-permute-start.19 = (bf16[128,256]{1,0:T(8,128)(2,1)S(1)}, bf16[128,256]{1,0:T(8,128)(2,1)S(1)}, u32[]{:S(2)}, u32[]{:S(2)}) collective-permute-start(bf16[128,256]{1,0:T(8,128)(2,1)S(1)} %fusion.16), channel_id=1, source_target_pairs={{2,0},{3,1},{4,2},{5,3},{6,4},{7,5},{0,6},{1,7},{10,8},{11,9},{12,... | collective-permute-start | bytes 196616 | tf_op jit(solution)/shard_map/ppermute | solution.py:424
  (20 other events, 522.6 us)

commit v13 on v12

--- a/solution.py
+++ b/solution.py
@@ -553,21 +553,25 @@
     met = met.astype(jnp.int32) == jnp.arange(steps)[:, None, None]
     own_here = jnp.any(met, axis=2).astype(jnp.int32).reshape(-1)
 
-    fanout_two = nbr_two.shape[2]
-    used_two = jnp.arange(fanout_two)[:, None] < deg_two
-    lists = jnp.concatenate([jnp.where(used_two, nbr_two[0].T, -1), deg_two], axis=0)
-    lists = in_order(spread_parts(lists))
-    upstream = in_order(spread_parts(cotangent[0])).reshape(seeds, hidden_width)
-
     fanout = nbr_one.shape[2]
     used = jnp.arange(fanout)[None, :] < deg_one[0][:, None]
     near = jnp.pad(jnp.where(used, near_first, -1), ((0, 0), (0, SLOTS - fanout)), constant_values=-1)
-    near, lists, upstream = lax.optimization_barrier((near, lists, upstream))
     me = feat_index.astype(jnp.int32).reshape(1)
     near = near.reshape(nodes // SLOTS, TILE)
     adj = adjacency(me, near, finder, steps * WIDE, parts, seeds)
     looked, answer_a, adj = lax.optimization_barrier((looked, answer_a, adj))
     answer_b = lax.all_to_all(looked, "batch", split_axis=0, concat_axis=0, tiled=True)
+
+    scalars = (spans_a, tally_a, starts_a, own_here)
+    total, found = gather_sum(input_count, scalars, answer_a, notes, adj)
+    second = (nbr_two[0], deg_two, cotangent[0])
+    total, second = lax.optimization_barrier((total, second))
+
+    fanout_two = nbr_two.shape[2]
+    used_two = jnp.arange(fanout_two)[:, None] < second[1]
+    lists = jnp.concatenate([jnp.where(used_two, second[0].T, -1), second[1]], axis=0)
+    lists = in_order(spread_parts(lists))
+    upstream = in_order(spread_parts(second[2])).reshape(seeds, hidden_width)
 
     near_two = lists[:, :fanout_two].transpose(1, 0, 2).reshape(fanout_two, seeds)
     deg_all = lists[:, fanout_two].reshape(seeds)
@@ -582,9 +586,7 @@
     adj_two = jnp.sum(
         place[:, :, None] == jnp.arange(share)[None, None, :], axis=0, dtype=jnp.float32
     ).astype(jnp.bfloat16)
-
-    scalars = (spans_a, tally_a, starts_a, own_here)
-    total, found = gather_sum(input_count, scalars, answer_a, notes, adj)
+    total, adj_two, upstream = lax.optimization_barrier((total, adj_two, upstream))
 
     def finish(begin, end):
         return gather_sum(

time: 277 us -> 277 us (level)
  waiting for transfers between devices: 88.2 us -> 74.5 us
  local copies, waits for them, and re-layouts: 10.2 us -> 17.5 us
  other arithmetic: 5.76 us -> 10.4 us
    all_to_all x1, waiting for transfers between devices: 39.3 us -> 24.2 us  [local(): lax.all_to_all(looked, 'batch', split_axis=0, concat_axis=0, tiled=True)]
    unnamed x40 -> x62, local copies, waits for them, and re-layouts: 5.4 us -> 9.19 us
    all_to_all x1, waiting for transfers between devices: 0.01 us -> 3.24 us  [local(): lax.all_to_all(looked_a, 'batch', split_axis=0, concat_axis=0, tiled=True)]
  transfers between devices with their start and end apart: 26 -> 26, of which waited for: 15 -> 15; matrix products, arithmetic and copies ran while one was open for 4% -> 7% of each run, Pallas kernels for 36% -> 36%
where the time goes in v13:
time: 277 us
  Pallas kernels  122 us (44%)
  waiting for transfers between devices  74.5 us (27%)
  starting transfers between devices  43 us (16%)
  local copies, waits for them, and re-layouts  17.5 us (6%)
  other arithmetic  10.4 us (4%)
  matrix products  6.17 us (2%)
  between operations  3.03 us (1%)
    pallas_call x4, Pallas kernels, gather_sum(): pl.pallas_call(functools.partial(gather_sum_body, piece, last, row0), out...  51.2 us
    pallas_call x1, Pallas kernels, adjacency(): pl.pallas_call(functools.partial(adjacency_body, tiles), out_shape=jax.Sh...  47.9 us
    ppermute x21, waiting for transfers between devices, passed(): lax.ppermute(part, axis, [((i + shift) % parts, i) for i in range(parts)])  40.7 us
    ppermute x21, starting transfers between devices, passed(): lax.ppermute(part, axis, [((i + shift) % parts, i) for i in range(parts)])  27.6 us
    all_to_all x1, waiting for transfers between devices, local(): lax.all_to_all(looked, 'batch', split_axis=0, concat_axis=0, tiled=True)  24.2 us
    pallas_call x2, Pallas kernels, lookup(): pl.pallas_call(functools.partial(lookup_body, places.shape[0] // groups,...  21.3 us
    unnamed x62, local copies, waits for them, and re-layouts  9.19 us
    all_to_all x1, starting transfers between devices, local(): lax.all_to_all(requests.reshape(batch_count, capacity), 'batch', split_ax...  6.33 us
  transfers between devices with their start and end apart: 26, of which 15 were waited for; matrix products, arithmetic and copies ran while one was open for 7% of the time, Pallas kernels for 36%

profile of v13, /device:TPU:0, one launch (start us, length us, event | category | flops | bytes accessed | tf_op | source)
XLA Modules:
  0.0 276.8 jit_solution(1628710183891275991)
XLA Ops:
  4.0 6.3 %all-to-all-start = ((s32[8,1,1536]{2,1,0:T(1,128)}), s32[8,1,1536]{2,1,0:T(1,128)S(1)}, u32[]{:S(2)}, u32[]{:S(2)}) async-start(s32[8,1,1536]{2,1,0:T(1,128)} %bitcast.9), calls=%async_computation | async-start | bytes 98304 | tf_op jit(solution)/shard_map/all_to_all | solution.py:517
  11.3 4.9 %all-to-all-done = s32[8,1,1536]{2,1,0:T(1,128)S(1)} async-done(((s32[8,1,1536]{2,1,0:T(1,128)}), s32[8,1,1536]{2,1,0:T(1,128)S(1)}, u32[]{:S(2)}, u32[]{:S(2)}) %all-to-all-start) | async-done | bytes 49184 | tf_op jit(solution)/shard_map/all_to_all | solution.py:517
  16.8 11.5 %lookup.3 = bf16[8,768,256]{2,1,0:T(8,128)(2,1)} custom-call(s32[12288]{0:T(1024)} %bitcast.159, bf16[8192,256]{1,0:T(8,128)(2,1)} %store_in.3), custom_call_target="tpu_custom_call" | custom-call | flops 62914560 | bytes 4194304 | tf_op jit(solution)/shard_map/lookup/pallas_call | solution.py:151
  28.3 4.5 %all-to-all-start.1 = ((bf16[8,768,256]{2,1,0:T(8,128)(2,1)}), bf16[8,768,256]{2,1,0:T(8,128)(2,1)}, u32[]{:S(2)}, u32[]{:S(2)}) async-start(bf16[8,768,256]{2,1,0:T(8,128)(2,1)} %lookup.3), calls=%async_computation.1 | async-start | bytes 6291456 | tf_op jit(solution)/shard_map/all_to_all | solution.py:524
  36.6 2.7 pad.12.clone
  43.4 9.8 %lookup.2 = bf16[8,768,256]{2,1,0:T(8,128)(2,1)} custom-call(s32[12288]{0:T(1024)S(1)} %bitcast.160, bf16[8192,256]{1,0:T(8,128)(2,1)S(1)} %copy-done.3), custom_call_target="tpu_custom_call" | custom-call | flops 62914560 | bytes 4194304 | tf_op jit(solution)/shard_map/lookup/pallas_call | solution.py:151
  53.2 47.9 %adjacency.1.adj_ref = f8e4m3fn[28,3072,256]{2,1,0:T(32,128)(4,1)} custom-call(s32[1]{0:T(128)} %bitcast.11.me_ref, s32[192,256]{1,0:T(8,128)S(1)} %reshape.242.near_ref, bf16[256,128]{1,0:T(8,128)(2,1)S(1)} %pad_maximum_fusion.4.table_ref), custom_call_target="tpu_custom_call" | custom-call | flops 22548578304 | bytes 22020096 | tf_op jit(solution)/shard_map/adjacency/pallas_call | solution.py:214
  101.1 3.2 %all-to-all-done.1.answer_ref = bf16[8,768,256]{2,1,0:T(8,128)(2,1)} async-done(((bf16[8,768,256]{2,1,0:T(8,128)(2,1)}), bf16[8,768,256]{2,1,0:T(8,128)(2,1)}, u32[]{:S(2)}, u32[]{:S(2)}) %all-to-all-start.1) | async-done | bytes 3145760 | tf_op jit(solution)/shard_map/all_to_all | solution.py:524
  104.3 4.4 %all-to-all-start.2 = ((bf16[8,768,256]{2,1,0:T(8,128)(2,1)}), bf16[8,768,256]{2,1,0:T(8,128)(2,1)}, u32[]{:S(2)}, u32[]{:S(2)}) async-start(bf16[8,768,256]{2,1,0:T(8,128)(2,1)} %lookup.2), calls=%async_computation.2 | async-start | bytes 6291456 | tf_op jit(solution)/shard_map/all_to_all | solution.py:563
  111.9 31.3 %gather_sum.4 = (f32[3072,256]{1,0:T(8,128)}, f32[3072,256]{1,0:T(8,128)}) custom-call(s32[2]{0:T(128)S(1)} %pad_add_fusion.4.spans_ref, s32[8]{0:T(128)S(1)} %get-tuple-element.88.counts_ref, s32[9]{0:T(128)S(1)} %get-tuple-element.90.starts_ref, s32[56]{0:T(128)S(1)} %reshape.248.own_here_ref, bf16[8,768,256]{2,1,0:T(8,128)(2,1)} %all-to-all-done.1.answer_ref, ...), custom_call_target="tpu_custom_call" | custom-call | flops 11274289152 | bytes 786432 | tf_op jit(solution)/shard_map/gather_sum/pallas_call | solution.py:393
  151.8 3.1 %convert_reduce_fusion = bf16[512,768]{1,0:T(8,128)(2,1)} fusion(s32[10,512]{1,0:T(8,128)S(1)} %fusion.35), kind=kLoop, calls=%fused_computation | loop fusion | flops 15335424 | bytes 806912 | tf_op jit(solution)/shard_map/reduce_sum | solution.py:586
  156.1 24.2 %all-to-all-done.2.answer_ref = bf16[8,768,256]{2,1,0:T(8,128)(2,1)} async-done(((bf16[8,768,256]{2,1,0:T(8,128)(2,1)}), bf16[8,768,256]{2,1,0:T(8,128)(2,1)}, u32[]{:S(2)}, u32[]{:S(2)}) %all-to-all-start.2) | async-done | bytes 3145760 | tf_op jit(solution)/shard_map/all_to_all | solution.py:563
  180.3 8.4 %gather_sum.5 = (bf16[1536,256]{1,0:T(8,128)(2,1)S(1)}, bf16[1536,256]{1,0:T(8,128)(2,1)S(1)}, bf16[768,256]{1,0:T(8,128)(2,1)}, bf16[768,256]{1,0:T(8,128)(2,1)}) custom-call(s32[2]{0:T(128)S(1)} %pad_add_fusion.5.spans_ref, s32[8]{0:T(128)S(1)} %get-tuple-element.87.counts_ref, s32[9]{0:T(128)S(1)} %get-tuple-element.89.starts_ref, ...), custom_call_target="tpu_custom_call" | custom-call | flops 1409286144 | bytes 393216 | tf_op jit(solution)/shard_map/gather_sum/pallas_call | solution.py:393
  191.7 6.3 %gather_sum.6 = (bf16[768,256]{1,0:T(8,128)(2,1)S(1)}, bf16[768,256]{1,0:T(8,128)(2,1)S(1)}, bf16[768,256]{1,0:T(8,128)(2,1)}) custom-call(s32[2]{0:T(128)S(1)} %pad_add_fusion.5.spans_ref, s32[8]{0:T(128)S(1)} %get-tuple-element.87.counts_ref, s32[9]{0:T(128)S(1)} %get-tuple-element.89.starts_ref, s32[56]{0:T(128)S(1)} %reshape.248.own_here_ref, ...), custom_call_target="tpu_custom_call" | custom-call | flops 704643072 | bytes 196608 | tf_op jit(solution)/shard_map/gather_sum/pallas_call | solution.py:393
  199.9 5.3 %gather_sum.7 = (bf16[768,256]{1,0:T(8,128)(2,1)S(1)}, bf16[768,256]{1,0:T(8,128)(2,1)S(1)}, bf16[768,256]{1,0:T(8,128)(2,1)S(1)}) custom-call(s32[2]{0:T(128)S(1)} %pad_add_fusion.5.spans_ref, s32[8]{0:T(128)S(1)} %get-tuple-element.87.counts_ref, s32[9]{0:T(128)S(1)} %get-tuple-element.89.starts_ref, s32[56]{0:T(128)S(1)} %reshape.248.own_here_ref, ...), custom_call_target="tpu_custom_call" | custom-call | flops 704643072 | bytes 196608 | tf_op jit(solution)/shard_map/gather_sum/pallas_call | solution.py:393
  205.3 5.5 %collective-permute-done.6 = bf16[768,256]{1,0:T(8,128)(2,1)} collective-permute-done((bf16[768,256]{1,0:T(8,128)(2,1)}, bf16[768,256]{1,0:T(8,128)(2,1)}, u32[]{:S(2)}, u32[]{:S(2)}) %collective-permute-start.6) | collective-permute-done | bytes 393248 | tf_op jit(solution)/shard_map/ppermute | solution.py:424
  214.5 2.8 %collective-permute-start.9 = (bf16[640,256]{1,0:T(8,128)(2,1)S(1)}, bf16[640,256]{1,0:T(8,128)(2,1)S(1)}, u32[]{:S(2)}, u32[]{:S(2)}) collective-permute-start(bf16[640,256]{1,0:T(8,128)(2,1)S(1)} %pad_maximum_fusion.2), channel_id=1, source_target_pairs={{8,0},{16,8},{24,16},{0,24},{9,1},{17,9},{25,17},{1,25},{10,2},{18... | collective-permute-start | bytes 983048 | tf_op jit(solution)/shard_map/ppermute | solution.py:424
  218.1 6.3 %collective-permute-done.11 = bf16[640,256]{1,0:T(8,128)(2,1)S(1)} collective-permute-done((bf16[640,256]{1,0:T(8,128)(2,1)S(1)}, bf16[640,256]{1,0:T(8,128)(2,1)S(1)}, u32[]{:S(2)}, u32[]{:S(2)}) %collective-permute-start.11) | collective-permute-done | bytes 327712 | tf_op jit(solution)/shard_map/ppermute | solution.py:424
  224.4 3.3 %collective-permute-done.10 = bf16[640,256]{1,0:T(8,128)(2,1)S(1)} collective-permute-done((bf16[640,256]{1,0:T(8,128)(2,1)S(1)}, bf16[640,256]{1,0:T(8,128)(2,1)S(1)}, u32[]{:S(2)}, u32[]{:S(2)}) %collective-permute-start.10) | collective-permute-done | bytes 327712 | tf_op jit(solution)/shard_map/ppermute | solution.py:424
  236.9 12.6 %collective-permute-done.12 = bf16[768,256]{1,0:T(8,128)(2,1)S(1)} collective-permute-done((bf16[768,256]{1,0:T(8,128)(2,1)S(1)}, bf16[768,256]{1,0:T(8,128)(2,1)S(1)}, u32[]{:S(2)}, u32[]{:S(2)}) %collective-permute-start.12) | collective-permute-done | bytes 393248 | tf_op jit(solution)/shard_map/ppermute | solution.py:424
  255.2 2.5 collective-permute-start.18
  257.7 2.5 collective-permute-start.17
  261.2 5.4 %collective-permute-done.17 = bf16[128,256]{1,0:T(8,128)(2,1)S(1)} collective-permute-done((bf16[128,256]{1,0:T(8,128)(2,1)S(1)}, bf16[128,256]{1,0:T(8,128)(2,1)S(1)}, u32[]{:S(2)}, u32[]{:S(2)}) %collective-permute-start.17) | collective-permute-done | bytes 65568 | tf_op jit(solution)/shard_map/ppermute | solution.py:424
  267.1 3.4 %collective-permute-start.19 = (bf16[128,256]{1,0:T(8,128)(2,1)S(1)}, bf16[128,256]{1,0:T(8,128)(2,1)S(1)}, u32[]{:S(2)}, u32[]{:S(2)}) collective-permute-start(bf16[128,256]{1,0:T(8,128)(2,1)S(1)} %fusion.16), channel_id=1, source_target_pairs={{2,0},{3,1},{4,2},{5,3},{6,4},{7,5},{0,6},{1,7},{10,8},{11,9},{12,... | collective-permute-start | bytes 196616 | tf_op jit(solution)/shard_map/ppermute | solution.py:424
  (188 shorter events, 55.8 us)
Async XLA Ops:
  4.0 12.2 %all-to-all-start = ((s32[8,1,1536]{2,1,0:T(1,128)}), s32[8,1,1536]{2,1,0:T(1,128)S(1)}, u32[]{:S(2)}, u32[]{:S(2)}) async-start(s32[8,1,1536]{2,1,0:T(1,128)} %bitcast.9), calls=%async_computation | async-start | bytes 98304 | tf_op jit(solution)/shard_map/all_to_all | solution.py:517
  28.3 76.0 %all-to-all-start.1 = ((bf16[8,768,256]{2,1,0:T(8,128)(2,1)}), bf16[8,768,256]{2,1,0:T(8,128)(2,1)}, u32[]{:S(2)}, u32[]{:S(2)}) async-start(bf16[8,768,256]{2,1,0:T(8,128)(2,1)} %lookup.3), calls=%async_computation.1 | async-start | bytes 6291456 | tf_op jit(solution)/shard_map/all_to_all | solution.py:524
  104.3 76.0 %all-to-all-start.2 = ((bf16[8,768,256]{2,1,0:T(8,128)(2,1)}), bf16[8,768,256]{2,1,0:T(8,128)(2,1)}, u32[]{:S(2)}, u32[]{:S(2)}) async-start(bf16[8,768,256]{2,1,0:T(8,128)(2,1)} %lookup.2), calls=%async_computation.2 | async-start | bytes 6291456 | tf_op jit(solution)/shard_map/all_to_all | solution.py:563
  143.2 7.6 %collective-permute-start = (s32[11,128]{1,0:T(8,128)S(1)}, s32[11,128]{1,0:T(8,128)S(1)}, u32[]{:S(2)}, u32[]{:S(2)}) collective-permute-start(s32[11,128]{1,0:T(8,128)S(1)} %pad_add_fusion.1), channel_id=1, source_target_pairs={{8,0},{16,8},{24,16},{0,24},{9,1},{17,9},{25,17},{1,25},{10,2},{18... | collective-permute-start | bytes 16904 | tf_op jit(solution)/shard_map/ppermute | solution.py:424
  145.7 5.2 %collective-permute-start.1 = (s32[11,128]{1,0:T(8,128)S(1)}, s32[11,128]{1,0:T(8,128)S(1)}, u32[]{:S(2)}, u32[]{:S(2)}) collective-permute-start(s32[11,128]{1,0:T(8,128)S(1)} %pad_add_fusion.1), channel_id=1, source_target_pairs={{16,0},{24,8},{0,16},{8,24},{17,1},{25,9},{1,17},{9,25},{18,2},{26... | collective-permute-start | bytes 16904 | tf_op jit(solution)/shard_map/ppermute | solution.py:424
  146.2 4.7 %collective-permute-start.2 = (s32[11,128]{1,0:T(8,128)S(1)}, s32[11,128]{1,0:T(8,128)S(1)}, u32[]{:S(2)}, u32[]{:S(2)}) collective-permute-start(s32[11,128]{1,0:T(8,128)S(1)} %pad_add_fusion.1), channel_id=1, source_target_pairs={{24,0},{0,8},{8,16},{16,24},{25,1},{1,9},{9,17},{17,25},{26,2},{2,... | collective-permute-start | bytes 16904 | tf_op jit(solution)/shard_map/ppermute | solution.py:424
  146.8 8.1 %collective-permute-start.3 = (bf16[128,256]{1,0:T(8,128)(2,1)S(1)}, bf16[128,256]{1,0:T(8,128)(2,1)S(1)}, u32[]{:S(2)}, u32[]{:S(2)}) collective-permute-start(bf16[128,256]{1,0:T(8,128)(2,1)S(1)} %bitcast.189), channel_id=1, source_target_pairs={{8,0},{16,8},{24,16},{0,24},{9,1},{17,9},{25,17},{1,25},{10,2},{18... | collective-permute-start | bytes 196616 | tf_op jit(solution)/shard_map/ppermute | solution.py:424
  149.2 5.7 %collective-permute-start.4 = (bf16[128,256]{1,0:T(8,128)(2,1)S(1)}, bf16[128,256]{1,0:T(8,128)(2,1)S(1)}, u32[]{:S(2)}, u32[]{:S(2)}) collective-permute-start(bf16[128,256]{1,0:T(8,128)(2,1)S(1)} %bitcast.190), channel_id=1, source_target_pairs={{16,0},{24,8},{0,16},{8,24},{17,1},{25,9},{1,17},{9,25},{18,2},{26... | collective-permute-start | bytes 196616 | tf_op jit(solution)/shard_map/ppermute | solution.py:424
  150.8 5.2 %collective-permute-start.5 = (bf16[128,256]{1,0:T(8,128)(2,1)S(1)}, bf16[128,256]{1,0:T(8,128)(2,1)S(1)}, u32[]{:S(2)}, u32[]{:S(2)}) collective-permute-start(bf16[128,256]{1,0:T(8,128)(2,1)S(1)} %bitcast.192), channel_id=1, source_target_pairs={{24,0},{0,8},{8,16},{16,24},{25,1},{1,9},{9,17},{17,25},{26,2},{2,... | collective-permute-start | bytes 196616 | tf_op jit(solution)/shard_map/ppermute | solution.py:424
  188.7 16.6 %collective-permute-start.8 = (bf16[768,256]{1,0:T(8,128)(2,1)}, bf16[768,256]{1,0:T(8,128)(2,1)}, u32[]{:S(2)}, u32[]{:S(2)}) collective-permute-start(bf16[768,256]{1,0:T(8,128)(2,1)} %get-tuple-element.62), channel_id=1, source_target_pairs={{8,0},{16,8},{24,16},{0,24},{9,1},{17,9},{25,17},{1,25},{10,2},{18... | collective-permute-start | bytes 1179656 | tf_op jit(solution)/shard_map/ppermute | solution.py:424
  191.0 14.2 %collective-permute-start.7 = (bf16[768,256]{1,0:T(8,128)(2,1)}, bf16[768,256]{1,0:T(8,128)(2,1)}, u32[]{:S(2)}, u32[]{:S(2)}) collective-permute-start(bf16[768,256]{1,0:T(8,128)(2,1)} %get-tuple-element.61), channel_id=1, source_target_pairs={{16,0},{24,8},{0,16},{8,24},{17,1},{25,9},{1,17},{9,25},{18,2},{26... | collective-permute-start | bytes 1179656 | tf_op jit(solution)/shard_map/ppermute | solution.py:424
  199.5 11.3 %collective-permute-start.6 = (bf16[768,256]{1,0:T(8,128)(2,1)}, bf16[768,256]{1,0:T(8,128)(2,1)}, u32[]{:S(2)}, u32[]{:S(2)}) collective-permute-start(bf16[768,256]{1,0:T(8,128)(2,1)} %get-tuple-element.60), channel_id=1, source_target_pairs={{24,0},{0,8},{8,16},{16,24},{25,1},{1,9},{9,17},{17,25},{26,2},{2,... | collective-permute-start | bytes 1179656 | tf_op jit(solution)/shard_map/ppermute | solution.py:424
  212.8 11.6 %collective-permute-start.11 = (bf16[640,256]{1,0:T(8,128)(2,1)S(1)}, bf16[640,256]{1,0:T(8,128)(2,1)S(1)}, u32[]{:S(2)}, u32[]{:S(2)}) collective-permute-start(bf16[640,256]{1,0:T(8,128)(2,1)S(1)} %pad_maximum_fusion.2), channel_id=1, source_target_pairs={{24,0},{0,8},{8,16},{16,24},{25,1},{1,9},{9,17},{17,25},{26,2},{2,... | collective-permute-start | bytes 983048 | tf_op jit(solution)/shard_map/ppermute | solution.py:424
  212.9 14.8 %collective-permute-start.10 = (bf16[640,256]{1,0:T(8,128)(2,1)S(1)}, bf16[640,256]{1,0:T(8,128)(2,1)S(1)}, u32[]{:S(2)}, u32[]{:S(2)}) collective-permute-start(bf16[640,256]{1,0:T(8,128)(2,1)S(1)} %pad_maximum_fusion.2), channel_id=1, source_target_pairs={{16,0},{24,8},{0,16},{8,24},{17,1},{25,9},{1,17},{9,25},{18,2},{26... | collective-permute-start | bytes 983048 | tf_op jit(solution)/shard_map/ppermute | solution.py:424
  214.5 14.2 %collective-permute-start.9 = (bf16[640,256]{1,0:T(8,128)(2,1)S(1)}, bf16[640,256]{1,0:T(8,128)(2,1)S(1)}, u32[]{:S(2)}, u32[]{:S(2)}) collective-permute-start(bf16[640,256]{1,0:T(8,128)(2,1)S(1)} %pad_maximum_fusion.2), channel_id=1, source_target_pairs={{8,0},{16,8},{24,16},{0,24},{9,1},{17,9},{25,17},{1,25},{10,2},{18... | collective-permute-start | bytes 983048 | tf_op jit(solution)/shard_map/ppermute | solution.py:424
  232.5 17.0 %collective-permute-start.14 = (bf16[768,256]{1,0:T(8,128)(2,1)S(1)}, bf16[768,256]{1,0:T(8,128)(2,1)S(1)}, u32[]{:S(2)}, u32[]{:S(2)}) collective-permute-start(bf16[768,256]{1,0:T(8,128)(2,1)S(1)} %fusion.2), channel_id=1, source_target_pairs={{8,0},{16,8},{24,16},{0,24},{9,1},{17,9},{25,17},{1,25},{10,2},{18... | collective-permute-start | bytes 1179656 | tf_op jit(solution)/shard_map/ppermute | solution.py:424
  234.1 15.4 %collective-permute-start.12 = (bf16[768,256]{1,0:T(8,128)(2,1)S(1)}, bf16[768,256]{1,0:T(8,128)(2,1)S(1)}, u32[]{:S(2)}, u32[]{:S(2)}) collective-permute-start(bf16[768,256]{1,0:T(8,128)(2,1)S(1)} %fusion.2), channel_id=1, source_target_pairs={{16,0},{24,8},{0,16},{8,24},{17,1},{25,9},{1,17},{9,25},{18,2},{26... | collective-permute-start | bytes 1179656 | tf_op jit(solution)/shard_map/ppermute | solution.py:424
  235.7 15.4 %collective-permute-start.13 = (bf16[768,256]{1,0:T(8,128)(2,1)S(1)}, bf16[768,256]{1,0:T(8,128)(2,1)S(1)}, u32[]{:S(2)}, u32[]{:S(2)}) collective-permute-start(bf16[768,256]{1,0:T(8,128)(2,1)S(1)} %fusion.2), channel_id=1, source_target_pairs={{24,0},{0,8},{8,16},{16,24},{25,1},{1,9},{9,17},{17,25},{26,2},{2,... | collective-permute-start | bytes 1179656 | tf_op jit(solution)/shard_map/ppermute | solution.py:424
  255.2 6.0 %collective-permute-start.18 = (bf16[128,256]{1,0:T(8,128)(2,1)S(1)}, bf16[128,256]{1,0:T(8,128)(2,1)S(1)}, u32[]{:S(2)}, u32[]{:S(2)}) collective-permute-start(bf16[128,256]{1,0:T(8,128)(2,1)S(1)} %get-tuple-element.80), channel_id=1, source_target_pairs={{2,0},{3,1},{4,2},{5,3},{6,4},{7,5},{0,6},{1,7},{10,8},{11,9},{12,... | collective-permute-start | bytes 196616 | tf_op jit(solution)/shard_map/ppermute | solution.py:424
  257.7 8.9 %collective-permute-start.17 = (bf16[128,256]{1,0:T(8,128)(2,1)S(1)}, bf16[128,256]{1,0:T(8,128)(2,1)S(1)}, u32[]{:S(2)}, u32[]{:S(2)}) collective-permute-start(bf16[128,256]{1,0:T(8,128)(2,1)S(1)} %get-tuple-element.81), channel_id=1, source_target_pairs={{4,0},{5,1},{6,2},{7,3},{0,4},{1,5},{2,6},{3,7},{12,8},{13,9},{14,... | collective-permute-start | bytes 196616 | tf_op jit(solution)/shard_map/ppermute | solution.py:424
  260.2 6.3 %collective-permute-start.16 = (bf16[128,256]{1,0:T(8,128)(2,1)S(1)}, bf16[128,256]{1,0:T(8,128)(2,1)S(1)}, u32[]{:S(2)}, u32[]{:S(2)}) collective-permute-start(bf16[128,256]{1,0:T(8,128)(2,1)S(1)} %get-tuple-element.79), channel_id=1, source_target_pairs={{6,0},{7,1},{0,2},{1,3},{2,4},{3,5},{4,6},{5,7},{14,8},{15,9},{8,1... | collective-permute-start | bytes 196616 | tf_op jit(solution)/shard_map/ppermute | solution.py:424
  266.6 6.2 %collective-permute-start.21 = (bf16[128,256]{1,0:T(8,128)(2,1)S(1)}, bf16[128,256]{1,0:T(8,128)(2,1)S(1)}, u32[]{:S(2)}, u32[]{:S(2)}) collective-permute-start(bf16[128,256]{1,0:T(8,128)(2,1)S(1)} %fusion.16), channel_id=1, source_target_pairs={{6,0},{7,1},{0,2},{1,3},{2,4},{3,5},{4,6},{5,7},{14,8},{15,9},{8,1... | collective-permute-start | bytes 196616 | tf_op jit(solution)/shard_map/ppermute | solution.py:424
  266.7 7.1 %collective-permute-start.20 = (bf16[128,256]{1,0:T(8,128)(2,1)S(1)}, bf16[128,256]{1,0:T(8,128)(2,1)S(1)}, u32[]{:S(2)}, u32[]{:S(2)}) collective-permute-start(bf16[128,256]{1,0:T(8,128)(2,1)S(1)} %fusion.16), channel_id=1, source_target_pairs={{4,0},{5,1},{6,2},{7,3},{0,4},{1,5},{2,6},{3,7},{12,8},{13,9},{14,... | collective-permute-start | bytes 196616 | tf_op jit(solution)/shard_map/ppermute | solution.py:424
  267.1 6.6 %collective-permute-start.19 = (bf16[128,256]{1,0:T(8,128)(2,1)S(1)}, bf16[128,256]{1,0:T(8,128)(2,1)S(1)}, u32[]{:S(2)}, u32[]{:S(2)}) collective-permute-start(bf16[128,256]{1,0:T(8,128)(2,1)S(1)} %fusion.16), channel_id=1, source_target_pairs={{2,0},{3,1},{4,2},{5,3},{6,4},{7,5},{0,6},{1,7},{10,8},{11,9},{12,... | collective-permute-start | bytes 196616 | tf_op jit(solution)/shard_map/ppermute | solution.py:424
  (30 other events, 668.3 us)

commit v14 on v13

--- a/solution.py
+++ b/solution.py
@@ -572,6 +572,7 @@
     lists = jnp.concatenate([jnp.where(used_two, second[0].T, -1), second[1]], axis=0)
     lists = in_order(spread_parts(lists))
     upstream = in_order(spread_parts(second[2])).reshape(seeds, hidden_width)
+    total, lists, upstream = lax.optimization_barrier((total, lists, upstream))
 
     near_two = lists[:, :fanout_two].transpose(1, 0, 2).reshape(fanout_two, seeds)
     deg_all = lists[:, fanout_two].reshape(seeds)
@@ -586,7 +587,6 @@
     adj_two = jnp.sum(
         place[:, :, None] == jnp.arange(share)[None, None, :], axis=0, dtype=jnp.float32
     ).astype(jnp.bfloat16)
-    total, adj_two, upstream = lax.optimization_barrier((total, adj_two, upstream))
 
     def finish(begin, end):
         return gather_sum(

time: 277 us -> 273 us (0.986)
  waiting for transfers between devices: 74.5 us -> 83.6 us
  local copies, waits for them, and re-layouts: 17.5 us -> 12.8 us
  other arithmetic: 10.4 us -> 5.76 us
    ppermute x21, waiting for transfers between devices: 40.7 us -> 46.5 us  [passed(): lax.ppermute(part, axis, [((i + shift) % parts, i) for i in range(parts)])]
    unnamed x62 -> x42, local copies, waits for them, and re-layouts: 9.19 us -> 5.89 us
  transfers between devices with their start and end apart: 26 -> 26, of which waited for: 15 -> 17; matrix products, arithmetic and copies ran while one was open for 7% -> 5% of each run, Pallas kernels for 36% -> 37%
where the time goes in v14:
time: 273 us; the launch traced here: 271 us
  Pallas kernels  120 us (44%)
  waiting for transfers between devices  83.6 us (31%)
  starting transfers between devices  40.5 us (15%)
  local copies, waits for them, and re-layouts  12.8 us (5%)
  other arithmetic  5.76 us (2%)
  matrix products  4.91 us (2%)
  between operations  2.92 us (1%)
    pallas_call x4, Pallas kernels, gather_sum(): pl.pallas_call(functools.partial(gather_sum_body, piece, last, row0), out...  49.1 us
    pallas_call x1, Pallas kernels, adjacency(): pl.pallas_call(functools.partial(adjacency_body, tiles), out_shape=jax.Sh...  47.8 us
    ppermute x21, waiting for transfers between devices, passed(): lax.ppermute(part, axis, [((i + shift) % parts, i) for i in range(parts)])  46.5 us
    ppermute x21, starting transfers between devices, passed(): lax.ppermute(part, axis, [((i + shift) % parts, i) for i in range(parts)])  25 us
    all_to_all x1, waiting for transfers between devices, local(): lax.all_to_all(looked, 'batch', split_axis=0, concat_axis=0, tiled=True)  24.1 us
    pallas_call x2, Pallas kernels, lookup(): pl.pallas_call(functools.partial(lookup_body, places.shape[0] // groups,...  21.3 us
    all_to_all x1, starting transfers between devices, local(): lax.all_to_all(requests.reshape(batch_count, capacity), 'batch', split_ax...  6.33 us
    unnamed x42, local copies, waits for them, and re-layouts  5.89 us
  transfers between devices with their start and end apart: 26, of which 17 were waited for; matrix products, arithmetic and copies ran while one was open for 5% of the time, Pallas kernels for 37%

profile of v14, /device:TPU:0, one launch (start us, length us, event | category | flops | bytes accessed | tf_op | source)
XLA Modules:
  0.0 270.5 jit_solution(4002359385488550646)
XLA Ops:
  4.0 6.3 %all-to-all-start = ((s32[8,1,1536]{2,1,0:T(1,128)}), s32[8,1,1536]{2,1,0:T(1,128)S(1)}, u32[]{:S(2)}, u32[]{:S(2)}) async-start(s32[8,1,1536]{2,1,0:T(1,128)} %bitcast.9), calls=%async_computation | async-start | bytes 98304 | tf_op jit(solution)/shard_map/all_to_all | solution.py:517
  11.3 4.9 %all-to-all-done = s32[8,1,1536]{2,1,0:T(1,128)S(1)} async-done(((s32[8,1,1536]{2,1,0:T(1,128)}), s32[8,1,1536]{2,1,0:T(1,128)S(1)}, u32[]{:S(2)}, u32[]{:S(2)}) %all-to-all-start) | async-done | bytes 49184 | tf_op jit(solution)/shard_map/all_to_all | solution.py:517
  16.8 11.5 %lookup.3 = bf16[8,768,256]{2,1,0:T(8,128)(2,1)} custom-call(s32[12288]{0:T(1024)} %bitcast.159, bf16[8192,256]{1,0:T(8,128)(2,1)} %store_in.3), custom_call_target="tpu_custom_call" | custom-call | flops 62914560 | bytes 4194304 | tf_op jit(solution)/shard_map/lookup/pallas_call | solution.py:151
  28.3 4.5 %all-to-all-start.1 = ((bf16[8,768,256]{2,1,0:T(8,128)(2,1)}), bf16[8,768,256]{2,1,0:T(8,128)(2,1)}, u32[]{:S(2)}, u32[]{:S(2)}) async-start(bf16[8,768,256]{2,1,0:T(8,128)(2,1)} %lookup.3), calls=%async_computation.1 | async-start | bytes 6291456 | tf_op jit(solution)/shard_map/all_to_all | solution.py:524
  40.9 9.8 %lookup.2 = bf16[8,768,256]{2,1,0:T(8,128)(2,1)} custom-call(s32[12288]{0:T(1024)S(1)} %bitcast.160, bf16[8192,256]{1,0:T(8,128)(2,1)S(1)} %copy-done.3), custom_call_target="tpu_custom_call" | custom-call | flops 62914560 | bytes 4194304 | tf_op jit(solution)/shard_map/lookup/pallas_call | solution.py:151
  50.7 47.8 %adjacency.1.adj_ref = f8e4m3fn[28,3072,256]{2,1,0:T(32,128)(4,1)} custom-call(s32[1]{0:T(128)} %bitcast.11.me_ref, s32[192,256]{1,0:T(8,128)S(1)} %reshape.242.near_ref, bf16[256,128]{1,0:T(8,128)(2,1)S(1)} %pad_maximum_fusion.4.table_ref), custom_call_target="tpu_custom_call" | custom-call | flops 22548578304 | bytes 22020096 | tf_op jit(solution)/shard_map/adjacency/pallas_call | solution.py:214
  98.5 5.8 %all-to-all-done.1.answer_ref = bf16[8,768,256]{2,1,0:T(8,128)(2,1)} async-done(((bf16[8,768,256]{2,1,0:T(8,128)(2,1)}), bf16[8,768,256]{2,1,0:T(8,128)(2,1)}, u32[]{:S(2)}, u32[]{:S(2)}) %all-to-all-start.1) | async-done | bytes 3145760 | tf_op jit(solution)/shard_map/all_to_all | solution.py:524
  104.3 4.5 %all-to-all-start.2 = ((bf16[8,768,256]{2,1,0:T(8,128)(2,1)}), bf16[8,768,256]{2,1,0:T(8,128)(2,1)}, u32[]{:S(2)}, u32[]{:S(2)}) async-start(bf16[8,768,256]{2,1,0:T(8,128)(2,1)} %lookup.2), calls=%async_computation.2 | async-start | bytes 6291456 | tf_op jit(solution)/shard_map/all_to_all | solution.py:563
  111.9 31.4 %gather_sum.4 = (f32[3072,256]{1,0:T(8,128)}, f32[3072,256]{1,0:T(8,128)}) custom-call(s32[2]{0:T(128)S(1)} %pad_add_fusion.4.spans_ref, s32[8]{0:T(128)S(1)} %get-tuple-element.88.counts_ref, s32[9]{0:T(128)S(1)} %get-tuple-element.90.starts_ref, s32[56]{0:T(128)S(1)} %reshape.248.own_here_ref, bf16[8,768,256]{2,1,0:T(8,128)(2,1)} %all-to-all-done.1.answer_ref, ...), custom_call_target="tpu_custom_call" | custom-call | flops 11274289152 | bytes 786432 | tf_op jit(solution)/shard_map/gather_sum/pallas_call | solution.py:393
  143.4 2.5 collective-permute-start
  151.8 2.5 collective-permute-done.4
  156.3 24.1 %all-to-all-done.2.answer_ref = bf16[8,768,256]{2,1,0:T(8,128)(2,1)} async-done(((bf16[8,768,256]{2,1,0:T(8,128)(2,1)}), bf16[8,768,256]{2,1,0:T(8,128)(2,1)}, u32[]{:S(2)}, u32[]{:S(2)}) %all-to-all-start.2) | async-done | bytes 3145760 | tf_op jit(solution)/shard_map/all_to_all | solution.py:563
  180.3 7.2 %gather_sum.5 = (bf16[1536,256]{1,0:T(8,128)(2,1)S(1)}, bf16[1536,256]{1,0:T(8,128)(2,1)S(1)}, bf16[768,256]{1,0:T(8,128)(2,1)S(1)}, bf16[768,256]{1,0:T(8,128)(2,1)S(1)}) custom-call(s32[2]{0:T(128)S(1)} %pad_add_fusion.5.spans_ref, s32[8]{0:T(128)S(1)} %get-tuple-element.87.counts_ref, s32[9]{0:T(128)S(1)} %get-tuple-element.89.starts_ref, ...), custom_call_target="tpu_custom_call" | custom-call | flops 1409286144 | bytes 393216 | tf_op jit(solution)/shard_map/gather_sum/pallas_call | solution.py:393
  187.6 2.5 collective-permute-start.8
  190.6 5.3 %gather_sum.6 = (bf16[768,256]{1,0:T(8,128)(2,1)S(1)}, bf16[768,256]{1,0:T(8,128)(2,1)S(1)}, bf16[768,256]{1,0:T(8,128)(2,1)S(1)}) custom-call(s32[2]{0:T(128)S(1)} %pad_add_fusion.5.spans_ref, s32[8]{0:T(128)S(1)} %get-tuple-element.87.counts_ref, s32[9]{0:T(128)S(1)} %get-tuple-element.89.starts_ref, s32[56]{0:T(128)S(1)} %reshape.248.own_here_ref, ...), custom_call_target="tpu_custom_call" | custom-call | flops 704643072 | bytes 196608 | tf_op jit(solution)/shard_map/gather_sum/pallas_call | solution.py:393
  198.9 5.3 %gather_sum.7 = (bf16[768,256]{1,0:T(8,128)(2,1)S(1)}, bf16[768,256]{1,0:T(8,128)(2,1)S(1)}, bf16[768,256]{1,0:T(8,128)(2,1)S(1)}) custom-call(s32[2]{0:T(128)S(1)} %pad_add_fusion.5.spans_ref, s32[8]{0:T(128)S(1)} %get-tuple-element.87.counts_ref, s32[9]{0:T(128)S(1)} %get-tuple-element.89.starts_ref, s32[56]{0:T(128)S(1)} %reshape.248.own_here_ref, ...), custom_call_target="tpu_custom_call" | custom-call | flops 704643072 | bytes 196608 | tf_op jit(solution)/shard_map/gather_sum/pallas_call | solution.py:393
  204.2 4.7 %collective-permute-done.7 = bf16[768,256]{1,0:T(8,128)(2,1)S(1)} collective-permute-done((bf16[768,256]{1,0:T(8,128)(2,1)S(1)}, bf16[768,256]{1,0:T(8,128)(2,1)S(1)}, u32[]{:S(2)}, u32[]{:S(2)}) %collective-permute-start.7) | collective-permute-done | bytes 393248 | tf_op jit(solution)/shard_map/ppermute | solution.py:424
  210.8 2.5 collective-permute-start.9
  213.4 7.9 %collective-permute-done.11 = bf16[640,256]{1,0:T(8,128)(2,1)S(1)} collective-permute-done((bf16[640,256]{1,0:T(8,128)(2,1)S(1)}, bf16[640,256]{1,0:T(8,128)(2,1)S(1)}, u32[]{:S(2)}, u32[]{:S(2)}) %collective-permute-start.11) | collective-permute-done | bytes 327712 | tf_op jit(solution)/shard_map/ppermute | solution.py:424
  221.3 3.5 %collective-permute-done.10 = bf16[640,256]{1,0:T(8,128)(2,1)S(1)} collective-permute-done((bf16[640,256]{1,0:T(8,128)(2,1)S(1)}, bf16[640,256]{1,0:T(8,128)(2,1)S(1)}, u32[]{:S(2)}, u32[]{:S(2)}) %collective-permute-start.10) | collective-permute-done | bytes 327712 | tf_op jit(solution)/shard_map/ppermute | solution.py:424
  231.4 7.9 %collective-permute-done.12 = bf16[768,256]{1,0:T(8,128)(2,1)S(1)} collective-permute-done((bf16[768,256]{1,0:T(8,128)(2,1)S(1)}, bf16[768,256]{1,0:T(8,128)(2,1)S(1)}, u32[]{:S(2)}, u32[]{:S(2)}) %collective-permute-start.12) | collective-permute-done | bytes 393248 | tf_op jit(solution)/shard_map/ppermute | solution.py:424
  239.7 7.4 %collective-permute-done.13 = bf16[768,256]{1,0:T(8,128)(2,1)S(1)} collective-permute-done((bf16[768,256]{1,0:T(8,128)(2,1)S(1)}, bf16[768,256]{1,0:T(8,128)(2,1)S(1)}, u32[]{:S(2)}, u32[]{:S(2)}) %collective-permute-start.13) | collective-permute-done | bytes 393248 | tf_op jit(solution)/shard_map/ppermute | solution.py:424
  254.7 4.5 %collective-permute-done.17 = bf16[128,256]{1,0:T(8,128)(2,1)S(1)} collective-permute-done((bf16[128,256]{1,0:T(8,128)(2,1)S(1)}, bf16[128,256]{1,0:T(8,128)(2,1)S(1)}, u32[]{:S(2)}, u32[]{:S(2)}) %collective-permute-start.17) | collective-permute-done | bytes 65568 | tf_op jit(solution)/shard_map/ppermute | solution.py:424
  263.7 2.4 collective-permute-done.21
  (168 shorter events, 51.0 us)
Async XLA Ops:
  4.0 12.2 %all-to-all-start = ((s32[8,1,1536]{2,1,0:T(1,128)}), s32[8,1,1536]{2,1,0:T(1,128)S(1)}, u32[]{:S(2)}, u32[]{:S(2)}) async-start(s32[8,1,1536]{2,1,0:T(1,128)} %bitcast.9), calls=%async_computation | async-start | bytes 98304 | tf_op jit(solution)/shard_map/all_to_all | solution.py:517
  28.3 76.0 %all-to-all-start.1 = ((bf16[8,768,256]{2,1,0:T(8,128)(2,1)}), bf16[8,768,256]{2,1,0:T(8,128)(2,1)}, u32[]{:S(2)}, u32[]{:S(2)}) async-start(bf16[8,768,256]{2,1,0:T(8,128)(2,1)} %lookup.3), calls=%async_computation.1 | async-start | bytes 6291456 | tf_op jit(solution)/shard_map/all_to_all | solution.py:524
  104.3 76.0 %all-to-all-start.2 = ((bf16[8,768,256]{2,1,0:T(8,128)(2,1)}), bf16[8,768,256]{2,1,0:T(8,128)(2,1)}, u32[]{:S(2)}, u32[]{:S(2)}) async-start(bf16[8,768,256]{2,1,0:T(8,128)(2,1)} %lookup.2), calls=%async_computation.2 | async-start | bytes 6291456 | tf_op jit(solution)/shard_map/all_to_all | solution.py:563
  143.4 7.6 %collective-permute-start = (s32[11,128]{1,0:T(8,128)S(1)}, s32[11,128]{1,0:T(8,128)S(1)}, u32[]{:S(2)}, u32[]{:S(2)}) collective-permute-start(s32[11,128]{1,0:T(8,128)S(1)} %pad_add_fusion.1), channel_id=1, source_target_pairs={{8,0},{16,8},{24,16},{0,24},{9,1},{17,9},{25,17},{1,25},{10,2},{18... | collective-permute-start | bytes 16904 | tf_op jit(solution)/shard_map/ppermute | solution.py:424
  145.9 5.2 %collective-permute-start.1 = (s32[11,128]{1,0:T(8,128)S(1)}, s32[11,128]{1,0:T(8,128)S(1)}, u32[]{:S(2)}, u32[]{:S(2)}) collective-permute-start(s32[11,128]{1,0:T(8,128)S(1)} %pad_add_fusion.1), channel_id=1, source_target_pairs={{16,0},{24,8},{0,16},{8,24},{17,1},{25,9},{1,17},{9,25},{18,2},{26... | collective-permute-start | bytes 16904 | tf_op jit(solution)/shard_map/ppermute | solution.py:424
  146.4 4.7 %collective-permute-start.2 = (s32[11,128]{1,0:T(8,128)S(1)}, s32[11,128]{1,0:T(8,128)S(1)}, u32[]{:S(2)}, u32[]{:S(2)}) collective-permute-start(s32[11,128]{1,0:T(8,128)S(1)} %pad_add_fusion.1), channel_id=1, source_target_pairs={{24,0},{0,8},{8,16},{16,24},{25,1},{1,9},{9,17},{17,25},{26,2},{2,... | collective-permute-start | bytes 16904 | tf_op jit(solution)/shard_map/ppermute | solution.py:424
  147.0 4.8 %collective-permute-start.3 = (bf16[128,256]{1,0:T(8,128)(2,1)S(1)}, bf16[128,256]{1,0:T(8,128)(2,1)S(1)}, u32[]{:S(2)}, u32[]{:S(2)}) collective-permute-start(bf16[128,256]{1,0:T(8,128)(2,1)S(1)} %bitcast.189), channel_id=1, source_target_pairs={{8,0},{16,8},{24,16},{0,24},{9,1},{17,9},{25,17},{1,25},{10,2},{18... | collective-permute-start | bytes 196616 | tf_op jit(solution)/shard_map/ppermute | solution.py:424
  149.3 5.0 %collective-permute-start.4 = (bf16[128,256]{1,0:T(8,128)(2,1)S(1)}, bf16[128,256]{1,0:T(8,128)(2,1)S(1)}, u32[]{:S(2)}, u32[]{:S(2)}) collective-permute-start(bf16[128,256]{1,0:T(8,128)(2,1)S(1)} %bitcast.190), channel_id=1, source_target_pairs={{16,0},{24,8},{0,16},{8,24},{17,1},{25,9},{1,17},{9,25},{18,2},{26... | collective-permute-start | bytes 196616 | tf_op jit(solution)/shard_map/ppermute | solution.py:424
  151.0 5.2 %collective-permute-start.5 = (bf16[128,256]{1,0:T(8,128)(2,1)S(1)}, bf16[128,256]{1,0:T(8,128)(2,1)S(1)}, u32[]{:S(2)}, u32[]{:S(2)}) collective-permute-start(bf16[128,256]{1,0:T(8,128)(2,1)S(1)} %bitcast.192), channel_id=1, source_target_pairs={{24,0},{0,8},{8,16},{16,24},{25,1},{1,9},{9,17},{17,25},{26,2},{2,... | collective-permute-start | bytes 196616 | tf_op jit(solution)/shard_map/ppermute | solution.py:424
  187.6 16.6 %collective-permute-start.8 = (bf16[768,256]{1,0:T(8,128)(2,1)S(1)}, bf16[768,256]{1,0:T(8,128)(2,1)S(1)}, u32[]{:S(2)}, u32[]{:S(2)}) collective-permute-start(bf16[768,256]{1,0:T(8,128)(2,1)S(1)} %get-tuple-element.62), channel_id=1, source_target_pairs={{8,0},{16,8},{24,16},{0,24},{9,1},{17,9},{25,17},{1,25},{10,2},{18... | collective-permute-start | bytes 1179656 | tf_op jit(solution)/shard_map/ppermute | solution.py:424
  190.1 18.8 %collective-permute-start.7 = (bf16[768,256]{1,0:T(8,128)(2,1)S(1)}, bf16[768,256]{1,0:T(8,128)(2,1)S(1)}, u32[]{:S(2)}, u32[]{:S(2)}) collective-permute-start(bf16[768,256]{1,0:T(8,128)(2,1)S(1)} %get-tuple-element.61), channel_id=1, source_target_pairs={{16,0},{24,8},{0,16},{8,24},{17,1},{25,9},{1,17},{9,25},{18,2},{26... | collective-permute-start | bytes 1179656 | tf_op jit(solution)/shard_map/ppermute | solution.py:424
  195.9 13.0 %collective-permute-start.6 = (bf16[768,256]{1,0:T(8,128)(2,1)S(1)}, bf16[768,256]{1,0:T(8,128)(2,1)S(1)}, u32[]{:S(2)}, u32[]{:S(2)}) collective-permute-start(bf16[768,256]{1,0:T(8,128)(2,1)S(1)} %get-tuple-element.60), channel_id=1, source_target_pairs={{24,0},{0,8},{8,16},{16,24},{25,1},{1,9},{9,17},{17,25},{26,2},{2,... | collective-permute-start | bytes 1179656 | tf_op jit(solution)/shard_map/ppermute | solution.py:424
  209.7 11.6 %collective-permute-start.11 = (bf16[640,256]{1,0:T(8,128)(2,1)S(1)}, bf16[640,256]{1,0:T(8,128)(2,1)S(1)}, u32[]{:S(2)}, u32[]{:S(2)}) collective-permute-start(bf16[640,256]{1,0:T(8,128)(2,1)S(1)} %pad_maximum_fusion.2), channel_id=1, source_target_pairs={{24,0},{0,8},{8,16},{16,24},{25,1},{1,9},{9,17},{17,25},{26,2},{2,... | collective-permute-start | bytes 983048 | tf_op jit(solution)/shard_map/ppermute | solution.py:424
  210.1 14.8 %collective-permute-start.10 = (bf16[640,256]{1,0:T(8,128)(2,1)S(1)}, bf16[640,256]{1,0:T(8,128)(2,1)S(1)}, u32[]{:S(2)}, u32[]{:S(2)}) collective-permute-start(bf16[640,256]{1,0:T(8,128)(2,1)S(1)} %pad_maximum_fusion.2), channel_id=1, source_target_pairs={{16,0},{24,8},{0,16},{8,24},{17,1},{25,9},{1,17},{9,25},{18,2},{26... | collective-permute-start | bytes 983048 | tf_op jit(solution)/shard_map/ppermute | solution.py:424
  210.8 14.0 %collective-permute-start.9 = (bf16[640,256]{1,0:T(8,128)(2,1)S(1)}, bf16[640,256]{1,0:T(8,128)(2,1)S(1)}, u32[]{:S(2)}, u32[]{:S(2)}) collective-permute-start(bf16[640,256]{1,0:T(8,128)(2,1)S(1)} %pad_maximum_fusion.2), channel_id=1, source_target_pairs={{8,0},{16,8},{24,16},{0,24},{9,1},{17,9},{25,17},{1,25},{10,2},{18... | collective-permute-start | bytes 983048 | tf_op jit(solution)/shard_map/ppermute | solution.py:424
  227.3 12.0 %collective-permute-start.14 = (bf16[768,256]{1,0:T(8,128)(2,1)S(1)}, bf16[768,256]{1,0:T(8,128)(2,1)S(1)}, u32[]{:S(2)}, u32[]{:S(2)}) collective-permute-start(bf16[768,256]{1,0:T(8,128)(2,1)S(1)} %fusion.2), channel_id=1, source_target_pairs={{8,0},{16,8},{24,16},{0,24},{9,1},{17,9},{25,17},{1,25},{10,2},{18... | collective-permute-start | bytes 1179656 | tf_op jit(solution)/shard_map/ppermute | solution.py:424
  229.3 10.0 %collective-permute-start.12 = (bf16[768,256]{1,0:T(8,128)(2,1)S(1)}, bf16[768,256]{1,0:T(8,128)(2,1)S(1)}, u32[]{:S(2)}, u32[]{:S(2)}) collective-permute-start(bf16[768,256]{1,0:T(8,128)(2,1)S(1)} %fusion.2), channel_id=1, source_target_pairs={{16,0},{24,8},{0,16},{8,24},{17,1},{25,9},{1,17},{9,25},{18,2},{26... | collective-permute-start | bytes 1179656 | tf_op jit(solution)/shard_map/ppermute | solution.py:424
  230.2 16.8 %collective-permute-start.13 = (bf16[768,256]{1,0:T(8,128)(2,1)S(1)}, bf16[768,256]{1,0:T(8,128)(2,1)S(1)}, u32[]{:S(2)}, u32[]{:S(2)}) collective-permute-start(bf16[768,256]{1,0:T(8,128)(2,1)S(1)} %fusion.2), channel_id=1, source_target_pairs={{24,0},{0,8},{8,16},{16,24},{25,1},{1,9},{9,17},{17,25},{26,2},{2,... | collective-permute-start | bytes 1179656 | tf_op jit(solution)/shard_map/ppermute | solution.py:424
  250.1 4.5 %collective-permute-start.18 = (bf16[128,256]{1,0:T(8,128)(2,1)S(1)}, bf16[128,256]{1,0:T(8,128)(2,1)S(1)}, u32[]{:S(2)}, u32[]{:S(2)}) collective-permute-start(bf16[128,256]{1,0:T(8,128)(2,1)S(1)} %get-tuple-element.80), channel_id=1, source_target_pairs={{2,0},{3,1},{4,2},{5,3},{6,4},{7,5},{0,6},{1,7},{10,8},{11,9},{12,... | collective-permute-start | bytes 196616 | tf_op jit(solution)/shard_map/ppermute | solution.py:424
  252.2 7.0 %collective-permute-start.17 = (bf16[128,256]{1,0:T(8,128)(2,1)S(1)}, bf16[128,256]{1,0:T(8,128)(2,1)S(1)}, u32[]{:S(2)}, u32[]{:S(2)}) collective-permute-start(bf16[128,256]{1,0:T(8,128)(2,1)S(1)} %get-tuple-element.81), channel_id=1, source_target_pairs={{4,0},{5,1},{6,2},{7,3},{0,4},{1,5},{2,6},{3,7},{12,8},{13,9},{14,... | collective-permute-start | bytes 196616 | tf_op jit(solution)/shard_map/ppermute | solution.py:424
  252.2 7.0 %collective-permute-start.16 = (bf16[128,256]{1,0:T(8,128)(2,1)S(1)}, bf16[128,256]{1,0:T(8,128)(2,1)S(1)}, u32[]{:S(2)}, u32[]{:S(2)}) collective-permute-start(bf16[128,256]{1,0:T(8,128)(2,1)S(1)} %get-tuple-element.79), channel_id=1, source_target_pairs={{6,0},{7,1},{0,2},{1,3},{2,4},{3,5},{4,6},{5,7},{14,8},{15,9},{8,1... | collective-permute-start | bytes 196616 | tf_op jit(solution)/shard_map/ppermute | solution.py:424
  259.3 6.9 %collective-permute-start.21 = (bf16[128,256]{1,0:T(8,128)(2,1)S(1)}, bf16[128,256]{1,0:T(8,128)(2,1)S(1)}, u32[]{:S(2)}, u32[]{:S(2)}) collective-permute-start(bf16[128,256]{1,0:T(8,128)(2,1)S(1)} %fusion.16), channel_id=1, source_target_pairs={{6,0},{7,1},{0,2},{1,3},{2,4},{3,5},{4,6},{5,7},{14,8},{15,9},{8,1... | collective-permute-start | bytes 196616 | tf_op jit(solution)/shard_map/ppermute | solution.py:424
  259.3 8.2 %collective-permute-start.20 = (bf16[128,256]{1,0:T(8,128)(2,1)S(1)}, bf16[128,256]{1,0:T(8,128)(2,1)S(1)}, u32[]{:S(2)}, u32[]{:S(2)}) collective-permute-start(bf16[128,256]{1,0:T(8,128)(2,1)S(1)} %fusion.16), channel_id=1, source_target_pairs={{4,0},{5,1},{6,2},{7,3},{0,4},{1,5},{2,6},{3,7},{12,8},{13,9},{14,... | collective-permute-start | bytes 196616 | tf_op jit(solution)/shard_map/ppermute | solution.py:424
  261.5 6.0 %collective-permute-start.19 = (bf16[128,256]{1,0:T(8,128)(2,1)S(1)}, bf16[128,256]{1,0:T(8,128)(2,1)S(1)}, u32[]{:S(2)}, u32[]{:S(2)}) collective-permute-start(bf16[128,256]{1,0:T(8,128)(2,1)S(1)} %fusion.16), channel_id=1, source_target_pairs={{2,0},{3,1},{4,2},{5,3},{6,4},{7,5},{0,6},{1,7},{10,8},{11,9},{12,... | collective-permute-start | bytes 196616 | tf_op jit(solution)/shard_map/ppermute | solution.py:424
  (20 other events, 549.8 us)

commit v15 on v14

--- a/solution.py
+++ b/solution.py
@@ -46,7 +46,27 @@
     return pl.CostEstimate(flops=int(flops), bytes_accessed=int(moved), transcendentals=0)
 
 
-def requests_body(batch_count, capacity, scale, owner_ref, row_ref, slot_ref, count_ref, request_ref):
+def requests_body(
+    batch_count,
+    capacity,
+    scale,
+    owner_in,
+    row_in,
+    slot_ref,
+    count_ref,
+    request_ref,
+    owner_ref,
+    row_ref,
+    came,
+):
+    copies = [
+        pltpu.make_async_copy(owner_in, owner_ref, came.at[0]),
+        pltpu.make_async_copy(row_in, row_ref, came.at[1]),
+    ]
+    for copy in copies:
+        copy.start()
+    for copy in copies:
+        copy.wait()
     blocks, width = owner_ref.shape[0] // 2, TILE
     places = request_ref.shape[0]
     line = lambda ref, b: jnp.concatenate([ref[2 * b : 2 * b + 1], ref[2 * b + 1 : 2 * b + 2]], axis=1)
@@ -96,9 +116,14 @@
             jax.ShapeDtypeStruct((batch_count, LANES), jnp.int32),
             jax.ShapeDtypeStruct((places, LANES), jnp.int32),
         ),
-        in_specs=[VMEM, VMEM],
+        in_specs=[ANY, ANY],
         out_specs=(VMEM, VMEM, VMEM),
-        compiler_params=params(16),
+        scratch_shapes=[
+            pltpu.VMEM(owners.shape, owners.dtype),
+            pltpu.VMEM(wanted.shape, wanted.dtype),
+            pltpu.SemaphoreType.DMA((2,)),
+        ],
+        compiler_params=params(58),
         cost_estimate=cost(4 * total * places * LANES, 24 * total),
         name="requests",
     )(owners, wanted)
@@ -364,7 +389,7 @@
     batch_count, width, features = answer.shape
     tiles, nodes, _ = adj.shape
     nodes = sum(shares) or nodes
-    piece = LANES if width % LANES == 0 else SLOTS
+    piece = math.gcd(width, LANES)
     last = rest is not None
     room = min(batch_count * width, inputs) + SLOTS * batch_count + 2 * WIDE * TILE
     in_specs = [SMEM, SMEM, SMEM, SMEM, ANY, HBM, HBM]
@@ -517,7 +542,7 @@
     received = lax.all_to_all(
         requests.reshape(batch_count, capacity), "batch", split_axis=0, concat_axis=0, tiled=True
     )
-    first = capacity // 2
+    first = capacity * 13 // (24 * SLOTS) * SLOTS
     places = received.reshape(batch_count * capacity)
     looked_a = lookup(store, places, batch_count, 0, first, 60)
     near_first, looked_a = lax.optimization_barrier((nbr_one[0], looked_a))

time: 273 us -> 273 us (level)
  starting transfers between devices: 40.5 us -> 43.5 us
    all_to_all x1, waiting for transfers between devices: 5.78 us -> 11.9 us  [local(): lax.all_to_all(looked_a, 'batch', split_axis=0, concat_axis=0, tiled=True)]
    all_to_all x1, waiting for transfers between devices: 24.1 us -> 18.4 us  [local(): lax.all_to_all(looked, 'batch', split_axis=0, concat_axis=0, tiled=True)]
    ppermute x21, starting transfers between devices: 25 us -> 28 us  [passed(): lax.ppermute(part, axis, [((i + shift) % parts, i) for i in range(parts)])]
  transfers between devices with their start and end apart: 26 -> 26, of which waited for: 17 -> 18; matrix products, arithmetic and copies ran while one was open for 5% -> 5% of each run, Pallas kernels for 37% -> 37%
where the time goes in v15:
time: 273 us
  Pallas kernels  122 us (45%)
  waiting for transfers between devices  82.3 us (30%)
  starting transfers between devices  43.5 us (16%)
  local copies, waits for them, and re-layouts  11.3 us (4%)
  other arithmetic  5.76 us (2%)
  matrix products  4.9 us (2%)
  between operations  2.93 us (1%)
    pallas_call x4, Pallas kernels, gather_sum(): pl.pallas_call(functools.partial(gather_sum_body, piece, last, row0), out...  50.4 us
    pallas_call x1, Pallas kernels, adjacency(): pl.pallas_call(functools.partial(adjacency_body, tiles), out_shape=jax.Sh...  47.8 us
    ppermute x21, waiting for transfers between devices, passed(): lax.ppermute(part, axis, [((i + shift) % parts, i) for i in range(parts)])  44.9 us
    ppermute x21, starting transfers between devices, passed(): lax.ppermute(part, axis, [((i + shift) % parts, i) for i in range(parts)])  28 us
    pallas_call x2, Pallas kernels, lookup(): pl.pallas_call(functools.partial(lookup_body, places.shape[0] // groups,...  21.4 us
    all_to_all x1, waiting for transfers between devices, local(): lax.all_to_all(looked, 'batch', split_axis=0, concat_axis=0, tiled=True)  18.4 us
    all_to_all x1, waiting for transfers between devices, local(): lax.all_to_all(looked_a, 'batch', split_axis=0, concat_axis=0, tiled=True)  11.9 us
    all_to_all x1, starting transfers between devices, local(): lax.all_to_all(requests.reshape(batch_count, capacity), 'batch', split_ax...  6.34 us
  transfers between devices with their start and end apart: 26, of which 18 were waited for; matrix products, arithmetic and copies ran while one was open for 5% of the time, Pallas kernels for 37%

profile of v15, /device:TPU:0, one launch (start us, length us, event | category | flops | bytes accessed | tf_op | source)
XLA Modules:
  0.0 272.9 jit_solution(2076573913191560910)
XLA Ops:
  0.6 2.6 requests.1
  3.3 6.3 %all-to-all-start = ((s32[8,1,1536]{2,1,0:T(1,128)}), s32[8,1,1536]{2,1,0:T(1,128)S(1)}, u32[]{:S(2)}, u32[]{:S(2)}) async-start(s32[8,1,1536]{2,1,0:T(1,128)} %bitcast.190), calls=%async_computation | async-start | bytes 98304 | tf_op jit(solution)/shard_map/all_to_all | solution.py:542
  10.6 4.9 %all-to-all-done = s32[8,1,1536]{2,1,0:T(1,128)S(1)} async-done(((s32[8,1,1536]{2,1,0:T(1,128)}), s32[8,1,1536]{2,1,0:T(1,128)S(1)}, u32[]{:S(2)}, u32[]{:S(2)}) %all-to-all-start) | async-done | bytes 49184 | tf_op jit(solution)/shard_map/all_to_all | solution.py:542
  16.1 12.1 %lookup.3 = bf16[8,832,256]{2,1,0:T(8,128)(2,1)} custom-call(s32[12288]{0:T(1024)} %bitcast.159, bf16[8192,256]{1,0:T(8,128)(2,1)} %store_in.3), custom_call_target="tpu_custom_call" | custom-call | flops 68157440 | bytes 4194304 | tf_op jit(solution)/shard_map/lookup/pallas_call | solution.py:176
  28.2 4.6 %all-to-all-start.1 = ((bf16[8,832,256]{2,1,0:T(8,128)(2,1)}), bf16[8,832,256]{2,1,0:T(8,128)(2,1)}, u32[]{:S(2)}, u32[]{:S(2)}) async-start(bf16[8,832,256]{2,1,0:T(8,128)(2,1)} %lookup.3), calls=%async_computation.1 | async-start | bytes 6815744 | tf_op jit(solution)/shard_map/all_to_all | solution.py:549
  41.0 9.3 %lookup.2 = bf16[8,704,256]{2,1,0:T(8,128)(2,1)} custom-call(s32[12288]{0:T(1024)S(1)} %bitcast.160, bf16[8192,256]{1,0:T(8,128)(2,1)S(1)} %copy-done.3), custom_call_target="tpu_custom_call" | custom-call | flops 57671680 | bytes 4194304 | tf_op jit(solution)/shard_map/lookup/pallas_call | solution.py:176
  50.2 47.8 %adjacency.1.adj_ref = f8e4m3fn[28,3072,256]{2,1,0:T(32,128)(4,1)} custom-call(s32[1]{0:T(128)} %bitcast.11.me_ref, s32[192,256]{1,0:T(8,128)S(1)} %reshape.242.near_ref, bf16[256,128]{1,0:T(8,128)(2,1)S(1)} %pad_maximum_fusion.4.table_ref), custom_call_target="tpu_custom_call" | custom-call | flops 22548578304 | bytes 22020096 | tf_op jit(solution)/shard_map/adjacency/pallas_call | solution.py:239
  98.1 11.9 %all-to-all-done.1.answer_ref = bf16[8,832,256]{2,1,0:T(8,128)(2,1)} async-done(((bf16[8,832,256]{2,1,0:T(8,128)(2,1)}), bf16[8,832,256]{2,1,0:T(8,128)(2,1)}, u32[]{:S(2)}, u32[]{:S(2)}) %all-to-all-start.1) | async-done | bytes 3407904 | tf_op jit(solution)/shard_map/all_to_all | solution.py:549
  110.0 4.4 %all-to-all-start.2 = ((bf16[8,704,256]{2,1,0:T(8,128)(2,1)}), bf16[8,704,256]{2,1,0:T(8,128)(2,1)}, u32[]{:S(2)}, u32[]{:S(2)}) async-start(bf16[8,704,256]{2,1,0:T(8,128)(2,1)} %lookup.2), calls=%async_computation.2 | async-start | bytes 5767168 | tf_op jit(solution)/shard_map/all_to_all | solution.py:588
  117.5 31.5 %gather_sum.4 = (f32[3072,256]{1,0:T(8,128)}, f32[3072,256]{1,0:T(8,128)}) custom-call(s32[2]{0:T(128)S(1)} %pad_add_fusion.4.spans_ref, s32[8]{0:T(128)S(1)} %get-tuple-element.88.counts_ref, s32[9]{0:T(128)S(1)} %get-tuple-element.90.starts_ref, s32[56]{0:T(128)S(1)} %reshape.248.own_here_ref, bf16[8,832,256]{2,1,0:T(8,128)(2,1)} %all-to-all-done.1.answer_ref, ...), custom_call_target="tpu_custom_call" | custom-call | flops 11274289152 | bytes 786432 | tf_op jit(solution)/shard_map/gather_sum/pallas_call | solution.py:418
  149.1 2.5 collective-permute-start
  159.4 2.6 collective-permute-done.5
  162.0 18.4 %all-to-all-done.2.answer_ref = bf16[8,704,256]{2,1,0:T(8,128)(2,1)} async-done(((bf16[8,704,256]{2,1,0:T(8,128)(2,1)}), bf16[8,704,256]{2,1,0:T(8,128)(2,1)}, u32[]{:S(2)}, u32[]{:S(2)}) %all-to-all-start.2) | async-done | bytes 2883616 | tf_op jit(solution)/shard_map/all_to_all | solution.py:588
  180.4 7.6 %gather_sum.5 = (bf16[1536,256]{1,0:T(8,128)(2,1)S(1)}, bf16[1536,256]{1,0:T(8,128)(2,1)S(1)}, bf16[768,256]{1,0:T(8,128)(2,1)S(1)}, bf16[768,256]{1,0:T(8,128)(2,1)S(1)}) custom-call(s32[2]{0:T(128)S(1)} %pad_add_fusion.5.spans_ref, s32[8]{0:T(128)S(1)} %get-tuple-element.87.counts_ref, s32[9]{0:T(128)S(1)} %get-tuple-element.89.starts_ref, ...), custom_call_target="tpu_custom_call" | custom-call | flops 1409286144 | bytes 393216 | tf_op jit(solution)/shard_map/gather_sum/pallas_call | solution.py:418
  187.9 2.5 collective-permute-start.8
  190.9 5.7 %gather_sum.6 = (bf16[768,256]{1,0:T(8,128)(2,1)S(1)}, bf16[768,256]{1,0:T(8,128)(2,1)S(1)}, bf16[768,256]{1,0:T(8,128)(2,1)S(1)}) custom-call(s32[2]{0:T(128)S(1)} %pad_add_fusion.5.spans_ref, s32[8]{0:T(128)S(1)} %get-tuple-element.87.counts_ref, s32[9]{0:T(128)S(1)} %get-tuple-element.89.starts_ref, s32[56]{0:T(128)S(1)} %reshape.248.own_here_ref, ...), custom_call_target="tpu_custom_call" | custom-call | flops 704643072 | bytes 196608 | tf_op jit(solution)/shard_map/gather_sum/pallas_call | solution.py:418
  199.6 5.6 %gather_sum.7 = (bf16[768,256]{1,0:T(8,128)(2,1)S(1)}, bf16[768,256]{1,0:T(8,128)(2,1)S(1)}, bf16[768,256]{1,0:T(8,128)(2,1)S(1)}) custom-call(s32[2]{0:T(128)S(1)} %pad_add_fusion.5.spans_ref, s32[8]{0:T(128)S(1)} %get-tuple-element.87.counts_ref, s32[9]{0:T(128)S(1)} %get-tuple-element.89.starts_ref, s32[56]{0:T(128)S(1)} %reshape.248.own_here_ref, ...), custom_call_target="tpu_custom_call" | custom-call | flops 704643072 | bytes 196608 | tf_op jit(solution)/shard_map/gather_sum/pallas_call | solution.py:418
  205.2 4.0 %collective-permute-done.7 = bf16[768,256]{1,0:T(8,128)(2,1)S(1)} collective-permute-done((bf16[768,256]{1,0:T(8,128)(2,1)S(1)}, bf16[768,256]{1,0:T(8,128)(2,1)S(1)}, u32[]{:S(2)}, u32[]{:S(2)}) %collective-permute-start.7) | collective-permute-done | bytes 393248 | tf_op jit(solution)/shard_map/ppermute | solution.py:449
  213.5 7.9 %collective-permute-done.11 = bf16[640,256]{1,0:T(8,128)(2,1)S(1)} collective-permute-done((bf16[640,256]{1,0:T(8,128)(2,1)S(1)}, bf16[640,256]{1,0:T(8,128)(2,1)S(1)}, u32[]{:S(2)}, u32[]{:S(2)}) %collective-permute-start.11) | collective-permute-done | bytes 327712 | tf_op jit(solution)/shard_map/ppermute | solution.py:449
  221.4 3.5 %collective-permute-done.10 = bf16[640,256]{1,0:T(8,128)(2,1)S(1)} collective-permute-done((bf16[640,256]{1,0:T(8,128)(2,1)S(1)}, bf16[640,256]{1,0:T(8,128)(2,1)S(1)}, u32[]{:S(2)}, u32[]{:S(2)}) %collective-permute-start.10) | collective-permute-done | bytes 327712 | tf_op jit(solution)/shard_map/ppermute | solution.py:449
  231.7 7.5 %collective-permute-done.12 = bf16[768,256]{1,0:T(8,128)(2,1)S(1)} collective-permute-done((bf16[768,256]{1,0:T(8,128)(2,1)S(1)}, bf16[768,256]{1,0:T(8,128)(2,1)S(1)}, u32[]{:S(2)}, u32[]{:S(2)}) %collective-permute-start.12) | collective-permute-done | bytes 393248 | tf_op jit(solution)/shard_map/ppermute | solution.py:449
  239.7 7.6 %collective-permute-done.13 = bf16[768,256]{1,0:T(8,128)(2,1)S(1)} collective-permute-done((bf16[768,256]{1,0:T(8,128)(2,1)S(1)}, bf16[768,256]{1,0:T(8,128)(2,1)S(1)}, u32[]{:S(2)}, u32[]{:S(2)}) %collective-permute-start.13) | collective-permute-done | bytes 393248 | tf_op jit(solution)/shard_map/ppermute | solution.py:449
  250.4 4.7 %collective-permute-start.18 = (bf16[128,256]{1,0:T(8,128)(2,1)S(1)}, bf16[128,256]{1,0:T(8,128)(2,1)S(1)}, u32[]{:S(2)}, u32[]{:S(2)}) collective-permute-start(bf16[128,256]{1,0:T(8,128)(2,1)S(1)} %get-tuple-element.80), channel_id=1, source_target_pairs={{2,0},{3,1},{4,2},{5,3},{6,4},{7,5},{0,6},{1,7},{10,8},{11,9},{12,... | collective-permute-start | bytes 196616 | tf_op jit(solution)/shard_map/ppermute | solution.py:449
  257.5 4.1 %collective-permute-done.17 = bf16[128,256]{1,0:T(8,128)(2,1)S(1)} collective-permute-done((bf16[128,256]{1,0:T(8,128)(2,1)S(1)}, bf16[128,256]{1,0:T(8,128)(2,1)S(1)}, u32[]{:S(2)}, u32[]{:S(2)}) %collective-permute-start.17) | collective-permute-done | bytes 65568 | tf_op jit(solution)/shard_map/ppermute | solution.py:449
  (168 shorter events, 50.5 us)
Async XLA Ops:
  3.3 12.2 %all-to-all-start = ((s32[8,1,1536]{2,1,0:T(1,128)}), s32[8,1,1536]{2,1,0:T(1,128)S(1)}, u32[]{:S(2)}, u32[]{:S(2)}) async-start(s32[8,1,1536]{2,1,0:T(1,128)} %bitcast.190), calls=%async_computation | async-start | bytes 98304 | tf_op jit(solution)/shard_map/all_to_all | solution.py:542
  28.2 81.8 %all-to-all-start.1 = ((bf16[8,832,256]{2,1,0:T(8,128)(2,1)}), bf16[8,832,256]{2,1,0:T(8,128)(2,1)}, u32[]{:S(2)}, u32[]{:S(2)}) async-start(bf16[8,832,256]{2,1,0:T(8,128)(2,1)} %lookup.3), calls=%async_computation.1 | async-start | bytes 6815744 | tf_op jit(solution)/shard_map/all_to_all | solution.py:549
  110.0 70.3 %all-to-all-start.2 = ((bf16[8,704,256]{2,1,0:T(8,128)(2,1)}), bf16[8,704,256]{2,1,0:T(8,128)(2,1)}, u32[]{:S(2)}, u32[]{:S(2)}) async-start(bf16[8,704,256]{2,1,0:T(8,128)(2,1)} %lookup.2), calls=%async_computation.2 | async-start | bytes 5767168 | tf_op jit(solution)/shard_map/all_to_all | solution.py:588
  149.1 7.6 %collective-permute-start = (s32[11,128]{1,0:T(8,128)S(1)}, s32[11,128]{1,0:T(8,128)S(1)}, u32[]{:S(2)}, u32[]{:S(2)}) collective-permute-start(s32[11,128]{1,0:T(8,128)S(1)} %pad_add_fusion.1), channel_id=1, source_target_pairs={{8,0},{16,8},{24,16},{0,24},{9,1},{17,9},{25,17},{1,25},{10,2},{18... | collective-permute-start | bytes 16904 | tf_op jit(solution)/shard_map/ppermute | solution.py:449
  151.6 5.2 %collective-permute-start.1 = (s32[11,128]{1,0:T(8,128)S(1)}, s32[11,128]{1,0:T(8,128)S(1)}, u32[]{:S(2)}, u32[]{:S(2)}) collective-permute-start(s32[11,128]{1,0:T(8,128)S(1)} %pad_add_fusion.1), channel_id=1, source_target_pairs={{16,0},{24,8},{0,16},{8,24},{17,1},{25,9},{1,17},{9,25},{18,2},{26... | collective-permute-start | bytes 16904 | tf_op jit(solution)/shard_map/ppermute | solution.py:449
  152.1 4.7 %collective-permute-start.2 = (s32[11,128]{1,0:T(8,128)S(1)}, s32[11,128]{1,0:T(8,128)S(1)}, u32[]{:S(2)}, u32[]{:S(2)}) collective-permute-start(s32[11,128]{1,0:T(8,128)S(1)} %pad_add_fusion.1), channel_id=1, source_target_pairs={{24,0},{0,8},{8,16},{16,24},{25,1},{1,9},{9,17},{17,25},{26,2},{2,... | collective-permute-start | bytes 16904 | tf_op jit(solution)/shard_map/ppermute | solution.py:449
  152.7 5.4 %collective-permute-start.3 = (bf16[128,256]{1,0:T(8,128)(2,1)S(1)}, bf16[128,256]{1,0:T(8,128)(2,1)S(1)}, u32[]{:S(2)}, u32[]{:S(2)}) collective-permute-start(bf16[128,256]{1,0:T(8,128)(2,1)S(1)} %bitcast.186), channel_id=1, source_target_pairs={{8,0},{16,8},{24,16},{0,24},{9,1},{17,9},{25,17},{1,25},{10,2},{18... | collective-permute-start | bytes 196616 | tf_op jit(solution)/shard_map/ppermute | solution.py:449
  155.1 4.3 %collective-permute-start.4 = (bf16[128,256]{1,0:T(8,128)(2,1)S(1)}, bf16[128,256]{1,0:T(8,128)(2,1)S(1)}, u32[]{:S(2)}, u32[]{:S(2)}) collective-permute-start(bf16[128,256]{1,0:T(8,128)(2,1)S(1)} %bitcast.187), channel_id=1, source_target_pairs={{16,0},{24,8},{0,16},{8,24},{17,1},{25,9},{1,17},{9,25},{18,2},{26... | collective-permute-start | bytes 196616 | tf_op jit(solution)/shard_map/ppermute | solution.py:449
  156.7 5.2 %collective-permute-start.5 = (bf16[128,256]{1,0:T(8,128)(2,1)S(1)}, bf16[128,256]{1,0:T(8,128)(2,1)S(1)}, u32[]{:S(2)}, u32[]{:S(2)}) collective-permute-start(bf16[128,256]{1,0:T(8,128)(2,1)S(1)} %bitcast.189), channel_id=1, source_target_pairs={{24,0},{0,8},{8,16},{16,24},{25,1},{1,9},{9,17},{17,25},{26,2},{2,... | collective-permute-start | bytes 196616 | tf_op jit(solution)/shard_map/ppermute | solution.py:449
  187.9 17.2 %collective-permute-start.8 = (bf16[768,256]{1,0:T(8,128)(2,1)S(1)}, bf16[768,256]{1,0:T(8,128)(2,1)S(1)}, u32[]{:S(2)}, u32[]{:S(2)}) collective-permute-start(bf16[768,256]{1,0:T(8,128)(2,1)S(1)} %get-tuple-element.62), channel_id=1, source_target_pairs={{8,0},{16,8},{24,16},{0,24},{9,1},{17,9},{25,17},{1,25},{10,2},{18... | collective-permute-start | bytes 1179656 | tf_op jit(solution)/shard_map/ppermute | solution.py:449
  190.4 18.8 %collective-permute-start.7 = (bf16[768,256]{1,0:T(8,128)(2,1)S(1)}, bf16[768,256]{1,0:T(8,128)(2,1)S(1)}, u32[]{:S(2)}, u32[]{:S(2)}) collective-permute-start(bf16[768,256]{1,0:T(8,128)(2,1)S(1)} %get-tuple-element.61), channel_id=1, source_target_pairs={{16,0},{24,8},{0,16},{8,24},{17,1},{25,9},{1,17},{9,25},{18,2},{26... | collective-permute-start | bytes 1179656 | tf_op jit(solution)/shard_map/ppermute | solution.py:449
  196.7 12.5 %collective-permute-start.6 = (bf16[768,256]{1,0:T(8,128)(2,1)S(1)}, bf16[768,256]{1,0:T(8,128)(2,1)S(1)}, u32[]{:S(2)}, u32[]{:S(2)}) collective-permute-start(bf16[768,256]{1,0:T(8,128)(2,1)S(1)} %get-tuple-element.60), channel_id=1, source_target_pairs={{24,0},{0,8},{8,16},{16,24},{25,1},{1,9},{9,17},{17,25},{26,2},{2,... | collective-permute-start | bytes 1179656 | tf_op jit(solution)/shard_map/ppermute | solution.py:449
  210.0 11.4 %collective-permute-start.11 = (bf16[640,256]{1,0:T(8,128)(2,1)S(1)}, bf16[640,256]{1,0:T(8,128)(2,1)S(1)}, u32[]{:S(2)}, u32[]{:S(2)}) collective-permute-start(bf16[640,256]{1,0:T(8,128)(2,1)S(1)} %pad_maximum_fusion.2), channel_id=1, source_target_pairs={{24,0},{0,8},{8,16},{16,24},{25,1},{1,9},{9,17},{17,25},{26,2},{2,... | collective-permute-start | bytes 983048 | tf_op jit(solution)/shard_map/ppermute | solution.py:449
  210.4 14.5 %collective-permute-start.10 = (bf16[640,256]{1,0:T(8,128)(2,1)S(1)}, bf16[640,256]{1,0:T(8,128)(2,1)S(1)}, u32[]{:S(2)}, u32[]{:S(2)}) collective-permute-start(bf16[640,256]{1,0:T(8,128)(2,1)S(1)} %pad_maximum_fusion.2), channel_id=1, source_target_pairs={{16,0},{24,8},{0,16},{8,24},{17,1},{25,9},{1,17},{9,25},{18,2},{26... | collective-permute-start | bytes 983048 | tf_op jit(solution)/shard_map/ppermute | solution.py:449
  211.1 13.7 %collective-permute-start.9 = (bf16[640,256]{1,0:T(8,128)(2,1)S(1)}, bf16[640,256]{1,0:T(8,128)(2,1)S(1)}, u32[]{:S(2)}, u32[]{:S(2)}) collective-permute-start(bf16[640,256]{1,0:T(8,128)(2,1)S(1)} %pad_maximum_fusion.2), channel_id=1, source_target_pairs={{8,0},{16,8},{24,16},{0,24},{9,1},{17,9},{25,17},{1,25},{10,2},{18... | collective-permute-start | bytes 983048 | tf_op jit(solution)/shard_map/ppermute | solution.py:449
  227.4 12.0 %collective-permute-start.14 = (bf16[768,256]{1,0:T(8,128)(2,1)S(1)}, bf16[768,256]{1,0:T(8,128)(2,1)S(1)}, u32[]{:S(2)}, u32[]{:S(2)}) collective-permute-start(bf16[768,256]{1,0:T(8,128)(2,1)S(1)} %fusion.2), channel_id=1, source_target_pairs={{8,0},{16,8},{24,16},{0,24},{9,1},{17,9},{25,17},{1,25},{10,2},{18... | collective-permute-start | bytes 1179656 | tf_op jit(solution)/shard_map/ppermute | solution.py:449
  229.6 9.5 %collective-permute-start.12 = (bf16[768,256]{1,0:T(8,128)(2,1)S(1)}, bf16[768,256]{1,0:T(8,128)(2,1)S(1)}, u32[]{:S(2)}, u32[]{:S(2)}) collective-permute-start(bf16[768,256]{1,0:T(8,128)(2,1)S(1)} %fusion.2), channel_id=1, source_target_pairs={{16,0},{24,8},{0,16},{8,24},{17,1},{25,9},{1,17},{9,25},{18,2},{26... | collective-permute-start | bytes 1179656 | tf_op jit(solution)/shard_map/ppermute | solution.py:449
  230.5 16.7 %collective-permute-start.13 = (bf16[768,256]{1,0:T(8,128)(2,1)S(1)}, bf16[768,256]{1,0:T(8,128)(2,1)S(1)}, u32[]{:S(2)}, u32[]{:S(2)}) collective-permute-start(bf16[768,256]{1,0:T(8,128)(2,1)S(1)} %fusion.2), channel_id=1, source_target_pairs={{24,0},{0,8},{8,16},{16,24},{25,1},{1,9},{9,17},{17,25},{26,2},{2,... | collective-permute-start | bytes 1179656 | tf_op jit(solution)/shard_map/ppermute | solution.py:449
  250.4 7.2 %collective-permute-start.18 = (bf16[128,256]{1,0:T(8,128)(2,1)S(1)}, bf16[128,256]{1,0:T(8,128)(2,1)S(1)}, u32[]{:S(2)}, u32[]{:S(2)}) collective-permute-start(bf16[128,256]{1,0:T(8,128)(2,1)S(1)} %get-tuple-element.80), channel_id=1, source_target_pairs={{2,0},{3,1},{4,2},{5,3},{6,4},{7,5},{0,6},{1,7},{10,8},{11,9},{12,... | collective-permute-start | bytes 196616 | tf_op jit(solution)/shard_map/ppermute | solution.py:449
  255.0 6.6 %collective-permute-start.17 = (bf16[128,256]{1,0:T(8,128)(2,1)S(1)}, bf16[128,256]{1,0:T(8,128)(2,1)S(1)}, u32[]{:S(2)}, u32[]{:S(2)}) collective-permute-start(bf16[128,256]{1,0:T(8,128)(2,1)S(1)} %get-tuple-element.81), channel_id=1, source_target_pairs={{4,0},{5,1},{6,2},{7,3},{0,4},{1,5},{2,6},{3,7},{12,8},{13,9},{14,... | collective-permute-start | bytes 196616 | tf_op jit(solution)/shard_map/ppermute | solution.py:449
  255.0 6.6 %collective-permute-start.16 = (bf16[128,256]{1,0:T(8,128)(2,1)S(1)}, bf16[128,256]{1,0:T(8,128)(2,1)S(1)}, u32[]{:S(2)}, u32[]{:S(2)}) collective-permute-start(bf16[128,256]{1,0:T(8,128)(2,1)S(1)} %get-tuple-element.79), channel_id=1, source_target_pairs={{6,0},{7,1},{0,2},{1,3},{2,4},{3,5},{4,6},{5,7},{14,8},{15,9},{8,1... | collective-permute-start | bytes 196616 | tf_op jit(solution)/shard_map/ppermute | solution.py:449
  261.7 6.9 %collective-permute-start.21 = (bf16[128,256]{1,0:T(8,128)(2,1)S(1)}, bf16[128,256]{1,0:T(8,128)(2,1)S(1)}, u32[]{:S(2)}, u32[]{:S(2)}) collective-permute-start(bf16[128,256]{1,0:T(8,128)(2,1)S(1)} %fusion.16), channel_id=1, source_target_pairs={{6,0},{7,1},{0,2},{1,3},{2,4},{3,5},{4,6},{5,7},{14,8},{15,9},{8,1... | collective-permute-start | bytes 196616 | tf_op jit(solution)/shard_map/ppermute | solution.py:449
  262.1 7.8 %collective-permute-start.20 = (bf16[128,256]{1,0:T(8,128)(2,1)S(1)}, bf16[128,256]{1,0:T(8,128)(2,1)S(1)}, u32[]{:S(2)}, u32[]{:S(2)}) collective-permute-start(bf16[128,256]{1,0:T(8,128)(2,1)S(1)} %fusion.16), channel_id=1, source_target_pairs={{4,0},{5,1},{6,2},{7,3},{0,4},{1,5},{2,6},{3,7},{12,8},{13,9},{14,... | collective-permute-start | bytes 196616 | tf_op jit(solution)/shard_map/ppermute | solution.py:449
  264.3 5.6 %collective-permute-start.19 = (bf16[128,256]{1,0:T(8,128)(2,1)S(1)}, bf16[128,256]{1,0:T(8,128)(2,1)S(1)}, u32[]{:S(2)}, u32[]{:S(2)}) collective-permute-start(bf16[128,256]{1,0:T(8,128)(2,1)S(1)} %fusion.16), channel_id=1, source_target_pairs={{2,0},{3,1},{4,2},{5,3},{6,4},{7,5},{0,6},{1,7},{10,8},{11,9},{12,... | collective-permute-start | bytes 196616 | tf_op jit(solution)/shard_map/ppermute | solution.py:449
  (20 other events, 563.5 us)

commit v16 on v15

--- a/solution.py
+++ b/solution.py
@@ -157,7 +157,7 @@
                     spot = pl.ds(pl.multiple_of(j * TILE * halves, TILE) + h, TILE, stride=halves)
                     table[spot, :] = store_ref[part, lane(h)].astype(jnp.float32)
 
-    @pl.loop(0, width // SLOTS, unroll=2)
+    @pl.loop(0, width // SLOTS, unroll=math.gcd(width // SLOTS, 4))
     def _(j):
         at = [want_ref[begin + j * SLOTS + u] for u in range(SLOTS)]
         rows = [table[pl.ds(pl.multiple_of(a, halves), halves), :] for a in at]

time: 273 us -> 271 us (level)
  transfers between devices with their start and end apart: 26 -> 26, of which waited for: 18 -> 17; matrix products, arithmetic and copies ran while one was open for 5% -> 5% of each run, Pallas kernels for 37% -> 37%
where the time goes in v16:
time: 271 us; the launch traced here: 270 us
  Pallas kernels  122 us (45%)
  waiting for transfers between devices  80.1 us (30%)
  starting transfers between devices  43.1 us (16%)
  local copies, waits for them, and re-layouts  11.3 us (4%)
  other arithmetic  5.76 us (2%)
  matrix products  4.92 us (2%)
  between operations  2.93 us (1%)
    pallas_call x4, Pallas kernels, gather_sum(): pl.pallas_call(functools.partial(gather_sum_body, piece, last, row0), out...  51.2 us
    pallas_call x1, Pallas kernels, adjacency(): pl.pallas_call(functools.partial(adjacency_body, tiles), out_shape=jax.Sh...  47.8 us
    ppermute x21, waiting for transfers between devices, passed(): lax.ppermute(part, axis, [((i + shift) % parts, i) for i in range(parts)])  42.8 us
    ppermute x21, starting transfers between devices, passed(): lax.ppermute(part, axis, [((i + shift) % parts, i) for i in range(parts)])  27.6 us
    pallas_call x2, Pallas kernels, lookup(): pl.pallas_call(functools.partial(lookup_body, places.shape[0] // groups,...  20 us
    all_to_all x1, waiting for transfers between devices, local(): lax.all_to_all(looked, 'batch', split_axis=0, concat_axis=0, tiled=True)  17.7 us
    all_to_all x1, waiting for transfers between devices, local(): lax.all_to_all(looked_a, 'batch', split_axis=0, concat_axis=0, tiled=True)  12.4 us
    all_to_all x1, starting transfers between devices, local(): lax.all_to_all(requests.reshape(batch_count, capacity), 'batch', split_ax...  6.34 us
  transfers between devices with their start and end apart: 26, of which 17 were waited for; matrix products, arithmetic and copies ran while one was open for 5% of the time, Pallas kernels for 37%

profile of v16, /device:TPU:0, one launch (start us, length us, event | category | flops | bytes accessed | tf_op | source)
XLA Modules:
  0.0 269.8 jit_solution(6180574629703402021)
XLA Ops:
  0.6 2.6 requests.1
  3.3 6.3 %all-to-all-start = ((s32[8,1,1536]{2,1,0:T(1,128)}), s32[8,1,1536]{2,1,0:T(1,128)S(1)}, u32[]{:S(2)}, u32[]{:S(2)}) async-start(s32[8,1,1536]{2,1,0:T(1,128)} %bitcast.190), calls=%async_computation | async-start | bytes 98304 | tf_op jit(solution)/shard_map/all_to_all | solution.py:542
  10.6 4.9 %all-to-all-done = s32[8,1,1536]{2,1,0:T(1,128)S(1)} async-done(((s32[8,1,1536]{2,1,0:T(1,128)}), s32[8,1,1536]{2,1,0:T(1,128)S(1)}, u32[]{:S(2)}, u32[]{:S(2)}) %all-to-all-start) | async-done | bytes 49184 | tf_op jit(solution)/shard_map/all_to_all | solution.py:542
  16.1 11.2 %lookup.3 = bf16[8,832,256]{2,1,0:T(8,128)(2,1)} custom-call(s32[12288]{0:T(1024)} %bitcast.159, bf16[8192,256]{1,0:T(8,128)(2,1)} %store_in.3), custom_call_target="tpu_custom_call" | custom-call | flops 68157440 | bytes 4194304 | tf_op jit(solution)/shard_map/lookup/pallas_call | solution.py:176
  27.3 4.6 %all-to-all-start.1 = ((bf16[8,832,256]{2,1,0:T(8,128)(2,1)}), bf16[8,832,256]{2,1,0:T(8,128)(2,1)}, u32[]{:S(2)}, u32[]{:S(2)}) async-start(bf16[8,832,256]{2,1,0:T(8,128)(2,1)} %lookup.3), calls=%async_computation.1 | async-start | bytes 6815744 | tf_op jit(solution)/shard_map/all_to_all | solution.py:549
  40.1 8.8 %lookup.2 = bf16[8,704,256]{2,1,0:T(8,128)(2,1)} custom-call(s32[12288]{0:T(1024)S(1)} %bitcast.160, bf16[8192,256]{1,0:T(8,128)(2,1)S(1)} %copy-done.3), custom_call_target="tpu_custom_call" | custom-call | flops 57671680 | bytes 4194304 | tf_op jit(solution)/shard_map/lookup/pallas_call | solution.py:176
  48.9 47.8 %adjacency.1.adj_ref = f8e4m3fn[28,3072,256]{2,1,0:T(32,128)(4,1)} custom-call(s32[1]{0:T(128)} %bitcast.11.me_ref, s32[192,256]{1,0:T(8,128)S(1)} %reshape.242.near_ref, bf16[256,128]{1,0:T(8,128)(2,1)S(1)} %pad_maximum_fusion.4.table_ref), custom_call_target="tpu_custom_call" | custom-call | flops 22548578304 | bytes 22020096 | tf_op jit(solution)/shard_map/adjacency/pallas_call | solution.py:239
  96.7 12.4 %all-to-all-done.1.answer_ref = bf16[8,832,256]{2,1,0:T(8,128)(2,1)} async-done(((bf16[8,832,256]{2,1,0:T(8,128)(2,1)}), bf16[8,832,256]{2,1,0:T(8,128)(2,1)}, u32[]{:S(2)}, u32[]{:S(2)}) %all-to-all-start.1) | async-done | bytes 3407904 | tf_op jit(solution)/shard_map/all_to_all | solution.py:549
  109.1 4.4 %all-to-all-start.2 = ((bf16[8,704,256]{2,1,0:T(8,128)(2,1)}), bf16[8,704,256]{2,1,0:T(8,128)(2,1)}, u32[]{:S(2)}, u32[]{:S(2)}) async-start(bf16[8,704,256]{2,1,0:T(8,128)(2,1)} %lookup.2), calls=%async_computation.2 | async-start | bytes 5767168 | tf_op jit(solution)/shard_map/all_to_all | solution.py:588
  116.7 32.2 %gather_sum.4 = (f32[3072,256]{1,0:T(8,128)}, f32[3072,256]{1,0:T(8,128)}) custom-call(s32[2]{0:T(128)S(1)} %pad_add_fusion.4.spans_ref, s32[8]{0:T(128)S(1)} %get-tuple-element.88.counts_ref, s32[9]{0:T(128)S(1)} %get-tuple-element.90.starts_ref, s32[56]{0:T(128)S(1)} %reshape.248.own_here_ref, bf16[8,832,256]{2,1,0:T(8,128)(2,1)} %all-to-all-done.1.answer_ref, ...), custom_call_target="tpu_custom_call" | custom-call | flops 11274289152 | bytes 786432 | tf_op jit(solution)/shard_map/gather_sum/pallas_call | solution.py:418
  148.9 2.5 collective-permute-start
  159.1 2.6 collective-permute-done.5
  161.8 17.7 %all-to-all-done.2.answer_ref = bf16[8,704,256]{2,1,0:T(8,128)(2,1)} async-done(((bf16[8,704,256]{2,1,0:T(8,128)(2,1)}), bf16[8,704,256]{2,1,0:T(8,128)(2,1)}, u32[]{:S(2)}, u32[]{:S(2)}) %all-to-all-start.2) | async-done | bytes 2883616 | tf_op jit(solution)/shard_map/all_to_all | solution.py:588
  179.5 7.6 %gather_sum.5 = (bf16[1536,256]{1,0:T(8,128)(2,1)S(1)}, bf16[1536,256]{1,0:T(8,128)(2,1)S(1)}, bf16[768,256]{1,0:T(8,128)(2,1)S(1)}, bf16[768,256]{1,0:T(8,128)(2,1)S(1)}) custom-call(s32[2]{0:T(128)S(1)} %pad_add_fusion.5.spans_ref, s32[8]{0:T(128)S(1)} %get-tuple-element.87.counts_ref, s32[9]{0:T(128)S(1)} %get-tuple-element.89.starts_ref, ...), custom_call_target="tpu_custom_call" | custom-call | flops 1409286144 | bytes 393216 | tf_op jit(solution)/shard_map/gather_sum/pallas_call | solution.py:418
  187.1 2.5 collective-permute-start.8
  190.1 5.8 %gather_sum.6 = (bf16[768,256]{1,0:T(8,128)(2,1)S(1)}, bf16[768,256]{1,0:T(8,128)(2,1)S(1)}, bf16[768,256]{1,0:T(8,128)(2,1)S(1)}) custom-call(s32[2]{0:T(128)S(1)} %pad_add_fusion.5.spans_ref, s32[8]{0:T(128)S(1)} %get-tuple-element.87.counts_ref, s32[9]{0:T(128)S(1)} %get-tuple-element.89.starts_ref, s32[56]{0:T(128)S(1)} %reshape.248.own_here_ref, ...), custom_call_target="tpu_custom_call" | custom-call | flops 704643072 | bytes 196608 | tf_op jit(solution)/shard_map/gather_sum/pallas_call | solution.py:418
  198.8 5.6 %gather_sum.7 = (bf16[768,256]{1,0:T(8,128)(2,1)S(1)}, bf16[768,256]{1,0:T(8,128)(2,1)S(1)}, bf16[768,256]{1,0:T(8,128)(2,1)S(1)}) custom-call(s32[2]{0:T(128)S(1)} %pad_add_fusion.5.spans_ref, s32[8]{0:T(128)S(1)} %get-tuple-element.87.counts_ref, s32[9]{0:T(128)S(1)} %get-tuple-element.89.starts_ref, s32[56]{0:T(128)S(1)} %reshape.248.own_here_ref, ...), custom_call_target="tpu_custom_call" | custom-call | flops 704643072 | bytes 196608 | tf_op jit(solution)/shard_map/gather_sum/pallas_call | solution.py:418
  204.4 3.9 %collective-permute-done.7 = bf16[768,256]{1,0:T(8,128)(2,1)S(1)} collective-permute-done((bf16[768,256]{1,0:T(8,128)(2,1)S(1)}, bf16[768,256]{1,0:T(8,128)(2,1)S(1)}, u32[]{:S(2)}, u32[]{:S(2)}) %collective-permute-start.7) | collective-permute-done | bytes 393248 | tf_op jit(solution)/shard_map/ppermute | solution.py:449
  212.7 7.8 %collective-permute-done.11 = bf16[640,256]{1,0:T(8,128)(2,1)S(1)} collective-permute-done((bf16[640,256]{1,0:T(8,128)(2,1)S(1)}, bf16[640,256]{1,0:T(8,128)(2,1)S(1)}, u32[]{:S(2)}, u32[]{:S(2)}) %collective-permute-start.11) | collective-permute-done | bytes 327712 | tf_op jit(solution)/shard_map/ppermute | solution.py:449
  220.5 3.4 %collective-permute-done.10 = bf16[640,256]{1,0:T(8,128)(2,1)S(1)} collective-permute-done((bf16[640,256]{1,0:T(8,128)(2,1)S(1)}, bf16[640,256]{1,0:T(8,128)(2,1)S(1)}, u32[]{:S(2)}, u32[]{:S(2)}) %collective-permute-start.10) | collective-permute-done | bytes 327712 | tf_op jit(solution)/shard_map/ppermute | solution.py:449
  230.9 7.4 %collective-permute-done.12 = bf16[768,256]{1,0:T(8,128)(2,1)S(1)} collective-permute-done((bf16[768,256]{1,0:T(8,128)(2,1)S(1)}, bf16[768,256]{1,0:T(8,128)(2,1)S(1)}, u32[]{:S(2)}, u32[]{:S(2)}) %collective-permute-start.12) | collective-permute-done | bytes 393248 | tf_op jit(solution)/shard_map/ppermute | solution.py:449
  238.8 7.5 %collective-permute-done.13 = bf16[768,256]{1,0:T(8,128)(2,1)S(1)} collective-permute-done((bf16[768,256]{1,0:T(8,128)(2,1)S(1)}, bf16[768,256]{1,0:T(8,128)(2,1)S(1)}, u32[]{:S(2)}, u32[]{:S(2)}) %collective-permute-start.13) | collective-permute-done | bytes 393248 | tf_op jit(solution)/shard_map/ppermute | solution.py:449
  254.5 4.9 %collective-permute-done.17 = bf16[128,256]{1,0:T(8,128)(2,1)S(1)} collective-permute-done((bf16[128,256]{1,0:T(8,128)(2,1)S(1)}, bf16[128,256]{1,0:T(8,128)(2,1)S(1)}, u32[]{:S(2)}, u32[]{:S(2)}) %collective-permute-start.17) | collective-permute-done | bytes 65568 | tf_op jit(solution)/shard_map/ppermute | solution.py:449
  261.3 2.8 %collective-permute-start.19 = (bf16[128,256]{1,0:T(8,128)(2,1)S(1)}, bf16[128,256]{1,0:T(8,128)(2,1)S(1)}, u32[]{:S(2)}, u32[]{:S(2)}) collective-permute-start(bf16[128,256]{1,0:T(8,128)(2,1)S(1)} %fusion.16), channel_id=1, source_target_pairs={{2,0},{3,1},{4,2},{5,3},{6,4},{7,5},{0,6},{1,7},{10,8},{11,9},{12,... | collective-permute-start | bytes 196616 | tf_op jit(solution)/shard_map/ppermute | solution.py:449
  (168 shorter events, 49.4 us)
Async XLA Ops:
  3.3 12.2 %all-to-all-start = ((s32[8,1,1536]{2,1,0:T(1,128)}), s32[8,1,1536]{2,1,0:T(1,128)S(1)}, u32[]{:S(2)}, u32[]{:S(2)}) async-start(s32[8,1,1536]{2,1,0:T(1,128)} %bitcast.190), calls=%async_computation | async-start | bytes 98304 | tf_op jit(solution)/shard_map/all_to_all | solution.py:542
  27.3 81.8 %all-to-all-start.1 = ((bf16[8,832,256]{2,1,0:T(8,128)(2,1)}), bf16[8,832,256]{2,1,0:T(8,128)(2,1)}, u32[]{:S(2)}, u32[]{:S(2)}) async-start(bf16[8,832,256]{2,1,0:T(8,128)(2,1)} %lookup.3), calls=%async_computation.1 | async-start | bytes 6815744 | tf_op jit(solution)/shard_map/all_to_all | solution.py:549
  109.1 70.3 %all-to-all-start.2 = ((bf16[8,704,256]{2,1,0:T(8,128)(2,1)}), bf16[8,704,256]{2,1,0:T(8,128)(2,1)}, u32[]{:S(2)}, u32[]{:S(2)}) async-start(bf16[8,704,256]{2,1,0:T(8,128)(2,1)} %lookup.2), calls=%async_computation.2 | async-start | bytes 5767168 | tf_op jit(solution)/shard_map/all_to_all | solution.py:588
  148.9 7.6 %collective-permute-start = (s32[11,128]{1,0:T(8,128)S(1)}, s32[11,128]{1,0:T(8,128)S(1)}, u32[]{:S(2)}, u32[]{:S(2)}) collective-permute-start(s32[11,128]{1,0:T(8,128)S(1)} %pad_add_fusion.1), channel_id=1, source_target_pairs={{8,0},{16,8},{24,16},{0,24},{9,1},{17,9},{25,17},{1,25},{10,2},{18... | collective-permute-start | bytes 16904 | tf_op jit(solution)/shard_map/ppermute | solution.py:449
  151.4 5.2 %collective-permute-start.1 = (s32[11,128]{1,0:T(8,128)S(1)}, s32[11,128]{1,0:T(8,128)S(1)}, u32[]{:S(2)}, u32[]{:S(2)}) collective-permute-start(s32[11,128]{1,0:T(8,128)S(1)} %pad_add_fusion.1), channel_id=1, source_target_pairs={{16,0},{24,8},{0,16},{8,24},{17,1},{25,9},{1,17},{9,25},{18,2},{26... | collective-permute-start | bytes 16904 | tf_op jit(solution)/shard_map/ppermute | solution.py:449
  151.9 4.7 %collective-permute-start.2 = (s32[11,128]{1,0:T(8,128)S(1)}, s32[11,128]{1,0:T(8,128)S(1)}, u32[]{:S(2)}, u32[]{:S(2)}) collective-permute-start(s32[11,128]{1,0:T(8,128)S(1)} %pad_add_fusion.1), channel_id=1, source_target_pairs={{24,0},{0,8},{8,16},{16,24},{25,1},{1,9},{9,17},{17,25},{26,2},{2,... | collective-permute-start | bytes 16904 | tf_op jit(solution)/shard_map/ppermute | solution.py:449
  152.5 4.8 %collective-permute-start.3 = (bf16[128,256]{1,0:T(8,128)(2,1)S(1)}, bf16[128,256]{1,0:T(8,128)(2,1)S(1)}, u32[]{:S(2)}, u32[]{:S(2)}) collective-permute-start(bf16[128,256]{1,0:T(8,128)(2,1)S(1)} %bitcast.186), channel_id=1, source_target_pairs={{8,0},{16,8},{24,16},{0,24},{9,1},{17,9},{25,17},{1,25},{10,2},{18... | collective-permute-start | bytes 196616 | tf_op jit(solution)/shard_map/ppermute | solution.py:449
  154.9 4.3 %collective-permute-start.4 = (bf16[128,256]{1,0:T(8,128)(2,1)S(1)}, bf16[128,256]{1,0:T(8,128)(2,1)S(1)}, u32[]{:S(2)}, u32[]{:S(2)}) collective-permute-start(bf16[128,256]{1,0:T(8,128)(2,1)S(1)} %bitcast.187), channel_id=1, source_target_pairs={{16,0},{24,8},{0,16},{8,24},{17,1},{25,9},{1,17},{9,25},{18,2},{26... | collective-permute-start | bytes 196616 | tf_op jit(solution)/shard_map/ppermute | solution.py:449
  156.5 5.2 %collective-permute-start.5 = (bf16[128,256]{1,0:T(8,128)(2,1)S(1)}, bf16[128,256]{1,0:T(8,128)(2,1)S(1)}, u32[]{:S(2)}, u32[]{:S(2)}) collective-permute-start(bf16[128,256]{1,0:T(8,128)(2,1)S(1)} %bitcast.189), channel_id=1, source_target_pairs={{24,0},{0,8},{8,16},{16,24},{25,1},{1,9},{9,17},{17,25},{26,2},{2,... | collective-permute-start | bytes 196616 | tf_op jit(solution)/shard_map/ppermute | solution.py:449
  187.1 17.4 %collective-permute-start.8 = (bf16[768,256]{1,0:T(8,128)(2,1)S(1)}, bf16[768,256]{1,0:T(8,128)(2,1)S(1)}, u32[]{:S(2)}, u32[]{:S(2)}) collective-permute-start(bf16[768,256]{1,0:T(8,128)(2,1)S(1)} %get-tuple-element.62), channel_id=1, source_target_pairs={{8,0},{16,8},{24,16},{0,24},{9,1},{17,9},{25,17},{1,25},{10,2},{18... | collective-permute-start | bytes 1179656 | tf_op jit(solution)/shard_map/ppermute | solution.py:449
  189.6 18.7 %collective-permute-start.7 = (bf16[768,256]{1,0:T(8,128)(2,1)S(1)}, bf16[768,256]{1,0:T(8,128)(2,1)S(1)}, u32[]{:S(2)}, u32[]{:S(2)}) collective-permute-start(bf16[768,256]{1,0:T(8,128)(2,1)S(1)} %get-tuple-element.61), channel_id=1, source_target_pairs={{16,0},{24,8},{0,16},{8,24},{17,1},{25,9},{1,17},{9,25},{18,2},{26... | collective-permute-start | bytes 1179656 | tf_op jit(solution)/shard_map/ppermute | solution.py:449
  195.9 12.4 %collective-permute-start.6 = (bf16[768,256]{1,0:T(8,128)(2,1)S(1)}, bf16[768,256]{1,0:T(8,128)(2,1)S(1)}, u32[]{:S(2)}, u32[]{:S(2)}) collective-permute-start(bf16[768,256]{1,0:T(8,128)(2,1)S(1)} %get-tuple-element.60), channel_id=1, source_target_pairs={{24,0},{0,8},{8,16},{16,24},{25,1},{1,9},{9,17},{17,25},{26,2},{2,... | collective-permute-start | bytes 1179656 | tf_op jit(solution)/shard_map/ppermute | solution.py:449
  209.1 11.4 %collective-permute-start.11 = (bf16[640,256]{1,0:T(8,128)(2,1)S(1)}, bf16[640,256]{1,0:T(8,128)(2,1)S(1)}, u32[]{:S(2)}, u32[]{:S(2)}) collective-permute-start(bf16[640,256]{1,0:T(8,128)(2,1)S(1)} %pad_maximum_fusion.2), channel_id=1, source_target_pairs={{24,0},{0,8},{8,16},{16,24},{25,1},{1,9},{9,17},{17,25},{26,2},{2,... | collective-permute-start | bytes 983048 | tf_op jit(solution)/shard_map/ppermute | solution.py:449
  209.5 14.5 %collective-permute-start.10 = (bf16[640,256]{1,0:T(8,128)(2,1)S(1)}, bf16[640,256]{1,0:T(8,128)(2,1)S(1)}, u32[]{:S(2)}, u32[]{:S(2)}) collective-permute-start(bf16[640,256]{1,0:T(8,128)(2,1)S(1)} %pad_maximum_fusion.2), channel_id=1, source_target_pairs={{16,0},{24,8},{0,16},{8,24},{17,1},{25,9},{1,17},{9,25},{18,2},{26... | collective-permute-start | bytes 983048 | tf_op jit(solution)/shard_map/ppermute | solution.py:449
  210.3 13.7 %collective-permute-start.9 = (bf16[640,256]{1,0:T(8,128)(2,1)S(1)}, bf16[640,256]{1,0:T(8,128)(2,1)S(1)}, u32[]{:S(2)}, u32[]{:S(2)}) collective-permute-start(bf16[640,256]{1,0:T(8,128)(2,1)S(1)} %pad_maximum_fusion.2), channel_id=1, source_target_pairs={{8,0},{16,8},{24,16},{0,24},{9,1},{17,9},{25,17},{1,25},{10,2},{18... | collective-permute-start | bytes 983048 | tf_op jit(solution)/shard_map/ppermute | solution.py:449
  226.5 12.0 %collective-permute-start.14 = (bf16[768,256]{1,0:T(8,128)(2,1)S(1)}, bf16[768,256]{1,0:T(8,128)(2,1)S(1)}, u32[]{:S(2)}, u32[]{:S(2)}) collective-permute-start(bf16[768,256]{1,0:T(8,128)(2,1)S(1)} %fusion.2), channel_id=1, source_target_pairs={{8,0},{16,8},{24,16},{0,24},{9,1},{17,9},{25,17},{1,25},{10,2},{18... | collective-permute-start | bytes 1179656 | tf_op jit(solution)/shard_map/ppermute | solution.py:449
  228.8 9.5 %collective-permute-start.12 = (bf16[768,256]{1,0:T(8,128)(2,1)S(1)}, bf16[768,256]{1,0:T(8,128)(2,1)S(1)}, u32[]{:S(2)}, u32[]{:S(2)}) collective-permute-start(bf16[768,256]{1,0:T(8,128)(2,1)S(1)} %fusion.2), channel_id=1, source_target_pairs={{16,0},{24,8},{0,16},{8,24},{17,1},{25,9},{1,17},{9,25},{18,2},{26... | collective-permute-start | bytes 1179656 | tf_op jit(solution)/shard_map/ppermute | solution.py:449
  229.7 16.7 %collective-permute-start.13 = (bf16[768,256]{1,0:T(8,128)(2,1)S(1)}, bf16[768,256]{1,0:T(8,128)(2,1)S(1)}, u32[]{:S(2)}, u32[]{:S(2)}) collective-permute-start(bf16[768,256]{1,0:T(8,128)(2,1)S(1)} %fusion.2), channel_id=1, source_target_pairs={{24,0},{0,8},{8,16},{16,24},{25,1},{1,9},{9,17},{17,25},{26,2},{2,... | collective-permute-start | bytes 1179656 | tf_op jit(solution)/shard_map/ppermute | solution.py:449
  249.4 5.0 %collective-permute-start.18 = (bf16[128,256]{1,0:T(8,128)(2,1)S(1)}, bf16[128,256]{1,0:T(8,128)(2,1)S(1)}, u32[]{:S(2)}, u32[]{:S(2)}) collective-permute-start(bf16[128,256]{1,0:T(8,128)(2,1)S(1)} %get-tuple-element.80), channel_id=1, source_target_pairs={{2,0},{3,1},{4,2},{5,3},{6,4},{7,5},{0,6},{1,7},{10,8},{11,9},{12,... | collective-permute-start | bytes 196616 | tf_op jit(solution)/shard_map/ppermute | solution.py:449
  251.8 7.6 %collective-permute-start.17 = (bf16[128,256]{1,0:T(8,128)(2,1)S(1)}, bf16[128,256]{1,0:T(8,128)(2,1)S(1)}, u32[]{:S(2)}, u32[]{:S(2)}) collective-permute-start(bf16[128,256]{1,0:T(8,128)(2,1)S(1)} %get-tuple-element.81), channel_id=1, source_target_pairs={{4,0},{5,1},{6,2},{7,3},{0,4},{1,5},{2,6},{3,7},{12,8},{13,9},{14,... | collective-permute-start | bytes 196616 | tf_op jit(solution)/shard_map/ppermute | solution.py:449
  252.5 6.8 %collective-permute-start.16 = (bf16[128,256]{1,0:T(8,128)(2,1)S(1)}, bf16[128,256]{1,0:T(8,128)(2,1)S(1)}, u32[]{:S(2)}, u32[]{:S(2)}) collective-permute-start(bf16[128,256]{1,0:T(8,128)(2,1)S(1)} %get-tuple-element.79), channel_id=1, source_target_pairs={{6,0},{7,1},{0,2},{1,3},{2,4},{3,5},{4,6},{5,7},{14,8},{15,9},{8,1... | collective-permute-start | bytes 196616 | tf_op jit(solution)/shard_map/ppermute | solution.py:449
  259.4 6.8 %collective-permute-start.21 = (bf16[128,256]{1,0:T(8,128)(2,1)S(1)}, bf16[128,256]{1,0:T(8,128)(2,1)S(1)}, u32[]{:S(2)}, u32[]{:S(2)}) collective-permute-start(bf16[128,256]{1,0:T(8,128)(2,1)S(1)} %fusion.16), channel_id=1, source_target_pairs={{6,0},{7,1},{0,2},{1,3},{2,4},{3,5},{4,6},{5,7},{14,8},{15,9},{8,1... | collective-permute-start | bytes 196616 | tf_op jit(solution)/shard_map/ppermute | solution.py:449
  259.4 7.3 %collective-permute-start.20 = (bf16[128,256]{1,0:T(8,128)(2,1)S(1)}, bf16[128,256]{1,0:T(8,128)(2,1)S(1)}, u32[]{:S(2)}, u32[]{:S(2)}) collective-permute-start(bf16[128,256]{1,0:T(8,128)(2,1)S(1)} %fusion.16), channel_id=1, source_target_pairs={{4,0},{5,1},{6,2},{7,3},{0,4},{1,5},{2,6},{3,7},{12,8},{13,9},{14,... | collective-permute-start | bytes 196616 | tf_op jit(solution)/shard_map/ppermute | solution.py:449
  261.3 5.5 %collective-permute-start.19 = (bf16[128,256]{1,0:T(8,128)(2,1)S(1)}, bf16[128,256]{1,0:T(8,128)(2,1)S(1)}, u32[]{:S(2)}, u32[]{:S(2)}) collective-permute-start(bf16[128,256]{1,0:T(8,128)(2,1)S(1)} %fusion.16), channel_id=1, source_target_pairs={{2,0},{3,1},{4,2},{5,3},{6,4},{7,5},{0,6},{1,7},{10,8},{11,9},{12,... | collective-permute-start | bytes 196616 | tf_op jit(solution)/shard_map/ppermute | solution.py:449
  (20 other events, 564.5 us)

commit v17 on v16

--- a/solution.py
+++ b/solution.py
@@ -299,12 +299,12 @@
 ):
     if last:
         (total_in, found_in, wself_in, wneigh_in, own_ref, mean_ref) = refs[:6]
-        share_refs = refs[6:-11]
-        packed, tiles_ref, ready, landed, arrived, notes_ref, carried = refs[-11:-4]
-        total_ref, found_ref, wself_ref, wneigh_ref = refs[-4:]
+        share_refs = refs[6:-13]
+        packed, tiles_ref, ready, landed, arrived, notes_ref, carried = refs[-13:-6]
+        total_ref, found_ref, before_ref, had_ref, wself_ref, wneigh_ref = refs[-6:]
         mine = pl.ds(row0, total_ref.shape[0])
-        pairs = ((notes_in.at[mine], notes_ref), (total_in.at[mine], total_ref))
-        pairs += ((found_in.at[mine], found_ref),)
+        pairs = ((notes_in.at[mine], notes_ref), (total_in.at[mine], before_ref))
+        pairs += ((found_in.at[mine], had_ref),)
         pairs += ((wself_in, wself_ref), (wneigh_in, wneigh_ref))
     else:
         total_ref, found_ref, packed, tiles_ref, ready, landed, arrived, notes_ref, carried = refs
@@ -328,11 +328,9 @@
     for copy in carry:
         copy.start()
     collect(piece, counts_ref, starts_ref, answer_ref, landed, arrived, packed)
-    for copy in carry:
-        copy.wait()
-    if not last:
-        total_ref[...] = jnp.zeros(total_ref.shape, jnp.float32)
-        found_ref[...] = jnp.zeros(found_ref.shape, jnp.float32)
+    total_ref[...] = jnp.zeros(total_ref.shape, jnp.float32)
+    found_ref[...] = jnp.zeros(found_ref.shape, jnp.float32)
+    carry[0].wait()
 
     @pl.loop(0, count)
     def _(step):
@@ -369,14 +367,16 @@
                 total_ref[part, :] += both[:rows]
                 found_ref[part, :] += both[rows:]
 
+    for copy in carry[1:]:
+        copy.wait()
     if last:
         share = share_refs[0].shape[0]
         step_rows = math.gcd(share, 3 * TILE)
         for p, share_ref in enumerate(share_refs):
             for r in range(share // step_rows):
                 part = pl.ds(p * share + r * step_rows, step_rows)
-                own = found_ref[part, :].astype(jnp.bfloat16)
-                mean = (total_ref[part, :] / notes_ref[part, 1:2]).astype(jnp.bfloat16)
+                own = (found_ref[part, :] + had_ref[part, :]).astype(jnp.bfloat16)
+                mean = ((total_ref[part, :] + before_ref[part, :]) / notes_ref[part, 1:2]).astype(jnp.bfloat16)
                 own_ref[part, :] = own
                 mean_ref[part, :] = mean
                 share_ref[pl.ds(r * step_rows, step_rows), :] = (
@@ -411,7 +411,7 @@
         out_shape += tuple(
             jax.ShapeDtypeStruct((n, rest[3].shape[1]), jnp.bfloat16) for n in shares
         )
-        scratch += [pltpu.VMEM((nodes, features), jnp.float32)] * 2
+        scratch += [pltpu.VMEM((nodes, features), jnp.float32)] * 4
         scratch += [pltpu.VMEM(x.shape, x.dtype) for x in rest[2:]]
     else:
         out_shape = (rows(jnp.float32), rows(jnp.float32))

time: 271 us -> 271 us (level)
    ppermute x21, waiting for transfers between devices: 42.8 us -> 45.7 us  [passed(): lax.ppermute(part, axis, [((i + shift) % parts, i) for i in range(parts)])]
  transfers between devices with their start and end apart: 26 -> 26, of which waited for: 17 -> 18; matrix products, arithmetic and copies ran while one was open for 5% -> 5% of each run, Pallas kernels for 37% -> 37%
where the time goes in v17:
time: 271 us
  Pallas kernels  123 us (45%)
  waiting for transfers between devices  82.3 us (30%)
  starting transfers between devices  40.7 us (15%)
  local copies, waits for them, and re-layouts  11.3 us (4%)
  other arithmetic  5.76 us (2%)
  matrix products  4.92 us (2%)
  between operations  2.93 us (1%)
    pallas_call x4, Pallas kernels, gather_sum(): pl.pallas_call(functools.partial(gather_sum_body, piece, last, row0), out...  52.2 us
    pallas_call x1, Pallas kernels, adjacency(): pl.pallas_call(functools.partial(adjacency_body, tiles), out_shape=jax.Sh...  47.8 us
    ppermute x21, waiting for transfers between devices, passed(): lax.ppermute(part, axis, [((i + shift) % parts, i) for i in range(parts)])  45.7 us
    ppermute x21, starting transfers between devices, passed(): lax.ppermute(part, axis, [((i + shift) % parts, i) for i in range(parts)])  25.2 us
    pallas_call x2, Pallas kernels, lookup(): pl.pallas_call(functools.partial(lookup_body, places.shape[0] // groups,...  20 us
    all_to_all x1, waiting for transfers between devices, local(): lax.all_to_all(looked, 'batch', split_axis=0, concat_axis=0, tiled=True)  17 us
    all_to_all x1, waiting for transfers between devices, local(): lax.all_to_all(looked_a, 'batch', split_axis=0, concat_axis=0, tiled=True)  12.4 us
    all_to_all x1, starting transfers between devices, local(): lax.all_to_all(requests.reshape(batch_count, capacity), 'batch', split_ax...  6.34 us
  transfers between devices with their start and end apart: 26, of which 18 were waited for; matrix products, arithmetic and copies ran while one was open for 5% of the time, Pallas kernels for 37%

profile of v17, /device:TPU:0, one launch (start us, length us, event | category | flops | bytes accessed | tf_op | source)
XLA Modules:
  0.0 270.5 jit_solution(4313614119910679956)
XLA Ops:
  0.6 2.6 requests.1
  3.3 6.3 %all-to-all-start = ((s32[8,1,1536]{2,1,0:T(1,128)}), s32[8,1,1536]{2,1,0:T(1,128)S(1)}, u32[]{:S(2)}, u32[]{:S(2)}) async-start(s32[8,1,1536]{2,1,0:T(1,128)} %bitcast.190), calls=%async_computation | async-start | bytes 98304 | tf_op jit(solution)/shard_map/all_to_all | solution.py:542
  10.6 4.9 %all-to-all-done = s32[8,1,1536]{2,1,0:T(1,128)S(1)} async-done(((s32[8,1,1536]{2,1,0:T(1,128)}), s32[8,1,1536]{2,1,0:T(1,128)S(1)}, u32[]{:S(2)}, u32[]{:S(2)}) %all-to-all-start) | async-done | bytes 49184 | tf_op jit(solution)/shard_map/all_to_all | solution.py:542
  16.1 11.2 %lookup.3 = bf16[8,832,256]{2,1,0:T(8,128)(2,1)} custom-call(s32[12288]{0:T(1024)} %bitcast.159, bf16[8192,256]{1,0:T(8,128)(2,1)} %store_in.3), custom_call_target="tpu_custom_call" | custom-call | flops 68157440 | bytes 4194304 | tf_op jit(solution)/shard_map/lookup/pallas_call | solution.py:176
  27.3 4.6 %all-to-all-start.1 = ((bf16[8,832,256]{2,1,0:T(8,128)(2,1)}), bf16[8,832,256]{2,1,0:T(8,128)(2,1)}, u32[]{:S(2)}, u32[]{:S(2)}) async-start(bf16[8,832,256]{2,1,0:T(8,128)(2,1)} %lookup.3), calls=%async_computation.1 | async-start | bytes 6815744 | tf_op jit(solution)/shard_map/all_to_all | solution.py:549
  40.1 8.8 %lookup.2 = bf16[8,704,256]{2,1,0:T(8,128)(2,1)} custom-call(s32[12288]{0:T(1024)S(1)} %bitcast.160, bf16[8192,256]{1,0:T(8,128)(2,1)S(1)} %copy-done.3), custom_call_target="tpu_custom_call" | custom-call | flops 57671680 | bytes 4194304 | tf_op jit(solution)/shard_map/lookup/pallas_call | solution.py:176
  48.9 47.8 %adjacency.1.adj_ref = f8e4m3fn[28,3072,256]{2,1,0:T(32,128)(4,1)} custom-call(s32[1]{0:T(128)} %bitcast.11.me_ref, s32[192,256]{1,0:T(8,128)S(1)} %reshape.242.near_ref, bf16[256,128]{1,0:T(8,128)(2,1)S(1)} %pad_maximum_fusion.4.table_ref), custom_call_target="tpu_custom_call" | custom-call | flops 22548578304 | bytes 22020096 | tf_op jit(solution)/shard_map/adjacency/pallas_call | solution.py:239
  96.7 12.4 %all-to-all-done.1.answer_ref = bf16[8,832,256]{2,1,0:T(8,128)(2,1)} async-done(((bf16[8,832,256]{2,1,0:T(8,128)(2,1)}), bf16[8,832,256]{2,1,0:T(8,128)(2,1)}, u32[]{:S(2)}, u32[]{:S(2)}) %all-to-all-start.1) | async-done | bytes 3407904 | tf_op jit(solution)/shard_map/all_to_all | solution.py:549
  109.1 4.4 %all-to-all-start.2 = ((bf16[8,704,256]{2,1,0:T(8,128)(2,1)}), bf16[8,704,256]{2,1,0:T(8,128)(2,1)}, u32[]{:S(2)}, u32[]{:S(2)}) async-start(bf16[8,704,256]{2,1,0:T(8,128)(2,1)} %lookup.2), calls=%async_computation.2 | async-start | bytes 5767168 | tf_op jit(solution)/shard_map/all_to_all | solution.py:588
  116.7 32.9 %gather_sum.4 = (f32[3072,256]{1,0:T(8,128)}, f32[3072,256]{1,0:T(8,128)}) custom-call(s32[2]{0:T(128)S(1)} %pad_add_fusion.4.spans_ref, s32[8]{0:T(128)S(1)} %get-tuple-element.88.counts_ref, s32[9]{0:T(128)S(1)} %get-tuple-element.90.starts_ref, s32[56]{0:T(128)S(1)} %reshape.248.own_here_ref, bf16[8,832,256]{2,1,0:T(8,128)(2,1)} %all-to-all-done.1.answer_ref, ...), custom_call_target="tpu_custom_call" | custom-call | flops 11274289152 | bytes 786432 | tf_op jit(solution)/shard_map/gather_sum/pallas_call | solution.py:418
  149.6 2.5 collective-permute-start
  157.9 2.4 collective-permute-done.4
  162.5 17.0 %all-to-all-done.2.answer_ref = bf16[8,704,256]{2,1,0:T(8,128)(2,1)} async-done(((bf16[8,704,256]{2,1,0:T(8,128)(2,1)}), bf16[8,704,256]{2,1,0:T(8,128)(2,1)}, u32[]{:S(2)}, u32[]{:S(2)}) %all-to-all-start.2) | async-done | bytes 2883616 | tf_op jit(solution)/shard_map/all_to_all | solution.py:588
  179.5 7.8 %gather_sum.5 = (bf16[1536,256]{1,0:T(8,128)(2,1)S(1)}, bf16[1536,256]{1,0:T(8,128)(2,1)S(1)}, bf16[768,256]{1,0:T(8,128)(2,1)S(1)}, bf16[768,256]{1,0:T(8,128)(2,1)S(1)}) custom-call(s32[2]{0:T(128)S(1)} %pad_add_fusion.5.spans_ref, s32[8]{0:T(128)S(1)} %get-tuple-element.87.counts_ref, s32[9]{0:T(128)S(1)} %get-tuple-element.89.starts_ref, ...), custom_call_target="tpu_custom_call" | custom-call | flops 1409286144 | bytes 393216 | tf_op jit(solution)/shard_map/gather_sum/pallas_call | solution.py:418
  187.3 2.5 collective-permute-start.8
  190.3 5.8 %gather_sum.6 = (bf16[768,256]{1,0:T(8,128)(2,1)S(1)}, bf16[768,256]{1,0:T(8,128)(2,1)S(1)}, bf16[768,256]{1,0:T(8,128)(2,1)S(1)}) custom-call(s32[2]{0:T(128)S(1)} %pad_add_fusion.5.spans_ref, s32[8]{0:T(128)S(1)} %get-tuple-element.87.counts_ref, s32[9]{0:T(128)S(1)} %get-tuple-element.89.starts_ref, s32[56]{0:T(128)S(1)} %reshape.248.own_here_ref, ...), custom_call_target="tpu_custom_call" | custom-call | flops 704643072 | bytes 196608 | tf_op jit(solution)/shard_map/gather_sum/pallas_call | solution.py:418
  199.0 5.7 %gather_sum.7 = (bf16[768,256]{1,0:T(8,128)(2,1)S(1)}, bf16[768,256]{1,0:T(8,128)(2,1)S(1)}, bf16[768,256]{1,0:T(8,128)(2,1)S(1)}) custom-call(s32[2]{0:T(128)S(1)} %pad_add_fusion.5.spans_ref, s32[8]{0:T(128)S(1)} %get-tuple-element.87.counts_ref, s32[9]{0:T(128)S(1)} %get-tuple-element.89.starts_ref, s32[56]{0:T(128)S(1)} %reshape.248.own_here_ref, ...), custom_call_target="tpu_custom_call" | custom-call | flops 704643072 | bytes 196608 | tf_op jit(solution)/shard_map/gather_sum/pallas_call | solution.py:418
  204.7 3.9 %collective-permute-done.7 = bf16[768,256]{1,0:T(8,128)(2,1)S(1)} collective-permute-done((bf16[768,256]{1,0:T(8,128)(2,1)S(1)}, bf16[768,256]{1,0:T(8,128)(2,1)S(1)}, u32[]{:S(2)}, u32[]{:S(2)}) %collective-permute-start.7) | collective-permute-done | bytes 393248 | tf_op jit(solution)/shard_map/ppermute | solution.py:449
  213.0 7.9 %collective-permute-done.11 = bf16[640,256]{1,0:T(8,128)(2,1)S(1)} collective-permute-done((bf16[640,256]{1,0:T(8,128)(2,1)S(1)}, bf16[640,256]{1,0:T(8,128)(2,1)S(1)}, u32[]{:S(2)}, u32[]{:S(2)}) %collective-permute-start.11) | collective-permute-done | bytes 327712 | tf_op jit(solution)/shard_map/ppermute | solution.py:449
  220.9 3.5 %collective-permute-done.10 = bf16[640,256]{1,0:T(8,128)(2,1)S(1)} collective-permute-done((bf16[640,256]{1,0:T(8,128)(2,1)S(1)}, bf16[640,256]{1,0:T(8,128)(2,1)S(1)}, u32[]{:S(2)}, u32[]{:S(2)}) %collective-permute-start.10) | collective-permute-done | bytes 327712 | tf_op jit(solution)/shard_map/ppermute | solution.py:449
  231.3 7.0 %collective-permute-done.12 = bf16[768,256]{1,0:T(8,128)(2,1)S(1)} collective-permute-done((bf16[768,256]{1,0:T(8,128)(2,1)S(1)}, bf16[768,256]{1,0:T(8,128)(2,1)S(1)}, u32[]{:S(2)}, u32[]{:S(2)}) %collective-permute-start.12) | collective-permute-done | bytes 393248 | tf_op jit(solution)/shard_map/ppermute | solution.py:449
  239.2 7.9 %collective-permute-done.13 = bf16[768,256]{1,0:T(8,128)(2,1)S(1)} collective-permute-done((bf16[768,256]{1,0:T(8,128)(2,1)S(1)}, bf16[768,256]{1,0:T(8,128)(2,1)S(1)}, u32[]{:S(2)}, u32[]{:S(2)}) %collective-permute-start.13) | collective-permute-done | bytes 393248 | tf_op jit(solution)/shard_map/ppermute | solution.py:449
  254.7 4.5 %collective-permute-done.17 = bf16[128,256]{1,0:T(8,128)(2,1)S(1)} collective-permute-done((bf16[128,256]{1,0:T(8,128)(2,1)S(1)}, bf16[128,256]{1,0:T(8,128)(2,1)S(1)}, u32[]{:S(2)}, u32[]{:S(2)}) %collective-permute-start.17) | collective-permute-done | bytes 65568 | tf_op jit(solution)/shard_map/ppermute | solution.py:449
  263.8 2.4 collective-permute-done.21
  (168 shorter events, 50.9 us)
Async XLA Ops:
  3.3 12.2 %all-to-all-start = ((s32[8,1,1536]{2,1,0:T(1,128)}), s32[8,1,1536]{2,1,0:T(1,128)S(1)}, u32[]{:S(2)}, u32[]{:S(2)}) async-start(s32[8,1,1536]{2,1,0:T(1,128)} %bitcast.190), calls=%async_computation | async-start | bytes 98304 | tf_op jit(solution)/shard_map/all_to_all | solution.py:542
  27.3 81.8 %all-to-all-start.1 = ((bf16[8,832,256]{2,1,0:T(8,128)(2,1)}), bf16[8,832,256]{2,1,0:T(8,128)(2,1)}, u32[]{:S(2)}, u32[]{:S(2)}) async-start(bf16[8,832,256]{2,1,0:T(8,128)(2,1)} %lookup.3), calls=%async_computation.1 | async-start | bytes 6815744 | tf_op jit(solution)/shard_map/all_to_all | solution.py:549
  109.1 70.3 %all-to-all-start.2 = ((bf16[8,704,256]{2,1,0:T(8,128)(2,1)}), bf16[8,704,256]{2,1,0:T(8,128)(2,1)}, u32[]{:S(2)}, u32[]{:S(2)}) async-start(bf16[8,704,256]{2,1,0:T(8,128)(2,1)} %lookup.2), calls=%async_computation.2 | async-start | bytes 5767168 | tf_op jit(solution)/shard_map/all_to_all | solution.py:588
  149.6 7.6 %collective-permute-start = (s32[11,128]{1,0:T(8,128)S(1)}, s32[11,128]{1,0:T(8,128)S(1)}, u32[]{:S(2)}, u32[]{:S(2)}) collective-permute-start(s32[11,128]{1,0:T(8,128)S(1)} %pad_add_fusion.1), channel_id=1, source_target_pairs={{8,0},{16,8},{24,16},{0,24},{9,1},{17,9},{25,17},{1,25},{10,2},{18... | collective-permute-start | bytes 16904 | tf_op jit(solution)/shard_map/ppermute | solution.py:449
  152.1 5.2 %collective-permute-start.1 = (s32[11,128]{1,0:T(8,128)S(1)}, s32[11,128]{1,0:T(8,128)S(1)}, u32[]{:S(2)}, u32[]{:S(2)}) collective-permute-start(s32[11,128]{1,0:T(8,128)S(1)} %pad_add_fusion.1), channel_id=1, source_target_pairs={{16,0},{24,8},{0,16},{8,24},{17,1},{25,9},{1,17},{9,25},{18,2},{26... | collective-permute-start | bytes 16904 | tf_op jit(solution)/shard_map/ppermute | solution.py:449
  152.6 4.7 %collective-permute-start.2 = (s32[11,128]{1,0:T(8,128)S(1)}, s32[11,128]{1,0:T(8,128)S(1)}, u32[]{:S(2)}, u32[]{:S(2)}) collective-permute-start(s32[11,128]{1,0:T(8,128)S(1)} %pad_add_fusion.1), channel_id=1, source_target_pairs={{24,0},{0,8},{8,16},{16,24},{25,1},{1,9},{9,17},{17,25},{26,2},{2,... | collective-permute-start | bytes 16904 | tf_op jit(solution)/shard_map/ppermute | solution.py:449
  153.2 4.7 %collective-permute-start.3 = (bf16[128,256]{1,0:T(8,128)(2,1)S(1)}, bf16[128,256]{1,0:T(8,128)(2,1)S(1)}, u32[]{:S(2)}, u32[]{:S(2)}) collective-permute-start(bf16[128,256]{1,0:T(8,128)(2,1)S(1)} %bitcast.186), channel_id=1, source_target_pairs={{8,0},{16,8},{24,16},{0,24},{9,1},{17,9},{25,17},{1,25},{10,2},{18... | collective-permute-start | bytes 196616 | tf_op jit(solution)/shard_map/ppermute | solution.py:449
  155.6 4.8 %collective-permute-start.4 = (bf16[128,256]{1,0:T(8,128)(2,1)S(1)}, bf16[128,256]{1,0:T(8,128)(2,1)S(1)}, u32[]{:S(2)}, u32[]{:S(2)}) collective-permute-start(bf16[128,256]{1,0:T(8,128)(2,1)S(1)} %bitcast.187), channel_id=1, source_target_pairs={{16,0},{24,8},{0,16},{8,24},{17,1},{25,9},{1,17},{9,25},{18,2},{26... | collective-permute-start | bytes 196616 | tf_op jit(solution)/shard_map/ppermute | solution.py:449
  157.2 5.2 %collective-permute-start.5 = (bf16[128,256]{1,0:T(8,128)(2,1)S(1)}, bf16[128,256]{1,0:T(8,128)(2,1)S(1)}, u32[]{:S(2)}, u32[]{:S(2)}) collective-permute-start(bf16[128,256]{1,0:T(8,128)(2,1)S(1)} %bitcast.189), channel_id=1, source_target_pairs={{24,0},{0,8},{8,16},{16,24},{25,1},{1,9},{9,17},{17,25},{26,2},{2,... | collective-permute-start | bytes 196616 | tf_op jit(solution)/shard_map/ppermute | solution.py:449
  187.3 17.4 %collective-permute-start.8 = (bf16[768,256]{1,0:T(8,128)(2,1)S(1)}, bf16[768,256]{1,0:T(8,128)(2,1)S(1)}, u32[]{:S(2)}, u32[]{:S(2)}) collective-permute-start(bf16[768,256]{1,0:T(8,128)(2,1)S(1)} %get-tuple-element.62), channel_id=1, source_target_pairs={{8,0},{16,8},{24,16},{0,24},{9,1},{17,9},{25,17},{1,25},{10,2},{18... | collective-permute-start | bytes 1179656 | tf_op jit(solution)/shard_map/ppermute | solution.py:449
  189.8 18.9 %collective-permute-start.7 = (bf16[768,256]{1,0:T(8,128)(2,1)S(1)}, bf16[768,256]{1,0:T(8,128)(2,1)S(1)}, u32[]{:S(2)}, u32[]{:S(2)}) collective-permute-start(bf16[768,256]{1,0:T(8,128)(2,1)S(1)} %get-tuple-element.61), channel_id=1, source_target_pairs={{16,0},{24,8},{0,16},{8,24},{17,1},{25,9},{1,17},{9,25},{18,2},{26... | collective-permute-start | bytes 1179656 | tf_op jit(solution)/shard_map/ppermute | solution.py:449
  196.1 12.5 %collective-permute-start.6 = (bf16[768,256]{1,0:T(8,128)(2,1)S(1)}, bf16[768,256]{1,0:T(8,128)(2,1)S(1)}, u32[]{:S(2)}, u32[]{:S(2)}) collective-permute-start(bf16[768,256]{1,0:T(8,128)(2,1)S(1)} %get-tuple-element.60), channel_id=1, source_target_pairs={{24,0},{0,8},{8,16},{16,24},{25,1},{1,9},{9,17},{17,25},{26,2},{2,... | collective-permute-start | bytes 1179656 | tf_op jit(solution)/shard_map/ppermute | solution.py:449
  209.4 11.4 %collective-permute-start.11 = (bf16[640,256]{1,0:T(8,128)(2,1)S(1)}, bf16[640,256]{1,0:T(8,128)(2,1)S(1)}, u32[]{:S(2)}, u32[]{:S(2)}) collective-permute-start(bf16[640,256]{1,0:T(8,128)(2,1)S(1)} %pad_maximum_fusion.2), channel_id=1, source_target_pairs={{24,0},{0,8},{8,16},{16,24},{25,1},{1,9},{9,17},{17,25},{26,2},{2,... | collective-permute-start | bytes 983048 | tf_op jit(solution)/shard_map/ppermute | solution.py:449
  209.8 14.5 %collective-permute-start.10 = (bf16[640,256]{1,0:T(8,128)(2,1)S(1)}, bf16[640,256]{1,0:T(8,128)(2,1)S(1)}, u32[]{:S(2)}, u32[]{:S(2)}) collective-permute-start(bf16[640,256]{1,0:T(8,128)(2,1)S(1)} %pad_maximum_fusion.2), channel_id=1, source_target_pairs={{16,0},{24,8},{0,16},{8,24},{17,1},{25,9},{1,17},{9,25},{18,2},{26... | collective-permute-start | bytes 983048 | tf_op jit(solution)/shard_map/ppermute | solution.py:449
  210.6 13.7 %collective-permute-start.9 = (bf16[640,256]{1,0:T(8,128)(2,1)S(1)}, bf16[640,256]{1,0:T(8,128)(2,1)S(1)}, u32[]{:S(2)}, u32[]{:S(2)}) collective-permute-start(bf16[640,256]{1,0:T(8,128)(2,1)S(1)} %pad_maximum_fusion.2), channel_id=1, source_target_pairs={{8,0},{16,8},{24,16},{0,24},{9,1},{17,9},{25,17},{1,25},{10,2},{18... | collective-permute-start | bytes 983048 | tf_op jit(solution)/shard_map/ppermute | solution.py:449
  226.8 12.0 %collective-permute-start.14 = (bf16[768,256]{1,0:T(8,128)(2,1)S(1)}, bf16[768,256]{1,0:T(8,128)(2,1)S(1)}, u32[]{:S(2)}, u32[]{:S(2)}) collective-permute-start(bf16[768,256]{1,0:T(8,128)(2,1)S(1)} %fusion.2), channel_id=1, source_target_pairs={{8,0},{16,8},{24,16},{0,24},{9,1},{17,9},{25,17},{1,25},{10,2},{18... | collective-permute-start | bytes 1179656 | tf_op jit(solution)/shard_map/ppermute | solution.py:449
  229.1 9.2 %collective-permute-start.12 = (bf16[768,256]{1,0:T(8,128)(2,1)S(1)}, bf16[768,256]{1,0:T(8,128)(2,1)S(1)}, u32[]{:S(2)}, u32[]{:S(2)}) collective-permute-start(bf16[768,256]{1,0:T(8,128)(2,1)S(1)} %fusion.2), channel_id=1, source_target_pairs={{16,0},{24,8},{0,16},{8,24},{17,1},{25,9},{1,17},{9,25},{18,2},{26... | collective-permute-start | bytes 1179656 | tf_op jit(solution)/shard_map/ppermute | solution.py:449
  230.0 17.1 %collective-permute-start.13 = (bf16[768,256]{1,0:T(8,128)(2,1)S(1)}, bf16[768,256]{1,0:T(8,128)(2,1)S(1)}, u32[]{:S(2)}, u32[]{:S(2)}) collective-permute-start(bf16[768,256]{1,0:T(8,128)(2,1)S(1)} %fusion.2), channel_id=1, source_target_pairs={{24,0},{0,8},{8,16},{16,24},{25,1},{1,9},{9,17},{17,25},{26,2},{2,... | collective-permute-start | bytes 1179656 | tf_op jit(solution)/shard_map/ppermute | solution.py:449
  250.1 4.6 %collective-permute-start.18 = (bf16[128,256]{1,0:T(8,128)(2,1)S(1)}, bf16[128,256]{1,0:T(8,128)(2,1)S(1)}, u32[]{:S(2)}, u32[]{:S(2)}) collective-permute-start(bf16[128,256]{1,0:T(8,128)(2,1)S(1)} %get-tuple-element.80), channel_id=1, source_target_pairs={{2,0},{3,1},{4,2},{5,3},{6,4},{7,5},{0,6},{1,7},{10,8},{11,9},{12,... | collective-permute-start | bytes 196616 | tf_op jit(solution)/shard_map/ppermute | solution.py:449
  252.2 7.0 %collective-permute-start.17 = (bf16[128,256]{1,0:T(8,128)(2,1)S(1)}, bf16[128,256]{1,0:T(8,128)(2,1)S(1)}, u32[]{:S(2)}, u32[]{:S(2)}) collective-permute-start(bf16[128,256]{1,0:T(8,128)(2,1)S(1)} %get-tuple-element.81), channel_id=1, source_target_pairs={{4,0},{5,1},{6,2},{7,3},{0,4},{1,5},{2,6},{3,7},{12,8},{13,9},{14,... | collective-permute-start | bytes 196616 | tf_op jit(solution)/shard_map/ppermute | solution.py:449
  252.2 7.0 %collective-permute-start.16 = (bf16[128,256]{1,0:T(8,128)(2,1)S(1)}, bf16[128,256]{1,0:T(8,128)(2,1)S(1)}, u32[]{:S(2)}, u32[]{:S(2)}) collective-permute-start(bf16[128,256]{1,0:T(8,128)(2,1)S(1)} %get-tuple-element.79), channel_id=1, source_target_pairs={{6,0},{7,1},{0,2},{1,3},{2,4},{3,5},{4,6},{5,7},{14,8},{15,9},{8,1... | collective-permute-start | bytes 196616 | tf_op jit(solution)/shard_map/ppermute | solution.py:449
  259.3 6.9 %collective-permute-start.21 = (bf16[128,256]{1,0:T(8,128)(2,1)S(1)}, bf16[128,256]{1,0:T(8,128)(2,1)S(1)}, u32[]{:S(2)}, u32[]{:S(2)}) collective-permute-start(bf16[128,256]{1,0:T(8,128)(2,1)S(1)} %fusion.16), channel_id=1, source_target_pairs={{6,0},{7,1},{0,2},{1,3},{2,4},{3,5},{4,6},{5,7},{14,8},{15,9},{8,1... | collective-permute-start | bytes 196616 | tf_op jit(solution)/shard_map/ppermute | solution.py:449
  259.3 8.2 %collective-permute-start.20 = (bf16[128,256]{1,0:T(8,128)(2,1)S(1)}, bf16[128,256]{1,0:T(8,128)(2,1)S(1)}, u32[]{:S(2)}, u32[]{:S(2)}) collective-permute-start(bf16[128,256]{1,0:T(8,128)(2,1)S(1)} %fusion.16), channel_id=1, source_target_pairs={{4,0},{5,1},{6,2},{7,3},{0,4},{1,5},{2,6},{3,7},{12,8},{13,9},{14,... | collective-permute-start | bytes 196616 | tf_op jit(solution)/shard_map/ppermute | solution.py:449
  261.5 6.0 %collective-permute-start.19 = (bf16[128,256]{1,0:T(8,128)(2,1)S(1)}, bf16[128,256]{1,0:T(8,128)(2,1)S(1)}, u32[]{:S(2)}, u32[]{:S(2)}) collective-permute-start(bf16[128,256]{1,0:T(8,128)(2,1)S(1)} %fusion.16), channel_id=1, source_target_pairs={{2,0},{3,1},{4,2},{5,3},{6,4},{7,5},{0,6},{1,7},{10,8},{11,9},{12,... | collective-permute-start | bytes 196616 | tf_op jit(solution)/shard_map/ppermute | solution.py:449
  (20 other events, 567.5 us)

commit v18 on v17

--- a/solution.py
+++ b/solution.py
@@ -183,7 +183,7 @@
             apart(rows_all),
             apart(width),
             pltpu.VMEM((rows_all, features), store.dtype),
-            pltpu.SemaphoreType.DMA((4,)),
+            pltpu.SemaphoreType.DMA((8,)),
         ],
         compiler_params=params(mib),
         cost_estimate=cost(groups * width * features * 40, 2 * rows_all * features),

time: 271 us -> 271 us (level)
  no operation moved by 1% of the time
where the time goes in v18:
time: 271 us; the launch traced here: 270 us
  Pallas kernels  123 us (45%)
  waiting for transfers between devices  81.7 us (30%)
  starting transfers between devices  40.9 us (15%)
  local copies, waits for them, and re-layouts  11.3 us (4%)
  other arithmetic  5.76 us (2%)
  matrix products  4.91 us (2%)
  between operations  2.94 us (1%)
    pallas_call x4, Pallas kernels, gather_sum(): pl.pallas_call(functools.partial(gather_sum_body, piece, last, row0), out...  52.1 us
    pallas_call x1, Pallas kernels, adjacency(): pl.pallas_call(functools.partial(adjacency_body, tiles), out_shape=jax.Sh...  47.8 us
    ppermute x21, waiting for transfers between devices, passed(): lax.ppermute(part, axis, [((i + shift) % parts, i) for i in range(parts)])  44.9 us
    ppermute x21, starting transfers between devices, passed(): lax.ppermute(part, axis, [((i + shift) % parts, i) for i in range(parts)])  25.4 us
    pallas_call x2, Pallas kernels, lookup(): pl.pallas_call(functools.partial(lookup_body, places.shape[0] // groups,...  20 us
    all_to_all x1, waiting for transfers between devices, local(): lax.all_to_all(looked, 'batch', split_axis=0, concat_axis=0, tiled=True)  17.2 us
    all_to_all x1, waiting for transfers between devices, local(): lax.all_to_all(looked_a, 'batch', split_axis=0, concat_axis=0, tiled=True)  12.3 us
    all_to_all x1, starting transfers between devices, local(): lax.all_to_all(requests.reshape(batch_count, capacity), 'batch', split_ax...  6.34 us
  transfers between devices with their start and end apart: 26, of which 18 were waited for; matrix products, arithmetic and copies ran while one was open for 5% of the time, Pallas kernels for 37%

profile of v18, /device:TPU:0, one launch (start us, length us, event | category | flops | bytes accessed | tf_op | source)
XLA Modules:
  0.0 270.0 jit_solution(13915751798412600689)
XLA Ops:
  0.6 2.6 requests.1
  3.3 6.3 %all-to-all-start = ((s32[8,1,1536]{2,1,0:T(1,128)}), s32[8,1,1536]{2,1,0:T(1,128)S(1)}, u32[]{:S(2)}, u32[]{:S(2)}) async-start(s32[8,1,1536]{2,1,0:T(1,128)} %bitcast.190), calls=%async_computation | async-start | bytes 98304 | tf_op jit(solution)/shard_map/all_to_all | solution.py:542
  10.6 4.9 %all-to-all-done = s32[8,1,1536]{2,1,0:T(1,128)S(1)} async-done(((s32[8,1,1536]{2,1,0:T(1,128)}), s32[8,1,1536]{2,1,0:T(1,128)S(1)}, u32[]{:S(2)}, u32[]{:S(2)}) %all-to-all-start) | async-done | bytes 49184 | tf_op jit(solution)/shard_map/all_to_all | solution.py:542
  16.1 11.1 %lookup.3 = bf16[8,832,256]{2,1,0:T(8,128)(2,1)} custom-call(s32[12288]{0:T(1024)} %bitcast.159, bf16[8192,256]{1,0:T(8,128)(2,1)} %store_in.3), custom_call_target="tpu_custom_call" | custom-call | flops 68157440 | bytes 4194304 | tf_op jit(solution)/shard_map/lookup/pallas_call | solution.py:176
  27.3 4.6 %all-to-all-start.1 = ((bf16[8,832,256]{2,1,0:T(8,128)(2,1)}), bf16[8,832,256]{2,1,0:T(8,128)(2,1)}, u32[]{:S(2)}, u32[]{:S(2)}) async-start(bf16[8,832,256]{2,1,0:T(8,128)(2,1)} %lookup.3), calls=%async_computation.1 | async-start | bytes 6815744 | tf_op jit(solution)/shard_map/all_to_all | solution.py:549
  40.0 8.9 %lookup.2 = bf16[8,704,256]{2,1,0:T(8,128)(2,1)} custom-call(s32[12288]{0:T(1024)S(1)} %bitcast.160, bf16[8192,256]{1,0:T(8,128)(2,1)S(1)} %copy-done.3), custom_call_target="tpu_custom_call" | custom-call | flops 57671680 | bytes 4194304 | tf_op jit(solution)/shard_map/lookup/pallas_call | solution.py:176
  48.9 47.8 %adjacency.1.adj_ref = f8e4m3fn[28,3072,256]{2,1,0:T(32,128)(4,1)} custom-call(s32[1]{0:T(128)} %bitcast.11.me_ref, s32[192,256]{1,0:T(8,128)S(1)} %reshape.242.near_ref, bf16[256,128]{1,0:T(8,128)(2,1)S(1)} %pad_maximum_fusion.4.table_ref), custom_call_target="tpu_custom_call" | custom-call | flops 22548578304 | bytes 22020096 | tf_op jit(solution)/shard_map/adjacency/pallas_call | solution.py:239
  96.7 12.3 %all-to-all-done.1.answer_ref = bf16[8,832,256]{2,1,0:T(8,128)(2,1)} async-done(((bf16[8,832,256]{2,1,0:T(8,128)(2,1)}), bf16[8,832,256]{2,1,0:T(8,128)(2,1)}, u32[]{:S(2)}, u32[]{:S(2)}) %all-to-all-start.1) | async-done | bytes 3407904 | tf_op jit(solution)/shard_map/all_to_all | solution.py:549
  109.1 4.4 %all-to-all-start.2 = ((bf16[8,704,256]{2,1,0:T(8,128)(2,1)}), bf16[8,704,256]{2,1,0:T(8,128)(2,1)}, u32[]{:S(2)}, u32[]{:S(2)}) async-start(bf16[8,704,256]{2,1,0:T(8,128)(2,1)} %lookup.2), calls=%async_computation.2 | async-start | bytes 5767168 | tf_op jit(solution)/shard_map/all_to_all | solution.py:588
  116.6 32.6 %gather_sum.4 = (f32[3072,256]{1,0:T(8,128)}, f32[3072,256]{1,0:T(8,128)}) custom-call(s32[2]{0:T(128)S(1)} %pad_add_fusion.4.spans_ref, s32[8]{0:T(128)S(1)} %get-tuple-element.88.counts_ref, s32[9]{0:T(128)S(1)} %get-tuple-element.90.starts_ref, s32[56]{0:T(128)S(1)} %reshape.248.own_here_ref, bf16[8,832,256]{2,1,0:T(8,128)(2,1)} %all-to-all-done.1.answer_ref, ...), custom_call_target="tpu_custom_call" | custom-call | flops 11274289152 | bytes 786432 | tf_op jit(solution)/shard_map/gather_sum/pallas_call | solution.py:418
  149.3 2.5 collective-permute-start
  159.5 2.6 collective-permute-done.5
  162.2 17.2 %all-to-all-done.2.answer_ref = bf16[8,704,256]{2,1,0:T(8,128)(2,1)} async-done(((bf16[8,704,256]{2,1,0:T(8,128)(2,1)}), bf16[8,704,256]{2,1,0:T(8,128)(2,1)}, u32[]{:S(2)}, u32[]{:S(2)}) %all-to-all-start.2) | async-done | bytes 2883616 | tf_op jit(solution)/shard_map/all_to_all | solution.py:588
  179.4 7.8 %gather_sum.5 = (bf16[1536,256]{1,0:T(8,128)(2,1)S(1)}, bf16[1536,256]{1,0:T(8,128)(2,1)S(1)}, bf16[768,256]{1,0:T(8,128)(2,1)S(1)}, bf16[768,256]{1,0:T(8,128)(2,1)S(1)}) custom-call(s32[2]{0:T(128)S(1)} %pad_add_fusion.5.spans_ref, s32[8]{0:T(128)S(1)} %get-tuple-element.87.counts_ref, s32[9]{0:T(128)S(1)} %get-tuple-element.89.starts_ref, ...), custom_call_target="tpu_custom_call" | custom-call | flops 1409286144 | bytes 393216 | tf_op jit(solution)/shard_map/gather_sum/pallas_call | solution.py:418
  187.3 2.5 collective-permute-start.8
  190.3 5.9 %gather_sum.6 = (bf16[768,256]{1,0:T(8,128)(2,1)S(1)}, bf16[768,256]{1,0:T(8,128)(2,1)S(1)}, bf16[768,256]{1,0:T(8,128)(2,1)S(1)}) custom-call(s32[2]{0:T(128)S(1)} %pad_add_fusion.5.spans_ref, s32[8]{0:T(128)S(1)} %get-tuple-element.87.counts_ref, s32[9]{0:T(128)S(1)} %get-tuple-element.89.starts_ref, s32[56]{0:T(128)S(1)} %reshape.248.own_here_ref, ...), custom_call_target="tpu_custom_call" | custom-call | flops 704643072 | bytes 196608 | tf_op jit(solution)/shard_map/gather_sum/pallas_call | solution.py:418
  199.1 5.7 %gather_sum.7 = (bf16[768,256]{1,0:T(8,128)(2,1)S(1)}, bf16[768,256]{1,0:T(8,128)(2,1)S(1)}, bf16[768,256]{1,0:T(8,128)(2,1)S(1)}) custom-call(s32[2]{0:T(128)S(1)} %pad_add_fusion.5.spans_ref, s32[8]{0:T(128)S(1)} %get-tuple-element.87.counts_ref, s32[9]{0:T(128)S(1)} %get-tuple-element.89.starts_ref, s32[56]{0:T(128)S(1)} %reshape.248.own_here_ref, ...), custom_call_target="tpu_custom_call" | custom-call | flops 704643072 | bytes 196608 | tf_op jit(solution)/shard_map/gather_sum/pallas_call | solution.py:418
  204.8 3.6 %collective-permute-done.7 = bf16[768,256]{1,0:T(8,128)(2,1)S(1)} collective-permute-done((bf16[768,256]{1,0:T(8,128)(2,1)S(1)}, bf16[768,256]{1,0:T(8,128)(2,1)S(1)}, u32[]{:S(2)}, u32[]{:S(2)}) %collective-permute-start.7) | collective-permute-done | bytes 393248 | tf_op jit(solution)/shard_map/ppermute | solution.py:449
  212.8 7.8 %collective-permute-done.11 = bf16[640,256]{1,0:T(8,128)(2,1)S(1)} collective-permute-done((bf16[640,256]{1,0:T(8,128)(2,1)S(1)}, bf16[640,256]{1,0:T(8,128)(2,1)S(1)}, u32[]{:S(2)}, u32[]{:S(2)}) %collective-permute-start.11) | collective-permute-done | bytes 327712 | tf_op jit(solution)/shard_map/ppermute | solution.py:449
  220.6 3.4 %collective-permute-done.10 = bf16[640,256]{1,0:T(8,128)(2,1)S(1)} collective-permute-done((bf16[640,256]{1,0:T(8,128)(2,1)S(1)}, bf16[640,256]{1,0:T(8,128)(2,1)S(1)}, u32[]{:S(2)}, u32[]{:S(2)}) %collective-permute-start.10) | collective-permute-done | bytes 327712 | tf_op jit(solution)/shard_map/ppermute | solution.py:449
  231.0 7.3 %collective-permute-done.12 = bf16[768,256]{1,0:T(8,128)(2,1)S(1)} collective-permute-done((bf16[768,256]{1,0:T(8,128)(2,1)S(1)}, bf16[768,256]{1,0:T(8,128)(2,1)S(1)}, u32[]{:S(2)}, u32[]{:S(2)}) %collective-permute-start.12) | collective-permute-done | bytes 393248 | tf_op jit(solution)/shard_map/ppermute | solution.py:449
  238.9 7.6 %collective-permute-done.13 = bf16[768,256]{1,0:T(8,128)(2,1)S(1)} collective-permute-done((bf16[768,256]{1,0:T(8,128)(2,1)S(1)}, bf16[768,256]{1,0:T(8,128)(2,1)S(1)}, u32[]{:S(2)}, u32[]{:S(2)}) %collective-permute-start.13) | collective-permute-done | bytes 393248 | tf_op jit(solution)/shard_map/ppermute | solution.py:449
  249.6 2.4 collective-permute-start.18
  254.5 4.9 %collective-permute-done.17 = bf16[128,256]{1,0:T(8,128)(2,1)S(1)} collective-permute-done((bf16[128,256]{1,0:T(8,128)(2,1)S(1)}, bf16[128,256]{1,0:T(8,128)(2,1)S(1)}, u32[]{:S(2)}, u32[]{:S(2)}) %collective-permute-start.17) | collective-permute-done | bytes 65568 | tf_op jit(solution)/shard_map/ppermute | solution.py:449
  (168 shorter events, 49.9 us)
Async XLA Ops:
  3.3 12.2 %all-to-all-start = ((s32[8,1,1536]{2,1,0:T(1,128)}), s32[8,1,1536]{2,1,0:T(1,128)S(1)}, u32[]{:S(2)}, u32[]{:S(2)}) async-start(s32[8,1,1536]{2,1,0:T(1,128)} %bitcast.190), calls=%async_computation | async-start | bytes 98304 | tf_op jit(solution)/shard_map/all_to_all | solution.py:542
  27.3 81.8 %all-to-all-start.1 = ((bf16[8,832,256]{2,1,0:T(8,128)(2,1)}), bf16[8,832,256]{2,1,0:T(8,128)(2,1)}, u32[]{:S(2)}, u32[]{:S(2)}) async-start(bf16[8,832,256]{2,1,0:T(8,128)(2,1)} %lookup.3), calls=%async_computation.1 | async-start | bytes 6815744 | tf_op jit(solution)/shard_map/all_to_all | solution.py:549
  109.1 70.3 %all-to-all-start.2 = ((bf16[8,704,256]{2,1,0:T(8,128)(2,1)}), bf16[8,704,256]{2,1,0:T(8,128)(2,1)}, u32[]{:S(2)}, u32[]{:S(2)}) async-start(bf16[8,704,256]{2,1,0:T(8,128)(2,1)} %lookup.2), calls=%async_computation.2 | async-start | bytes 5767168 | tf_op jit(solution)/shard_map/all_to_all | solution.py:588
  149.3 7.6 %collective-permute-start = (s32[11,128]{1,0:T(8,128)S(1)}, s32[11,128]{1,0:T(8,128)S(1)}, u32[]{:S(2)}, u32[]{:S(2)}) collective-permute-start(s32[11,128]{1,0:T(8,128)S(1)} %pad_add_fusion.1), channel_id=1, source_target_pairs={{8,0},{16,8},{24,16},{0,24},{9,1},{17,9},{25,17},{1,25},{10,2},{18... | collective-permute-start | bytes 16904 | tf_op jit(solution)/shard_map/ppermute | solution.py:449
  151.8 5.2 %collective-permute-start.1 = (s32[11,128]{1,0:T(8,128)S(1)}, s32[11,128]{1,0:T(8,128)S(1)}, u32[]{:S(2)}, u32[]{:S(2)}) collective-permute-start(s32[11,128]{1,0:T(8,128)S(1)} %pad_add_fusion.1), channel_id=1, source_target_pairs={{16,0},{24,8},{0,16},{8,24},{17,1},{25,9},{1,17},{9,25},{18,2},{26... | collective-permute-start | bytes 16904 | tf_op jit(solution)/shard_map/ppermute | solution.py:449
  152.3 4.7 %collective-permute-start.2 = (s32[11,128]{1,0:T(8,128)S(1)}, s32[11,128]{1,0:T(8,128)S(1)}, u32[]{:S(2)}, u32[]{:S(2)}) collective-permute-start(s32[11,128]{1,0:T(8,128)S(1)} %pad_add_fusion.1), channel_id=1, source_target_pairs={{24,0},{0,8},{8,16},{16,24},{25,1},{1,9},{9,17},{17,25},{26,2},{2,... | collective-permute-start | bytes 16904 | tf_op jit(solution)/shard_map/ppermute | solution.py:449
  152.9 4.8 %collective-permute-start.3 = (bf16[128,256]{1,0:T(8,128)(2,1)S(1)}, bf16[128,256]{1,0:T(8,128)(2,1)S(1)}, u32[]{:S(2)}, u32[]{:S(2)}) collective-permute-start(bf16[128,256]{1,0:T(8,128)(2,1)S(1)} %bitcast.186), channel_id=1, source_target_pairs={{8,0},{16,8},{24,16},{0,24},{9,1},{17,9},{25,17},{1,25},{10,2},{18... | collective-permute-start | bytes 196616 | tf_op jit(solution)/shard_map/ppermute | solution.py:449
  155.2 4.3 %collective-permute-start.4 = (bf16[128,256]{1,0:T(8,128)(2,1)S(1)}, bf16[128,256]{1,0:T(8,128)(2,1)S(1)}, u32[]{:S(2)}, u32[]{:S(2)}) collective-permute-start(bf16[128,256]{1,0:T(8,128)(2,1)S(1)} %bitcast.187), channel_id=1, source_target_pairs={{16,0},{24,8},{0,16},{8,24},{17,1},{25,9},{1,17},{9,25},{18,2},{26... | collective-permute-start | bytes 196616 | tf_op jit(solution)/shard_map/ppermute | solution.py:449
  156.9 5.2 %collective-permute-start.5 = (bf16[128,256]{1,0:T(8,128)(2,1)S(1)}, bf16[128,256]{1,0:T(8,128)(2,1)S(1)}, u32[]{:S(2)}, u32[]{:S(2)}) collective-permute-start(bf16[128,256]{1,0:T(8,128)(2,1)S(1)} %bitcast.189), channel_id=1, source_target_pairs={{24,0},{0,8},{8,16},{16,24},{25,1},{1,9},{9,17},{17,25},{26,2},{2,... | collective-permute-start | bytes 196616 | tf_op jit(solution)/shard_map/ppermute | solution.py:449
  187.3 17.6 %collective-permute-start.8 = (bf16[768,256]{1,0:T(8,128)(2,1)S(1)}, bf16[768,256]{1,0:T(8,128)(2,1)S(1)}, u32[]{:S(2)}, u32[]{:S(2)}) collective-permute-start(bf16[768,256]{1,0:T(8,128)(2,1)S(1)} %get-tuple-element.62), channel_id=1, source_target_pairs={{8,0},{16,8},{24,16},{0,24},{9,1},{17,9},{25,17},{1,25},{10,2},{18... | collective-permute-start | bytes 1179656 | tf_op jit(solution)/shard_map/ppermute | solution.py:449
  189.8 18.7 %collective-permute-start.7 = (bf16[768,256]{1,0:T(8,128)(2,1)S(1)}, bf16[768,256]{1,0:T(8,128)(2,1)S(1)}, u32[]{:S(2)}, u32[]{:S(2)}) collective-permute-start(bf16[768,256]{1,0:T(8,128)(2,1)S(1)} %get-tuple-element.61), channel_id=1, source_target_pairs={{16,0},{24,8},{0,16},{8,24},{17,1},{25,9},{1,17},{9,25},{18,2},{26... | collective-permute-start | bytes 1179656 | tf_op jit(solution)/shard_map/ppermute | solution.py:449
  196.2 12.3 %collective-permute-start.6 = (bf16[768,256]{1,0:T(8,128)(2,1)S(1)}, bf16[768,256]{1,0:T(8,128)(2,1)S(1)}, u32[]{:S(2)}, u32[]{:S(2)}) collective-permute-start(bf16[768,256]{1,0:T(8,128)(2,1)S(1)} %get-tuple-element.60), channel_id=1, source_target_pairs={{24,0},{0,8},{8,16},{16,24},{25,1},{1,9},{9,17},{17,25},{26,2},{2,... | collective-permute-start | bytes 1179656 | tf_op jit(solution)/shard_map/ppermute | solution.py:449
  209.3 11.4 %collective-permute-start.11 = (bf16[640,256]{1,0:T(8,128)(2,1)S(1)}, bf16[640,256]{1,0:T(8,128)(2,1)S(1)}, u32[]{:S(2)}, u32[]{:S(2)}) collective-permute-start(bf16[640,256]{1,0:T(8,128)(2,1)S(1)} %pad_maximum_fusion.2), channel_id=1, source_target_pairs={{24,0},{0,8},{8,16},{16,24},{25,1},{1,9},{9,17},{17,25},{26,2},{2,... | collective-permute-start | bytes 983048 | tf_op jit(solution)/shard_map/ppermute | solution.py:449
  209.6 14.4 %collective-permute-start.10 = (bf16[640,256]{1,0:T(8,128)(2,1)S(1)}, bf16[640,256]{1,0:T(8,128)(2,1)S(1)}, u32[]{:S(2)}, u32[]{:S(2)}) collective-permute-start(bf16[640,256]{1,0:T(8,128)(2,1)S(1)} %pad_maximum_fusion.2), channel_id=1, source_target_pairs={{16,0},{24,8},{0,16},{8,24},{17,1},{25,9},{1,17},{9,25},{18,2},{26... | collective-permute-start | bytes 983048 | tf_op jit(solution)/shard_map/ppermute | solution.py:449
  210.4 13.6 %collective-permute-start.9 = (bf16[640,256]{1,0:T(8,128)(2,1)S(1)}, bf16[640,256]{1,0:T(8,128)(2,1)S(1)}, u32[]{:S(2)}, u32[]{:S(2)}) collective-permute-start(bf16[640,256]{1,0:T(8,128)(2,1)S(1)} %pad_maximum_fusion.2), channel_id=1, source_target_pairs={{8,0},{16,8},{24,16},{0,24},{9,1},{17,9},{25,17},{1,25},{10,2},{18... | collective-permute-start | bytes 983048 | tf_op jit(solution)/shard_map/ppermute | solution.py:449
  226.6 12.0 %collective-permute-start.14 = (bf16[768,256]{1,0:T(8,128)(2,1)S(1)}, bf16[768,256]{1,0:T(8,128)(2,1)S(1)}, u32[]{:S(2)}, u32[]{:S(2)}) collective-permute-start(bf16[768,256]{1,0:T(8,128)(2,1)S(1)} %fusion.2), channel_id=1, source_target_pairs={{8,0},{16,8},{24,16},{0,24},{9,1},{17,9},{25,17},{1,25},{10,2},{18... | collective-permute-start | bytes 1179656 | tf_op jit(solution)/shard_map/ppermute | solution.py:449
  228.9 9.4 %collective-permute-start.12 = (bf16[768,256]{1,0:T(8,128)(2,1)S(1)}, bf16[768,256]{1,0:T(8,128)(2,1)S(1)}, u32[]{:S(2)}, u32[]{:S(2)}) collective-permute-start(bf16[768,256]{1,0:T(8,128)(2,1)S(1)} %fusion.2), channel_id=1, source_target_pairs={{16,0},{24,8},{0,16},{8,24},{17,1},{25,9},{1,17},{9,25},{18,2},{26... | collective-permute-start | bytes 1179656 | tf_op jit(solution)/shard_map/ppermute | solution.py:449
  229.8 16.7 %collective-permute-start.13 = (bf16[768,256]{1,0:T(8,128)(2,1)S(1)}, bf16[768,256]{1,0:T(8,128)(2,1)S(1)}, u32[]{:S(2)}, u32[]{:S(2)}) collective-permute-start(bf16[768,256]{1,0:T(8,128)(2,1)S(1)} %fusion.2), channel_id=1, source_target_pairs={{24,0},{0,8},{8,16},{16,24},{25,1},{1,9},{9,17},{17,25},{26,2},{2,... | collective-permute-start | bytes 1179656 | tf_op jit(solution)/shard_map/ppermute | solution.py:449
  249.6 4.9 %collective-permute-start.18 = (bf16[128,256]{1,0:T(8,128)(2,1)S(1)}, bf16[128,256]{1,0:T(8,128)(2,1)S(1)}, u32[]{:S(2)}, u32[]{:S(2)}) collective-permute-start(bf16[128,256]{1,0:T(8,128)(2,1)S(1)} %get-tuple-element.80), channel_id=1, source_target_pairs={{2,0},{3,1},{4,2},{5,3},{6,4},{7,5},{0,6},{1,7},{10,8},{11,9},{12,... | collective-permute-start | bytes 196616 | tf_op jit(solution)/shard_map/ppermute | solution.py:449
  252.0 7.4 %collective-permute-start.17 = (bf16[128,256]{1,0:T(8,128)(2,1)S(1)}, bf16[128,256]{1,0:T(8,128)(2,1)S(1)}, u32[]{:S(2)}, u32[]{:S(2)}) collective-permute-start(bf16[128,256]{1,0:T(8,128)(2,1)S(1)} %get-tuple-element.81), channel_id=1, source_target_pairs={{4,0},{5,1},{6,2},{7,3},{0,4},{1,5},{2,6},{3,7},{12,8},{13,9},{14,... | collective-permute-start | bytes 196616 | tf_op jit(solution)/shard_map/ppermute | solution.py:449
  253.0 6.5 %collective-permute-start.16 = (bf16[128,256]{1,0:T(8,128)(2,1)S(1)}, bf16[128,256]{1,0:T(8,128)(2,1)S(1)}, u32[]{:S(2)}, u32[]{:S(2)}) collective-permute-start(bf16[128,256]{1,0:T(8,128)(2,1)S(1)} %get-tuple-element.79), channel_id=1, source_target_pairs={{6,0},{7,1},{0,2},{1,3},{2,4},{3,5},{4,6},{5,7},{14,8},{15,9},{8,1... | collective-permute-start | bytes 196616 | tf_op jit(solution)/shard_map/ppermute | solution.py:449
  259.5 6.3 %collective-permute-start.21 = (bf16[128,256]{1,0:T(8,128)(2,1)S(1)}, bf16[128,256]{1,0:T(8,128)(2,1)S(1)}, u32[]{:S(2)}, u32[]{:S(2)}) collective-permute-start(bf16[128,256]{1,0:T(8,128)(2,1)S(1)} %fusion.16), channel_id=1, source_target_pairs={{6,0},{7,1},{0,2},{1,3},{2,4},{3,5},{4,6},{5,7},{14,8},{15,9},{8,1... | collective-permute-start | bytes 196616 | tf_op jit(solution)/shard_map/ppermute | solution.py:449
  259.6 7.5 %collective-permute-start.20 = (bf16[128,256]{1,0:T(8,128)(2,1)S(1)}, bf16[128,256]{1,0:T(8,128)(2,1)S(1)}, u32[]{:S(2)}, u32[]{:S(2)}) collective-permute-start(bf16[128,256]{1,0:T(8,128)(2,1)S(1)} %fusion.16), channel_id=1, source_target_pairs={{4,0},{5,1},{6,2},{7,3},{0,4},{1,5},{2,6},{3,7},{12,8},{13,9},{14,... | collective-permute-start | bytes 196616 | tf_op jit(solution)/shard_map/ppermute | solution.py:449
  261.3 5.7 %collective-permute-start.19 = (bf16[128,256]{1,0:T(8,128)(2,1)S(1)}, bf16[128,256]{1,0:T(8,128)(2,1)S(1)}, u32[]{:S(2)}, u32[]{:S(2)}) collective-permute-start(bf16[128,256]{1,0:T(8,128)(2,1)S(1)} %fusion.16), channel_id=1, source_target_pairs={{2,0},{3,1},{4,2},{5,3},{6,4},{7,5},{0,6},{1,7},{10,8},{11,9},{12,... | collective-permute-start | bytes 196616 | tf_op jit(solution)/shard_map/ppermute | solution.py:449
  (20 other events, 565.4 us)
